TPU v7x, 32 devices: a whole 2x2x4 slice. The times are simulated.
32 devices in a mesh: grp: 4 (over x, core), wide: 8 (over z, y).
Axes of the slice: x: 2, y: 2, z: 4, core: 2. Of those that a mesh axis runs over, the one named last changes fastest.
Arguments:
- amplitudes: float32 [1024, 64, 512], P(('grp', 'wide')), may hold values from -6 to 6
- integrals: float32 [4, 512, 512], P('grp'), may hold values from -0.25 to 0.25
- base_residual: float32 [32, 64, 512], P(('grp', 'wide')), may hold values from -6 to 6
- occ_gap: float32 [32, 64], P(('grp', 'wide')), may hold values from 0.5 to 4
- virt_sum: float32 [512], replicated, may hold values from 0.5 to 4
- task_amp: int32 [32, 96], P(('grp', 'wide')), may hold values from 0 to 255, as said below
- task_int: int32 [32, 96], P(('grp', 'wide')), may hold values from 0 to 3
- task_res: int32 [32, 96], P(('grp', 'wide')), may hold values from 0 to 7, as said below
- task_count: int32 [32], P(('grp', 'wide')), may hold values from 12 to 96, as said below
- res_owner: int32 [4, 8], P('grp'), may hold values from 0 to 7, as said below
- amp_label: int32 [1024], P(('grp', 'wide')), may hold values from 0 to 3
- int_label: int32 [4], replicated, may hold values from 0 to 3
Outputs:
- doubles_residual: float32 [32, 64, 512], P(('grp', 'wide'))
Inputs may be any that keep to these rules, and one draw needn't show every extreme that they name: `task_amp`: amplitude block t of a grp row is kept by the device of wide index t // 32 of that row, at its local position t % 32. Among the used slots of one device at most 12 name blocks kept by one device. `task_res`: among the used slots of one device at most 12 name tiles whose position (see res_owner) lies on one device. Slots from task_count on are unused; their entries are arbitrary values within the stated ranges. `res_owner`: each row is a permutation; position p of a grp row lies on the device of wide index p, at its local position p % 1.
All inputs are finite; a program needn't handle non-finite values.
Results may differ from a plain program's by a relative error of at most 0.0001.
Values sent between devices are 32-bit elements; how exact they have to be, the bound alone decides.
No kernel may reach another device: no remote copies, remote signals or barrier semaphores. Data moves between devices by JAX's collectives and lax.ppermute only.
A program may use at most 128 MiB of HBM per device.

v0:
```python
import jax
import jax.numpy as jnp
from jax import lax
from jax.sharding import PartitionSpec as P


def bucket_ranks(holder, usable, lane_count):
    owner_hits = ((holder[:, None] == jnp.arange(lane_count)[None, :]) & usable[:, None]).astype(
        jnp.int32
    )
    before = jnp.cumsum(owner_hits, axis=0) - owner_hits
    return jnp.sum(before * owner_hits, axis=1)


def run_tasks(tile_source, tile_index, all_integrals, int_ids, signs, slot_count):
    slot_index = jnp.arange(slot_count, dtype=jnp.int32)

    def block_product(task_block):
        tiles_here = jnp.take(tile_source, tile_index[task_block], axis=0)
        weights_here = jnp.take(all_integrals, int_ids[task_block], axis=0)
        product = jnp.einsum(
            "kij,kjl->kil", tiles_here, weights_here, precision=lax.Precision.HIGHEST
        )
        return product * signs[task_block][:, None, None]

    result = lax.map(block_product, slot_index.reshape(-1, 8))
    return result.reshape(slot_count, result.shape[2], result.shape[3])


def owner_image(contribution, res_pos, usable, positions):
    slot_count = contribution.shape[0]
    tile_hits = ((res_pos[:, None] == jnp.arange(positions)[None, :]) & usable[:, None]).astype(
        jnp.float32
    )
    return jnp.einsum(
        "sp,sx->px",
        tile_hits,
        contribution.reshape(slot_count, -1),
        precision=lax.Precision.HIGHEST,
    )


def on_device(
    amplitudes,
    integrals,
    base_residual,
    occ_gap,
    virt_sum,
    task_amp,
    task_int,
    task_res,
    task_count,
    res_owner,
    amp_label,
    int_label,
):
    lane_count = lax.axis_size("wide")
    amp_dev = amplitudes.shape[0]
    res_dev = base_residual.shape[0]
    tile_rows = amplitudes.shape[1]
    window = base_residual.shape[2]
    slot_count = task_amp.shape[1]
    bucket = slot_count // lane_count
    all_integrals = lax.all_gather(integrals, "grp", axis=0, tiled=True)
    slot_index = jnp.arange(slot_count, dtype=jnp.int32)
    where_kept = jnp.argsort(res_owner[0])
    lists_amp, lists_int, lists_res, lists_count = (
        lax.all_gather(task_amp, "wide", axis=0, tiled=True),
        lax.all_gather(task_int, "wide", axis=0, tiled=True),
        lax.all_gather(task_res, "wide", axis=0, tiled=True),
        lax.all_gather(task_count, "wide", axis=0, tiled=True),
    )
    own_lane = lax.axis_index("wide")

    def pick(list_amp, list_count):
        list_usable = slot_index < list_count
        list_holder = list_amp // amp_dev
        list_rank = bucket_ranks(list_holder, list_usable, lane_count)
        mine = list_usable & (list_holder == own_lane)
        return (jnp.where(mine, list_rank, bucket), mine)

    local_rank, mine = jax.vmap(pick)(lists_amp, lists_count)
    lane_ids = jnp.arange(lane_count, dtype=jnp.int32)
    target = jnp.where(mine, lane_ids[:, None] * bucket + local_rank, lane_count * bucket).reshape(
        -1
    )
    kept_amp = (
        jnp.zeros((slot_count,), jnp.int32)
        .at[target]
        .set((lists_amp % amp_dev).reshape(-1), mode="drop")
    )
    kept_int = (
        jnp.zeros((slot_count,), jnp.int32).at[target].set(lists_int.reshape(-1), mode="drop")
    )
    kept_res = (
        jnp.zeros((slot_count,), jnp.int32)
        .at[target]
        .set(jnp.take(where_kept, lists_res.reshape(-1), axis=0), mode="drop")
    )
    kept_used = jnp.zeros((slot_count,), jnp.bool_).at[target].set(True, mode="drop")
    parity = (jnp.take(amp_label, kept_amp, axis=0) + jnp.take(int_label, kept_int, axis=0)) % 2
    signs = jnp.where(kept_used, 1.0 - 2.0 * parity.astype(jnp.float32), 0.0)
    contribution = run_tasks(amplitudes, kept_amp, all_integrals, kept_int, signs, slot_count)
    image = owner_image(contribution, kept_res, kept_used, lane_count * res_dev)
    arrived = lax.all_to_all(
        image.reshape(lane_count, res_dev, tile_rows, window),
        "wide",
        split_axis=0,
        concat_axis=0,
        tiled=True,
    )
    summed = jnp.sum(arrived, axis=0)
    divisor = occ_gap[:, :, None] + virt_sum[None, None, :]
    return (base_residual + summed) / divisor


def solution(mesh):
    return jax.shard_map(
        on_device,
        mesh=mesh,
        in_specs=(
            P(("grp", "wide"), None, None),
            P("grp", None, None),
            P(("grp", "wide"), None, None),
            P(("grp", "wide"), None),
            P(),
            P(("grp", "wide"), None),
            P(("grp", "wide"), None),
            P(("grp", "wide"), None),
            P(("grp", "wide")),
            P("grp", None),
            P(("grp", "wide")),
            P(),
        ),
        out_specs=P(("grp", "wide"), None, None),
        check_vma=False,
    )
```

profile of v0, /device:TPU:0, one launch (start us, length us, event | category | flops | bytes accessed | tf_op | source)
XLA Modules:
  0.0 392.2 jit_solution(10716480026393786675)
XLA Ops:
  10.0 13.1 %all-reduce = s32[8]{0:T(128)S(1)} all-reduce(s32[8]{0:T(128)S(1)} %dynamic-update-slice), channel_id=1, replica_groups=mesh['grp'=4,'wide'=8] {'wide'}, use_global_device_ids=true, to_apply=%add | all-reduce | flops 8 | bytes 64
  23.1 17.8 %all-gather.1 = s32[8,1,96]{2,1,0:T(1,128)S(1)} all-gather(s32[1,1,96]{2,1,0:T(1,128)} %bitcast.102), channel_id=1, replica_groups=mesh['grp'=4,'wide'=8] {'wide'}, dimensions={0}, use_global_device_ids=true | all-gather | bytes 3456 | tf_op jit(solution)/shard_map/all_gather | solution.py:70
  42.2 16.8 %all-gather.2 = s32[8,1,96]{2,1,0:T(1,128)S(1)} all-gather(s32[1,1,96]{2,1,0:T(1,128)} %bitcast.103), channel_id=1, replica_groups=mesh['grp'=4,'wide'=8] {'wide'}, dimensions={0}, use_global_device_ids=true | all-gather | bytes 3456 | tf_op jit(solution)/shard_map/all_gather | solution.py:69
  59.7 17.8 %all-gather = s32[8,1,96]{2,1,0:T(1,128)S(1)} all-gather(s32[1,1,96]{2,1,0:T(1,128)} %bitcast.104), channel_id=1, replica_groups=mesh['grp'=4,'wide'=8] {'wide'}, dimensions={0}, use_global_device_ids=true | all-gather | bytes 3456 | tf_op jit(solution)/shard_map/all_gather | solution.py:68
  80.2 3.4 scatter_custom_fusion.2
  83.6 3.4 scatter_custom_fusion.3
  89.3 4.5 %fusion.41 = s32[768]{0:T(1024)S(1)} fusion(s32[]{:T(128)} %bitcast.13, s32[]{:T(128)} %bitcast.14, s32[]{:T(128)} %bitcast.15, s32[]{:T(128)} %bitcast.16, s32[]{:T(128)} %bitcast.17, s32[]{:T(128)} %bitcast.19, s32[]{:T(128)} %bitcast.18, s32[768,1]{0,1:T(1,128)S(1)} %reshape.251), kind=kLoop, calls=%fused_computation.76 | loop fusion | flops 11520 | bytes 6172 | tf_op jit(solution)/shard_map/jit(_take)/gather | solution.py:98
  94.4 3.4 scatter_custom_fusion
  97.8 3.6 scatter_custom_fusion.1
  106.8 243.2 %while.10 = (s32[]{:T(128)}, f32[12,8,64,512]{3,2,1,0:T(8,128)}, s32[12,8]{1,0:T(8,128)S(1)}, s32[96]{0:T(128)S(1)}, f32[32,64,512]{2,1,0:T(8,128)}, /*index=5*/...) while((s32[]{:T(128)}, f32[12,8,64,512]{3,2,1,0:T(8,128)}, s32[12,8]{1,0:T(8,128)S(1)}, ...), condition=%wide.region_8.9_spmd, body=%wide.region_7.8_spmd.sunk | while | flops 1613237376 | bytes 29373292 | solution.py:26
  108.8 2.8 gather_fusion.3
  111.6 6.5 %gather_fusion.2 = f32[8,512,512]{2,1,0:T(8,128)} fusion(f32[4,512,512]{2,1,0:T(8,128)} %get-tuple-element.165, s32[1024]{0:T(1024)S(1)} %pad_clamp_fusion.8), kind=kCustom, calls=%fused_computation.3.clone.1 | custom fusion | bytes 16777248 | tf_op jit(solution)/shard_map/while/body/eval_jaxpr/jit(_take)/gather | solution.py:20
  118.1 9.0 %fusion.70 = f32[12,8,64,512]{3,2,1,0:T(8,128)} fusion(f32[12,8,64,512]{3,2,1,0:T(8,128)} %get-tuple-element.151, s32[]{:T(128)S(6)} %copy.41, f32[8,512,512]{2,1,0:T(8,128)} %gather_fusion.2, pred[8]{0:T(512)(128)(4,1)S(1)} %get-tuple-element.138, f32[8,64,512]{2,1,0:T(8,128)S(1)} %gather_fusion.3, f32[8]{0:T(128)S(1)} %gather_fusion.4, ...), kind=kOutput, calls=%fused_computation.16.clone.1 | convolution fusion | flops 1613234176 | bytes 10485812 | tf_op jit(solution)/shard_map/while/body/eval_jaxpr/kij,kjl->kil/dot_general | solution.py:21
  129.1 2.8 gather_fusion.3
  131.9 6.5 %gather_fusion.2 = f32[8,512,512]{2,1,0:T(8,128)} fusion(f32[4,512,512]{2,1,0:T(8,128)} %get-tuple-element.165, s32[1024]{0:T(1024)S(1)} %pad_clamp_fusion.8), kind=kCustom, calls=%fused_computation.3.clone.1 | custom fusion | bytes 16777248 | tf_op jit(solution)/shard_map/while/body/eval_jaxpr/jit(_take)/gather | solution.py:20
  138.4 9.0 %fusion.70 = f32[12,8,64,512]{3,2,1,0:T(8,128)} fusion(f32[12,8,64,512]{3,2,1,0:T(8,128)} %get-tuple-element.151, s32[]{:T(128)S(6)} %copy.41, f32[8,512,512]{2,1,0:T(8,128)} %gather_fusion.2, pred[8]{0:T(512)(128)(4,1)S(1)} %get-tuple-element.138, f32[8,64,512]{2,1,0:T(8,128)S(1)} %gather_fusion.3, f32[8]{0:T(128)S(1)} %gather_fusion.4, ...), kind=kOutput, calls=%fused_computation.16.clone.1 | convolution fusion | flops 1613234176 | bytes 10485812 | tf_op jit(solution)/shard_map/while/body/eval_jaxpr/kij,kjl->kil/dot_general | solution.py:21
  149.4 2.8 gather_fusion.3
  152.2 6.5 %gather_fusion.2 = f32[8,512,512]{2,1,0:T(8,128)} fusion(f32[4,512,512]{2,1,0:T(8,128)} %get-tuple-element.165, s32[1024]{0:T(1024)S(1)} %pad_clamp_fusion.8), kind=kCustom, calls=%fused_computation.3.clone.1 | custom fusion | bytes 16777248 | tf_op jit(solution)/shard_map/while/body/eval_jaxpr/jit(_take)/gather | solution.py:20
  158.7 9.0 %fusion.70 = f32[12,8,64,512]{3,2,1,0:T(8,128)} fusion(f32[12,8,64,512]{3,2,1,0:T(8,128)} %get-tuple-element.151, s32[]{:T(128)S(6)} %copy.41, f32[8,512,512]{2,1,0:T(8,128)} %gather_fusion.2, pred[8]{0:T(512)(128)(4,1)S(1)} %get-tuple-element.138, f32[8,64,512]{2,1,0:T(8,128)S(1)} %gather_fusion.3, f32[8]{0:T(128)S(1)} %gather_fusion.4, ...), kind=kOutput, calls=%fused_computation.16.clone.1 | convolution fusion | flops 1613234176 | bytes 10485812 | tf_op jit(solution)/shard_map/while/body/eval_jaxpr/kij,kjl->kil/dot_general | solution.py:21
  169.6 2.8 gather_fusion.3
  172.5 6.5 %gather_fusion.2 = f32[8,512,512]{2,1,0:T(8,128)} fusion(f32[4,512,512]{2,1,0:T(8,128)} %get-tuple-element.165, s32[1024]{0:T(1024)S(1)} %pad_clamp_fusion.8), kind=kCustom, calls=%fused_computation.3.clone.1 | custom fusion | bytes 16777248 | tf_op jit(solution)/shard_map/while/body/eval_jaxpr/jit(_take)/gather | solution.py:20
  178.9 9.0 %fusion.70 = f32[12,8,64,512]{3,2,1,0:T(8,128)} fusion(f32[12,8,64,512]{3,2,1,0:T(8,128)} %get-tuple-element.151, s32[]{:T(128)S(6)} %copy.41, f32[8,512,512]{2,1,0:T(8,128)} %gather_fusion.2, pred[8]{0:T(512)(128)(4,1)S(1)} %get-tuple-element.138, f32[8,64,512]{2,1,0:T(8,128)S(1)} %gather_fusion.3, f32[8]{0:T(128)S(1)} %gather_fusion.4, ...), kind=kOutput, calls=%fused_computation.16.clone.1 | convolution fusion | flops 1613234176 | bytes 10485812 | tf_op jit(solution)/shard_map/while/body/eval_jaxpr/kij,kjl->kil/dot_general | solution.py:21
  189.9 2.8 gather_fusion.3
  192.7 6.5 %gather_fusion.2 = f32[8,512,512]{2,1,0:T(8,128)} fusion(f32[4,512,512]{2,1,0:T(8,128)} %get-tuple-element.165, s32[1024]{0:T(1024)S(1)} %pad_clamp_fusion.8), kind=kCustom, calls=%fused_computation.3.clone.1 | custom fusion | bytes 16777248 | tf_op jit(solution)/shard_map/while/body/eval_jaxpr/jit(_take)/gather | solution.py:20
  199.2 9.0 %fusion.70 = f32[12,8,64,512]{3,2,1,0:T(8,128)} fusion(f32[12,8,64,512]{3,2,1,0:T(8,128)} %get-tuple-element.151, s32[]{:T(128)S(6)} %copy.41, f32[8,512,512]{2,1,0:T(8,128)} %gather_fusion.2, pred[8]{0:T(512)(128)(4,1)S(1)} %get-tuple-element.138, f32[8,64,512]{2,1,0:T(8,128)S(1)} %gather_fusion.3, f32[8]{0:T(128)S(1)} %gather_fusion.4, ...), kind=kOutput, calls=%fused_computation.16.clone.1 | convolution fusion | flops 1613234176 | bytes 10485812 | tf_op jit(solution)/shard_map/while/body/eval_jaxpr/kij,kjl->kil/dot_general | solution.py:21
  210.1 2.8 gather_fusion.3
  213.0 6.5 %gather_fusion.2 = f32[8,512,512]{2,1,0:T(8,128)} fusion(f32[4,512,512]{2,1,0:T(8,128)} %get-tuple-element.165, s32[1024]{0:T(1024)S(1)} %pad_clamp_fusion.8), kind=kCustom, calls=%fused_computation.3.clone.1 | custom fusion | bytes 16777248 | tf_op jit(solution)/shard_map/while/body/eval_jaxpr/jit(_take)/gather | solution.py:20
  219.4 9.0 %fusion.70 = f32[12,8,64,512]{3,2,1,0:T(8,128)} fusion(f32[12,8,64,512]{3,2,1,0:T(8,128)} %get-tuple-element.151, s32[]{:T(128)S(6)} %copy.41, f32[8,512,512]{2,1,0:T(8,128)} %gather_fusion.2, pred[8]{0:T(512)(128)(4,1)S(1)} %get-tuple-element.138, f32[8,64,512]{2,1,0:T(8,128)S(1)} %gather_fusion.3, f32[8]{0:T(128)S(1)} %gather_fusion.4, ...), kind=kOutput, calls=%fused_computation.16.clone.1 | convolution fusion | flops 1613234176 | bytes 10485812 | tf_op jit(solution)/shard_map/while/body/eval_jaxpr/kij,kjl->kil/dot_general | solution.py:21
  230.4 2.8 gather_fusion.3
  233.2 6.5 %gather_fusion.2 = f32[8,512,512]{2,1,0:T(8,128)} fusion(f32[4,512,512]{2,1,0:T(8,128)} %get-tuple-element.165, s32[1024]{0:T(1024)S(1)} %pad_clamp_fusion.8), kind=kCustom, calls=%fused_computation.3.clone.1 | custom fusion | bytes 16777248 | tf_op jit(solution)/shard_map/while/body/eval_jaxpr/jit(_take)/gather | solution.py:20
  239.7 9.0 %fusion.70 = f32[12,8,64,512]{3,2,1,0:T(8,128)} fusion(f32[12,8,64,512]{3,2,1,0:T(8,128)} %get-tuple-element.151, s32[]{:T(128)S(6)} %copy.41, f32[8,512,512]{2,1,0:T(8,128)} %gather_fusion.2, pred[8]{0:T(512)(128)(4,1)S(1)} %get-tuple-element.138, f32[8,64,512]{2,1,0:T(8,128)S(1)} %gather_fusion.3, f32[8]{0:T(128)S(1)} %gather_fusion.4, ...), kind=kOutput, calls=%fused_computation.16.clone.1 | convolution fusion | flops 1613234176 | bytes 10485812 | tf_op jit(solution)/shard_map/while/body/eval_jaxpr/kij,kjl->kil/dot_general | solution.py:21
  250.7 2.8 gather_fusion.3
  253.5 6.5 %gather_fusion.2 = f32[8,512,512]{2,1,0:T(8,128)} fusion(f32[4,512,512]{2,1,0:T(8,128)} %get-tuple-element.165, s32[1024]{0:T(1024)S(1)} %pad_clamp_fusion.8), kind=kCustom, calls=%fused_computation.3.clone.1 | custom fusion | bytes 16777248 | tf_op jit(solution)/shard_map/while/body/eval_jaxpr/jit(_take)/gather | solution.py:20
  260.0 9.0 %fusion.70 = f32[12,8,64,512]{3,2,1,0:T(8,128)} fusion(f32[12,8,64,512]{3,2,1,0:T(8,128)} %get-tuple-element.151, s32[]{:T(128)S(6)} %copy.41, f32[8,512,512]{2,1,0:T(8,128)} %gather_fusion.2, pred[8]{0:T(512)(128)(4,1)S(1)} %get-tuple-element.138, f32[8,64,512]{2,1,0:T(8,128)S(1)} %gather_fusion.3, f32[8]{0:T(128)S(1)} %gather_fusion.4, ...), kind=kOutput, calls=%fused_computation.16.clone.1 | convolution fusion | flops 1613234176 | bytes 10485812 | tf_op jit(solution)/shard_map/while/body/eval_jaxpr/kij,kjl->kil/dot_general | solution.py:21
  271.0 2.8 gather_fusion.3
  273.8 6.5 %gather_fusion.2 = f32[8,512,512]{2,1,0:T(8,128)} fusion(f32[4,512,512]{2,1,0:T(8,128)} %get-tuple-element.165, s32[1024]{0:T(1024)S(1)} %pad_clamp_fusion.8), kind=kCustom, calls=%fused_computation.3.clone.1 | custom fusion | bytes 16777248 | tf_op jit(solution)/shard_map/while/body/eval_jaxpr/jit(_take)/gather | solution.py:20
  280.2 9.0 %fusion.70 = f32[12,8,64,512]{3,2,1,0:T(8,128)} fusion(f32[12,8,64,512]{3,2,1,0:T(8,128)} %get-tuple-element.151, s32[]{:T(128)S(6)} %copy.41, f32[8,512,512]{2,1,0:T(8,128)} %gather_fusion.2, pred[8]{0:T(512)(128)(4,1)S(1)} %get-tuple-element.138, f32[8,64,512]{2,1,0:T(8,128)S(1)} %gather_fusion.3, f32[8]{0:T(128)S(1)} %gather_fusion.4, ...), kind=kOutput, calls=%fused_computation.16.clone.1 | convolution fusion | flops 1613234176 | bytes 10485812 | tf_op jit(solution)/shard_map/while/body/eval_jaxpr/kij,kjl->kil/dot_general | solution.py:21
  291.3 2.8 gather_fusion.3
  294.1 6.5 %gather_fusion.2 = f32[8,512,512]{2,1,0:T(8,128)} fusion(f32[4,512,512]{2,1,0:T(8,128)} %get-tuple-element.165, s32[1024]{0:T(1024)S(1)} %pad_clamp_fusion.8), kind=kCustom, calls=%fused_computation.3.clone.1 | custom fusion | bytes 16777248 | tf_op jit(solution)/shard_map/while/body/eval_jaxpr/jit(_take)/gather | solution.py:20
  300.6 9.0 %fusion.70 = f32[12,8,64,512]{3,2,1,0:T(8,128)} fusion(f32[12,8,64,512]{3,2,1,0:T(8,128)} %get-tuple-element.151, s32[]{:T(128)S(6)} %copy.41, f32[8,512,512]{2,1,0:T(8,128)} %gather_fusion.2, pred[8]{0:T(512)(128)(4,1)S(1)} %get-tuple-element.138, f32[8,64,512]{2,1,0:T(8,128)S(1)} %gather_fusion.3, f32[8]{0:T(128)S(1)} %gather_fusion.4, ...), kind=kOutput, calls=%fused_computation.16.clone.1 | convolution fusion | flops 1613234176 | bytes 10485812 | tf_op jit(solution)/shard_map/while/body/eval_jaxpr/kij,kjl->kil/dot_general | solution.py:21
  311.5 2.8 gather_fusion.3
  314.4 6.5 %gather_fusion.2 = f32[8,512,512]{2,1,0:T(8,128)} fusion(f32[4,512,512]{2,1,0:T(8,128)} %get-tuple-element.165, s32[1024]{0:T(1024)S(1)} %pad_clamp_fusion.8), kind=kCustom, calls=%fused_computation.3.clone.1 | custom fusion | bytes 16777248 | tf_op jit(solution)/shard_map/while/body/eval_jaxpr/jit(_take)/gather | solution.py:20
  320.8 9.0 %fusion.70 = f32[12,8,64,512]{3,2,1,0:T(8,128)} fusion(f32[12,8,64,512]{3,2,1,0:T(8,128)} %get-tuple-element.151, s32[]{:T(128)S(6)} %copy.41, f32[8,512,512]{2,1,0:T(8,128)} %gather_fusion.2, pred[8]{0:T(512)(128)(4,1)S(1)} %get-tuple-element.138, f32[8,64,512]{2,1,0:T(8,128)S(1)} %gather_fusion.3, f32[8]{0:T(128)S(1)} %gather_fusion.4, ...), kind=kOutput, calls=%fused_computation.16.clone.1 | convolution fusion | flops 1613234176 | bytes 10485812 | tf_op jit(solution)/shard_map/while/body/eval_jaxpr/kij,kjl->kil/dot_general | solution.py:21
  331.8 2.8 gather_fusion.3
  334.6 6.5 %gather_fusion.2 = f32[8,512,512]{2,1,0:T(8,128)} fusion(f32[4,512,512]{2,1,0:T(8,128)} %get-tuple-element.165, s32[1024]{0:T(1024)S(1)} %pad_clamp_fusion.8), kind=kCustom, calls=%fused_computation.3.clone.1 | custom fusion | bytes 16777248 | tf_op jit(solution)/shard_map/while/body/eval_jaxpr/jit(_take)/gather | solution.py:20
  341.1 8.9 %fusion.70 = f32[12,8,64,512]{3,2,1,0:T(8,128)} fusion(f32[12,8,64,512]{3,2,1,0:T(8,128)} %get-tuple-element.151, s32[]{:T(128)S(6)} %copy.41, f32[8,512,512]{2,1,0:T(8,128)} %gather_fusion.2, pred[8]{0:T(512)(128)(4,1)S(1)} %get-tuple-element.138, f32[8,64,512]{2,1,0:T(8,128)S(1)} %gather_fusion.3, f32[8]{0:T(128)S(1)} %gather_fusion.4, ...), kind=kOutput, calls=%fused_computation.16.clone.1 | convolution fusion | flops 1613234176 | bytes 10485812 | tf_op jit(solution)/shard_map/while/body/eval_jaxpr/kij,kjl->kil/dot_general | solution.py:21
  350.0 15.5 %fusion.23 = f32[8,1,64,512]{3,0,2,1:T(8,128)S(1)} fusion(s32[96]{0:T(128)S(1)} %scatter_custom_fusion, pred[96]{0:T(512)(128)(4,1)S(1)} %scatter_custom_fusion.1, f32[12,8,64,512]{3,2,1,0:T(8,128)} %get-tuple-element.49), kind=kOutput, calls=%fused_computation.37 | convolution fusion | flops 301991424 | bytes 13631968 | tf_op jit(solution)/shard_map/sp,sx->px/dot_general | solution.py:35
  366.1 18.4 %all_to_all.5 = f32[8,1,64,512]{3,2,1,0:T(8,128)S(1)} all-to-all(f32[8,1,64,512]{3,2,1,0:T(8,128)S(1)} %copy.25), channel_id=1, replica_groups=mesh['grp'=4,'wide'=8] {'wide'}, dimensions={0} | all-to-all | bytes 2097152 | tf_op jit(solution)/shard_map/all_to_all | solution.py:105
  (155 shorter events, 41.0 us)
Async XLA Ops:
  6.5 94.9 %copy-start = (s32[32]{0:T(128)S(1)}, s32[32]{0:T(128)}, u32[]{:S(2)}) copy-start(s32[32]{0:T(128)} %param.24) | copy-start | bytes 388
  6.5 100.2 %all-gather.5.cloned.1.call-start = ((), (), s32[]{:S(2)}) async-start(), calls=%async_computation.1 | async-start | bytes 5242880 | tf_op jit(solution)/shard_map/all_gather | solution.py:64
  350.0 34.6 %copy-start.1 = (f32[1,64,512]{2,1,0:T(8,128)S(1)}, f32[1,64,512]{2,1,0:T(8,128)}, u32[]{:S(2)}) copy-start(f32[1,64,512]{2,1,0:T(8,128)} %param.16) | copy-start | bytes 393220
  350.0 34.6 %copy-start.2 = (f32[512]{0:T(512)S(1)}, f32[512]{0:T(512)}, u32[]{:S(2)}) copy-start(f32[512]{0:T(512)} %param.18) | copy-start | bytes 6148
  350.0 34.6 %copy-start.3 = (f32[1,64]{1,0:T(1,128)S(1)}, f32[1,64]{1,0:T(1,128)}, u32[]{:S(2)}) copy-start(f32[1,64]{1,0:T(1,128)} %param.17) | copy-start | bytes 772
Sparse Core Ops, SparseCore 0:
  8.9 37.1 all-gather.4
where the time goes:
time: 393 us; the launch traced here: 392 us
  local copies, waits for them, and re-layouts  155 us (39%)
  matrix products  123 us (31%)
  blocking collectives  83.9 us (21%)
  other arithmetic  14.2 us (4%)
  between operations  14.2 us (4%)
    dot_general x12, matrix products, block_product(): jnp.einsum('kij,kjl->kil', tiles_here, weights_here, precision=lax.Precis...  108 us
    gather x24, local copies, waits for them, and re-layouts, block_product(): weights_here = jnp.take(all_integrals, int_ids[task_block], axis=0)  85.3 us
    gather x24, local copies, waits for them, and re-layouts, block_product(): tiles_here = jnp.take(tile_source, tile_index[task_block], axis=0)  41.4 us
    all_to_all x1, blocking collectives, on_device(): lax.all_to_all(image.reshape(lane_count, res_dev, tile_rows, window), 'wi...  18.4 us
    all_gather x1, blocking collectives, on_device(): lax.all_gather(task_amp, 'wide', axis=0, tiled=True)  17.8 us
    all_gather x1, blocking collectives, on_device(): lax.all_gather(task_res, 'wide', axis=0, tiled=True)  17.8 us
    all_gather x1, blocking collectives, on_device(): lax.all_gather(task_int, 'wide', axis=0, tiled=True)  16.8 us
    dot_general x1, matrix products, owner_image(): jnp.einsum('sp,sx->px', tile_hits, contribution.reshape(slot_count, -1),...  15.5 us
  transfers between devices with their start and end apart: 1, of which 0 were waited for; matrix products, arithmetic and copies ran while one was open for 8% of the time, Pallas kernels for 0%

commit v1 on v0

v1 whole, which is shorter than its diff:
```python
import functools

import jax
import jax.numpy as jnp
from jax import lax
from jax.experimental import pallas as pl
from jax.experimental.pallas import tpu as pltpu
from jax.sharding import PartitionSpec as P

LANES = 128


def split(x):
    hi = x.astype(jnp.bfloat16)
    return hi, (x - hi.astype(jnp.float32)).astype(jnp.bfloat16)


def swap(x, axis, k):
    n = lax.axis_size(axis)
    return lax.ppermute(x, axis, [(i, i ^ k) for i in range(n)])


def coefficients(lists_ref, amp_label_ref, owner_ref, int_label_ref, amp_dev, lanes, blocks):
    lane = lax.axis_index("wide")
    grp = lax.axis_index("grp")
    amp, cint, res, count = (lists_ref[i] for i in range(4))
    slot = lax.broadcasted_iota(jnp.int32, amp.shape, 1)
    local = amp - lane * amp_dev
    valid = (slot < count) & (local >= 0) & (local < amp_dev)
    pos = jnp.zeros_like(res)
    for p in range(lanes):
        pos = jnp.where(res == owner_ref[0, p], p, pos)
    seg = (pos ^ lane) * blocks + (cint ^ grp)
    seg = jnp.where(valid, seg, -1)
    rows = lanes * blocks
    row_id = lax.broadcasted_iota(jnp.int32, (rows, amp.shape[1]), 0)
    col_id = lax.broadcasted_iota(jnp.int32, (LANES, amp.shape[1]), 0)
    counts = jnp.zeros((rows, LANES), jnp.float32)
    for src in range(lanes):
        hit_row = jnp.where(row_id == seg[src : src + 1, :], 1.0, 0.0)
        hit_col = jnp.where(col_id == local[src : src + 1, :], 1.0, 0.0)
        counts += lax.dot_general(
            hit_row.astype(jnp.bfloat16),
            hit_col.astype(jnp.bfloat16),
            (((1,), (1,)), ((), ())),
            preferred_element_type=jnp.float32,
        )
    row = lax.broadcasted_iota(jnp.int32, (rows, LANES), 0)
    label = jnp.zeros((rows, LANES), jnp.int32)
    for c in range(blocks):
        label = jnp.where((row & (blocks - 1)) == c, int_label_ref[c ^ grp], label)
    odd = (label + amp_label_ref[...]) & 1
    weight = jnp.where(odd == 1, -counts, counts)
    col = lax.broadcasted_iota(jnp.int32, (rows, LANES), 1)
    follow = jnp.where(counts > 0.5, col, LANES)
    step = 1
    while step < amp_dev:
        follow = jnp.minimum(follow, pltpu.roll(follow, LANES - step, 1))
        step *= 2
    return weight, follow


def product_kernel(
    lanes,
    blocks,
    owner_ref,
    int_label_ref,
    lists_ref,
    amp_label_ref,
    amp_ref,
    *rest,
):
    int_refs = rest[:blocks]
    out_ref, weight_v, follow_v, weight_s, follow_s, st_hi, st_lo, in_hi, in_lo, sems = rest[blocks:]
    amp_dev, tile_rows, depth = amp_ref.shape
    weight, follow = coefficients(
        lists_ref, amp_label_ref, owner_ref, int_label_ref, amp_dev, lanes, blocks
    )
    weight_v[...] = weight
    follow_v[...] = follow
    one = pltpu.make_async_copy(weight_v, weight_s, sems.at[0])
    two = pltpu.make_async_copy(follow_v, follow_s, sems.at[1])
    one.start()
    two.start()
    for c in range(blocks):
        hi, lo = split(int_refs[c][...])
        in_hi[c] = hi
        in_lo[c] = lo
    one.wait()
    two.wait()

    def stack(s, _):
        def more(carry):
            return carry[0] < amp_dev

        def add(carry):
            a, total = carry
            return follow_s[s, a + 1], total + weight_s[s, a] * amp_ref[a]

        _, total = lax.while_loop(
            more, add, (follow_s[s, 0], jnp.zeros((tile_rows, depth), jnp.float32))
        )
        hi, lo = split(total)
        st_hi[s] = hi
        st_lo[s] = lo
        return 0

    lax.fori_loop(0, lanes * blocks, stack, 0)
    group = max(1, 256 // tile_rows)
    for p in range(0, lanes, group):
        total = None
        for c in range(blocks):
            pick = [(p + q) * blocks + c for q in range(group)]
            hi = jnp.concatenate([st_hi[s] for s in pick], 0)
            lo = jnp.concatenate([st_lo[s] for s in pick], 0)
            part = (
                jnp.dot(hi, in_hi[c], preferred_element_type=jnp.float32)
                + jnp.dot(hi, in_lo[c], preferred_element_type=jnp.float32)
                + jnp.dot(lo, in_hi[c], preferred_element_type=jnp.float32)
            )
            total = part if total is None else total + part
        out_ref[p : p + group] = total.reshape(group, tile_rows, total.shape[1])


def products(owner, int_label, lists, amp_label, amplitudes, ints, lanes):
    blocks = len(ints)
    amp_dev, tile_rows, depth = amplitudes.shape
    window = ints[0].shape[1]
    rows = lanes * blocks
    smem = pl.BlockSpec(memory_space=pltpu.SMEM)
    vmem = pl.BlockSpec(memory_space=pltpu.VMEM)
    return pl.pallas_call(
        functools.partial(product_kernel, lanes, blocks),
        out_shape=jax.ShapeDtypeStruct((lanes, tile_rows, window), jnp.float32),
        in_specs=[smem, smem, vmem, vmem, vmem] + [vmem] * blocks,
        out_specs=vmem,
        scratch_shapes=[
            pltpu.VMEM((rows, LANES), jnp.float32),
            pltpu.VMEM((rows, LANES), jnp.int32),
            pltpu.SMEM((rows, LANES), jnp.float32),
            pltpu.SMEM((rows, LANES), jnp.int32),
            pltpu.VMEM((rows, tile_rows, depth), jnp.bfloat16),
            pltpu.VMEM((rows, tile_rows, depth), jnp.bfloat16),
            pltpu.VMEM((blocks, depth, window), jnp.bfloat16),
            pltpu.VMEM((blocks, depth, window), jnp.bfloat16),
            pltpu.SemaphoreType.DMA((2,)),
        ],
        compiler_params=pltpu.CompilerParams(vmem_limit_bytes=48 * 1024 * 1024),
        cost_estimate=pl.CostEstimate(
            flops=6 * lanes * tile_rows * blocks * depth * window,
            bytes_accessed=amplitudes.size * 4 + blocks * depth * window * 4,
            transcendentals=0,
        ),
        name="products",
    )(owner, int_label, lists, amp_label, amplitudes, *ints)


def on_device(
    amplitudes,
    integrals,
    base_residual,
    occ_gap,
    virt_sum,
    task_amp,
    task_int,
    task_res,
    task_count,
    res_owner,
    amp_label,
    int_label,
):
    lanes = lax.axis_size("wide")
    grps = lax.axis_size("grp")
    slots = task_amp.shape[1]
    ints = [integrals] + [None] * (grps - 1)
    for k in range(2, grps, 2):
        ints[k] = swap(integrals, "grp", k)
    ints[1] = swap(integrals, "grp", 1)
    for k in range(2, grps, 2):
        ints[k + 1] = swap(ints[k], "grp", 1)
    lists = jnp.stack(
        [task_amp, task_int, task_res, jnp.broadcast_to(task_count[:, None], (1, slots))]
    )
    k = 1
    while k < lanes:
        lists = jnp.concatenate([lists, swap(lists, "wide", k)], axis=1)
        k *= 2
    labels = jnp.pad(amp_label, (0, LANES - amp_label.shape[0]))[None, :]
    image = products(
        res_owner, int_label, lists, labels, amplitudes, [x[0] for x in ints], lanes
    )
    far = list(range(lanes - 2, lanes // 2 - 1, -2))
    near = list(range(lanes // 2 - 2, -1, -2))
    total = {}
    for part in (far, near):
        got = swap(jnp.concatenate([image[k + 1 : k + 2] for k in part], 0), "wide", 1)
        for i, k in enumerate(part):
            total[k] = image[k : k + 1] + got[i : i + 1]
    summed = base_residual + total[0]
    for k in far + near:
        if k:
            summed = summed + swap(total[k], "wide", k)
    divisor = occ_gap[:, :, None] + virt_sum[None, None, :]
    return summed / divisor


def solution(mesh):
    return jax.shard_map(
        on_device,
        mesh=mesh,
        in_specs=(
            P(("grp", "wide"), None, None),
            P("grp", None, None),
            P(("grp", "wide"), None, None),
            P(("grp", "wide"), None),
            P(),
            P(("grp", "wide"), None),
            P(("grp", "wide"), None),
            P(("grp", "wide"), None),
            P(("grp", "wide")),
            P("grp", None),
            P(("grp", "wide")),
            P(),
        ),
        out_specs=P(("grp", "wide"), None, None),
        check_vma=False,
    )
```

time: 393 us -> 78.2 us (0.20)
  local copies, waits for them, and re-layouts: 155 us -> 3.24 us
  matrix products: 123 us -> 0 us
  blocking collectives: 83.9 us -> 0 us
  waiting for transfers between devices: 0.73 us -> 43.6 us
  starting transfers between devices: 0.01 us -> 16.7 us
  between operations: 14.2 us -> 0.75 us
  other arithmetic: 14.2 us -> 3.65 us
  Pallas kernels: 0 us -> 9.72 us
    gather x63 -> x0, local copies, waits for them, and re-layouts: 138 us -> none  [the longest x24 85.3 us: block_product(): weights_here = jnp.take(all_integrals, int_ids[task_block], axis=0)]
    dot_general x13 -> x0, matrix products: 123 us -> none  [the longest x12 108 us: block_product(): jnp.einsum('kij,kjl->kil', tiles_here, weights_here, precision=lax.Precis...]
    all_gather x3 -> x0, blocking collectives: 52.4 us -> none  [the longest x1 17.8 us: on_device(): lax.all_gather(task_amp, 'wide', axis=0, tiled=True)]
    ppermute x0 -> x11, waiting for transfers between devices: none -> 43.6 us  [swap(): return lax.ppermute(x, axis, [(i, i ^ k) for i in range(n)])]
    all_to_all x1 -> x0, blocking collectives: 18.4 us -> none  [on_device(): lax.all_to_all(image.reshape(lane_count, res_dev, tile_rows, window), 'wi...]
    ppermute x0 -> x11, starting transfers between devices: none -> 16.7 us  [swap(): return lax.ppermute(x, axis, [(i, i ^ k) for i in range(n)])]
    scatter x4 -> x0, local copies, waits for them, and re-layouts: 13.7 us -> none  [the longest x1 3.56 us: on_device(): jnp.zeros((slot_count,), jnp.bool_).at[target].set(True, mode='drop')]
    unnamed x1 -> x0, blocking collectives: 13.1 us -> none
  transfers between devices with their start and end apart: 1 -> 11, of which waited for: 0 -> 8; matrix products, arithmetic and copies ran while one was open for 8% -> 4% of each run, Pallas kernels for 0% -> 0%
where the time goes in v1:
time: 78.2 us; the launch traced here: 77.7 us
  waiting for transfers between devices  43.6 us (56%)
  starting transfers between devices  16.7 us (21%)
  Pallas kernels  9.72 us (12%)
  other arithmetic  3.65 us (5%)
  local copies, waits for them, and re-layouts  3.24 us (4%)
    ppermute x11, waiting for transfers between devices, swap(): return lax.ppermute(x, axis, [(i, i ^ k) for i in range(n)])  43.6 us
    ppermute x11, starting transfers between devices, swap(): return lax.ppermute(x, axis, [(i, i ^ k) for i in range(n)])  16.7 us
    pallas_call x1, Pallas kernels, products(): pl.pallas_call(functools.partial(product_kernel, lanes, blocks), out_shap...  9.72 us
    unnamed x12, local copies, waits for them, and re-layouts  2.54 us
    concatenate x3, other arithmetic, on_device(): lists = jnp.concatenate([lists, swap(lists, 'wide', k)], axis=1)  2.1 us
  transfers between devices with their start and end apart: 11, of which 8 were waited for; matrix products, arithmetic and copies ran while one was open for 4% of the time, Pallas kernels for 0%

profile of v1, /device:TPU:0, one launch (start us, length us, event | category | flops | bytes accessed | tf_op | source)
XLA Modules:
  0.0 77.7 jit_solution(12741210425550649087)
XLA Ops:
  0.0 2.9 %collective-permute-start.4 = (f32[1,512,512]{2,1,0:T(8,128)}, f32[1,512,512]{2,1,0:T(8,128)S(1)}, u32[]{:S(2)}, u32[]{:S(2)}) collective-permute-start(f32[1,512,512]{2,1,0:T(8,128)} %param.13), channel_id=1, source_target_pairs={{0,16},{8,24},{16,0},{24,8},{1,17},{9,25},{17,1},{25,9},{2,18},{10... | collective-permute-start | bytes 3145736 | tf_op jit(solution)/shard_map/ppermute | solution.py:20
  2.9 0.0 collective-permute-start.3
  2.9 23.4 %collective-permute-done.4 = f32[1,512,512]{2,1,0:T(8,128)S(1)} collective-permute-done((f32[1,512,512]{2,1,0:T(8,128)}, f32[1,512,512]{2,1,0:T(8,128)S(1)}, u32[]{:S(2)}, u32[]{:S(2)}) %collective-permute-start.4) | collective-permute-done | bytes 1048608 | tf_op jit(solution)/shard_map/ppermute | solution.py:20
  26.3 0.0 collective-permute-start.5
  27.0 0.7 pad_add_fusion.3
  27.7 1.8 %collective-permute-start = (s32[4,1,96]{2,1,0:T(1,128)S(1)}, s32[4,1,96]{2,1,0:T(1,128)S(1)}, u32[]{:S(2)}, u32[]{:S(2)}) collective-permute-start(s32[4,1,96]{2,1,0:T(1,128)S(1)} %pad_add_fusion.3), channel_id=1, source_target_pairs={{0,1},{1,0},{2,3},{3,2},{4,5},{5,4},{6,7},{7,6},{8,9},{9,8},{10,11... | collective-permute-start | bytes 4616 | tf_op jit(solution)/shard_map/ppermute | solution.py:20
  29.4 1.8 %collective-permute-done = s32[4,1,96]{2,1,0:T(1,128)S(1)} collective-permute-done((s32[4,1,96]{2,1,0:T(1,128)S(1)}, s32[4,1,96]{2,1,0:T(1,128)S(1)}, u32[]{:S(2)}, u32[]{:S(2)}) %collective-permute-start) | collective-permute-done | bytes 1568 | tf_op jit(solution)/shard_map/ppermute | solution.py:20
  31.3 0.7 pad_add_fusion.2
  31.9 1.9 %collective-permute-start.1 = (s32[4,2,96]{2,1,0:T(2,128)S(1)}, s32[4,2,96]{2,1,0:T(2,128)S(1)}, u32[]{:S(2)}, u32[]{:S(2)}) collective-permute-start(s32[4,2,96]{2,1,0:T(2,128)S(1)} %pad_add_fusion.2), channel_id=1, source_target_pairs={{0,2},{1,3},{2,0},{3,1},{4,6},{5,7},{6,4},{7,5},{8,10},{9,11},{10,... | collective-permute-start | bytes 9224 | tf_op jit(solution)/shard_map/ppermute | solution.py:20
  33.8 1.8 %collective-permute-done.1 = s32[4,2,96]{2,1,0:T(2,128)S(1)} collective-permute-done((s32[4,2,96]{2,1,0:T(2,128)S(1)}, s32[4,2,96]{2,1,0:T(2,128)S(1)}, u32[]{:S(2)}, u32[]{:S(2)}) %collective-permute-start.1) | collective-permute-done | bytes 3104 | tf_op jit(solution)/shard_map/ppermute | solution.py:20
  35.6 0.7 pad_add_fusion.1
  36.3 2.9 %collective-permute-start.2 = (s32[4,4,96]{2,1,0:T(4,128)S(1)}, s32[4,4,96]{2,1,0:T(4,128)S(1)}, u32[]{:S(2)}, u32[]{:S(2)}) collective-permute-start(s32[4,4,96]{2,1,0:T(4,128)S(1)} %pad_add_fusion.1), channel_id=1, source_target_pairs={{0,4},{1,5},{2,6},{3,7},{4,0},{5,1},{6,2},{7,3},{8,12},{9,13},{10,... | collective-permute-start | bytes 18440 | tf_op jit(solution)/shard_map/ppermute | solution.py:20
  39.2 0.7 pad_bitcast_fusion.amp_label_ref
  39.9 1.1 %collective-permute-done.2 = s32[4,4,96]{2,1,0:T(4,128)S(1)} collective-permute-done((s32[4,4,96]{2,1,0:T(4,128)S(1)}, s32[4,4,96]{2,1,0:T(4,128)S(1)}, u32[]{:S(2)}, u32[]{:S(2)}) %collective-permute-start.2) | collective-permute-done | bytes 6176 | tf_op jit(solution)/shard_map/ppermute | solution.py:20
  40.9 0.7 pad_add_fusion.lists_ref
  41.6 0.0 collective-permute-done.3
  41.6 0.0 collective-permute-done.5
  41.7 0.0 copy-start
  41.7 1.2 %copy-done = f32[1,512,512]{2,1,0:T(8,128)S(1)} copy-done((f32[1,512,512]{2,1,0:T(8,128)S(1)}, f32[1,512,512]{2,1,0:T(8,128)}, u32[]{:S(2)}) %copy-start) | copy-done | bytes 1048600
  42.9 0.0 copy-start.1
  42.9 0.7 copy-done.1
  43.5 0.0 copy-start.2
  43.5 0.7 copy-done.2
  44.2 0.0 copy-start.3
  44.2 0.0 copy-start.4
  44.2 0.0 copy-start.5
  44.2 9.7 %products.1 = f32[8,64,512]{2,1,0:T(8,128)S(1)} custom-call(s32[1,8]{1,0:T(1,128)S(1)} %copy-done.1, s32[4]{0:T(128)S(1)} %copy-done.2, s32[4,8,96]{2,1,0:T(8,128)S(1)} %pad_add_fusion.lists_ref, s32[1,128]{1,0:T(1,128)S(1)} %pad_bitcast_fusion.amp_label_ref, f32[32,64,512]{2,1,0:T(8,128)} %amp_ref.1, f32[512,512]{1,0:T(8,128)S(1)} %bitcast.12, ...), custom_call_target="tpu_custom_call" | custom-call | flops 3221225472 | bytes 8388608 | tf_op jit(solution)/shard_map/products/pallas_call | solution.py:132
  54.0 2.7 %collective-permute-start.6 = (f32[2,64,512]{2,1,0:T(8,128)S(1)}, f32[2,64,512]{2,1,0:T(8,128)S(1)}, u32[]{:S(2)}, u32[]{:S(2)}) collective-permute-start(f32[2,64,512]{2,1,0:T(8,128)S(1)} %pad_maximum_fusion), channel_id=1, source_target_pairs={{0,1},{1,0},{2,3},{3,2},{4,5},{5,4},{6,7},{7,6},{8,9},{9,8},{10,11... | collective-permute-start | bytes 786440 | tf_op jit(solution)/shard_map/ppermute | solution.py:20
  56.7 0.1 collective-permute-start.7
  56.8 5.5 %collective-permute-done.6 = f32[2,64,512]{2,1,0:T(8,128)S(1)} collective-permute-done((f32[2,64,512]{2,1,0:T(8,128)S(1)}, f32[2,64,512]{2,1,0:T(8,128)S(1)}, u32[]{:S(2)}, u32[]{:S(2)}) %collective-permute-start.6) | collective-permute-done | bytes 262176 | tf_op jit(solution)/shard_map/ppermute | solution.py:20
  62.3 2.8 %collective-permute-done.7 = f32[2,64,512]{2,1,0:T(8,128)S(1)} collective-permute-done((f32[2,64,512]{2,1,0:T(8,128)S(1)}, f32[2,64,512]{2,1,0:T(8,128)S(1)}, u32[]{:S(2)}, u32[]{:S(2)}) %collective-permute-start.7) | collective-permute-done | bytes 262176 | tf_op jit(solution)/shard_map/ppermute | solution.py:20
  65.1 0.1 slice_add_fusion.2
  65.2 3.6 %collective-permute-start.8 = (f32[1,64,512]{2,1,0:T(8,128)S(1)}, f32[1,64,512]{2,1,0:T(8,128)S(1)}, u32[]{:S(2)}, u32[]{:S(2)}) collective-permute-start(f32[1,64,512]{2,1,0:T(8,128)S(1)} %get-tuple-element.5), channel_id=1, source_target_pairs={{0,6},{1,7},{2,4},{3,5},{4,2},{5,3},{6,0},{7,1},{8,14},{9,15},{10,... | collective-permute-start | bytes 393224 | tf_op jit(solution)/shard_map/ppermute | solution.py:20
  68.8 0.6 collective-permute-start.9
  69.4 0.2 collective-permute-start.10
  69.7 2.6 %collective-permute-done.8 = f32[1,64,512]{2,1,0:T(8,128)S(1)} collective-permute-done((f32[1,64,512]{2,1,0:T(8,128)S(1)}, f32[1,64,512]{2,1,0:T(8,128)S(1)}, u32[]{:S(2)}, u32[]{:S(2)}) %collective-permute-start.8) | collective-permute-done | bytes 131104 | tf_op jit(solution)/shard_map/ppermute | solution.py:20
  72.3 4.6 %collective-permute-done.9 = f32[1,64,512]{2,1,0:T(8,128)S(1)} collective-permute-done((f32[1,64,512]{2,1,0:T(8,128)S(1)}, f32[1,64,512]{2,1,0:T(8,128)S(1)}, u32[]{:S(2)}, u32[]{:S(2)}) %collective-permute-start.9) | collective-permute-done | bytes 131104 | tf_op jit(solution)/shard_map/ppermute | solution.py:20
  76.9 0.0 collective-permute-done.10
  76.9 0.0 copy-done.3
  76.9 0.0 copy-done.4
  76.9 0.0 copy-done.5
  76.9 0.8 fusion.4
  (4 shorter events, 0.1 us)
Async XLA Ops:
  0.0 26.3 %collective-permute-start.4 = (f32[1,512,512]{2,1,0:T(8,128)}, f32[1,512,512]{2,1,0:T(8,128)S(1)}, u32[]{:S(2)}, u32[]{:S(2)}) collective-permute-start(f32[1,512,512]{2,1,0:T(8,128)} %param.13), channel_id=1, source_target_pairs={{0,16},{8,24},{16,0},{24,8},{1,17},{9,25},{17,1},{25,9},{2,18},{10... | collective-permute-start | bytes 3145736 | tf_op jit(solution)/shard_map/ppermute | solution.py:20
  2.9 38.7 %collective-permute-start.3 = (f32[1,512,512]{2,1,0:T(8,128)}, f32[1,512,512]{2,1,0:T(8,128)S(1)}, u32[]{:S(2)}, u32[]{:S(2)}) collective-permute-start(f32[1,512,512]{2,1,0:T(8,128)} %param.13), channel_id=1, source_target_pairs={{0,8},{8,0},{16,24},{24,16},{1,9},{9,1},{17,25},{25,17},{2,10},{10... | collective-permute-start | bytes 3145736 | tf_op jit(solution)/shard_map/ppermute | solution.py:20
  26.3 15.3 %collective-permute-start.5 = (f32[1,512,512]{2,1,0:T(8,128)S(1)}, f32[1,512,512]{2,1,0:T(8,128)S(1)}, u32[]{:S(2)}, u32[]{:S(2)}) collective-permute-start(f32[1,512,512]{2,1,0:T(8,128)S(1)} %collective-permute-done.4), channel_id=1, source_target_pairs={{0,8},{8,0},{16,24},{24,16},{1,9},{9,1},{17,25},{25,17},{2,10},{10... | collective-permute-start | bytes 3145736 | tf_op jit(solution)/shard_map/ppermute | solution.py:20
  27.7 3.6 %collective-permute-start = (s32[4,1,96]{2,1,0:T(1,128)S(1)}, s32[4,1,96]{2,1,0:T(1,128)S(1)}, u32[]{:S(2)}, u32[]{:S(2)}) collective-permute-start(s32[4,1,96]{2,1,0:T(1,128)S(1)} %pad_add_fusion.3), channel_id=1, source_target_pairs={{0,1},{1,0},{2,3},{3,2},{4,5},{5,4},{6,7},{7,6},{8,9},{9,8},{10,11... | collective-permute-start | bytes 4616 | tf_op jit(solution)/shard_map/ppermute | solution.py:20
  31.9 3.7 %collective-permute-start.1 = (s32[4,2,96]{2,1,0:T(2,128)S(1)}, s32[4,2,96]{2,1,0:T(2,128)S(1)}, u32[]{:S(2)}, u32[]{:S(2)}) collective-permute-start(s32[4,2,96]{2,1,0:T(2,128)S(1)} %pad_add_fusion.2), channel_id=1, source_target_pairs={{0,2},{1,3},{2,0},{3,1},{4,6},{5,7},{6,4},{7,5},{8,10},{9,11},{10,... | collective-permute-start | bytes 9224 | tf_op jit(solution)/shard_map/ppermute | solution.py:20
  36.3 4.6 %collective-permute-start.2 = (s32[4,4,96]{2,1,0:T(4,128)S(1)}, s32[4,4,96]{2,1,0:T(4,128)S(1)}, u32[]{:S(2)}, u32[]{:S(2)}) collective-permute-start(s32[4,4,96]{2,1,0:T(4,128)S(1)} %pad_add_fusion.1), channel_id=1, source_target_pairs={{0,4},{1,5},{2,6},{3,7},{4,0},{5,1},{6,2},{7,3},{8,12},{9,13},{10,... | collective-permute-start | bytes 18440 | tf_op jit(solution)/shard_map/ppermute | solution.py:20
  41.7 1.2 %copy-start = (f32[1,512,512]{2,1,0:T(8,128)S(1)}, f32[1,512,512]{2,1,0:T(8,128)}, u32[]{:S(2)}) copy-start(f32[1,512,512]{2,1,0:T(8,128)} %param.13) | copy-start | bytes 3145732
  42.9 0.7 copy-start.1
  43.5 0.7 copy-start.2
  44.2 32.7 %copy-start.3 = (f32[1,64,512]{2,1,0:T(8,128)S(1)}, f32[1,64,512]{2,1,0:T(8,128)}, u32[]{:S(2)}) copy-start(f32[1,64,512]{2,1,0:T(8,128)} %param.14) | copy-start | bytes 393220
  44.2 32.7 %copy-start.4 = (f32[512]{0:T(512)S(1)}, f32[512]{0:T(512)}, u32[]{:S(2)}) copy-start(f32[512]{0:T(512)} %param.16) | copy-start | bytes 6148
  44.2 32.7 %copy-start.5 = (f32[1,64]{1,0:T(1,128)S(1)}, f32[1,64]{1,0:T(1,128)}, u32[]{:S(2)}) copy-start(f32[1,64]{1,0:T(1,128)} %param.15) | copy-start | bytes 772
  54.0 8.3 %collective-permute-start.6 = (f32[2,64,512]{2,1,0:T(8,128)S(1)}, f32[2,64,512]{2,1,0:T(8,128)S(1)}, u32[]{:S(2)}, u32[]{:S(2)}) collective-permute-start(f32[2,64,512]{2,1,0:T(8,128)S(1)} %pad_maximum_fusion), channel_id=1, source_target_pairs={{0,1},{1,0},{2,3},{3,2},{4,5},{5,4},{6,7},{7,6},{8,9},{9,8},{10,11... | collective-permute-start | bytes 786440 | tf_op jit(solution)/shard_map/ppermute | solution.py:20
  56.7 8.4 %collective-permute-start.7 = (f32[2,64,512]{2,1,0:T(8,128)S(1)}, f32[2,64,512]{2,1,0:T(8,128)S(1)}, u32[]{:S(2)}, u32[]{:S(2)}) collective-permute-start(f32[2,64,512]{2,1,0:T(8,128)S(1)} %pad_maximum_fusion.1), channel_id=1, source_target_pairs={{0,1},{1,0},{2,3},{3,2},{4,5},{5,4},{6,7},{7,6},{8,9},{9,8},{10,11... | collective-permute-start | bytes 786440 | tf_op jit(solution)/shard_map/ppermute | solution.py:20
  65.2 7.1 %collective-permute-start.8 = (f32[1,64,512]{2,1,0:T(8,128)S(1)}, f32[1,64,512]{2,1,0:T(8,128)S(1)}, u32[]{:S(2)}, u32[]{:S(2)}) collective-permute-start(f32[1,64,512]{2,1,0:T(8,128)S(1)} %get-tuple-element.5), channel_id=1, source_target_pairs={{0,6},{1,7},{2,4},{3,5},{4,2},{5,3},{6,0},{7,1},{8,14},{9,15},{10,... | collective-permute-start | bytes 393224 | tf_op jit(solution)/shard_map/ppermute | solution.py:20
  68.8 8.1 %collective-permute-start.9 = (f32[1,64,512]{2,1,0:T(8,128)S(1)}, f32[1,64,512]{2,1,0:T(8,128)S(1)}, u32[]{:S(2)}, u32[]{:S(2)}) collective-permute-start(f32[1,64,512]{2,1,0:T(8,128)S(1)} %get-tuple-element.6), channel_id=1, source_target_pairs={{0,4},{1,5},{2,6},{3,7},{4,0},{5,1},{6,2},{7,3},{8,12},{9,13},{10,... | collective-permute-start | bytes 393224 | tf_op jit(solution)/shard_map/ppermute | solution.py:20
  69.4 7.5 %collective-permute-start.10 = (f32[1,64,512]{2,1,0:T(8,128)S(1)}, f32[1,64,512]{2,1,0:T(8,128)S(1)}, u32[]{:S(2)}, u32[]{:S(2)}) collective-permute-start(f32[1,64,512]{2,1,0:T(8,128)S(1)} %get-tuple-element.7), channel_id=1, source_target_pairs={{0,2},{1,3},{2,0},{3,1},{4,6},{5,7},{6,4},{7,5},{8,10},{9,11},{10,... | collective-permute-start | bytes 393224 | tf_op jit(solution)/shard_map/ppermute | solution.py:20

commit v2 on v1

v2 whole, which is shorter than its diff:
```python
import functools

import jax
import jax.numpy as jnp
from jax import lax
from jax.experimental import pallas as pl
from jax.experimental.pallas import tpu as pltpu
from jax.sharding import PartitionSpec as P

LANES = 128
MIB = 1024 * 1024
VMEM = pl.BlockSpec(memory_space=pltpu.VMEM)


def split(x):
    hi = x.astype(jnp.bfloat16)
    return hi, (x - hi.astype(jnp.float32)).astype(jnp.bfloat16)


def swap(x, axis, k):
    n = lax.axis_size(axis)
    return lax.ppermute(x, axis, [(i, i ^ k) for i in range(n)])


def after(x, *others):
    return lax.optimization_barrier((x, *others))[0]


def tile_order(lanes):
    side = list(range(lanes // 2, lanes, 2)) + list(range(lanes // 2 - 2, -1, -2))
    return [k + 1 for k in side], side


def quarter_ids(lane):
    low = lane & 1
    side = low ^ ((lane >> 1) & 1)
    return (2 * side + low, 2 * side + 1 - low, 3 - 2 * side - low, 2 - 2 * side + low)


def coefficients(lists_ref, table_ref, amp_dev, lanes, blocks):
    lane = lax.axis_index("wide")
    grp = lax.axis_index("grp")
    amp, cint, res, count = (lists_ref[i] for i in range(4))
    slot = lax.broadcasted_iota(jnp.int32, amp.shape, 1)
    local = amp - lane * amp_dev
    valid = (slot < count) & (local >= 0) & (local < amp_dev)
    away, side = tile_order(lanes)
    pos = jnp.zeros_like(res)
    for p in range(lanes):
        pos = jnp.where(res == table_ref[1:2, p : p + 1], p, pos)
    offset = pos ^ lane
    place = jnp.zeros_like(res)
    for j, k in enumerate(away + side):
        place = jnp.where(offset == k, j, place)
    seg = jnp.where(valid, place * blocks + (cint ^ grp), -1)
    rows = lanes * blocks
    row_id = lax.broadcasted_iota(jnp.int32, (rows, amp.shape[1]), 0)
    col_id = lax.broadcasted_iota(jnp.int32, (LANES, amp.shape[1]), 0)
    counts = jnp.zeros((rows, LANES), jnp.float32)
    for src in range(lanes):
        hit_row = jnp.where(row_id == seg[src : src + 1, :], 1.0, 0.0)
        hit_col = jnp.where(col_id == local[src : src + 1, :], 1.0, 0.0)
        counts += lax.dot_general(
            hit_row.astype(jnp.bfloat16),
            hit_col.astype(jnp.bfloat16),
            (((1,), (1,)), ((), ())),
            preferred_element_type=jnp.float32,
        )
    row = lax.broadcasted_iota(jnp.int32, (rows, LANES), 0)
    block = (row & (blocks - 1)) ^ grp
    label = jnp.zeros((rows, LANES), jnp.int32)
    for c in range(blocks):
        label = jnp.where(block == c, table_ref[2:3, c : c + 1], label)
    odd = (label + table_ref[0:1, :]) & 1
    weight = jnp.where(odd == 1, -counts, counts)
    col = lax.broadcasted_iota(jnp.int32, (rows, LANES), 1)
    follow = jnp.where(counts > 0.5, col, LANES)
    step = 1
    while step < amp_dev:
        follow = jnp.minimum(follow, pltpu.roll(follow, LANES - step, 1))
        step *= 2
    return weight, follow


def passes(st_hi, st_lo, in_hi, in_lo, first, count):
    hi = st_hi[first : first + count, :]
    lo = st_lo[first : first + count, :]
    dot = functools.partial(jnp.dot, preferred_element_type=jnp.float32)
    return dot(hi, in_hi[...]) + dot(hi, in_lo[...]) + dot(lo, in_hi[...])


def store_tiles(refs, out):
    tile_rows = refs[0].shape[1]
    for i, ref in enumerate(refs):
        ref[0] = out[i * tile_rows : (i + 1) * tile_rows]


def load_kernel(amp_hbm, amp_ref, sems):
    n = sems.shape[0]
    step = amp_ref.shape[0] // n
    copies = [
        pltpu.make_async_copy(
            amp_hbm.at[pl.ds(i * step, step)], amp_ref.at[pl.ds(i * step, step)], sems.at[i]
        )
        for i in range(n)
    ]
    for copy in copies:
        copy.start()
    for copy in copies:
        copy.wait()


def load(amplitudes):
    size = amplitudes.size * 4
    return pl.pallas_call(
        load_kernel,
        out_shape=pltpu.VMEM(amplitudes.shape, amplitudes.dtype),
        in_specs=[pl.BlockSpec(memory_space=pltpu.HBM)],
        out_specs=VMEM,
        scratch_shapes=[pltpu.SemaphoreType.DMA((4,))],
        compiler_params=pltpu.CompilerParams(vmem_limit_bytes=size + MIB),
        cost_estimate=pl.CostEstimate(flops=0, bytes_accessed=2 * size, transcendentals=0),
        name="load_amplitudes",
    )(pltpu.with_memory_space_constraint(amplitudes, pltpu.HBM))


def sums_kernel(lanes, blocks, lists_ref, table_ref, amp_ref, *rest):
    whole, parts = rest[:2], rest[2 : 2 + 4 * (blocks - 2)]
    rest = rest[2 + 4 * (blocks - 2) :]
    away = lanes // 2
    away_refs, rest = rest[:away], rest[away:]
    st_hi, st_lo, in_hi, in_lo, weight_v, follow_v, weight_s, follow_s, sems = rest
    amp_dev, tile_rows, depth = amp_ref.shape
    weight, follow = coefficients(lists_ref, table_ref, amp_dev, lanes, blocks)
    weight_v[...] = weight
    follow_v[...] = follow
    one = pltpu.make_async_copy(weight_v, weight_s, sems.at[0])
    two = pltpu.make_async_copy(follow_v, follow_s, sems.at[1])
    one.start()
    two.start()
    for c in range(2):
        hi, lo = split(whole[c][...])
        in_hi[c * depth : (c + 1) * depth, :] = hi
        in_lo[c * depth : (c + 1) * depth, :] = lo
    ids = quarter_ids(lax.axis_index("wide"))
    quarter = depth // 4
    for c in range(2, blocks):
        for i in range(4):
            hi, lo = split(parts[4 * (c - 2) + i][...])
            at = pl.ds(pl.multiple_of(c * depth + ids[i] * quarter, quarter), quarter)
            in_hi[at, :] = hi
            in_lo[at, :] = lo
    one.wait()
    two.wait()

    def stack(j, _):
        for c in range(blocks):
            s = j * blocks + c

            def more(carry):
                return carry[0] < amp_dev

            def add(carry, s=s):
                a, total = carry
                return follow_s[s, a + 1], total + weight_s[s, a] * amp_ref[a]

            _, total = lax.while_loop(
                more, add, (follow_s[s, 0], jnp.zeros((tile_rows, depth), jnp.float32))
            )
            hi, lo = split(total)
            at = pl.ds(pl.multiple_of(j * tile_rows, tile_rows), tile_rows)
            st_hi[at, c * depth : (c + 1) * depth] = hi
            st_lo[at, c * depth : (c + 1) * depth] = lo
        return 0

    lax.fori_loop(0, lanes, stack, 0)
    store_tiles(away_refs, passes(st_hi, st_lo, in_hi, in_lo, 0, away * tile_rows))


def side_kernel(st_hi, st_lo, in_hi, in_lo, *side_refs):
    rows = len(side_refs) * side_refs[0].shape[1]
    store_tiles(side_refs, passes(st_hi, st_lo, in_hi, in_lo, rows, rows))


def products(lists, table, amplitudes, whole, parts, lanes):
    blocks = 2 + len(parts)
    amp_dev, tile_rows, depth = amplitudes.shape
    window = whole[0].shape[1]
    rows = lanes * blocks
    half = lanes // 2
    tiles = [jax.ShapeDtypeStruct((1, tile_rows, window), jnp.float32)] * half
    packed_shapes = [pltpu.VMEM((lanes * tile_rows, blocks * depth), jnp.bfloat16)] * 2 + [
        pltpu.VMEM((blocks * depth, window), jnp.bfloat16)
    ] * 2
    packed_bytes = 4 * (lanes * tile_rows + window) * blocks * depth
    tile_bytes = half * tile_rows * window * 4
    int_bytes = 4 * blocks * depth * window

    cost = pl.CostEstimate(
        flops=3 * lanes * tile_rows * blocks * depth * window,
        bytes_accessed=packed_bytes,
        transcendentals=0,
    )

    out = pl.pallas_call(
        functools.partial(sums_kernel, lanes, blocks),
        out_shape=tiles + packed_shapes,
        in_specs=[VMEM] * (5 + 4 * len(parts)),
        out_specs=[VMEM] * (half + 4),
        scratch_shapes=[
            pltpu.VMEM((rows, LANES), jnp.float32),
            pltpu.VMEM((rows, LANES), jnp.int32),
            pltpu.SMEM((rows, LANES), jnp.float32),
            pltpu.SMEM((rows, LANES), jnp.int32),
            pltpu.SemaphoreType.DMA((2,)),
        ],
        compiler_params=pltpu.CompilerParams(
            vmem_limit_bytes=min(56 * MIB, int_bytes + 2 * tile_bytes + 8 * MIB)
        ),
        cost_estimate=cost,
        name="sums_and_away_products",
    )(lists, table, amplitudes, *whole, *[x for four in parts for x in four])
    away, packed = out[:half], out[half:]
    packed = [pltpu.with_memory_space_constraint(x, pltpu.VMEM) for x in packed]
    side = pl.pallas_call(
        side_kernel,
        out_shape=tiles,
        in_specs=[VMEM] * 4,
        out_specs=[VMEM] * half,
        compiler_params=pltpu.CompilerParams(vmem_limit_bytes=2 * tile_bytes + 8 * MIB),
        cost_estimate=cost,
        name="side_products",
    )(*packed)
    return away, side


def on_device(
    amplitudes,
    integrals,
    base_residual,
    occ_gap,
    virt_sum,
    task_amp,
    task_int,
    task_res,
    task_count,
    res_owner,
    amp_label,
    int_label,
):
    lanes = lax.axis_size("wide")
    grps = lax.axis_size("grp")
    slots = task_amp.shape[1]
    own = integrals[0]
    quarter = own.shape[0] // 4
    ids = quarter_ids(lax.axis_index("wide"))
    send = [lax.dynamic_slice_in_dim(own, ids[i] * quarter, quarter, 0) for i in range(2)]
    fetched = {k: [swap(x, "grp", k) for x in send] for k in range(2, grps, 2)}
    whole = [own, swap(own, "grp", 1)]

    lists = jnp.stack(
        [task_amp, task_int, task_res, jnp.broadcast_to(task_count[:, None], (1, slots))]
    )
    amplitudes = load(amplitudes)
    k = 1
    while k < lanes:
        lists = jnp.concatenate([lists, swap(lists, "wide", k)], axis=1)
        if k == 1:
            lists = early = after(lists, amplitudes)
        k *= 2
    table = jnp.stack(
        [jnp.pad(x, (0, LANES - x.shape[0])) for x in (amp_label, res_owner[0], int_label)]
    )

    parts = [None] * (grps - 2)
    for k, (one, two) in fetched.items():
        relay = after(one, early)
        four = [one, two, swap(relay, "wide", 1), swap(relay, "wide", 2)]
        parts[k - 2] = four
        parts[k - 1] = [swap(after(x, lists), "grp", 1) for x in four]

    amplitudes = pltpu.with_memory_space_constraint(amplitudes, pltpu.VMEM)
    away, mine = products(lists, table, amplitudes, whole, parts, lanes)
    _, offsets = tile_order(lanes)
    got = [swap(x, "wide", 1) for x in away]
    summed = base_residual
    for k, here, there in zip(offsets, mine, got):
        part = here + there
        summed = summed + (swap(part, "wide", k) if k else part)
    divisor = occ_gap[:, :, None] + virt_sum[None, None, :]
    return summed / divisor


def solution(mesh):
    return jax.shard_map(
        on_device,
        mesh=mesh,
        in_specs=(
            P(("grp", "wide"), None, None),
            P("grp", None, None),
            P(("grp", "wide"), None, None),
            P(("grp", "wide"), None),
            P(),
            P(("grp", "wide"), None),
            P(("grp", "wide"), None),
            P(("grp", "wide"), None),
            P(("grp", "wide")),
            P("grp", None),
            P(("grp", "wide")),
            P(),
        ),
        out_specs=P(("grp", "wide"), None, None),
        check_vma=False,
    )
```

time: 78.2 us -> 54.1 us (0.69)
  waiting for transfers between devices: 43.6 us -> 14.7 us
  starting transfers between devices: 16.7 us -> 25 us
  local copies, waits for them, and re-layouts: 3.24 us -> 1.12 us
  other arithmetic: 3.65 us -> 1.54 us
  Pallas kernels: 9.72 us -> 10.6 us
    ppermute x11 -> x19, waiting for transfers between devices: 43.6 us -> 14.7 us  [swap(): return lax.ppermute(x, axis, [(i, i ^ k) for i in range(n)])]
    ppermute x11 -> x19, starting transfers between devices: 16.7 us -> 25 us  [swap(): return lax.ppermute(x, axis, [(i, i ^ k) for i in range(n)])]
    unnamed x12 -> x20, local copies, waits for them, and re-layouts: 2.54 us -> 0.04 us
    concatenate x3, other arithmetic: 2.1 us -> 0.03 us  [on_device(): lists = jnp.concatenate([lists, swap(lists, 'wide', k)], axis=1)]
    dynamic_slice x0 -> x1, local copies, waits for them, and re-layouts: none -> 1.06 us  [on_device(): lax.dynamic_slice_in_dim(own, ids[i] * quarter, quarter, 0)]
    pallas_call x1 -> x3, Pallas kernels: 9.72 us -> 10.6 us  [the longest x1 6.65 us: products(): pl.pallas_call(functools.partial(sums_kernel, lanes, blocks), out_shape=t...]
  transfers between devices with their start and end apart: 11 -> 19, of which waited for: 8 -> 10; matrix products, arithmetic and copies ran while one was open for 4% -> 3% of each run, Pallas kernels for 0% -> 7%
where the time goes in v2:
time: 54.1 us; the launch traced here: 53.9 us
  starting transfers between devices  25 us (46%)
  waiting for transfers between devices  14.7 us (27%)
  Pallas kernels  10.6 us (20%)
  other arithmetic  1.54 us (3%)
  local copies, waits for them, and re-layouts  1.12 us (2%)
  between operations  0.83 us (2%)
    ppermute x19, starting transfers between devices, swap(): return lax.ppermute(x, axis, [(i, i ^ k) for i in range(n)])  25 us
    ppermute x19, waiting for transfers between devices, swap(): return lax.ppermute(x, axis, [(i, i ^ k) for i in range(n)])  14.7 us
    pallas_call x1, Pallas kernels, products(): pl.pallas_call(functools.partial(sums_kernel, lanes, blocks), out_shape=t...  6.65 us
    pallas_call x1, Pallas kernels, load(): pl.pallas_call(load_kernel, out_shape=pltpu.VMEM(amplitudes.shape, amplit...  2.2 us
    pallas_call x1, Pallas kernels, products(): pl.pallas_call(side_kernel, out_shape=tiles, in_specs=[VMEM] * 4, out_spe...  1.78 us
  transfers between devices with their start and end apart: 19, of which 10 were waited for; matrix products, arithmetic and copies ran while one was open for 3% of the time, Pallas kernels for 7%

profile of v2, /device:TPU:0, one launch (start us, length us, event | category | flops | bytes accessed | tf_op | source)
XLA Modules:
  0.0 53.9 jit_solution(14165809003641403058)
XLA Ops:
  0.0 0.5 collective-permute-start.3
  0.5 1.1 %dynamic-slice_bitcast_fusion = (f32[128,512]{1,0:T(8,128)S(1)}, f32[128,512]{1,0:T(8,128)S(1)}) fusion(f32[1,512,512]{2,1,0:T(8,128)} %param.13, s32[]{:T(128)S(6)} %select_n.7, s32[]{:T(128)S(6)} %select_n.6), kind=kLoop, calls=%fused_computation | loop fusion | bytes 1048584 | tf_op jit(solution)/shard_map/dynamic_slice | solution.py:257
  1.5 2.6 %collective-permute-start.4 = (f32[128,512]{1,0:T(8,128)S(1)}, f32[128,512]{1,0:T(8,128)S(1)}, u32[]{:S(2)}, u32[]{:S(2)}) collective-permute-start(f32[128,512]{1,0:T(8,128)S(1)} %get-tuple-element.42), channel_id=1, source_target_pairs={{0,16},{8,24},{16,0},{24,8},{1,17},{9,25},{17,1},{25,9},{2,18},{10... | collective-permute-start | bytes 786440 | tf_op jit(solution)/shard_map/ppermute | solution.py:22
  4.7 0.7 %pad_add_fusion.3 = s32[4,1,96]{2,1,0:T(1,128)S(1)} fusion(s32[1,1,96]{2,1,0:T(1,128)S(1)} %stack_broadcast_in_dim.8, s32[1,1,96]{2,1,0:T(1,128)} %bitcast.20, s32[1,1,96]{2,1,0:T(1,128)} %bitcast.22, s32[1,1,96]{2,1,0:T(1,128)} %bitcast.24), kind=kLoop, calls=%fused_computation.6 | loop fusion | flops 1152 | bytes 3072 | tf_op jit(solution)/shard_map/stack | solution.py:261
  5.4 1.5 %collective-permute-start = (s32[4,1,96]{2,1,0:T(1,128)S(1)}, s32[4,1,96]{2,1,0:T(1,128)S(1)}, u32[]{:S(2)}, u32[]{:S(2)}) collective-permute-start(s32[4,1,96]{2,1,0:T(1,128)S(1)} %pad_add_fusion.3), channel_id=1, source_target_pairs={{0,1},{1,0},{2,3},{3,2},{4,5},{5,4},{6,7},{7,6},{8,9},{9,8},{10,11... | collective-permute-start | bytes 4616 | tf_op jit(solution)/shard_map/ppermute | solution.py:22
  7.0 0.0 copy-start.7
  7.0 0.0 copy-start.8
  7.0 0.0 copy-start
  7.0 0.6 %collective-permute-start.5 = (f32[128,512]{1,0:T(8,128)S(1)}, f32[128,512]{1,0:T(8,128)S(1)}, u32[]{:S(2)}, u32[]{:S(2)}) collective-permute-start(f32[128,512]{1,0:T(8,128)S(1)} %get-tuple-element.41), channel_id=1, source_target_pairs={{0,16},{8,24},{16,0},{24,8},{1,17},{9,25},{17,1},{25,9},{2,18},{10... | collective-permute-start | bytes 786440 | tf_op jit(solution)/shard_map/ppermute | solution.py:22
  7.6 2.2 %load_amplitudes.1.amp_ref = f32[32,64,512]{2,1,0:T(8,128)S(1)} custom-call(f32[32,64,512]{2,1,0:T(8,128)} %amp_hbm.1), custom_call_target="tpu_custom_call" | custom-call | bytes 8388608 | tf_op jit(solution)/shard_map/load_amplitudes/pallas_call | solution.py:115
  9.8 0.0 collective-permute-done
  9.9 1.4 %collective-permute-done.4.rest_2_ = f32[128,512]{1,0:T(8,128)S(1)} collective-permute-done((f32[128,512]{1,0:T(8,128)S(1)}, f32[128,512]{1,0:T(8,128)S(1)}, u32[]{:S(2)}, u32[]{:S(2)}) %collective-permute-start.4) | collective-permute-done | bytes 262176 | tf_op jit(solution)/shard_map/ppermute | solution.py:22
  11.2 2.0 %collective-permute-start.7 = (f32[128,512]{1,0:T(8,128)S(1)}, f32[128,512]{1,0:T(8,128)S(1)}, u32[]{:S(2)}, u32[]{:S(2)}) collective-permute-start(f32[128,512]{1,0:T(8,128)S(1)} %collective-permute-done.4.rest_2_), channel_id=1, source_target_pairs={{0,2},{1,3},{2,0},{3,1},{4,6},{5,7},{6,4},{7,5},{8,10},{9,11},{10,... | collective-permute-start | bytes 786440 | tf_op jit(solution)/shard_map/ppermute | solution.py:22
  13.3 1.5 %collective-permute-start.6 = (f32[128,512]{1,0:T(8,128)S(1)}, f32[128,512]{1,0:T(8,128)S(1)}, u32[]{:S(2)}, u32[]{:S(2)}) collective-permute-start(f32[128,512]{1,0:T(8,128)S(1)} %collective-permute-done.4.rest_2_), channel_id=1, source_target_pairs={{0,1},{1,0},{2,3},{3,2},{4,5},{5,4},{6,7},{7,6},{8,9},{9,8},{10,11... | collective-permute-start | bytes 786440 | tf_op jit(solution)/shard_map/ppermute | solution.py:22
  14.8 0.4 collective-permute-start.1
  15.2 4.0 %collective-permute-done.1 = s32[4,2,96]{2,1,0:T(2,128)S(1)} collective-permute-done((s32[4,2,96]{2,1,0:T(2,128)S(1)}, s32[4,2,96]{2,1,0:T(2,128)S(1)}, u32[]{:S(2)}, u32[]{:S(2)}) %collective-permute-start.1) | collective-permute-done | bytes 3104 | tf_op jit(solution)/shard_map/ppermute | solution.py:22
  19.3 2.7 %collective-permute-start.2 = (s32[4,4,96]{2,1,0:T(4,128)S(1)}, s32[4,4,96]{2,1,0:T(4,128)S(1)}, u32[]{:S(2)}, u32[]{:S(2)}) collective-permute-start(s32[4,4,96]{2,1,0:T(4,128)S(1)} %pad_add_fusion.1), channel_id=1, source_target_pairs={{0,4},{1,5},{2,6},{3,7},{4,0},{5,1},{6,2},{7,3},{8,12},{9,13},{10,... | collective-permute-start | bytes 18440 | tf_op jit(solution)/shard_map/ppermute | solution.py:22
  22.0 1.9 %collective-permute-done.2 = s32[4,4,96]{2,1,0:T(4,128)S(1)} collective-permute-done((s32[4,4,96]{2,1,0:T(4,128)S(1)}, s32[4,4,96]{2,1,0:T(4,128)S(1)}, u32[]{:S(2)}, u32[]{:S(2)}) %collective-permute-start.2) | collective-permute-done | bytes 6176 | tf_op jit(solution)/shard_map/ppermute | solution.py:22
  23.9 0.0 collective-permute-done.5.rest_3_
  23.9 0.1 collective-permute-start.8
  24.0 0.5 collective-permute-start.9
  24.5 0.0 collective-permute-done.7.rest_5_
  24.5 0.1 collective-permute-start.11
  24.6 0.0 collective-permute-done.6.rest_4_
  24.6 0.4 collective-permute-start.10
  25.0 0.0 copy-done.7
  25.1 0.5 collective-permute-done.8.rest_6_
  25.5 0.4 collective-permute-done.9.rest_7_
  25.9 0.4 collective-permute-done.11.rest_9_
  26.3 0.4 collective-permute-done.10.rest_8_
  26.7 0.0 collective-permute-done.3.rest_1_
  26.7 6.7 %sums_and_away_products.1 = (f32[1,64,512]{2,1,0:T(8,128)S(1)}, f32[1,64,512]{2,1,0:T(8,128)S(1)}, f32[1,64,512]{2,1,0:T(8,128)S(1)}, f32[1,64,512]{2,1,0:T(8,12...) custom-call(s32[4,8,96]{2,1,0:T(8,128)S(1)} %pad_add_fusion.lists_re, ...), custom_call_target="tpu_custom_call" | custom-call | flops 1610612736 | bytes 8388608 | tf_op jit(solution)/shard_map/sums_and_away_products/pallas_call | solution.py:205
  33.3 1.9 %collective-permute-start.12 = (f32[1,64,512]{2,1,0:T(8,128)S(1)}, f32[1,64,512]{2,1,0:T(8,128)S(1)}, u32[]{:S(2)}, u32[]{:S(2)}) collective-permute-start(f32[1,64,512]{2,1,0:T(8,128)S(1)} %get-tuple-element.34), channel_id=1, source_target_pairs={{0,1},{1,0},{2,3},{3,2},{4,5},{5,4},{6,7},{7,6},{8,9},{9,8},{10,11... | collective-permute-start | bytes 393224 | tf_op jit(solution)/shard_map/ppermute | solution.py:22
  35.2 0.2 collective-permute-start.14
  35.4 1.8 %collective-permute-start.16 = (f32[1,64,512]{2,1,0:T(8,128)S(1)}, f32[1,64,512]{2,1,0:T(8,128)S(1)}, u32[]{:S(2)}, u32[]{:S(2)}) collective-permute-start(f32[1,64,512]{2,1,0:T(8,128)S(1)} %get-tuple-element.38), channel_id=1, source_target_pairs={{0,1},{1,0},{2,3},{3,2},{4,5},{5,4},{6,7},{7,6},{8,9},{9,8},{10,11... | collective-permute-start | bytes 393224 | tf_op jit(solution)/shard_map/ppermute | solution.py:22
  37.2 0.2 collective-permute-start.18
  37.5 1.8 %side_products.1 = (f32[1,64,512]{2,1,0:T(8,128)S(1)}, f32[1,64,512]{2,1,0:T(8,128)S(1)}, f32[1,64,512]{2,1,0:T(8,128)S(1)}, f32[1,64,512]{2,1,0:T(8,128)S(1)}) custom-call(bf16[512,2048]{1,0:T(8,128)(2,1)S(1)} %get-tuple-element.29.st_hi, bf16[512,2048]{1,0:T(8,128)(2,1)S(1)} %get-tuple-element.30.st_lo, bf16[2048,512]{1,0:T(8,128)(2,1)S(1)} %get-tuple-element.31.in_hi, ...), custom_call_target="tpu_custom_call" | custom-call | flops 1610612736 | bytes 8388608 | tf_op jit(solution)/shard_map/side_products/pallas_call | solution.py:225
  39.2 0.5 collective-permute-done.12
  39.8 3.2 %collective-permute-start.13 = (f32[1,64,512]{2,1,0:T(8,128)S(1)}, f32[1,64,512]{2,1,0:T(8,128)S(1)}, u32[]{:S(2)}, u32[]{:S(2)}) collective-permute-start(f32[1,64,512]{2,1,0:T(8,128)S(1)} %add.67), channel_id=1, source_target_pairs={{0,4},{1,5},{2,6},{3,7},{4,0},{5,1},{6,2},{7,3},{8,12},{9,13},{10,... | collective-permute-start | bytes 393224 | tf_op jit(solution)/shard_map/ppermute | solution.py:22
  42.9 0.0 collective-permute-done.14
  43.0 3.6 %collective-permute-start.15 = (f32[1,64,512]{2,1,0:T(8,128)S(1)}, f32[1,64,512]{2,1,0:T(8,128)S(1)}, u32[]{:S(2)}, u32[]{:S(2)}) collective-permute-start(f32[1,64,512]{2,1,0:T(8,128)S(1)} %add.69), channel_id=1, source_target_pairs={{0,6},{1,7},{2,4},{3,5},{4,2},{5,3},{6,0},{7,1},{8,14},{9,15},{10,... | collective-permute-start | bytes 393224 | tf_op jit(solution)/shard_map/ppermute | solution.py:22
  46.5 0.0 collective-permute-done.16
  46.6 1.3 %collective-permute-start.17 = (f32[1,64,512]{2,1,0:T(8,128)S(1)}, f32[1,64,512]{2,1,0:T(8,128)S(1)}, u32[]{:S(2)}, u32[]{:S(2)}) collective-permute-start(f32[1,64,512]{2,1,0:T(8,128)S(1)} %add.71), channel_id=1, source_target_pairs={{0,2},{1,3},{2,0},{3,1},{4,6},{5,7},{6,4},{7,5},{8,10},{9,11},{10,... | collective-permute-start | bytes 393224 | tf_op jit(solution)/shard_map/ppermute | solution.py:22
  47.8 0.0 collective-permute-done.18
  47.8 3.8 %collective-permute-done.13 = f32[1,64,512]{2,1,0:T(8,128)S(1)} collective-permute-done((f32[1,64,512]{2,1,0:T(8,128)S(1)}, f32[1,64,512]{2,1,0:T(8,128)S(1)}, u32[]{:S(2)}, u32[]{:S(2)}) %collective-permute-start.13) | collective-permute-done | bytes 131104 | tf_op jit(solution)/shard_map/ppermute | solution.py:22
  51.7 0.0 collective-permute-done.15
  51.7 1.5 %collective-permute-done.17 = f32[1,64,512]{2,1,0:T(8,128)S(1)} collective-permute-done((f32[1,64,512]{2,1,0:T(8,128)S(1)}, f32[1,64,512]{2,1,0:T(8,128)S(1)}, u32[]{:S(2)}, u32[]{:S(2)}) %collective-permute-start.17) | collective-permute-done | bytes 131104 | tf_op jit(solution)/shard_map/ppermute | solution.py:22
  53.1 0.8 %add_divide_fusion = f32[1,64,512]{2,1,0:T(8,128)} fusion(f32[1,64,512]{2,1,0:T(8,128)S(1)} %get-tuple-element.39, f32[1,64,512]{2,1,0:T(8,128)S(1)} %collective-permute-done.18, f32[1,64,512]{2,1,0:T(8,128)S(1)} %collective-permute-done.17, f32[1,64,512]{2,1,0:T(8,128)S(1)} %collective-permute-done.15, f32[1,64,512]{2,1,0:T(8,128)S(1)} %copy-done.1, ...), kind=kLoop, calls=%fused_computation.2 | loop fusion | flops 229376 | bytes 919808 | tf_op jit(solution)/shard_map/div | solution.py:291
  (26 shorter events, 0.1 us)
Async XLA Ops:
  0.0 26.7 %collective-permute-start.3 = (f32[512,512]{1,0:T(8,128)}, f32[512,512]{1,0:T(8,128)S(1)}, u32[]{:S(2)}, u32[]{:S(2)}) collective-permute-start(f32[512,512]{1,0:T(8,128)} %bitcast.18), channel_id=1, source_target_pairs={{0,8},{8,0},{16,24},{24,16},{1,9},{9,1},{17,25},{25,17},{2,10},{10... | collective-permute-start | bytes 3145736 | tf_op jit(solution)/shard_map/ppermute | solution.py:22
  1.5 9.7 %collective-permute-start.4 = (f32[128,512]{1,0:T(8,128)S(1)}, f32[128,512]{1,0:T(8,128)S(1)}, u32[]{:S(2)}, u32[]{:S(2)}) collective-permute-start(f32[128,512]{1,0:T(8,128)S(1)} %get-tuple-element.42), channel_id=1, source_target_pairs={{0,16},{8,24},{16,0},{24,8},{1,17},{9,25},{17,1},{25,9},{2,18},{10... | collective-permute-start | bytes 786440 | tf_op jit(solution)/shard_map/ppermute | solution.py:22
  5.4 4.4 %collective-permute-start = (s32[4,1,96]{2,1,0:T(1,128)S(1)}, s32[4,1,96]{2,1,0:T(1,128)S(1)}, u32[]{:S(2)}, u32[]{:S(2)}) collective-permute-start(s32[4,1,96]{2,1,0:T(1,128)S(1)} %pad_add_fusion.3), channel_id=1, source_target_pairs={{0,1},{1,0},{2,3},{3,2},{4,5},{5,4},{6,7},{7,6},{8,9},{9,8},{10,11... | collective-permute-start | bytes 4616 | tf_op jit(solution)/shard_map/ppermute | solution.py:22
  7.0 2.9 %copy-start.3 = (s32[1,96]{1,0:T(1,128)S(1)}, s32[1,96]{1,0:T(1,128)}, u32[]{:S(2)}) copy-start(s32[1,96]{1,0:T(1,128)} %param.19) | copy-start | bytes 1156
  7.0 2.9 %copy-start.4 = (s32[1,96]{1,0:T(1,128)S(1)}, s32[1,96]{1,0:T(1,128)}, u32[]{:S(2)}) copy-start(s32[1,96]{1,0:T(1,128)} %param.18) | copy-start | bytes 1156
  7.0 2.9 %copy-start.5 = (s32[1,96]{1,0:T(1,128)S(1)}, s32[1,96]{1,0:T(1,128)}, u32[]{:S(2)}) copy-start(s32[1,96]{1,0:T(1,128)} %param.17) | copy-start | bytes 1156
  7.0 18.1 %copy-start.9 = (s32[32]{0:T(128)S(1)}, s32[32]{0:T(128)}, u32[]{:S(2)}) copy-start(s32[32]{0:T(128)} %param.22) | copy-start | bytes 388
  7.0 18.1 %copy-start.7 = (s32[4]{0:T(128)S(1)}, s32[4]{0:T(128)}, u32[]{:S(2)}) copy-start(s32[4]{0:T(128)} %param.23) | copy-start | bytes 52
  7.0 18.1 %copy-start.8 = (s32[1,8]{1,0:T(1,128)S(1)}, s32[1,8]{1,0:T(1,128)}, u32[]{:S(2)}) copy-start(s32[1,8]{1,0:T(1,128)} %param.21) | copy-start | bytes 100
  7.0 19.7 %copy-start = (f32[1,512,512]{2,1,0:T(8,128)S(1)}, f32[1,512,512]{2,1,0:T(8,128)}, u32[]{:S(2)}) copy-start(f32[1,512,512]{2,1,0:T(8,128)} %param.13) | copy-start | bytes 3145732
  7.0 16.9 %collective-permute-start.5 = (f32[128,512]{1,0:T(8,128)S(1)}, f32[128,512]{1,0:T(8,128)S(1)}, u32[]{:S(2)}, u32[]{:S(2)}) collective-permute-start(f32[128,512]{1,0:T(8,128)S(1)} %get-tuple-element.41), channel_id=1, source_target_pairs={{0,16},{8,24},{16,0},{24,8},{1,17},{9,25},{17,1},{25,9},{2,18},{10... | collective-permute-start | bytes 786440 | tf_op jit(solution)/shard_map/ppermute | solution.py:22
  11.2 13.3 %collective-permute-start.7 = (f32[128,512]{1,0:T(8,128)S(1)}, f32[128,512]{1,0:T(8,128)S(1)}, u32[]{:S(2)}, u32[]{:S(2)}) collective-permute-start(f32[128,512]{1,0:T(8,128)S(1)} %collective-permute-done.4.rest_2_), channel_id=1, source_target_pairs={{0,2},{1,3},{2,0},{3,1},{4,6},{5,7},{6,4},{7,5},{8,10},{9,11},{10,... | collective-permute-start | bytes 786440 | tf_op jit(solution)/shard_map/ppermute | solution.py:22
  13.3 11.3 %collective-permute-start.6 = (f32[128,512]{1,0:T(8,128)S(1)}, f32[128,512]{1,0:T(8,128)S(1)}, u32[]{:S(2)}, u32[]{:S(2)}) collective-permute-start(f32[128,512]{1,0:T(8,128)S(1)} %collective-permute-done.4.rest_2_), channel_id=1, source_target_pairs={{0,1},{1,0},{2,3},{3,2},{4,5},{5,4},{6,7},{7,6},{8,9},{9,8},{10,11... | collective-permute-start | bytes 786440 | tf_op jit(solution)/shard_map/ppermute | solution.py:22
  14.8 4.5 %collective-permute-start.1 = (s32[4,2,96]{2,1,0:T(2,128)S(1)}, s32[4,2,96]{2,1,0:T(2,128)S(1)}, u32[]{:S(2)}, u32[]{:S(2)}) collective-permute-start(s32[4,2,96]{2,1,0:T(2,128)S(1)} %pad_add_fusion.2), channel_id=1, source_target_pairs={{0,2},{1,3},{2,0},{3,1},{4,6},{5,7},{6,4},{7,5},{8,10},{9,11},{10,... | collective-permute-start | bytes 9224 | tf_op jit(solution)/shard_map/ppermute | solution.py:22
  19.3 4.6 %collective-permute-start.2 = (s32[4,4,96]{2,1,0:T(4,128)S(1)}, s32[4,4,96]{2,1,0:T(4,128)S(1)}, u32[]{:S(2)}, u32[]{:S(2)}) collective-permute-start(s32[4,4,96]{2,1,0:T(4,128)S(1)} %pad_add_fusion.1), channel_id=1, source_target_pairs={{0,4},{1,5},{2,6},{3,7},{4,0},{5,1},{6,2},{7,3},{8,12},{9,13},{10,... | collective-permute-start | bytes 18440 | tf_op jit(solution)/shard_map/ppermute | solution.py:22
  23.9 1.6 %collective-permute-start.8 = (f32[128,512]{1,0:T(8,128)S(1)}, f32[128,512]{1,0:T(8,128)S(1)}, u32[]{:S(2)}, u32[]{:S(2)}) collective-permute-start(f32[128,512]{1,0:T(8,128)S(1)} %collective-permute-done.4.rest_2_), channel_id=1, source_target_pairs={{0,8},{8,0},{16,24},{24,16},{1,9},{9,1},{17,25},{25,17},{2,10},{10... | collective-permute-start | bytes 786440 | tf_op jit(solution)/shard_map/ppermute | solution.py:22
  24.0 1.9 %collective-permute-start.9 = (f32[128,512]{1,0:T(8,128)S(1)}, f32[128,512]{1,0:T(8,128)S(1)}, u32[]{:S(2)}, u32[]{:S(2)}) collective-permute-start(f32[128,512]{1,0:T(8,128)S(1)} %collective-permute-done.5.rest_3_), channel_id=1, source_target_pairs={{0,8},{8,0},{16,24},{24,16},{1,9},{9,1},{17,25},{25,17},{2,10},{10... | collective-permute-start | bytes 786440 | tf_op jit(solution)/shard_map/ppermute | solution.py:22
  24.5 1.8 %collective-permute-start.11 = (f32[128,512]{1,0:T(8,128)S(1)}, f32[128,512]{1,0:T(8,128)S(1)}, u32[]{:S(2)}, u32[]{:S(2)}) collective-permute-start(f32[128,512]{1,0:T(8,128)S(1)} %collective-permute-done.7.rest_5_), channel_id=1, source_target_pairs={{0,8},{8,0},{16,24},{24,16},{1,9},{9,1},{17,25},{25,17},{2,10},{10... | collective-permute-start | bytes 786440 | tf_op jit(solution)/shard_map/ppermute | solution.py:22
  24.6 2.1 %collective-permute-start.10 = (f32[128,512]{1,0:T(8,128)S(1)}, f32[128,512]{1,0:T(8,128)S(1)}, u32[]{:S(2)}, u32[]{:S(2)}) collective-permute-start(f32[128,512]{1,0:T(8,128)S(1)} %collective-permute-done.6.rest_4_), channel_id=1, source_target_pairs={{0,8},{8,0},{16,24},{24,16},{1,9},{9,1},{17,25},{25,17},{2,10},{10... | collective-permute-start | bytes 786440 | tf_op jit(solution)/shard_map/ppermute | solution.py:22
  33.3 6.4 %collective-permute-start.12 = (f32[1,64,512]{2,1,0:T(8,128)S(1)}, f32[1,64,512]{2,1,0:T(8,128)S(1)}, u32[]{:S(2)}, u32[]{:S(2)}) collective-permute-start(f32[1,64,512]{2,1,0:T(8,128)S(1)} %get-tuple-element.34), channel_id=1, source_target_pairs={{0,1},{1,0},{2,3},{3,2},{4,5},{5,4},{6,7},{7,6},{8,9},{9,8},{10,11... | collective-permute-start | bytes 393224 | tf_op jit(solution)/shard_map/ppermute | solution.py:22
  35.2 7.8 %collective-permute-start.14 = (f32[1,64,512]{2,1,0:T(8,128)S(1)}, f32[1,64,512]{2,1,0:T(8,128)S(1)}, u32[]{:S(2)}, u32[]{:S(2)}) collective-permute-start(f32[1,64,512]{2,1,0:T(8,128)S(1)} %get-tuple-element.36), channel_id=1, source_target_pairs={{0,1},{1,0},{2,3},{3,2},{4,5},{5,4},{6,7},{7,6},{8,9},{9,8},{10,11... | collective-permute-start | bytes 393224 | tf_op jit(solution)/shard_map/ppermute | solution.py:22
  35.4 11.1 %collective-permute-start.16 = (f32[1,64,512]{2,1,0:T(8,128)S(1)}, f32[1,64,512]{2,1,0:T(8,128)S(1)}, u32[]{:S(2)}, u32[]{:S(2)}) collective-permute-start(f32[1,64,512]{2,1,0:T(8,128)S(1)} %get-tuple-element.38), channel_id=1, source_target_pairs={{0,1},{1,0},{2,3},{3,2},{4,5},{5,4},{6,7},{7,6},{8,9},{9,8},{10,11... | collective-permute-start | bytes 393224 | tf_op jit(solution)/shard_map/ppermute | solution.py:22
  37.2 10.6 %collective-permute-start.18 = (f32[1,64,512]{2,1,0:T(8,128)S(1)}, f32[1,64,512]{2,1,0:T(8,128)S(1)}, u32[]{:S(2)}, u32[]{:S(2)}) collective-permute-start(f32[1,64,512]{2,1,0:T(8,128)S(1)} %get-tuple-element.40), channel_id=1, source_target_pairs={{0,1},{1,0},{2,3},{3,2},{4,5},{5,4},{6,7},{7,6},{8,9},{9,8},{10,11... | collective-permute-start | bytes 393224 | tf_op jit(solution)/shard_map/ppermute | solution.py:22
  37.4 15.7 %copy-start.1 = (f32[1,64,512]{2,1,0:T(8,128)S(1)}, f32[1,64,512]{2,1,0:T(8,128)}, u32[]{:S(2)}) copy-start(f32[1,64,512]{2,1,0:T(8,128)} %param.14) | copy-start | bytes 393220
  37.4 15.7 %copy-start.2 = (f32[512]{0:T(512)S(1)}, f32[512]{0:T(512)}, u32[]{:S(2)}) copy-start(f32[512]{0:T(512)} %param.16) | copy-start | bytes 6148
  37.4 15.7 %copy-start.6 = (f32[1,64]{1,0:T(1,128)S(1)}, f32[1,64]{1,0:T(1,128)}, u32[]{:S(2)}) copy-start(f32[1,64]{1,0:T(1,128)} %param.15) | copy-start | bytes 772
  39.8 11.9 %collective-permute-start.13 = (f32[1,64,512]{2,1,0:T(8,128)S(1)}, f32[1,64,512]{2,1,0:T(8,128)S(1)}, u32[]{:S(2)}, u32[]{:S(2)}) collective-permute-start(f32[1,64,512]{2,1,0:T(8,128)S(1)} %add.67), channel_id=1, source_target_pairs={{0,4},{1,5},{2,6},{3,7},{4,0},{5,1},{6,2},{7,3},{8,12},{9,13},{10,... | collective-permute-start | bytes 393224 | tf_op jit(solution)/shard_map/ppermute | solution.py:22
  43.0 8.7 %collective-permute-start.15 = (f32[1,64,512]{2,1,0:T(8,128)S(1)}, f32[1,64,512]{2,1,0:T(8,128)S(1)}, u32[]{:S(2)}, u32[]{:S(2)}) collective-permute-start(f32[1,64,512]{2,1,0:T(8,128)S(1)} %add.69), channel_id=1, source_target_pairs={{0,6},{1,7},{2,4},{3,5},{4,2},{5,3},{6,0},{7,1},{8,14},{9,15},{10,... | collective-permute-start | bytes 393224 | tf_op jit(solution)/shard_map/ppermute | solution.py:22
  46.6 6.6 %collective-permute-start.17 = (f32[1,64,512]{2,1,0:T(8,128)S(1)}, f32[1,64,512]{2,1,0:T(8,128)S(1)}, u32[]{:S(2)}, u32[]{:S(2)}) collective-permute-start(f32[1,64,512]{2,1,0:T(8,128)S(1)} %add.71), channel_id=1, source_target_pairs={{0,2},{1,3},{2,0},{3,1},{4,6},{5,7},{6,4},{7,5},{8,10},{9,11},{10,... | collective-permute-start | bytes 393224 | tf_op jit(solution)/shard_map/ppermute | solution.py:22

commit v3 on v2

v3 whole, which is shorter than its diff:
```python
import functools

import jax
import jax.numpy as jnp
from jax import lax
from jax.experimental import pallas as pl
from jax.experimental.pallas import tpu as pltpu
from jax.sharding import PartitionSpec as P

LANES = 128
MIB = 1024 * 1024
VMEM = pl.BlockSpec(memory_space=pltpu.VMEM)


def split(x):
    hi = x.astype(jnp.bfloat16)
    return hi, (x - hi.astype(jnp.float32)).astype(jnp.bfloat16)


def swap(x, axis, k):
    n = lax.axis_size(axis)
    return lax.ppermute(x, axis, [(i, i ^ k) for i in range(n)])


def after(x, *others):
    return lax.optimization_barrier((x, *others))[0]


def tile_order(lanes):
    side = list(range(lanes // 2, lanes, 2)) + list(range(lanes // 2 - 2, -1, -2))
    return [k + 1 for k in side], side


def row_cuts(depth):
    end = depth * 9 // 32 // 16 * 16
    return end, depth - 2 * end


def end_offsets(depth):
    low = lax.axis_index("wide") & 1
    last = depth - row_cuts(depth)[0]
    return pl.multiple_of(low * last, 16), pl.multiple_of(last - low * last, 16)


def prepare_kernel(*refs):
    count_ref, small, own_hbm = refs[0], refs[1:7], refs[7]
    one_ref, two_ref, lists_ref, table_ref = refs[8:12]
    (amp, cint, res, amp_label, owner, int_label), sems = refs[12:18], refs[18]
    end, middle = one_ref.shape[0], two_ref.shape[0]
    mine, _ = end_offsets(own_hbm.shape[0])
    moves = list(zip(small, refs[12:18]))
    moves.append((own_hbm.at[pl.ds(mine, end), :], one_ref))
    moves.append((own_hbm.at[pl.ds(end, middle), :], two_ref))
    copies = [pltpu.make_async_copy(a, b, sems.at[i]) for i, (a, b) in enumerate(moves)]
    for copy in copies:
        copy.start()
    table_ref[...] = jnp.zeros(table_ref.shape, jnp.int32)
    for copy in copies:
        copy.wait()
    slot = lax.broadcasted_iota(jnp.int32, amp.shape, 1)
    lists_ref[0] = amp[...]
    lists_ref[1] = cint[...]
    lists_ref[2] = jnp.where(slot < count_ref[0], res[...], -1)
    for i, ref in enumerate((amp_label, owner, int_label)):
        table_ref[i : i + 1, 0 : ref.shape[1]] = ref[...]


def prepare(task_amp, task_int, task_res, task_count, amp_label, owner, int_label, own):
    pieces = [pltpu.VMEM((n, own.shape[1]), own.dtype) for n in row_cuts(own.shape[0])]
    args = [task_amp, task_int, task_res, amp_label[None, :], owner, int_label[None, :], own]
    return pl.pallas_call(
        prepare_kernel,
        out_shape=[
            *pieces,
            pltpu.VMEM((3,) + task_amp.shape, jnp.int32),
            pltpu.VMEM((3, LANES), jnp.int32),
        ],
        in_specs=[pl.BlockSpec(memory_space=pltpu.SMEM)] + [pl.BlockSpec(memory_space=pltpu.HBM)] * 7,
        out_specs=[VMEM] * 4,
        scratch_shapes=[pltpu.VMEM(x.shape, x.dtype) for x in args[:6]]
        + [pltpu.SemaphoreType.DMA((8,))],
        compiler_params=pltpu.CompilerParams(vmem_limit_bytes=8 * MIB),
        cost_estimate=pl.CostEstimate(flops=0, bytes_accessed=own.size * 4, transcendentals=0),
        name="prepare",
    )(task_count, *[pltpu.with_memory_space_constraint(x, pltpu.HBM) for x in args])


def load_kernel(amp_hbm, amp_ref, sems):
    n = sems.shape[0]
    step = amp_ref.shape[0] // n
    copies = [
        pltpu.make_async_copy(
            amp_hbm.at[pl.ds(i * step, step)], amp_ref.at[pl.ds(i * step, step)], sems.at[i]
        )
        for i in range(n)
    ]
    for copy in copies:
        copy.start()
    for copy in copies:
        copy.wait()


def load(amplitudes):
    size = amplitudes.size * 4
    return pl.pallas_call(
        load_kernel,
        out_shape=pltpu.VMEM(amplitudes.shape, amplitudes.dtype),
        in_specs=[pl.BlockSpec(memory_space=pltpu.HBM)],
        out_specs=VMEM,
        scratch_shapes=[pltpu.SemaphoreType.DMA((4,))],
        compiler_params=pltpu.CompilerParams(vmem_limit_bytes=size + MIB),
        cost_estimate=pl.CostEstimate(flops=0, bytes_accessed=2 * size, transcendentals=0),
        name="load_amplitudes",
    )(pltpu.with_memory_space_constraint(amplitudes, pltpu.HBM))


def coefficients(lists_ref, table_ref, amp_dev, lanes, blocks):
    lane = lax.axis_index("wide")
    grp = lax.axis_index("grp")
    amp, cint, res = (lists_ref[i] for i in range(3))
    local = amp - lane * amp_dev
    valid = (res >= 0) & (local >= 0) & (local < amp_dev)
    away, side = tile_order(lanes)
    pos = jnp.zeros_like(res)
    for p in range(lanes):
        pos = jnp.where(res == table_ref[1:2, p : p + 1], p, pos)
    offset = pos ^ lane
    place = jnp.zeros_like(res)
    for j, k in enumerate(away + side):
        place = jnp.where(offset == k, j, place)
    seg = jnp.where(valid, place * blocks + (cint ^ grp), -1)
    rows = lanes * blocks
    row_id = lax.broadcasted_iota(jnp.int32, (rows, amp.shape[1]), 0)
    col_id = lax.broadcasted_iota(jnp.int32, (LANES, amp.shape[1]), 0)
    counts = jnp.zeros((rows, LANES), jnp.float32)
    for src in range(lanes):
        hit_row = jnp.where(row_id == seg[src : src + 1, :], 1.0, 0.0)
        hit_col = jnp.where(col_id == local[src : src + 1, :], 1.0, 0.0)
        counts += lax.dot_general(
            hit_row.astype(jnp.bfloat16),
            hit_col.astype(jnp.bfloat16),
            (((1,), (1,)), ((), ())),
            preferred_element_type=jnp.float32,
        )
    row = lax.broadcasted_iota(jnp.int32, (rows, LANES), 0)
    block = (row & (blocks - 1)) ^ grp
    label = jnp.zeros((rows, LANES), jnp.int32)
    for c in range(blocks):
        label = jnp.where(block == c, table_ref[2:3, c : c + 1], label)
    odd = (label + table_ref[0:1, :]) & 1
    weight = jnp.where(odd == 1, -counts, counts)
    col = lax.broadcasted_iota(jnp.int32, (rows, LANES), 1)
    follow = jnp.where(counts > 0.5, col, LANES)
    step = 1
    while step < amp_dev:
        follow = jnp.minimum(follow, pltpu.roll(follow, LANES - step, 1))
        step *= 2
    return weight, follow


def passes(hi, lo, in_hi, in_lo):
    dot = functools.partial(jnp.dot, preferred_element_type=jnp.float32)
    return dot(hi, in_hi[...]) + dot(hi, in_lo[...]) + dot(lo, in_hi[...])


def sums_kernel(lanes, blocks, lists_ref, table_ref, amp_ref, *rest):
    st_hi, st_lo, weight_v, follow_v, weight_s, follow_s, sems = rest
    amp_dev, tile_rows, depth = amp_ref.shape
    weight, follow = coefficients(lists_ref, table_ref, amp_dev, lanes, blocks)
    weight_v[...] = weight
    follow_v[...] = follow
    moves = [
        pltpu.make_async_copy(weight_v, weight_s, sems.at[0]),
        pltpu.make_async_copy(follow_v, follow_s, sems.at[1]),
    ]
    for copy in moves:
        copy.start()
    for copy in moves:
        copy.wait()

    def stack(j, _):
        for c in range(blocks):
            s = j * blocks + c

            def more(carry):
                return carry[0] < amp_dev

            def add(carry, s=s):
                a, total = carry
                return follow_s[s, a + 1], total + weight_s[s, a] * amp_ref[a]

            _, total = lax.while_loop(
                more, add, (follow_s[s, 0], jnp.zeros((tile_rows, depth), jnp.float32))
            )
            hi, lo = split(total)
            at = pl.ds(pl.multiple_of(j * tile_rows, tile_rows), tile_rows)
            st_hi[at, c * depth : (c + 1) * depth] = hi
            st_lo[at, c * depth : (c + 1) * depth] = lo
        return 0

    lax.fori_loop(0, lanes, stack, 0)


def local_kernel(st_hi, st_lo, own_ref, pair_ref, local_ref, in_hi, in_lo):
    depth = own_ref.shape[0]
    for c, ref in enumerate((own_ref, pair_ref)):
        hi, lo = split(ref[...])
        in_hi[c * depth : (c + 1) * depth, :] = hi
        in_lo[c * depth : (c + 1) * depth, :] = lo
    local_ref[...] = passes(st_hi[:, : 2 * depth], st_lo[:, : 2 * depth], in_hi, in_lo)


def add_remote(st_hi, st_lo, local_ref, in_hi, in_lo, first, out_refs):
    tile_rows = out_refs[0].shape[1]
    remote = in_hi.shape[0]
    at = slice(first * tile_rows, (first + len(out_refs)) * tile_rows)
    lead = st_hi.shape[1] - remote
    out = local_ref[at, :] + passes(st_hi[at, lead:], st_lo[at, lead:], in_hi, in_lo)
    for i, ref in enumerate(out_refs):
        ref[0] = out[i * tile_rows : (i + 1) * tile_rows]


def first_kernel(blocks, st_hi, st_lo, local_ref, *rest):
    parts, rest = rest[: 3 * (blocks - 2)], rest[3 * (blocks - 2) :]
    out_refs, (in_hi, in_lo) = rest[:-2], rest[-2:]
    depth = in_hi.shape[0] // (blocks - 2)
    mine, theirs = end_offsets(depth)
    for c in range(blocks - 2):
        starts = (mine, row_cuts(depth)[0], theirs)
        for start, part in zip(starts, parts[3 * c : 3 * c + 3]):
            hi, lo = split(part[...])
            at = pl.ds(pl.multiple_of(c * depth + start, 16), part.shape[0])
            in_hi[at, :] = hi
            in_lo[at, :] = lo
    add_remote(st_hi, st_lo, local_ref, in_hi, in_lo, 0, out_refs)


def second_kernel(first, st_hi, st_lo, local_ref, in_hi, in_lo, *out_refs):
    add_remote(st_hi, st_lo, local_ref, in_hi, in_lo, first, out_refs)


def limit(n):
    return pltpu.CompilerParams(vmem_limit_bytes=min(n + 12 * MIB, 56 * MIB))


def sums(lists, table, amplitudes, lanes, blocks):
    amp_dev, tile_rows, depth = amplitudes.shape
    rows = lanes * blocks
    held = pltpu.VMEM((lanes * tile_rows, blocks * depth), jnp.bfloat16)
    return pl.pallas_call(
        functools.partial(sums_kernel, lanes, blocks),
        out_shape=[held, held],
        in_specs=[VMEM] * 3,
        out_specs=[VMEM] * 2,
        scratch_shapes=[
            pltpu.VMEM((rows, LANES), jnp.float32),
            pltpu.VMEM((rows, LANES), jnp.int32),
            pltpu.SMEM((rows, LANES), jnp.float32),
            pltpu.SMEM((rows, LANES), jnp.int32),
            pltpu.SemaphoreType.DMA((2,)),
        ],
        compiler_params=limit(amplitudes.size * 4),
        cost_estimate=pl.CostEstimate(
            flops=0, bytes_accessed=4 * amplitudes.size, transcendentals=0
        ),
        name="sums",
    )(lists, table, pltpu.with_memory_space_constraint(amplitudes, pltpu.VMEM))


def local_products(held, own, pair):
    depth, window = own.shape
    rows = held[0].shape[0]
    half = pltpu.VMEM((2 * depth, window), jnp.bfloat16)
    return pl.pallas_call(
        local_kernel,
        out_shape=pltpu.VMEM((rows, window), jnp.float32),
        in_specs=[VMEM] * 4,
        out_specs=VMEM,
        scratch_shapes=[half, half],
        compiler_params=limit(16 * depth * window),
        cost_estimate=pl.CostEstimate(
            flops=12 * rows * depth * window, bytes_accessed=0, transcendentals=0
        ),
        name="local_products",
    )(*[pltpu.with_memory_space_constraint(x, pltpu.VMEM) for x in held], own, pair)


def add_products(held, parts, lanes, tile_rows):
    blocks = 2 + len(parts)
    depth = held[0].shape[1] // blocks
    window = held[2].shape[1]
    tile = jax.ShapeDtypeStruct((1, tile_rows, window), jnp.float32)
    remote = pltpu.VMEM(((blocks - 2) * depth, window), jnp.bfloat16)
    first = lanes // 2 + 1
    held = [pltpu.with_memory_space_constraint(x, pltpu.VMEM) for x in held]

    def cost(n):
        return pl.CostEstimate(
            flops=6 * n * tile_rows * (blocks - 2) * depth * window,
            bytes_accessed=4 * n * tile_rows * window,
            transcendentals=0,
        )

    *tiles, in_hi, in_lo = pl.pallas_call(
        functools.partial(first_kernel, blocks),
        out_shape=[tile] * first + [remote] * 2,
        in_specs=[VMEM] * (3 + 3 * len(parts)),
        out_specs=[VMEM] * (first + 2),
        compiler_params=limit(4 * blocks * depth * window),
        cost_estimate=cost(first),
        name="first_products",
    )(*held, *[x for three in parts for x in three])
    packed = [pltpu.with_memory_space_constraint(x, pltpu.VMEM) for x in (in_hi, in_lo)]
    others = pl.pallas_call(
        functools.partial(second_kernel, first),
        out_shape=[tile] * (lanes - first),
        in_specs=[VMEM] * 5,
        out_specs=[VMEM] * (lanes - first),
        compiler_params=limit(0),
        cost_estimate=cost(lanes - first),
        name="second_products",
    )(*held, *packed)
    return [*tiles, *others]


def on_device(
    amplitudes,
    integrals,
    base_residual,
    occ_gap,
    virt_sum,
    task_amp,
    task_int,
    task_res,
    task_count,
    res_owner,
    amp_label,
    int_label,
):
    lanes = lax.axis_size("wide")
    grps = lax.axis_size("grp")
    own = integrals[0]
    one, two, lists, table = prepare(
        task_amp, task_int, task_res, task_count, amp_label, res_owner, int_label, own
    )
    fetched = {k: [swap(x, "grp", k) for x in (one, two)] for k in range(2, grps, 2)}
    amplitudes = load(amplitudes)
    k = 1
    while k < lanes:
        if k == 2:
            lists = after(lists, amplitudes)
        lists = jnp.concatenate([lists, swap(lists, "wide", k)], axis=1)
        k *= 2
    pair = swap(own, "grp", 1)
    held = sums(lists, table, amplitudes, lanes, grps)

    parts = [None] * (grps - 2)
    for k, (one, two) in fetched.items():
        three = [one, two, swap(one, "wide", 1)]
        parts[k - 2] = three
        parts[k - 1] = [swap(after(x, y), "grp", 1) for x, y in zip(three, (lists, held[0], held[0]))]

    held = [*held, local_products(held, own, pair)]
    tiles = add_products(held, parts, lanes, amplitudes.shape[1])
    _, offsets = tile_order(lanes)
    got = [swap(x, "wide", 1) for x in tiles[: lanes // 2]]
    summed = base_residual
    for k, here, there in zip(offsets, tiles[lanes // 2 :], got):
        part = here + there
        summed = summed + (swap(part, "wide", k) if k else part)
    divisor = occ_gap[:, :, None] + virt_sum[None, None, :]
    return summed / divisor


def solution(mesh):
    return jax.shard_map(
        on_device,
        mesh=mesh,
        in_specs=(
            P(("grp", "wide"), None, None),
            P("grp", None, None),
            P(("grp", "wide"), None, None),
            P(("grp", "wide"), None),
            P(),
            P(("grp", "wide"), None),
            P(("grp", "wide"), None),
            P(("grp", "wide"), None),
            P(("grp", "wide")),
            P("grp", None),
            P(("grp", "wide")),
            P(),
        ),
        out_specs=P(("grp", "wide"), None, None),
        check_vma=False,
    )
```

time: 54.1 us -> 48 us (0.89)
  waiting for transfers between devices: 14.7 us -> 11.4 us
  starting transfers between devices: 25 us -> 23.8 us
  local copies, waits for them, and re-layouts: 1.12 us -> 0.02 us
  other arithmetic: 1.54 us -> 0.84 us
    ppermute x19 -> x17, waiting for transfers between devices: 14.7 us -> 11.4 us  [swap(): return lax.ppermute(x, axis, [(i, i ^ k) for i in range(n)])]
    ppermute x19 -> x17, starting transfers between devices: 25 us -> 23.8 us  [swap(): return lax.ppermute(x, axis, [(i, i ^ k) for i in range(n)])]
    dynamic_slice x1 -> x0, local copies, waits for them, and re-layouts: 1.06 us -> none  [on_device(): lax.dynamic_slice_in_dim(own, ids[i] * quarter, quarter, 0)]
    another operation x2 -> x0, other arithmetic: 0.71 us -> none  [the longest x1 0.7 us: on_device(): jnp.stack([task_amp, task_int, task_res, jnp.broadcast_to(task_count[:, N...]
    pallas_call x2 -> x5, Pallas kernels: 8.44 us -> 8.56 us  [the longest x1 3.34 us: sums(): pl.pallas_call(functools.partial(sums_kernel, lanes, blocks), out_shape=[...]
  transfers between devices with their start and end apart: 19 -> 17, of which waited for: 10 -> 6; matrix products, arithmetic and copies ran while one was open for 3% -> 0% of each run, Pallas kernels for 7% -> 20%
where the time goes in v3:
time: 48 us; the launch traced here: 47.6 us
  starting transfers between devices  23.8 us (50%)
  waiting for transfers between devices  11.4 us (24%)
  Pallas kernels  10.8 us (22%)
  other arithmetic  0.84 us (2%)
  between operations  0.78 us (2%)
    ppermute x17, starting transfers between devices, swap(): return lax.ppermute(x, axis, [(i, i ^ k) for i in range(n)])  23.8 us
    ppermute x17, waiting for transfers between devices, swap(): return lax.ppermute(x, axis, [(i, i ^ k) for i in range(n)])  11.4 us
    pallas_call x1, Pallas kernels, sums(): pl.pallas_call(functools.partial(sums_kernel, lanes, blocks), out_shape=[...  3.34 us
    pallas_call x1, Pallas kernels, load(): pl.pallas_call(load_kernel, out_shape=pltpu.VMEM(amplitudes.shape, amplit...  2.2 us
    pallas_call x1, Pallas kernels, local_products(): pl.pallas_call(local_kernel, out_shape=pltpu.VMEM((rows, window), jnp.flo...  1.81 us
    pallas_call x1, Pallas kernels, add_products(): pl.pallas_call(functools.partial(first_kernel, blocks), out_shape=[tile]...  1.35 us
    pallas_call x1, Pallas kernels, prepare(): pl.pallas_call(prepare_kernel, out_shape=[*pieces, pltpu.VMEM((3,) + task...  1.28 us
  transfers between devices with their start and end apart: 17, of which 6 were waited for; matrix products, arithmetic and copies ran while one was open for 0% of the time, Pallas kernels for 20%

profile of v3, /device:TPU:0, one launch (start us, length us, event | category | flops | bytes accessed | tf_op | source)
XLA Modules:
  0.0 47.6 jit_solution(11942562184082567399)
XLA Ops:
  0.0 0.5 collective-permute-start.3
  1.1 1.3 %prepare.1 = (f32[144,512]{1,0:T(8,128)S(1)}, f32[224,512]{1,0:T(8,128)S(1)}, s32[3,1,96]{2,1,0:T(1,128)S(1)}, s32[3,128]{1,0:T(4,128)S(1)}) custom-call(s32[1]{0:T(128)S(6)} %copy.13.refs_0_, s32[1,96]{1,0:T(1,128)} %refs_1_.1, s32[1,96]{1,0:T(1,128)} %refs_2_.1, s32[1,96]{1,0:T(1,128)} %refs_3_.1, s32[1,32]{1,0:T(1,128)} %bitcast.7, s32[1,8]{1,0:T(1,128)} %refs_5_.1, ...), custom_call_target="tpu_custom_call" | custom-call | bytes 1048576 | tf_op jit(solution)/shard_map/prepare/pallas_call | solution.py:71
  2.4 2.6 %collective-permute-start.4 = (f32[144,512]{1,0:T(8,128)S(1)}, f32[144,512]{1,0:T(8,128)S(1)}, u32[]{:S(2)}, u32[]{:S(2)}) collective-permute-start(f32[144,512]{1,0:T(8,128)S(1)} %get-tuple-element.30), channel_id=1, source_target_pairs={{0,16},{8,24},{16,0},{24,8},{1,17},{9,25},{17,1},{25,9},{2,18},{10... | collective-permute-start | bytes 884744 | tf_op jit(solution)/shard_map/ppermute | solution.py:22
  4.9 0.1 collective-permute-start.5
  5.0 2.0 %collective-permute-start = (s32[3,1,96]{2,1,0:T(1,128)S(1)}, s32[3,1,96]{2,1,0:T(1,128)S(1)}, u32[]{:S(2)}, u32[]{:S(2)}) collective-permute-start(s32[3,1,96]{2,1,0:T(1,128)S(1)} %get-tuple-element.25), channel_id=1, source_target_pairs={{0,1},{1,0},{2,3},{3,2},{4,5},{5,4},{6,7},{7,6},{8,9},{9,8},{10,11... | collective-permute-start | bytes 3464 | tf_op jit(solution)/shard_map/ppermute | solution.py:22
  7.0 2.2 %load_amplitudes.1.amp_ref = f32[32,64,512]{2,1,0:T(8,128)S(1)} custom-call(f32[32,64,512]{2,1,0:T(8,128)} %amp_hbm.1), custom_call_target="tpu_custom_call" | custom-call | bytes 8388608 | tf_op jit(solution)/shard_map/load_amplitudes/pallas_call | solution.py:105
  9.2 0.0 copy-start
  9.2 0.0 collective-permute-done
  9.3 1.6 %collective-permute-start.1 = (s32[3,2,96]{2,1,0:T(2,128)S(1)}, s32[3,2,96]{2,1,0:T(2,128)S(1)}, u32[]{:S(2)}, u32[]{:S(2)}) collective-permute-start(s32[3,2,96]{2,1,0:T(2,128)S(1)} %pad_add_fusion.2), channel_id=1, source_target_pairs={{0,2},{1,3},{2,0},{3,1},{4,6},{5,7},{6,4},{7,5},{8,10},{9,11},{10,... | collective-permute-start | bytes 6920 | tf_op jit(solution)/shard_map/ppermute | solution.py:22
  10.9 1.9 %collective-permute-done.4.rest_0_ = f32[144,512]{1,0:T(8,128)S(1)} collective-permute-done((f32[144,512]{1,0:T(8,128)S(1)}, f32[144,512]{1,0:T(8,128)S(1)}, u32[]{:S(2)}, u32[]{:S(2)}) %collective-permute-start.4) | collective-permute-done | bytes 294944 | tf_op jit(solution)/shard_map/ppermute | solution.py:22
  12.8 2.0 %collective-permute-start.6 = (f32[144,512]{1,0:T(8,128)S(1)}, f32[144,512]{1,0:T(8,128)S(1)}, u32[]{:S(2)}, u32[]{:S(2)}) collective-permute-start(f32[144,512]{1,0:T(8,128)S(1)} %collective-permute-done.4.rest_0_), channel_id=1, source_target_pairs={{0,1},{1,0},{2,3},{3,2},{4,5},{5,4},{6,7},{7,6},{8,9},{9,8},{10,11... | collective-permute-start | bytes 884744 | tf_op jit(solution)/shard_map/ppermute | solution.py:22
  14.8 0.0 collective-permute-done.1
  14.8 2.7 %collective-permute-start.2 = (s32[3,4,96]{2,1,0:T(4,128)S(1)}, s32[3,4,96]{2,1,0:T(4,128)S(1)}, u32[]{:S(2)}, u32[]{:S(2)}) collective-permute-start(s32[3,4,96]{2,1,0:T(4,128)S(1)} %pad_add_fusion.1), channel_id=1, source_target_pairs={{0,4},{1,5},{2,6},{3,7},{4,0},{5,1},{6,2},{7,3},{8,12},{9,13},{10,... | collective-permute-start | bytes 13832 | tf_op jit(solution)/shard_map/ppermute | solution.py:22
  17.4 1.9 %collective-permute-done.2 = s32[3,4,96]{2,1,0:T(4,128)S(1)} collective-permute-done((s32[3,4,96]{2,1,0:T(4,128)S(1)}, s32[3,4,96]{2,1,0:T(4,128)S(1)}, u32[]{:S(2)}, u32[]{:S(2)}) %collective-permute-start.2) | collective-permute-done | bytes 4640 | tf_op jit(solution)/shard_map/ppermute | solution.py:22
  19.4 3.3 %sums.1 = (bf16[512,2048]{1,0:T(8,128)(2,1)S(1)}, bf16[512,2048]{1,0:T(8,128)(2,1)S(1)}) custom-call(s32[3,8,96]{2,1,0:T(8,128)S(1)} %pad_add_fusion.lists_ref, s32[3,128]{1,0:T(4,128)S(1)} %get-tuple-element.27.table_ref, f32[32,64,512]{2,1,0:T(8,128)S(1)} %load_amplitudes.1.amp_ref), custom_call_target="tpu_custom_call" | custom-call | bytes 4194304 | tf_op jit(solution)/shard_map/sums/pallas_call | solution.py:250
  22.7 0.0 collective-permute-done.5.rest_1_
  22.8 0.1 collective-permute-start.8
  22.8 0.5 %collective-permute-start.7 = (f32[144,512]{1,0:T(8,128)S(1)}, f32[144,512]{1,0:T(8,128)S(1)}, u32[]{:S(2)}, u32[]{:S(2)}) collective-permute-start(f32[144,512]{1,0:T(8,128)S(1)} %collective-permute-done.4.rest_0_), channel_id=1, source_target_pairs={{0,8},{8,0},{16,24},{24,16},{1,9},{9,1},{17,25},{25,17},{2,10},{10... | collective-permute-start | bytes 884744 | tf_op jit(solution)/shard_map/ppermute | solution.py:22
  23.3 0.0 collective-permute-done.6.rest_2_
  23.3 0.1 collective-permute-start.9
  23.4 0.0 collective-permute-done.3.pair_ref
  23.4 0.0 copy-done
  23.4 1.8 %local_products.1.local_ref = f32[512,512]{1,0:T(8,128)S(1)} custom-call(bf16[512,2048]{1,0:T(8,128)(2,1)S(1)} %get-tuple-element.28.st_hi, bf16[512,2048]{1,0:T(8,128)(2,1)S(1)} %get-tuple-element.29.st_lo, f32[512,512]{1,0:T(8,128)S(1)} %bitcast.6, f32[512,512]{1,0:T(8,128)S(1)} %collective-permute-done.3.pair_ref), custom_call_target="tpu_custom_call" | custom-call | flops 1610612736 | tf_op jit(solution)/shard_map/local_products/pallas_call | solution.py:274
  25.2 0.0 collective-permute-done.7.rest_3_
  25.2 0.2 collective-permute-done.9.rest_5_
  25.5 0.0 collective-permute-done.8.rest_4_
  25.5 1.3 %first_products.1 = (f32[1,64,512]{2,1,0:T(8,128)S(1)}, f32[1,64,512]{2,1,0:T(8,128)S(1)}, f32[1,64,512]{2,1,0:T(8,128)S(1)}, f32[1,64,512]{2,1,0:T(8,128)S(1)},...) custom-call(bf16[512,2048]{1,0:T(8,128)(2,1)S(1)} %get-tuple-element.28.st_hi, ...), custom_call_target="tpu_custom_call" | custom-call | flops 1006632960 | bytes 655360 | tf_op jit(solution)/shard_map/first_products/pallas_call | solution.py:304
  26.8 1.5 %collective-permute-start.10 = (f32[1,64,512]{2,1,0:T(8,128)S(1)}, f32[1,64,512]{2,1,0:T(8,128)S(1)}, u32[]{:S(2)}, u32[]{:S(2)}) collective-permute-start(f32[1,64,512]{2,1,0:T(8,128)S(1)} %get-tuple-element.36), channel_id=1, source_target_pairs={{0,1},{1,0},{2,3},{3,2},{4,5},{5,4},{6,7},{7,6},{8,9},{9,8},{10,11... | collective-permute-start | bytes 393224 | tf_op jit(solution)/shard_map/ppermute | solution.py:22
  28.3 0.6 %collective-permute-start.12 = (f32[1,64,512]{2,1,0:T(8,128)S(1)}, f32[1,64,512]{2,1,0:T(8,128)S(1)}, u32[]{:S(2)}, u32[]{:S(2)}) collective-permute-start(f32[1,64,512]{2,1,0:T(8,128)S(1)} %get-tuple-element.40), channel_id=1, source_target_pairs={{0,1},{1,0},{2,3},{3,2},{4,5},{5,4},{6,7},{7,6},{8,9},{9,8},{10,11... | collective-permute-start | bytes 393224 | tf_op jit(solution)/shard_map/ppermute | solution.py:22
  28.9 1.4 %collective-permute-start.14 = (f32[1,64,512]{2,1,0:T(8,128)S(1)}, f32[1,64,512]{2,1,0:T(8,128)S(1)}, u32[]{:S(2)}, u32[]{:S(2)}) collective-permute-start(f32[1,64,512]{2,1,0:T(8,128)S(1)} %get-tuple-element.42), channel_id=1, source_target_pairs={{0,1},{1,0},{2,3},{3,2},{4,5},{5,4},{6,7},{7,6},{8,9},{9,8},{10,11... | collective-permute-start | bytes 393224 | tf_op jit(solution)/shard_map/ppermute | solution.py:22
  30.3 0.6 %collective-permute-start.16 = (f32[1,64,512]{2,1,0:T(8,128)S(1)}, f32[1,64,512]{2,1,0:T(8,128)S(1)}, u32[]{:S(2)}, u32[]{:S(2)}) collective-permute-start(f32[1,64,512]{2,1,0:T(8,128)S(1)} %get-tuple-element.44), channel_id=1, source_target_pairs={{0,1},{1,0},{2,3},{3,2},{4,5},{5,4},{6,7},{7,6},{8,9},{9,8},{10,11... | collective-permute-start | bytes 393224 | tf_op jit(solution)/shard_map/ppermute | solution.py:22
  31.0 0.0 copy-start.1
  31.0 0.0 copy-start.2
  31.0 0.8 %second_products.1 = (f32[1,64,512]{2,1,0:T(8,128)S(1)}, f32[1,64,512]{2,1,0:T(8,128)S(1)}, f32[1,64,512]{2,1,0:T(8,128)S(1)}) custom-call(bf16[512,2048]{1,0:T(8,128)(2,1)S(1)} %get-tuple-element.28.st_hi, bf16[512,2048]{1,0:T(8,128)(2,1)S(1)} %get-tuple-element.29.st_lo, f32[512,512]{1,0:T(8,128)S(1)} %local_products.1.local_ref, ...), custom_call_target="tpu_custom_call" | custom-call | flops 603979776 | bytes 393216 | tf_op jit(solution)/shard_map/second_products/pallas_call | solution.py:314
  31.8 1.5 %collective-permute-done.10 = f32[1,64,512]{2,1,0:T(8,128)S(1)} collective-permute-done((f32[1,64,512]{2,1,0:T(8,128)S(1)}, f32[1,64,512]{2,1,0:T(8,128)S(1)}, u32[]{:S(2)}, u32[]{:S(2)}) %collective-permute-start.10) | collective-permute-done | bytes 131104 | tf_op jit(solution)/shard_map/ppermute | solution.py:22
  33.3 3.2 %collective-permute-start.11 = (f32[1,64,512]{2,1,0:T(8,128)S(1)}, f32[1,64,512]{2,1,0:T(8,128)S(1)}, u32[]{:S(2)}, u32[]{:S(2)}) collective-permute-start(f32[1,64,512]{2,1,0:T(8,128)S(1)} %add.45), channel_id=1, source_target_pairs={{0,4},{1,5},{2,6},{3,7},{4,0},{5,1},{6,2},{7,3},{8,12},{9,13},{10,... | collective-permute-start | bytes 393224 | tf_op jit(solution)/shard_map/ppermute | solution.py:22
  36.5 0.0 collective-permute-done.12
  36.5 3.3 %collective-permute-start.13 = (f32[1,64,512]{2,1,0:T(8,128)S(1)}, f32[1,64,512]{2,1,0:T(8,128)S(1)}, u32[]{:S(2)}, u32[]{:S(2)}) collective-permute-start(f32[1,64,512]{2,1,0:T(8,128)S(1)} %add.47), channel_id=1, source_target_pairs={{0,6},{1,7},{2,4},{3,5},{4,2},{5,3},{6,0},{7,1},{8,14},{9,15},{10,... | collective-permute-start | bytes 393224 | tf_op jit(solution)/shard_map/ppermute | solution.py:22
  39.8 0.0 collective-permute-done.14
  39.8 1.2 %collective-permute-start.15 = (f32[1,64,512]{2,1,0:T(8,128)S(1)}, f32[1,64,512]{2,1,0:T(8,128)S(1)}, u32[]{:S(2)}, u32[]{:S(2)}) collective-permute-start(f32[1,64,512]{2,1,0:T(8,128)S(1)} %add.49), channel_id=1, source_target_pairs={{0,2},{1,3},{2,0},{3,1},{4,6},{5,7},{6,4},{7,5},{8,10},{9,11},{10,... | collective-permute-start | bytes 393224 | tf_op jit(solution)/shard_map/ppermute | solution.py:22
  41.0 0.0 collective-permute-done.16
  41.0 4.6 %collective-permute-done.11 = f32[1,64,512]{2,1,0:T(8,128)S(1)} collective-permute-done((f32[1,64,512]{2,1,0:T(8,128)S(1)}, f32[1,64,512]{2,1,0:T(8,128)S(1)}, u32[]{:S(2)}, u32[]{:S(2)}) %collective-permute-start.11) | collective-permute-done | bytes 131104 | tf_op jit(solution)/shard_map/ppermute | solution.py:22
  45.6 0.0 collective-permute-done.13
  45.6 1.2 %collective-permute-done.15 = f32[1,64,512]{2,1,0:T(8,128)S(1)} collective-permute-done((f32[1,64,512]{2,1,0:T(8,128)S(1)}, f32[1,64,512]{2,1,0:T(8,128)S(1)}, u32[]{:S(2)}, u32[]{:S(2)}) %collective-permute-start.15) | collective-permute-done | bytes 131104 | tf_op jit(solution)/shard_map/ppermute | solution.py:22
  46.8 0.0 copy-done.1
  46.8 0.0 copy-done.2
  46.8 0.0 copy-done.3
  46.8 0.8 %add_divide_fusion = f32[1,64,512]{2,1,0:T(8,128)} fusion(f32[1,64,512]{2,1,0:T(8,128)S(1)} %get-tuple-element.43, f32[1,64,512]{2,1,0:T(8,128)S(1)} %collective-permute-done.16, f32[1,64,512]{2,1,0:T(8,128)S(1)} %collective-permute-done.15, f32[1,64,512]{2,1,0:T(8,128)S(1)} %collective-permute-done.13, f32[1,64,512]{2,1,0:T(8,128)S(1)} %copy-done.1, ...), kind=kLoop, calls=%fused_computation | loop fusion | flops 229376 | bytes 919808 | tf_op jit(solution)/shard_map/div | solution.py:372
  (7 shorter events, 0.1 us)
Async XLA Ops:
  0.0 23.4 %collective-permute-start.3 = (f32[512,512]{1,0:T(8,128)}, f32[512,512]{1,0:T(8,128)S(1)}, u32[]{:S(2)}, u32[]{:S(2)}) collective-permute-start(f32[512,512]{1,0:T(8,128)} %bitcast.4), channel_id=1, source_target_pairs={{0,8},{8,0},{16,24},{24,16},{1,9},{9,1},{17,25},{25,17},{2,10},{10... | collective-permute-start | bytes 3145736 | tf_op jit(solution)/shard_map/ppermute | solution.py:22
  2.4 10.4 %collective-permute-start.4 = (f32[144,512]{1,0:T(8,128)S(1)}, f32[144,512]{1,0:T(8,128)S(1)}, u32[]{:S(2)}, u32[]{:S(2)}) collective-permute-start(f32[144,512]{1,0:T(8,128)S(1)} %get-tuple-element.30), channel_id=1, source_target_pairs={{0,16},{8,24},{16,0},{24,8},{1,17},{9,25},{17,1},{25,9},{2,18},{10... | collective-permute-start | bytes 884744 | tf_op jit(solution)/shard_map/ppermute | solution.py:22
  4.9 17.8 %collective-permute-start.5 = (f32[224,512]{1,0:T(8,128)S(1)}, f32[224,512]{1,0:T(8,128)S(1)}, u32[]{:S(2)}, u32[]{:S(2)}) collective-permute-start(f32[224,512]{1,0:T(8,128)S(1)} %get-tuple-element.31), channel_id=1, source_target_pairs={{0,16},{8,24},{16,0},{24,8},{1,17},{9,25},{17,1},{25,9},{2,18},{10... | collective-permute-start | bytes 1376264 | tf_op jit(solution)/shard_map/ppermute | solution.py:22
  5.0 4.2 %collective-permute-start = (s32[3,1,96]{2,1,0:T(1,128)S(1)}, s32[3,1,96]{2,1,0:T(1,128)S(1)}, u32[]{:S(2)}, u32[]{:S(2)}) collective-permute-start(s32[3,1,96]{2,1,0:T(1,128)S(1)} %get-tuple-element.25), channel_id=1, source_target_pairs={{0,1},{1,0},{2,3},{3,2},{4,5},{5,4},{6,7},{7,6},{8,9},{9,8},{10,11... | collective-permute-start | bytes 3464 | tf_op jit(solution)/shard_map/ppermute | solution.py:22
  9.2 14.2 %copy-start = (f32[1,512,512]{2,1,0:T(8,128)S(1)}, f32[1,512,512]{2,1,0:T(8,128)}, u32[]{:S(2)}) copy-start(f32[1,512,512]{2,1,0:T(8,128)} %param.13) | copy-start | bytes 3145732
  9.3 5.5 %collective-permute-start.1 = (s32[3,2,96]{2,1,0:T(2,128)S(1)}, s32[3,2,96]{2,1,0:T(2,128)S(1)}, u32[]{:S(2)}, u32[]{:S(2)}) collective-permute-start(s32[3,2,96]{2,1,0:T(2,128)S(1)} %pad_add_fusion.2), channel_id=1, source_target_pairs={{0,2},{1,3},{2,0},{3,1},{4,6},{5,7},{6,4},{7,5},{8,10},{9,11},{10,... | collective-permute-start | bytes 6920 | tf_op jit(solution)/shard_map/ppermute | solution.py:22
  12.8 10.5 %collective-permute-start.6 = (f32[144,512]{1,0:T(8,128)S(1)}, f32[144,512]{1,0:T(8,128)S(1)}, u32[]{:S(2)}, u32[]{:S(2)}) collective-permute-start(f32[144,512]{1,0:T(8,128)S(1)} %collective-permute-done.4.rest_0_), channel_id=1, source_target_pairs={{0,1},{1,0},{2,3},{3,2},{4,5},{5,4},{6,7},{7,6},{8,9},{9,8},{10,11... | collective-permute-start | bytes 884744 | tf_op jit(solution)/shard_map/ppermute | solution.py:22
  14.8 4.6 %collective-permute-start.2 = (s32[3,4,96]{2,1,0:T(4,128)S(1)}, s32[3,4,96]{2,1,0:T(4,128)S(1)}, u32[]{:S(2)}, u32[]{:S(2)}) collective-permute-start(s32[3,4,96]{2,1,0:T(4,128)S(1)} %pad_add_fusion.1), channel_id=1, source_target_pairs={{0,4},{1,5},{2,6},{3,7},{4,0},{5,1},{6,2},{7,3},{8,12},{9,13},{10,... | collective-permute-start | bytes 13832 | tf_op jit(solution)/shard_map/ppermute | solution.py:22
  22.8 2.7 %collective-permute-start.8 = (f32[224,512]{1,0:T(8,128)S(1)}, f32[224,512]{1,0:T(8,128)S(1)}, u32[]{:S(2)}, u32[]{:S(2)}) collective-permute-start(f32[224,512]{1,0:T(8,128)S(1)} %collective-permute-done.5.rest_1_), channel_id=1, source_target_pairs={{0,8},{8,0},{16,24},{24,16},{1,9},{9,1},{17,25},{25,17},{2,10},{10... | collective-permute-start | bytes 1376264 | tf_op jit(solution)/shard_map/ppermute | solution.py:22
  22.8 2.4 %collective-permute-start.7 = (f32[144,512]{1,0:T(8,128)S(1)}, f32[144,512]{1,0:T(8,128)S(1)}, u32[]{:S(2)}, u32[]{:S(2)}) collective-permute-start(f32[144,512]{1,0:T(8,128)S(1)} %collective-permute-done.4.rest_0_), channel_id=1, source_target_pairs={{0,8},{8,0},{16,24},{24,16},{1,9},{9,1},{17,25},{25,17},{2,10},{10... | collective-permute-start | bytes 884744 | tf_op jit(solution)/shard_map/ppermute | solution.py:22
  23.3 2.1 %collective-permute-start.9 = (f32[144,512]{1,0:T(8,128)S(1)}, f32[144,512]{1,0:T(8,128)S(1)}, u32[]{:S(2)}, u32[]{:S(2)}) collective-permute-start(f32[144,512]{1,0:T(8,128)S(1)} %collective-permute-done.6.rest_2_), channel_id=1, source_target_pairs={{0,8},{8,0},{16,24},{24,16},{1,9},{9,1},{17,25},{25,17},{2,10},{10... | collective-permute-start | bytes 884744 | tf_op jit(solution)/shard_map/ppermute | solution.py:22
  26.8 6.4 %collective-permute-start.10 = (f32[1,64,512]{2,1,0:T(8,128)S(1)}, f32[1,64,512]{2,1,0:T(8,128)S(1)}, u32[]{:S(2)}, u32[]{:S(2)}) collective-permute-start(f32[1,64,512]{2,1,0:T(8,128)S(1)} %get-tuple-element.36), channel_id=1, source_target_pairs={{0,1},{1,0},{2,3},{3,2},{4,5},{5,4},{6,7},{7,6},{8,9},{9,8},{10,11... | collective-permute-start | bytes 393224 | tf_op jit(solution)/shard_map/ppermute | solution.py:22
  28.3 8.2 %collective-permute-start.12 = (f32[1,64,512]{2,1,0:T(8,128)S(1)}, f32[1,64,512]{2,1,0:T(8,128)S(1)}, u32[]{:S(2)}, u32[]{:S(2)}) collective-permute-start(f32[1,64,512]{2,1,0:T(8,128)S(1)} %get-tuple-element.40), channel_id=1, source_target_pairs={{0,1},{1,0},{2,3},{3,2},{4,5},{5,4},{6,7},{7,6},{8,9},{9,8},{10,11... | collective-permute-start | bytes 393224 | tf_op jit(solution)/shard_map/ppermute | solution.py:22
  28.9 10.9 %collective-permute-start.14 = (f32[1,64,512]{2,1,0:T(8,128)S(1)}, f32[1,64,512]{2,1,0:T(8,128)S(1)}, u32[]{:S(2)}, u32[]{:S(2)}) collective-permute-start(f32[1,64,512]{2,1,0:T(8,128)S(1)} %get-tuple-element.42), channel_id=1, source_target_pairs={{0,1},{1,0},{2,3},{3,2},{4,5},{5,4},{6,7},{7,6},{8,9},{9,8},{10,11... | collective-permute-start | bytes 393224 | tf_op jit(solution)/shard_map/ppermute | solution.py:22
  30.3 10.7 %collective-permute-start.16 = (f32[1,64,512]{2,1,0:T(8,128)S(1)}, f32[1,64,512]{2,1,0:T(8,128)S(1)}, u32[]{:S(2)}, u32[]{:S(2)}) collective-permute-start(f32[1,64,512]{2,1,0:T(8,128)S(1)} %get-tuple-element.44), channel_id=1, source_target_pairs={{0,1},{1,0},{2,3},{3,2},{4,5},{5,4},{6,7},{7,6},{8,9},{9,8},{10,11... | collective-permute-start | bytes 393224 | tf_op jit(solution)/shard_map/ppermute | solution.py:22
  31.0 15.8 %copy-start.1 = (f32[1,64,512]{2,1,0:T(8,128)S(1)}, f32[1,64,512]{2,1,0:T(8,128)}, u32[]{:S(2)}) copy-start(f32[1,64,512]{2,1,0:T(8,128)} %param.14) | copy-start | bytes 393220
  31.0 15.8 %copy-start.2 = (f32[512]{0:T(512)S(1)}, f32[512]{0:T(512)}, u32[]{:S(2)}) copy-start(f32[512]{0:T(512)} %param.16) | copy-start | bytes 6148
  31.0 15.8 %copy-start.3 = (f32[1,64]{1,0:T(1,128)S(1)}, f32[1,64]{1,0:T(1,128)}, u32[]{:S(2)}) copy-start(f32[1,64]{1,0:T(1,128)} %param.15) | copy-start | bytes 772
  33.3 12.3 %collective-permute-start.11 = (f32[1,64,512]{2,1,0:T(8,128)S(1)}, f32[1,64,512]{2,1,0:T(8,128)S(1)}, u32[]{:S(2)}, u32[]{:S(2)}) collective-permute-start(f32[1,64,512]{2,1,0:T(8,128)S(1)} %add.45), channel_id=1, source_target_pairs={{0,4},{1,5},{2,6},{3,7},{4,0},{5,1},{6,2},{7,3},{8,12},{9,13},{10,... | collective-permute-start | bytes 393224 | tf_op jit(solution)/shard_map/ppermute | solution.py:22
  36.5 9.1 %collective-permute-start.13 = (f32[1,64,512]{2,1,0:T(8,128)S(1)}, f32[1,64,512]{2,1,0:T(8,128)S(1)}, u32[]{:S(2)}, u32[]{:S(2)}) collective-permute-start(f32[1,64,512]{2,1,0:T(8,128)S(1)} %add.47), channel_id=1, source_target_pairs={{0,6},{1,7},{2,4},{3,5},{4,2},{5,3},{6,0},{7,1},{8,14},{9,15},{10,... | collective-permute-start | bytes 393224 | tf_op jit(solution)/shard_map/ppermute | solution.py:22
  39.8 7.0 %collective-permute-start.15 = (f32[1,64,512]{2,1,0:T(8,128)S(1)}, f32[1,64,512]{2,1,0:T(8,128)S(1)}, u32[]{:S(2)}, u32[]{:S(2)}) collective-permute-start(f32[1,64,512]{2,1,0:T(8,128)S(1)} %add.49), channel_id=1, source_target_pairs={{0,2},{1,3},{2,0},{3,1},{4,6},{5,7},{6,4},{7,5},{8,10},{9,11},{10,... | collective-permute-start | bytes 393224 | tf_op jit(solution)/shard_map/ppermute | solution.py:22

commit v4 on v0

v4 whole, which is shorter than its diff:
```python
import functools

import jax
import jax.numpy as jnp
from jax import lax
from jax.experimental import pallas as pl
from jax.experimental.pallas import tpu as pltpu
from jax.sharding import PartitionSpec as P

LANES = 128
MIB = 1024 * 1024
DEEP = 256
VMEM = pl.BlockSpec(memory_space=pltpu.VMEM)
HBM = pl.BlockSpec(memory_space=pltpu.HBM)


def in_vmem(x):
    return pltpu.with_memory_space_constraint(x, pltpu.VMEM)


def in_hbm(x):
    return pltpu.with_memory_space_constraint(x, pltpu.HBM)


def limit(n):
    return pltpu.CompilerParams(vmem_limit_bytes=min(n + 12 * MIB, 56 * MIB))


def cost(flops, nbytes):
    return pl.CostEstimate(flops=flops, bytes_accessed=nbytes, transcendentals=0)


def split(x):
    hi = x.astype(jnp.bfloat16)
    return hi, (x - hi.astype(jnp.float32)).astype(jnp.bfloat16)


def swap(x, axis, k):
    n = lax.axis_size(axis)
    return lax.ppermute(x, axis, [(i, i ^ k) for i in range(n)])


def after(x, *others):
    return lax.optimization_barrier((x, *others))[0]


def tile_order(lanes):
    side = list(range(lanes // 2, lanes, 2)) + list(range(lanes // 2 - 2, -1, -2))
    return [k + 1 for k in side], side


def row_cuts(depth):
    end = depth * 9 // 32 // 16 * 16
    return end, depth - 2 * end


def end_offsets(depth):
    low = lax.axis_index("wide") & 1
    last = depth - row_cuts(depth)[0]
    return pl.multiple_of(low * last, 16), pl.multiple_of(last - low * last, 16)


def pieces_kernel(own_hbm, one_ref, two_ref, sems):
    end, middle = one_ref.shape[0], two_ref.shape[0]
    mine, _ = end_offsets(own_hbm.shape[0])
    copies = [
        pltpu.make_async_copy(own_hbm.at[pl.ds(mine, end), :], one_ref, sems.at[0]),
        pltpu.make_async_copy(own_hbm.at[pl.ds(end, middle), :], two_ref, sems.at[1]),
    ]
    for copy in copies:
        copy.start()
    for copy in copies:
        copy.wait()


def pieces(own):
    return pl.pallas_call(
        pieces_kernel,
        out_shape=[pltpu.VMEM((n, own.shape[1]), own.dtype) for n in row_cuts(own.shape[0])],
        in_specs=[HBM],
        out_specs=[VMEM] * 2,
        scratch_shapes=[pltpu.SemaphoreType.DMA((2,))],
        compiler_params=limit(0),
        cost_estimate=cost(0, own.size * 4),
        name="pieces",
    )(in_hbm(own))


def lists_kernel(count_ref, *refs):
    small, (lists_ref, table_ref) = refs[:6], refs[6:8]
    held, sems = refs[8:14], refs[14]
    amp, cint, res, amp_label, owner, int_label = held
    copies = [pltpu.make_async_copy(a, b, sems.at[i]) for i, (a, b) in enumerate(zip(small, held))]
    for copy in copies:
        copy.start()
    table_ref[...] = jnp.zeros(table_ref.shape, jnp.int32)
    for copy in copies:
        copy.wait()
    slot = lax.broadcasted_iota(jnp.int32, amp.shape, 1)
    lists_ref[0] = amp[...]
    lists_ref[1] = cint[...]
    lists_ref[2] = jnp.where(slot < count_ref[0], res[...], -1)
    amp_dev = amp_label.shape[1]
    for at in range(0, DEEP, amp_dev):
        table_ref[0:1, at : at + amp_dev] = amp_label[...]
    table_ref[1:2, 0 : owner.shape[1]] = owner[...]
    table_ref[2:3, 0 : int_label.shape[1]] = int_label[...]


def pack_lists(task_amp, task_int, task_res, task_count, amp_label, owner, int_label):
    args = [task_amp, task_int, task_res, amp_label[None, :], owner, int_label[None, :]]
    return pl.pallas_call(
        lists_kernel,
        out_shape=[
            pltpu.VMEM((3,) + task_amp.shape, jnp.int32),
            pltpu.VMEM((3, DEEP), jnp.int32),
        ],
        in_specs=[pl.BlockSpec(memory_space=pltpu.SMEM)] + [HBM] * 6,
        out_specs=[VMEM] * 2,
        scratch_shapes=[pltpu.VMEM(x.shape, x.dtype) for x in args]
        + [pltpu.SemaphoreType.DMA((6,))],
        compiler_params=limit(0),
        cost_estimate=cost(0, 4096),
        name="pack_lists",
    )(task_count, *[in_hbm(x) for x in args])


def load_kernel(first, amp_hbm, out_ref, rows_ref, sems):
    amp_dev = amp_hbm.shape[0]
    rows = rows_ref.shape[0]
    copies = [
        pltpu.make_async_copy(amp_hbm.at[:, first + i, :], rows_ref.at[i], sems.at[i])
        for i in range(rows)
    ]
    for copy in copies:
        copy.start()
    for i, copy in enumerate(copies):
        copy.wait()
        hi, lo = split(rows_ref[i])
        at = 2 * amp_dev * i
        out_ref[at : at + amp_dev, :] = hi
        out_ref[at + amp_dev : at + 2 * amp_dev, :] = lo


def load(amplitudes, first, rows):
    amp_dev, _, depth = amplitudes.shape
    return pl.pallas_call(
        functools.partial(load_kernel, first),
        out_shape=pltpu.VMEM((rows * 2 * amp_dev, depth), jnp.bfloat16),
        in_specs=[HBM],
        out_specs=VMEM,
        scratch_shapes=[
            pltpu.VMEM((rows, amp_dev, depth), jnp.float32),
            pltpu.SemaphoreType.DMA((rows,)),
        ],
        compiler_params=limit(8 * rows * amp_dev * depth),
        cost_estimate=cost(0, 8 * rows * amp_dev * depth),
        name="load_amplitudes",
    )(in_hbm(amplitudes))


def local_kernel(own_ref, pair_ref, in_hi, in_lo):
    depth = own_ref.shape[0]
    for c, ref in enumerate((own_ref, pair_ref)):
        hi, lo = split(ref[...])
        in_hi[c * depth : (c + 1) * depth, :] = hi
        in_lo[c * depth : (c + 1) * depth, :] = lo


def split_local(own, pair):
    depth, window = own.shape
    return pl.pallas_call(
        local_kernel,
        out_shape=[pltpu.VMEM((2 * depth, window), jnp.bfloat16)] * 2,
        in_specs=[VMEM] * 2,
        out_specs=[VMEM] * 2,
        compiler_params=limit(16 * depth * window),
        cost_estimate=cost(0, 16 * depth * window),
        name="split_local",
    )(own, pair)


def coefficients(lists_ref, table_ref, amp_dev, lanes, blocks):
    lane = lax.axis_index("wide")
    grp = lax.axis_index("grp")
    amp, cint, res = (lists_ref[i] for i in range(3))
    local = amp - lane * amp_dev
    valid = (res >= 0) & (local >= 0) & (local < amp_dev)
    pos = jnp.zeros_like(res)
    for p in range(lanes):
        pos = jnp.where(res == table_ref[1:2, p : p + 1], p, pos)
    offset = pos ^ lane
    place = jnp.zeros_like(res)
    away, side = tile_order(lanes)
    for j, k in enumerate(away + side):
        place = jnp.where(offset == k, j, place)
    seg = jnp.where(valid, place * blocks + (cint ^ grp), -1)
    half = lanes // 2
    group = DEEP // (2 * amp_dev)
    rows = 2 * blocks * group * half
    slots = amp.shape[1]

    def parts(row):
        tile = row & (half - 1)
        inner = (row >> (half.bit_length() - 1)) & (group - 1)
        outer = row >> ((half * group).bit_length() - 1)
        return tile, inner, outer & (blocks - 1), outer >> (blocks.bit_length() - 1)

    tile, _, block, away_or_side = parts(lax.broadcasted_iota(jnp.int32, (rows, slots), 0))
    row_seg = (away_or_side * half + tile) * blocks + block
    col_amp = lax.broadcasted_iota(jnp.int32, (DEEP, slots), 0) & (amp_dev - 1)
    counts = jnp.zeros((rows, DEEP), jnp.float32)
    for src in range(lanes):
        hit_row = jnp.where(row_seg == seg[src : src + 1, :], 1.0, 0.0)
        hit_col = jnp.where(col_amp == local[src : src + 1, :], 1.0, 0.0)
        counts += lax.dot_general(
            hit_row.astype(jnp.bfloat16),
            hit_col.astype(jnp.bfloat16),
            (((1,), (1,)), ((), ())),
            preferred_element_type=jnp.float32,
        )
    _, inner, block, _ = parts(lax.broadcasted_iota(jnp.int32, (rows, DEEP), 0))
    block = block ^ grp
    label = jnp.zeros((rows, DEEP), jnp.int32)
    for c in range(blocks):
        label = jnp.where(block == c, table_ref[2:3, c : c + 1], label)
    odd = (label + table_ref[0:1, :]) & 1
    col = lax.broadcasted_iota(jnp.int32, (rows, DEEP), 1)
    same = inner == (col >> ((2 * amp_dev).bit_length() - 1))
    weight = jnp.where(odd == 1, -counts, counts)
    return jnp.where(same, weight, 0.0).astype(jnp.bfloat16)


def sums_kernel(lanes, blocks, amp_dev, lists_ref, table_ref, *refs):
    amp_refs, sums_refs = refs[:-4], refs[-4:]
    weight = coefficients(lists_ref, table_ref, amp_dev, lanes, blocks)
    depth = amp_refs[0].shape[1]
    step = weight.shape[0] // (2 * blocks)
    first = 0
    for ref in amp_refs:
        count = ref.shape[0] // DEEP

        def add(g, _, ref=ref, first=first):
            rows = ref[pl.ds(pl.multiple_of(g * DEEP, DEEP), DEEP), :]
            total = jnp.dot(weight, rows, preferred_element_type=jnp.float32)
            at = pl.ds(pl.multiple_of((first + g) * step, step), step)
            for k in range(2):
                for c in range(blocks):
                    r = (k * blocks + c) * step
                    hi, lo = split(total[r : r + step, :])
                    sums_refs[2 * k][at, c * depth : (c + 1) * depth] = hi
                    sums_refs[2 * k + 1][at, c * depth : (c + 1) * depth] = lo
            return 0

        lax.fori_loop(0, count, add, 0)
        first += count


def sums(lists, table, rows, amp_dev, tile_rows, lanes, blocks):
    depth = rows[0].shape[1]
    held = pltpu.VMEM((lanes // 2 * tile_rows, blocks * depth), jnp.bfloat16)
    return pl.pallas_call(
        functools.partial(sums_kernel, lanes, blocks, amp_dev),
        out_shape=[held] * 4,
        in_specs=[VMEM] * (2 + len(rows)),
        out_specs=[VMEM] * 4,
        compiler_params=limit(0),
        cost_estimate=cost(0, 16 * tile_rows * amp_dev * depth),
        name="sums",
    )(lists, table, *[in_vmem(x) for x in rows])


def passes(hi, lo, in_hi, in_lo):
    dot = functools.partial(jnp.dot, preferred_element_type=jnp.float32)
    return dot(hi, in_hi) + dot(hi, in_lo) + dot(lo, in_hi)


def store_tiles(out, out_refs, held):
    tiles = len(out_refs)
    rows = out.shape[0] // tiles
    for b in range(held.shape[0]):
        held[b] = out[:, b * LANES : (b + 1) * LANES]
    for j, ref in enumerate(out_refs):
        for b in range(held.shape[0]):
            ref[0, :, b * LANES : (b + 1) * LANES] = held[b, pl.ds(j, rows, stride=tiles), :]


def local_products_kernel(hi, lo, in_hi, in_lo, out_ref):
    depth = in_hi.shape[0]
    out_ref[...] = passes(hi[:, :depth], lo[:, :depth], in_hi[...], in_lo[...])


def local_products(hi, lo, in_hi, in_lo):
    depth, window = in_hi.shape
    return pl.pallas_call(
        local_products_kernel,
        out_shape=pltpu.VMEM((hi.shape[0], window), jnp.float32),
        in_specs=[VMEM] * 4,
        out_specs=VMEM,
        compiler_params=limit(0),
        cost_estimate=cost(6 * hi.shape[0] * depth * window, 0),
        name="local_products",
    )(*[in_vmem(x) for x in (hi, lo, in_hi, in_lo)])


def away_kernel(tiles, blocks, hi, lo, local_ref, *rest):
    n = 3 * (blocks - 2)
    parts, out_refs, (in_hi, in_lo, held) = rest[:n], rest[n : n + tiles], rest[n + tiles :]
    depth = in_hi.shape[0] // (blocks - 2)
    mine, theirs = end_offsets(depth)
    for c in range(blocks - 2):
        starts = (mine, row_cuts(depth)[0], theirs)
        for start, part in zip(starts, parts[3 * c : 3 * c + 3]):
            high, low = split(part[...])
            at = pl.ds(pl.multiple_of(c * depth + start, 16), part.shape[0])
            in_hi[at, :] = high
            in_lo[at, :] = low
    out = passes(hi[:, 2 * depth :], lo[:, 2 * depth :], in_hi[...], in_lo[...])
    store_tiles(local_ref[...] + out, out_refs, held)


def side_kernel(tiles, hi, lo, local_hi, local_lo, in_hi, in_lo, *rest):
    out_refs, held = rest[:tiles], rest[tiles]
    depth = local_hi.shape[0]
    out = passes(hi[:, :depth], lo[:, :depth], local_hi[...], local_lo[...])
    out += passes(hi[:, depth:], lo[:, depth:], in_hi[...], in_lo[...])
    store_tiles(out, out_refs, held)


def away_products(hi, lo, local, parts, tiles):
    blocks = 2 + len(parts)
    depth = hi.shape[1] // blocks
    rows, window = local.shape
    remote = pltpu.VMEM(((blocks - 2) * depth, window), jnp.bfloat16)
    *out, in_hi, in_lo = pl.pallas_call(
        functools.partial(away_kernel, tiles, blocks),
        out_shape=[jax.ShapeDtypeStruct((1, rows // tiles, window), jnp.float32)] * tiles
        + [remote] * 2,
        in_specs=[VMEM] * (3 + 3 * len(parts)),
        out_specs=[VMEM] * (tiles + 2),
        scratch_shapes=[pltpu.VMEM((window // LANES, rows, LANES), jnp.float32)],
        compiler_params=limit(4 * blocks * depth * window),
        cost_estimate=cost(6 * rows * (blocks - 2) * depth * window, 0),
        name="away_products",
    )(*[in_vmem(x) for x in (hi, lo, local)], *[x for three in parts for x in three])
    return out, in_hi, in_lo


def side_products(hi, lo, local_hi, local_lo, in_hi, in_lo, tiles):
    rows, depth = hi.shape
    window = in_hi.shape[1]
    return pl.pallas_call(
        functools.partial(side_kernel, tiles),
        out_shape=[jax.ShapeDtypeStruct((1, rows // tiles, window), jnp.float32)] * tiles,
        in_specs=[VMEM] * 6,
        out_specs=[VMEM] * tiles,
        scratch_shapes=[pltpu.VMEM((window // LANES, rows, LANES), jnp.float32)],
        compiler_params=limit(0),
        cost_estimate=cost(6 * rows * depth * window, 0),
        name="side_products",
    )(*[in_vmem(x) for x in (hi, lo, local_hi, local_lo, in_hi, in_lo)])


def on_device(
    amplitudes,
    integrals,
    base_residual,
    occ_gap,
    virt_sum,
    task_amp,
    task_int,
    task_res,
    task_count,
    res_owner,
    amp_label,
    int_label,
):
    lanes = lax.axis_size("wide")
    grps = lax.axis_size("grp")
    amp_dev, tile_rows, _ = amplitudes.shape
    half = lanes // 2
    own = integrals[0]
    one, two = pieces(own)
    fetched = {k: [swap(x, "grp", k) for x in (one, two)] for k in range(2, grps, 2)}
    lists, table = pack_lists(
        task_amp, task_int, after(task_res, one), task_count, amp_label, res_owner, int_label
    )
    pair = swap(own, "grp", 1)
    rows = [load(amplitudes, i * tile_rows // 2, tile_rows // 2) for i in range(2)]
    local_hi, local_lo = split_local(own, pair)
    k = 1
    while k < lanes:
        if k in (2, 4):
            lists = after(lists, rows[k // 4])
        lists = jnp.concatenate([lists, swap(lists, "wide", k)], axis=1)
        k *= 2
    away_hi, away_lo, side_hi, side_lo = sums(lists, table, rows, amp_dev, tile_rows, lanes, grps)

    parts = [None] * (grps - 2)
    for k, (one, two) in fetched.items():
        three = [one, two, swap(one, "wide", 1)]
        parts[k - 2] = three
        parts[k - 1] = [
            swap(after(x, y), "grp", 1) for x, y in zip(three, (lists, away_hi, away_hi))
        ]

    local = local_products(away_hi, away_lo, local_hi, local_lo)
    away, in_hi, in_lo = away_products(away_hi, away_lo, local, parts, half)
    side = side_products(side_hi, side_lo, local_hi, local_lo, in_hi, in_lo, half)
    _, offsets = tile_order(lanes)
    got = [swap(x, "wide", 1) for x in away]
    summed = base_residual
    for k, here, there in reversed(list(zip(offsets, side, got))):
        part = here + there
        summed = summed + (swap(part, "wide", k) if k else part)
    divisor = occ_gap[:, :, None] + virt_sum[None, None, :]
    return summed / divisor


def solution(mesh):
    return jax.shard_map(
        on_device,
        mesh=mesh,
        in_specs=(
            P(("grp", "wide"), None, None),
            P("grp", None, None),
            P(("grp", "wide"), None, None),
            P(("grp", "wide"), None),
            P(),
            P(("grp", "wide"), None),
            P(("grp", "wide"), None),
            P(("grp", "wide"), None),
            P(("grp", "wide")),
            P("grp", None),
            P(("grp", "wide")),
            P(),
        ),
        out_specs=P(("grp", "wide"), None, None),
        check_vma=False,
    )
```

time: 393 us -> 48.1 us (0.12)
  local copies, waits for them, and re-layouts: 155 us -> 0.02 us
  matrix products: 123 us -> 0 us
  blocking collectives: 83.9 us -> 0 us
  starting transfers between devices: 0.01 us -> 21.4 us
  Pallas kernels: 0 us -> 14 us
  between operations: 14.2 us -> 0.8 us
  other arithmetic: 14.2 us -> 0.84 us
  waiting for transfers between devices: 0.73 us -> 10.7 us
    gather x63 -> x0, local copies, waits for them, and re-layouts: 138 us -> none  [the longest x24 85.3 us: block_product(): weights_here = jnp.take(all_integrals, int_ids[task_block], axis=0)]
    dot_general x13 -> x0, matrix products: 123 us -> none  [the longest x12 108 us: block_product(): jnp.einsum('kij,kjl->kil', tiles_here, weights_here, precision=lax.Precis...]
    all_gather x3 -> x0, blocking collectives: 52.4 us -> none  [the longest x1 17.8 us: on_device(): lax.all_gather(task_amp, 'wide', axis=0, tiled=True)]
    ppermute x0 -> x17, starting transfers between devices: none -> 21.4 us  [swap(): return lax.ppermute(x, axis, [(i, i ^ k) for i in range(n)])]
    all_to_all x1 -> x0, blocking collectives: 18.4 us -> none  [on_device(): lax.all_to_all(image.reshape(lane_count, res_dev, tile_rows, window), 'wi...]
    pallas_call x0 -> x9, Pallas kernels: none -> 14 us  [the longest x2 4.26 us: load(): pl.pallas_call(functools.partial(load_kernel, first), out_shape=pltpu.VME...]
    scatter x4 -> x0, local copies, waits for them, and re-layouts: 13.7 us -> none  [the longest x1 3.56 us: on_device(): jnp.zeros((slot_count,), jnp.bool_).at[target].set(True, mode='drop')]
    unnamed x1 -> x0, blocking collectives: 13.1 us -> none
  transfers between devices with their start and end apart: 1 -> 17, of which waited for: 0 -> 9; matrix products, arithmetic and copies ran while one was open for 8% -> 0% of each run, Pallas kernels for 0% -> 27%
where the time goes in v4:
time: 48.1 us; the launch traced here: 47.8 us
  starting transfers between devices  21.4 us (44%)
  Pallas kernels  14 us (29%)
  waiting for transfers between devices  10.7 us (22%)
  other arithmetic  0.84 us (2%)
  between operations  0.8 us (2%)
    ppermute x17, starting transfers between devices, swap(): return lax.ppermute(x, axis, [(i, i ^ k) for i in range(n)])  21.4 us
    ppermute x17, waiting for transfers between devices, swap(): return lax.ppermute(x, axis, [(i, i ^ k) for i in range(n)])  10.7 us
    pallas_call x2, Pallas kernels, load(): pl.pallas_call(functools.partial(load_kernel, first), out_shape=pltpu.VME...  4.26 us
    pallas_call x1, Pallas kernels, sums(): pl.pallas_call(functools.partial(sums_kernel, lanes, blocks, amp_dev), ou...  3.5 us
    pallas_call x1, Pallas kernels, side_products(): pl.pallas_call(functools.partial(side_kernel, tiles), out_shape=[jax.Shap...  1.81 us
    pallas_call x1, Pallas kernels, away_products(): pl.pallas_call(functools.partial(away_kernel, tiles, blocks), out_shape=[...  1.23 us
    pallas_call x1, Pallas kernels, pieces(): pl.pallas_call(pieces_kernel, out_shape=[pltpu.VMEM((n, own.shape[1]), ow...  1.12 us
    pallas_call x1, Pallas kernels, local_products(): pl.pallas_call(local_products_kernel, out_shape=pltpu.VMEM((hi.shape[0],...  0.97 us
  transfers between devices with their start and end apart: 17, of which 9 were waited for; matrix products, arithmetic and copies ran while one was open for 0% of the time, Pallas kernels for 27%

profile of v4, /device:TPU:0, one launch (start us, length us, event | category | flops | bytes accessed | tf_op | source)
XLA Modules:
  0.0 47.8 jit_solution(4244898864441344407)
XLA Ops:
  0.0 0.5 collective-permute-start.3
  0.5 1.1 %pieces.1 = (f32[144,512]{1,0:T(8,128)S(1)}, f32[224,512]{1,0:T(8,128)S(1)}) custom-call(f32[512,512]{1,0:T(8,128)} %bitcast.5), custom_call_target="tpu_custom_call" | custom-call | bytes 1048576 | tf_op jit(solution)/shard_map/pieces/pallas_call | solution.py:77
  1.6 2.6 %collective-permute-start.4 = (f32[144,512]{1,0:T(8,128)S(1)}, f32[144,512]{1,0:T(8,128)S(1)}, u32[]{:S(2)}, u32[]{:S(2)}) collective-permute-start(f32[144,512]{1,0:T(8,128)S(1)} %get-tuple-element.31), channel_id=1, source_target_pairs={{0,16},{8,24},{16,0},{24,8},{1,17},{9,25},{17,1},{25,9},{2,18},{10... | collective-permute-start | bytes 884744 | tf_op jit(solution)/shard_map/ppermute | solution.py:40
  4.1 0.1 collective-permute-start.5
  4.9 0.9 %pack_lists.1 = (s32[3,1,96]{2,1,0:T(1,128)S(1)}, s32[3,256]{1,0:T(4,128)S(1)}) custom-call(s32[1]{0:T(128)S(6)} %copy.13.count_ref, s32[1,96]{1,0:T(1,128)} %refs_0_.1, s32[1,96]{1,0:T(1,128)} %refs_1_.1, s32[1,96]{1,0:T(1,128)} %refs_2_, s32[1,32]{1,0:T(1,128)} %bitcast.8, s32[1,8]{1,0:T(1,128)} %refs_4_.1, s32[1,4]{1,0:T(1,128)} %bitcast.9), custom_call_target="tpu_custom_call" | custom-call | bytes 4096 | tf_op jit(solution)/shard_map/pack_lists/pallas_call | solution.py:112
  5.7 2.0 %collective-permute-start = (s32[3,1,96]{2,1,0:T(1,128)S(1)}, s32[3,1,96]{2,1,0:T(1,128)S(1)}, u32[]{:S(2)}, u32[]{:S(2)}) collective-permute-start(s32[3,1,96]{2,1,0:T(1,128)S(1)} %get-tuple-element.33), channel_id=1, source_target_pairs={{0,1},{1,0},{2,3},{3,2},{4,5},{5,4},{6,7},{7,6},{8,9},{9,8},{10,11... | collective-permute-start | bytes 3464 | tf_op jit(solution)/shard_map/ppermute | solution.py:40
  7.8 2.1 %load_amplitudes.2.refs_0_ = bf16[2048,512]{1,0:T(8,128)(2,1)S(1)} custom-call(f32[32,64,512]{2,1,0:T(8,128)} %amp_hbm.3), custom_call_target="tpu_custom_call" | custom-call | bytes 4194304 | tf_op jit(solution)/shard_map/load_amplitudes/pallas_call | solution.py:147
  9.9 0.0 collective-permute-done
  10.0 1.6 %collective-permute-start.1 = (s32[3,2,96]{2,1,0:T(2,128)S(1)}, s32[3,2,96]{2,1,0:T(2,128)S(1)}, u32[]{:S(2)}, u32[]{:S(2)}) collective-permute-start(s32[3,2,96]{2,1,0:T(2,128)S(1)} %pad_add_fusion.2), channel_id=1, source_target_pairs={{0,2},{1,3},{2,0},{3,1},{4,6},{5,7},{6,4},{7,5},{8,10},{9,11},{10,... | collective-permute-start | bytes 6920 | tf_op jit(solution)/shard_map/ppermute | solution.py:40
  11.6 2.1 %load_amplitudes.3.refs_1_ = bf16[2048,512]{1,0:T(8,128)(2,1)S(1)} custom-call(f32[32,64,512]{2,1,0:T(8,128)} %amp_hbm.3), custom_call_target="tpu_custom_call" | custom-call | bytes 4194304 | tf_op jit(solution)/shard_map/load_amplitudes/pallas_call | solution.py:147
  13.7 0.0 collective-permute-done.4.rest_0_
  13.7 1.5 %collective-permute-start.6 = (f32[144,512]{1,0:T(8,128)S(1)}, f32[144,512]{1,0:T(8,128)S(1)}, u32[]{:S(2)}, u32[]{:S(2)}) collective-permute-start(f32[144,512]{1,0:T(8,128)S(1)} %collective-permute-done.4.rest_0_), channel_id=1, source_target_pairs={{0,1},{1,0},{2,3},{3,2},{4,5},{5,4},{6,7},{7,6},{8,9},{9,8},{10,11... | collective-permute-start | bytes 884744 | tf_op jit(solution)/shard_map/ppermute | solution.py:40
  15.2 0.0 collective-permute-done.1
  15.3 2.7 %collective-permute-start.2 = (s32[3,4,96]{2,1,0:T(4,128)S(1)}, s32[3,4,96]{2,1,0:T(4,128)S(1)}, u32[]{:S(2)}, u32[]{:S(2)}) collective-permute-start(s32[3,4,96]{2,1,0:T(4,128)S(1)} %pad_add_fusion.1), channel_id=1, source_target_pairs={{0,4},{1,5},{2,6},{3,7},{4,0},{5,1},{6,2},{7,3},{8,12},{9,13},{10,... | collective-permute-start | bytes 13832 | tf_op jit(solution)/shard_map/ppermute | solution.py:40
  17.9 1.9 %collective-permute-done.2 = s32[3,4,96]{2,1,0:T(4,128)S(1)} collective-permute-done((s32[3,4,96]{2,1,0:T(4,128)S(1)}, s32[3,4,96]{2,1,0:T(4,128)S(1)}, u32[]{:S(2)}, u32[]{:S(2)}) %collective-permute-start.2) | collective-permute-done | bytes 4640 | tf_op jit(solution)/shard_map/ppermute | solution.py:40
  19.9 0.0 copy-start
  19.9 3.5 %sums.1 = (bf16[256,2048]{1,0:T(8,128)(2,1)S(1)}, bf16[256,2048]{1,0:T(8,128)(2,1)S(1)}, bf16[256,2048]{1,0:T(8,128)(2,1)S(1)}, bf16[256,2048]{1,0:T(8,128)(2,1)S(1)}) custom-call(s32[3,8,96]{2,1,0:T(8,128)S(1)} %pad_add_fusion.lists_ref, s32[3,256]{1,0:T(4,128)S(1)} %get-tuple-element.36.table_ref, bf16[2048,512]{1,0:T(8,128)(2,1)S(1)} %load_amplitudes.2.refs_0_, ...), custom_call_target="tpu_custom_call" | custom-call | bytes 16777216 | tf_op jit(solution)/shard_map/sums/pallas_call | solution.py:262
  23.4 0.0 collective-permute-done.5.rest_1_
  23.4 0.1 collective-permute-start.8
  23.5 0.5 %collective-permute-start.7 = (f32[144,512]{1,0:T(8,128)S(1)}, f32[144,512]{1,0:T(8,128)S(1)}, u32[]{:S(2)}, u32[]{:S(2)}) collective-permute-start(f32[144,512]{1,0:T(8,128)S(1)} %collective-permute-done.4.rest_0_), channel_id=1, source_target_pairs={{0,8},{8,0},{16,24},{24,16},{1,9},{9,1},{17,25},{25,17},{2,10},{10... | collective-permute-start | bytes 884744 | tf_op jit(solution)/shard_map/ppermute | solution.py:40
  24.0 0.0 collective-permute-done.6.rest_2_
  24.0 0.1 collective-permute-start.9
  24.0 0.0 collective-permute-done.3.pair_ref
  24.0 0.0 copy-done
  24.1 0.3 split_local.1
  24.3 1.0 %local_products.1.local_ref = f32[256,512]{1,0:T(8,128)S(1)} custom-call(bf16[256,2048]{1,0:T(8,128)(2,1)S(1)} %get-tuple-element.41.hi, bf16[256,2048]{1,0:T(8,128)(2,1)S(1)} %get-tuple-element.42.lo, bf16[1024,512]{1,0:T(8,128)(2,1)S(1)} %get-tuple-element.39.in_hi.local_hi, bf16[1024,512]{1,0:T(8,128)(2,1)S(1)} %get-tuple-element.40.in_lo.local_lo), custom_call_target="tpu_custom_call" | custom-call | flops 805306368 | tf_op jit(solution)/shard_map/local_products/pallas_call | solution.py:295
  25.3 0.4 collective-permute-done.7.rest_3_
  25.7 0.4 collective-permute-done.9.rest_5_
  26.1 0.0 collective-permute-done.8.rest_4_
  26.1 1.2 %away_products.1 = (f32[1,64,512]{2,1,0:T(8,128)S(1)}, f32[1,64,512]{2,1,0:T(8,128)S(1)}, f32[1,64,512]{2,1,0:T(8,128)S(1)}, f32[1,64,512]{2,1,0:T(8,128)S(1)}, ...) custom-call(bf16[256,2048]{1,0:T(8,128)(2,1)S(1)} %get-tuple-element.41.hi, ...), custom_call_target="tpu_custom_call" | custom-call | flops 805306368 | tf_op jit(solution)/shard_map/away_products/pallas_call | solution.py:335
  27.4 0.7 %collective-permute-start.15 = (f32[1,64,512]{2,1,0:T(8,128)S(1)}, f32[1,64,512]{2,1,0:T(8,128)S(1)}, u32[]{:S(2)}, u32[]{:S(2)}) collective-permute-start(f32[1,64,512]{2,1,0:T(8,128)S(1)} %get-tuple-element.56), channel_id=1, source_target_pairs={{0,1},{1,0},{2,3},{3,2},{4,5},{5,4},{6,7},{7,6},{8,9},{9,8},{10,11... | collective-permute-start | bytes 393224 | tf_op jit(solution)/shard_map/ppermute | solution.py:40
  28.0 1.4 %collective-permute-start.13 = (f32[1,64,512]{2,1,0:T(8,128)S(1)}, f32[1,64,512]{2,1,0:T(8,128)S(1)}, u32[]{:S(2)}, u32[]{:S(2)}) collective-permute-start(f32[1,64,512]{2,1,0:T(8,128)S(1)} %get-tuple-element.54), channel_id=1, source_target_pairs={{0,1},{1,0},{2,3},{3,2},{4,5},{5,4},{6,7},{7,6},{8,9},{9,8},{10,11... | collective-permute-start | bytes 393224 | tf_op jit(solution)/shard_map/ppermute | solution.py:40
  29.4 0.6 %collective-permute-start.11 = (f32[1,64,512]{2,1,0:T(8,128)S(1)}, f32[1,64,512]{2,1,0:T(8,128)S(1)}, u32[]{:S(2)}, u32[]{:S(2)}) collective-permute-start(f32[1,64,512]{2,1,0:T(8,128)S(1)} %get-tuple-element.52), channel_id=1, source_target_pairs={{0,1},{1,0},{2,3},{3,2},{4,5},{5,4},{6,7},{7,6},{8,9},{9,8},{10,11... | collective-permute-start | bytes 393224 | tf_op jit(solution)/shard_map/ppermute | solution.py:40
  30.0 1.4 %collective-permute-start.10 = (f32[1,64,512]{2,1,0:T(8,128)S(1)}, f32[1,64,512]{2,1,0:T(8,128)S(1)}, u32[]{:S(2)}, u32[]{:S(2)}) collective-permute-start(f32[1,64,512]{2,1,0:T(8,128)S(1)} %get-tuple-element.50), channel_id=1, source_target_pairs={{0,1},{1,0},{2,3},{3,2},{4,5},{5,4},{6,7},{7,6},{8,9},{9,8},{10,11... | collective-permute-start | bytes 393224 | tf_op jit(solution)/shard_map/ppermute | solution.py:40
  31.5 1.8 %side_products.1 = (f32[1,64,512]{2,1,0:T(8,128)S(1)}, f32[1,64,512]{2,1,0:T(8,128)S(1)}, f32[1,64,512]{2,1,0:T(8,128)S(1)}, f32[1,64,512]{2,1,0:T(8,128)S(1)}) custom-call(bf16[256,2048]{1,0:T(8,128)(2,1)S(1)} %get-tuple-element.37.hi, bf16[256,2048]{1,0:T(8,128)(2,1)S(1)} %get-tuple-element.38.lo, bf16[1024,512]{1,0:T(8,128)(2,1)S(1)} %get-tuple-element.39.in_hi.local_hi, ...), custom_call_target="tpu_custom_call" | custom-call | flops 1610612736 | tf_op jit(solution)/shard_map/side_products/pallas_call | solution.py:352
  33.3 0.5 collective-permute-done.15
  33.8 2.7 %collective-permute-start.16 = (f32[1,64,512]{2,1,0:T(8,128)S(1)}, f32[1,64,512]{2,1,0:T(8,128)S(1)}, u32[]{:S(2)}, u32[]{:S(2)}) collective-permute-start(f32[1,64,512]{2,1,0:T(8,128)S(1)} %add.51), channel_id=1, source_target_pairs={{0,4},{1,5},{2,6},{3,7},{4,0},{5,1},{6,2},{7,3},{8,12},{9,13},{10,... | collective-permute-start | bytes 393224 | tf_op jit(solution)/shard_map/ppermute | solution.py:40
  36.4 0.1 collective-permute-done.13
  36.6 2.5 %collective-permute-start.14 = (f32[1,64,512]{2,1,0:T(8,128)S(1)}, f32[1,64,512]{2,1,0:T(8,128)S(1)}, u32[]{:S(2)}, u32[]{:S(2)}) collective-permute-start(f32[1,64,512]{2,1,0:T(8,128)S(1)} %add.49), channel_id=1, source_target_pairs={{0,6},{1,7},{2,4},{3,5},{4,2},{5,3},{6,0},{7,1},{8,14},{9,15},{10,... | collective-permute-start | bytes 393224 | tf_op jit(solution)/shard_map/ppermute | solution.py:40
  39.1 0.2 collective-permute-done.11
  39.4 0.5 %collective-permute-start.12 = (f32[1,64,512]{2,1,0:T(8,128)S(1)}, f32[1,64,512]{2,1,0:T(8,128)S(1)}, u32[]{:S(2)}, u32[]{:S(2)}) collective-permute-start(f32[1,64,512]{2,1,0:T(8,128)S(1)} %add.47), channel_id=1, source_target_pairs={{0,2},{1,3},{2,0},{3,1},{4,6},{5,7},{6,4},{7,5},{8,10},{9,11},{10,... | collective-permute-start | bytes 393224 | tf_op jit(solution)/shard_map/ppermute | solution.py:40
  39.9 1.5 %collective-permute-done.10 = f32[1,64,512]{2,1,0:T(8,128)S(1)} collective-permute-done((f32[1,64,512]{2,1,0:T(8,128)S(1)}, f32[1,64,512]{2,1,0:T(8,128)S(1)}, u32[]{:S(2)}, u32[]{:S(2)}) %collective-permute-start.10) | collective-permute-done | bytes 131104 | tf_op jit(solution)/shard_map/ppermute | solution.py:40
  41.4 4.0 %collective-permute-done.16 = f32[1,64,512]{2,1,0:T(8,128)S(1)} collective-permute-done((f32[1,64,512]{2,1,0:T(8,128)S(1)}, f32[1,64,512]{2,1,0:T(8,128)S(1)}, u32[]{:S(2)}, u32[]{:S(2)}) %collective-permute-start.16) | collective-permute-done | bytes 131104 | tf_op jit(solution)/shard_map/ppermute | solution.py:40
  45.4 0.0 collective-permute-done.14
  45.4 1.6 %collective-permute-done.12 = f32[1,64,512]{2,1,0:T(8,128)S(1)} collective-permute-done((f32[1,64,512]{2,1,0:T(8,128)S(1)}, f32[1,64,512]{2,1,0:T(8,128)S(1)}, u32[]{:S(2)}, u32[]{:S(2)}) %collective-permute-start.12) | collective-permute-done | bytes 131104 | tf_op jit(solution)/shard_map/ppermute | solution.py:40
  47.0 0.0 copy-done.1
  47.0 0.0 copy-done.2
  47.0 0.8 %add_divide_fusion = f32[1,64,512]{2,1,0:T(8,128)} fusion(f32[1,64,512]{2,1,0:T(8,128)S(1)} %collective-permute-done.16, f32[1,64,512]{2,1,0:T(8,128)S(1)} %collective-permute-done.14, f32[1,64,512]{2,1,0:T(8,128)S(1)} %collective-permute-done.12, f32[1,64,512]{2,1,0:T(8,128)S(1)} %copy-done.1, f32[1,64,512]{2,1,0:T(8,128)S(1)} %get-tuple-element.49, ...), kind=kLoop, calls=%fused_computation | loop fusion | flops 229376 | bytes 919808 | tf_op jit(solution)/shard_map/div | solution.py:417
  (10 shorter events, 0.1 us)
Async XLA Ops:
  0.0 24.0 %collective-permute-start.3 = (f32[512,512]{1,0:T(8,128)}, f32[512,512]{1,0:T(8,128)S(1)}, u32[]{:S(2)}, u32[]{:S(2)}) collective-permute-start(f32[512,512]{1,0:T(8,128)} %bitcast.4), channel_id=1, source_target_pairs={{0,8},{8,0},{16,24},{24,16},{1,9},{9,1},{17,25},{25,17},{2,10},{10... | collective-permute-start | bytes 3145736 | tf_op jit(solution)/shard_map/ppermute | solution.py:40
  1.6 12.2 %collective-permute-start.4 = (f32[144,512]{1,0:T(8,128)S(1)}, f32[144,512]{1,0:T(8,128)S(1)}, u32[]{:S(2)}, u32[]{:S(2)}) collective-permute-start(f32[144,512]{1,0:T(8,128)S(1)} %get-tuple-element.31), channel_id=1, source_target_pairs={{0,16},{8,24},{16,0},{24,8},{1,17},{9,25},{17,1},{25,9},{2,18},{10... | collective-permute-start | bytes 884744 | tf_op jit(solution)/shard_map/ppermute | solution.py:40
  4.1 19.2 %collective-permute-start.5 = (f32[224,512]{1,0:T(8,128)S(1)}, f32[224,512]{1,0:T(8,128)S(1)}, u32[]{:S(2)}, u32[]{:S(2)}) collective-permute-start(f32[224,512]{1,0:T(8,128)S(1)} %get-tuple-element.43), channel_id=1, source_target_pairs={{0,16},{8,24},{16,0},{24,8},{1,17},{9,25},{17,1},{25,9},{2,18},{10... | collective-permute-start | bytes 1376264 | tf_op jit(solution)/shard_map/ppermute | solution.py:40
  5.7 4.2 %collective-permute-start = (s32[3,1,96]{2,1,0:T(1,128)S(1)}, s32[3,1,96]{2,1,0:T(1,128)S(1)}, u32[]{:S(2)}, u32[]{:S(2)}) collective-permute-start(s32[3,1,96]{2,1,0:T(1,128)S(1)} %get-tuple-element.33), channel_id=1, source_target_pairs={{0,1},{1,0},{2,3},{3,2},{4,5},{5,4},{6,7},{7,6},{8,9},{9,8},{10,11... | collective-permute-start | bytes 3464 | tf_op jit(solution)/shard_map/ppermute | solution.py:40
  10.0 5.3 %collective-permute-start.1 = (s32[3,2,96]{2,1,0:T(2,128)S(1)}, s32[3,2,96]{2,1,0:T(2,128)S(1)}, u32[]{:S(2)}, u32[]{:S(2)}) collective-permute-start(s32[3,2,96]{2,1,0:T(2,128)S(1)} %pad_add_fusion.2), channel_id=1, source_target_pairs={{0,2},{1,3},{2,0},{3,1},{4,6},{5,7},{6,4},{7,5},{8,10},{9,11},{10,... | collective-permute-start | bytes 6920 | tf_op jit(solution)/shard_map/ppermute | solution.py:40
  13.7 10.2 %collective-permute-start.6 = (f32[144,512]{1,0:T(8,128)S(1)}, f32[144,512]{1,0:T(8,128)S(1)}, u32[]{:S(2)}, u32[]{:S(2)}) collective-permute-start(f32[144,512]{1,0:T(8,128)S(1)} %collective-permute-done.4.rest_0_), channel_id=1, source_target_pairs={{0,1},{1,0},{2,3},{3,2},{4,5},{5,4},{6,7},{7,6},{8,9},{9,8},{10,11... | collective-permute-start | bytes 884744 | tf_op jit(solution)/shard_map/ppermute | solution.py:40
  15.3 4.6 %collective-permute-start.2 = (s32[3,4,96]{2,1,0:T(4,128)S(1)}, s32[3,4,96]{2,1,0:T(4,128)S(1)}, u32[]{:S(2)}, u32[]{:S(2)}) collective-permute-start(s32[3,4,96]{2,1,0:T(4,128)S(1)} %pad_add_fusion.1), channel_id=1, source_target_pairs={{0,4},{1,5},{2,6},{3,7},{4,0},{5,1},{6,2},{7,3},{8,12},{9,13},{10,... | collective-permute-start | bytes 13832 | tf_op jit(solution)/shard_map/ppermute | solution.py:40
  19.9 4.2 %copy-start = (f32[1,512,512]{2,1,0:T(8,128)S(1)}, f32[1,512,512]{2,1,0:T(8,128)}, u32[]{:S(2)}) copy-start(f32[1,512,512]{2,1,0:T(8,128)} %param.13) | copy-start | bytes 3145732
  23.4 2.7 %collective-permute-start.8 = (f32[224,512]{1,0:T(8,128)S(1)}, f32[224,512]{1,0:T(8,128)S(1)}, u32[]{:S(2)}, u32[]{:S(2)}) collective-permute-start(f32[224,512]{1,0:T(8,128)S(1)} %collective-permute-done.5.rest_1_), channel_id=1, source_target_pairs={{0,8},{8,0},{16,24},{24,16},{1,9},{9,1},{17,25},{25,17},{2,10},{10... | collective-permute-start | bytes 1376264 | tf_op jit(solution)/shard_map/ppermute | solution.py:40
  23.5 2.2 %collective-permute-start.7 = (f32[144,512]{1,0:T(8,128)S(1)}, f32[144,512]{1,0:T(8,128)S(1)}, u32[]{:S(2)}, u32[]{:S(2)}) collective-permute-start(f32[144,512]{1,0:T(8,128)S(1)} %collective-permute-done.4.rest_0_), channel_id=1, source_target_pairs={{0,8},{8,0},{16,24},{24,16},{1,9},{9,1},{17,25},{25,17},{2,10},{10... | collective-permute-start | bytes 884744 | tf_op jit(solution)/shard_map/ppermute | solution.py:40
  24.0 2.1 %collective-permute-start.9 = (f32[144,512]{1,0:T(8,128)S(1)}, f32[144,512]{1,0:T(8,128)S(1)}, u32[]{:S(2)}, u32[]{:S(2)}) collective-permute-start(f32[144,512]{1,0:T(8,128)S(1)} %collective-permute-done.6.rest_2_), channel_id=1, source_target_pairs={{0,8},{8,0},{16,24},{24,16},{1,9},{9,1},{17,25},{25,17},{2,10},{10... | collective-permute-start | bytes 884744 | tf_op jit(solution)/shard_map/ppermute | solution.py:40
  27.4 6.4 %collective-permute-start.15 = (f32[1,64,512]{2,1,0:T(8,128)S(1)}, f32[1,64,512]{2,1,0:T(8,128)S(1)}, u32[]{:S(2)}, u32[]{:S(2)}) collective-permute-start(f32[1,64,512]{2,1,0:T(8,128)S(1)} %get-tuple-element.56), channel_id=1, source_target_pairs={{0,1},{1,0},{2,3},{3,2},{4,5},{5,4},{6,7},{7,6},{8,9},{9,8},{10,11... | collective-permute-start | bytes 393224 | tf_op jit(solution)/shard_map/ppermute | solution.py:40
  28.0 8.5 %collective-permute-start.13 = (f32[1,64,512]{2,1,0:T(8,128)S(1)}, f32[1,64,512]{2,1,0:T(8,128)S(1)}, u32[]{:S(2)}, u32[]{:S(2)}) collective-permute-start(f32[1,64,512]{2,1,0:T(8,128)S(1)} %get-tuple-element.54), channel_id=1, source_target_pairs={{0,1},{1,0},{2,3},{3,2},{4,5},{5,4},{6,7},{7,6},{8,9},{9,8},{10,11... | collective-permute-start | bytes 393224 | tf_op jit(solution)/shard_map/ppermute | solution.py:40
  29.4 9.9 %collective-permute-start.11 = (f32[1,64,512]{2,1,0:T(8,128)S(1)}, f32[1,64,512]{2,1,0:T(8,128)S(1)}, u32[]{:S(2)}, u32[]{:S(2)}) collective-permute-start(f32[1,64,512]{2,1,0:T(8,128)S(1)} %get-tuple-element.52), channel_id=1, source_target_pairs={{0,1},{1,0},{2,3},{3,2},{4,5},{5,4},{6,7},{7,6},{8,9},{9,8},{10,11... | collective-permute-start | bytes 393224 | tf_op jit(solution)/shard_map/ppermute | solution.py:40
  30.0 11.3 %collective-permute-start.10 = (f32[1,64,512]{2,1,0:T(8,128)S(1)}, f32[1,64,512]{2,1,0:T(8,128)S(1)}, u32[]{:S(2)}, u32[]{:S(2)}) collective-permute-start(f32[1,64,512]{2,1,0:T(8,128)S(1)} %get-tuple-element.50), channel_id=1, source_target_pairs={{0,1},{1,0},{2,3},{3,2},{4,5},{5,4},{6,7},{7,6},{8,9},{9,8},{10,11... | collective-permute-start | bytes 393224 | tf_op jit(solution)/shard_map/ppermute | solution.py:40
  31.5 15.6 %copy-start.1 = (f32[1,64,512]{2,1,0:T(8,128)S(1)}, f32[1,64,512]{2,1,0:T(8,128)}, u32[]{:S(2)}) copy-start(f32[1,64,512]{2,1,0:T(8,128)} %param.14) | copy-start | bytes 393220
  31.5 15.6 %copy-start.2 = (f32[512]{0:T(512)S(1)}, f32[512]{0:T(512)}, u32[]{:S(2)}) copy-start(f32[512]{0:T(512)} %param.16) | copy-start | bytes 6148
  31.5 15.6 %copy-start.3 = (f32[1,64]{1,0:T(1,128)S(1)}, f32[1,64]{1,0:T(1,128)}, u32[]{:S(2)}) copy-start(f32[1,64]{1,0:T(1,128)} %param.15) | copy-start | bytes 772
  33.8 11.6 %collective-permute-start.16 = (f32[1,64,512]{2,1,0:T(8,128)S(1)}, f32[1,64,512]{2,1,0:T(8,128)S(1)}, u32[]{:S(2)}, u32[]{:S(2)}) collective-permute-start(f32[1,64,512]{2,1,0:T(8,128)S(1)} %add.51), channel_id=1, source_target_pairs={{0,4},{1,5},{2,6},{3,7},{4,0},{5,1},{6,2},{7,3},{8,12},{9,13},{10,... | collective-permute-start | bytes 393224 | tf_op jit(solution)/shard_map/ppermute | solution.py:40
  36.6 8.8 %collective-permute-start.14 = (f32[1,64,512]{2,1,0:T(8,128)S(1)}, f32[1,64,512]{2,1,0:T(8,128)S(1)}, u32[]{:S(2)}, u32[]{:S(2)}) collective-permute-start(f32[1,64,512]{2,1,0:T(8,128)S(1)} %add.49), channel_id=1, source_target_pairs={{0,6},{1,7},{2,4},{3,5},{4,2},{5,3},{6,0},{7,1},{8,14},{9,15},{10,... | collective-permute-start | bytes 393224 | tf_op jit(solution)/shard_map/ppermute | solution.py:40
  39.4 7.6 %collective-permute-start.12 = (f32[1,64,512]{2,1,0:T(8,128)S(1)}, f32[1,64,512]{2,1,0:T(8,128)S(1)}, u32[]{:S(2)}, u32[]{:S(2)}) collective-permute-start(f32[1,64,512]{2,1,0:T(8,128)S(1)} %add.47), channel_id=1, source_target_pairs={{0,2},{1,3},{2,0},{3,1},{4,6},{5,7},{6,4},{7,5},{8,10},{9,11},{10,... | collective-permute-start | bytes 393224 | tf_op jit(solution)/shard_map/ppermute | solution.py:40

commit v5 on v4

--- a/solution.py
+++ b/solution.py
@@ -157,27 +157,6 @@
         cost_estimate=cost(0, 8 * rows * amp_dev * depth),
         name="load_amplitudes",
     )(in_hbm(amplitudes))
-
-
-def local_kernel(own_ref, pair_ref, in_hi, in_lo):
-    depth = own_ref.shape[0]
-    for c, ref in enumerate((own_ref, pair_ref)):
-        hi, lo = split(ref[...])
-        in_hi[c * depth : (c + 1) * depth, :] = hi
-        in_lo[c * depth : (c + 1) * depth, :] = lo
-
-
-def split_local(own, pair):
-    depth, window = own.shape
-    return pl.pallas_call(
-        local_kernel,
-        out_shape=[pltpu.VMEM((2 * depth, window), jnp.bfloat16)] * 2,
-        in_specs=[VMEM] * 2,
-        out_specs=[VMEM] * 2,
-        compiler_params=limit(16 * depth * window),
-        cost_estimate=cost(0, 16 * depth * window),
-        name="split_local",
-    )(own, pair)
 
 
 def coefficients(lists_ref, table_ref, amp_dev, lanes, blocks):
@@ -231,45 +210,6 @@
     return jnp.where(same, weight, 0.0).astype(jnp.bfloat16)
 
 
-def sums_kernel(lanes, blocks, amp_dev, lists_ref, table_ref, *refs):
-    amp_refs, sums_refs = refs[:-4], refs[-4:]
-    weight = coefficients(lists_ref, table_ref, amp_dev, lanes, blocks)
-    depth = amp_refs[0].shape[1]
-    step = weight.shape[0] // (2 * blocks)
-    first = 0
-    for ref in amp_refs:
-        count = ref.shape[0] // DEEP
-
-        def add(g, _, ref=ref, first=first):
-            rows = ref[pl.ds(pl.multiple_of(g * DEEP, DEEP), DEEP), :]
-            total = jnp.dot(weight, rows, preferred_element_type=jnp.float32)
-            at = pl.ds(pl.multiple_of((first + g) * step, step), step)
-            for k in range(2):
-                for c in range(blocks):
-                    r = (k * blocks + c) * step
-                    hi, lo = split(total[r : r + step, :])
-                    sums_refs[2 * k][at, c * depth : (c + 1) * depth] = hi
-                    sums_refs[2 * k + 1][at, c * depth : (c + 1) * depth] = lo
-            return 0
-
-        lax.fori_loop(0, count, add, 0)
-        first += count
-
-
-def sums(lists, table, rows, amp_dev, tile_rows, lanes, blocks):
-    depth = rows[0].shape[1]
-    held = pltpu.VMEM((lanes // 2 * tile_rows, blocks * depth), jnp.bfloat16)
-    return pl.pallas_call(
-        functools.partial(sums_kernel, lanes, blocks, amp_dev),
-        out_shape=[held] * 4,
-        in_specs=[VMEM] * (2 + len(rows)),
-        out_specs=[VMEM] * 4,
-        compiler_params=limit(0),
-        cost_estimate=cost(0, 16 * tile_rows * amp_dev * depth),
-        name="sums",
-    )(lists, table, *[in_vmem(x) for x in rows])
-
-
 def passes(hi, lo, in_hi, in_lo):
     dot = functools.partial(jnp.dot, preferred_element_type=jnp.float32)
     return dot(hi, in_hi) + dot(hi, in_lo) + dot(lo, in_hi)
@@ -285,27 +225,55 @@
             ref[0, :, b * LANES : (b + 1) * LANES] = held[b, pl.ds(j, rows, stride=tiles), :]
 
 
-def local_products_kernel(hi, lo, in_hi, in_lo, out_ref):
-    depth = in_hi.shape[0]
-    out_ref[...] = passes(hi[:, :depth], lo[:, :depth], in_hi[...], in_lo[...])
-
-
-def local_products(hi, lo, in_hi, in_lo):
-    depth, window = in_hi.shape
+def sums_kernel(lanes, blocks, amp_dev, lists_ref, table_ref, own_ref, pair_ref, *refs):
+    amp_refs, sums_refs, local_refs, (in_hi, in_lo) = refs[:2], refs[2:6], refs[6:8], refs[8:]
+    weight = coefficients(lists_ref, table_ref, amp_dev, lanes, blocks)
+    depth = own_ref.shape[0]
+    step = weight.shape[0] // (2 * blocks)
+    first = 0
+    for ref in amp_refs:
+        count = ref.shape[0] // DEEP
+        for g in range(count):
+            rows = ref[g * DEEP : (g + 1) * DEEP, :]
+            total = jnp.dot(weight, rows, preferred_element_type=jnp.float32)
+            at = slice((first + g) * step, (first + g + 1) * step)
+            for k in range(2):
+                for c in range(blocks):
+                    r = (k * blocks + c) * step
+                    hi, lo = split(total[r : r + step, :])
+                    sums_refs[2 * k][at, c * depth : (c + 1) * depth] = hi
+                    sums_refs[2 * k + 1][at, c * depth : (c + 1) * depth] = lo
+        first += count
+    for c, ref in enumerate((own_ref, pair_ref)):
+        hi, lo = split(ref[...])
+        in_hi[c * depth : (c + 1) * depth, :] = hi
+        in_lo[c * depth : (c + 1) * depth, :] = lo
+    for k, ref in enumerate(local_refs):
+        hi, lo = (x[:, : 2 * depth] for x in sums_refs[2 * k : 2 * k + 2])
+        ref[...] = passes(hi, lo, in_hi[...], in_lo[...])
+
+
+def sums(lists, table, own, pair, rows, amp_dev, tile_rows, lanes, blocks):
+    depth, window = own.shape
+    kept = lanes // 2 * tile_rows
+    held = pltpu.VMEM((kept, blocks * depth), jnp.bfloat16)
+    local = pltpu.VMEM((2 * depth, window), jnp.bfloat16)
+    product = pltpu.VMEM((kept, window), jnp.float32)
     return pl.pallas_call(
-        local_products_kernel,
-        out_shape=pltpu.VMEM((hi.shape[0], window), jnp.float32),
-        in_specs=[VMEM] * 4,
-        out_specs=VMEM,
-        compiler_params=limit(0),
-        cost_estimate=cost(6 * hi.shape[0] * depth * window, 0),
-        name="local_products",
-    )(*[in_vmem(x) for x in (hi, lo, in_hi, in_lo)])
-
-
-def away_kernel(tiles, blocks, hi, lo, local_ref, *rest):
+        functools.partial(sums_kernel, lanes, blocks, amp_dev),
+        out_shape=[held] * 4 + [product] * 2,
+        in_specs=[VMEM] * (4 + len(rows)),
+        out_specs=[VMEM] * 6,
+        scratch_shapes=[local] * 2,
+        compiler_params=limit(16 * depth * window),
+        cost_estimate=cost(0, 16 * tile_rows * amp_dev * depth),
+        name="sums",
+    )(lists, table, own, pair, *[in_vmem(x) for x in rows])
+
+
+def away_kernel(blocks, hi, lo, local_ref, *rest):
     n = 3 * (blocks - 2)
-    parts, out_refs, (in_hi, in_lo, held) = rest[:n], rest[n : n + tiles], rest[n + tiles :]
+    parts, out_refs, (in_hi, in_lo, held) = rest[:n], rest[n:-3], rest[-3:]
     depth = in_hi.shape[0] // (blocks - 2)
     mine, theirs = end_offsets(depth)
     for c in range(blocks - 2):
@@ -319,12 +287,11 @@
     store_tiles(local_ref[...] + out, out_refs, held)
 
 
-def side_kernel(tiles, hi, lo, local_hi, local_lo, in_hi, in_lo, *rest):
-    out_refs, held = rest[:tiles], rest[tiles]
-    depth = local_hi.shape[0]
-    out = passes(hi[:, :depth], lo[:, :depth], local_hi[...], local_lo[...])
-    out += passes(hi[:, depth:], lo[:, depth:], in_hi[...], in_lo[...])
-    store_tiles(out, out_refs, held)
+def side_kernel(hi, lo, local_ref, in_hi, in_lo, *rest):
+    out_refs, held = rest[:-1], rest[-1]
+    lead = hi.shape[1] - in_hi.shape[0]
+    out = passes(hi[:, lead:], lo[:, lead:], in_hi[...], in_lo[...])
+    store_tiles(local_ref[...] + out, out_refs, held)
 
 
 def away_products(hi, lo, local, parts, tiles):
@@ -332,12 +299,12 @@
     depth = hi.shape[1] // blocks
     rows, window = local.shape
     remote = pltpu.VMEM(((blocks - 2) * depth, window), jnp.bfloat16)
+    shapes = [jax.ShapeDtypeStruct((1, rows // tiles, window), jnp.float32)] * tiles
     *out, in_hi, in_lo = pl.pallas_call(
-        functools.partial(away_kernel, tiles, blocks),
-        out_shape=[jax.ShapeDtypeStruct((1, rows // tiles, window), jnp.float32)] * tiles
-        + [remote] * 2,
+        functools.partial(away_kernel, blocks),
+        out_shape=shapes + [remote] * 2,
         in_specs=[VMEM] * (3 + 3 * len(parts)),
-        out_specs=[VMEM] * (tiles + 2),
+        out_specs=[VMEM] * (len(shapes) + 2),
         scratch_shapes=[pltpu.VMEM((window // LANES, rows, LANES), jnp.float32)],
         compiler_params=limit(4 * blocks * depth * window),
         cost_estimate=cost(6 * rows * (blocks - 2) * depth * window, 0),
@@ -346,19 +313,19 @@
     return out, in_hi, in_lo
 
 
-def side_products(hi, lo, local_hi, local_lo, in_hi, in_lo, tiles):
-    rows, depth = hi.shape
-    window = in_hi.shape[1]
+def side_products(hi, lo, local, in_hi, in_lo, tiles):
+    rows, window = local.shape
+    shapes = [jax.ShapeDtypeStruct((1, rows // tiles, window), jnp.float32)] * tiles
     return pl.pallas_call(
-        functools.partial(side_kernel, tiles),
-        out_shape=[jax.ShapeDtypeStruct((1, rows // tiles, window), jnp.float32)] * tiles,
-        in_specs=[VMEM] * 6,
-        out_specs=[VMEM] * tiles,
+        side_kernel,
+        out_shape=shapes,
+        in_specs=[VMEM] * 5,
+        out_specs=[VMEM] * len(shapes),
         scratch_shapes=[pltpu.VMEM((window // LANES, rows, LANES), jnp.float32)],
         compiler_params=limit(0),
-        cost_estimate=cost(6 * rows * depth * window, 0),
+        cost_estimate=cost(6 * rows * in_hi.size, 0),
         name="side_products",
-    )(*[in_vmem(x) for x in (hi, lo, local_hi, local_lo, in_hi, in_lo)])
+    )(*[in_vmem(x) for x in (hi, lo, local, in_hi, in_lo)])
 
 
 def on_device(
@@ -387,14 +354,16 @@
     )
     pair = swap(own, "grp", 1)
     rows = [load(amplitudes, i * tile_rows // 2, tile_rows // 2) for i in range(2)]
-    local_hi, local_lo = split_local(own, pair)
     k = 1
     while k < lanes:
-        if k in (2, 4):
-            lists = after(lists, rows[k // 4])
+        if k == 2:
+            lists = after(lists, rows[0])
         lists = jnp.concatenate([lists, swap(lists, "wide", k)], axis=1)
         k *= 2
-    away_hi, away_lo, side_hi, side_lo = sums(lists, table, rows, amp_dev, tile_rows, lanes, grps)
+    lists = after(lists, rows[1])
+    away_hi, away_lo, side_hi, side_lo, *local = sums(
+        lists, table, own, pair, rows, amp_dev, tile_rows, lanes, grps
+    )
 
     parts = [None] * (grps - 2)
     for k, (one, two) in fetched.items():
@@ -404,13 +373,12 @@
             swap(after(x, y), "grp", 1) for x, y in zip(three, (lists, away_hi, away_hi))
         ]
 
-    local = local_products(away_hi, away_lo, local_hi, local_lo)
-    away, in_hi, in_lo = away_products(away_hi, away_lo, local, parts, half)
-    side = side_products(side_hi, side_lo, local_hi, local_lo, in_hi, in_lo, half)
+    away, in_hi, in_lo = away_products(away_hi, away_lo, local[0], parts, half)
+    side = side_products(side_hi, side_lo, local[1], in_hi, in_lo, half)
     _, offsets = tile_order(lanes)
     got = [swap(x, "wide", 1) for x in away]
     summed = base_residual
-    for k, here, there in reversed(list(zip(offsets, side, got))):
+    for k, here, there in zip(offsets, side, got):
         part = here + there
         summed = summed + (swap(part, "wide", k) if k else part)
     divisor = occ_gap[:, :, None] + virt_sum[None, None, :]

time: 48.1 us -> 46.5 us (0.967)
  Pallas kernels: 14 us -> 11.5 us
  starting transfers between devices: 21.4 us -> 23.2 us
  waiting for transfers between devices: 10.7 us -> 9.8 us
    pallas_call x4 -> x2, Pallas kernels: 4.28 us -> 2.23 us  [the longest x1 1.23 us: away_products(): pl.pallas_call(functools.partial(away_kernel, blocks), out_shape=shapes +...]
    ppermute x17, starting transfers between devices: 21.4 us -> 23.2 us  [swap(): return lax.ppermute(x, axis, [(i, i ^ k) for i in range(n)])]
    ppermute x17, waiting for transfers between devices: 10.7 us -> 9.8 us  [swap(): return lax.ppermute(x, axis, [(i, i ^ k) for i in range(n)])]
  transfers between devices with their start and end apart: 17 -> 17, of which waited for: 9 -> 8; matrix products, arithmetic and copies ran while one was open for 0% -> 0% of each run, Pallas kernels for 27% -> 22%
where the time goes in v5:
time: 46.5 us; the launch traced here: 46.2 us
  starting transfers between devices  23.2 us (50%)
  Pallas kernels  11.5 us (25%)
  waiting for transfers between devices  9.8 us (21%)
  other arithmetic  0.84 us (2%)
  between operations  0.8 us (2%)
    ppermute x17, starting transfers between devices, swap(): return lax.ppermute(x, axis, [(i, i ^ k) for i in range(n)])  23.2 us
    ppermute x17, waiting for transfers between devices, swap(): return lax.ppermute(x, axis, [(i, i ^ k) for i in range(n)])  9.8 us
    pallas_call x2, Pallas kernels, load(): pl.pallas_call(functools.partial(load_kernel, first), out_shape=pltpu.VME...  4.26 us
    pallas_call x1, Pallas kernels, sums(): pl.pallas_call(functools.partial(sums_kernel, lanes, blocks, amp_dev), ou...  3.03 us
    pallas_call x1, Pallas kernels, away_products(): pl.pallas_call(functools.partial(away_kernel, blocks), out_shape=shapes +...  1.23 us
    pallas_call x1, Pallas kernels, pieces(): pl.pallas_call(pieces_kernel, out_shape=[pltpu.VMEM((n, own.shape[1]), ow...  1.12 us
    pallas_call x1, Pallas kernels, side_products(): pl.pallas_call(side_kernel, out_shape=shapes, in_specs=[VMEM] * 5, out_sp...  1 us
  transfers between devices with their start and end apart: 17, of which 8 were waited for; matrix products, arithmetic and copies ran while one was open for 0% of the time, Pallas kernels for 22%

profile of v5, /device:TPU:0, one launch (start us, length us, event | category | flops | bytes accessed | tf_op | source)
XLA Modules:
  0.0 46.2 jit_solution(1209842625148586253)
XLA Ops:
  0.0 0.5 collective-permute-start.3
  0.5 1.1 %pieces.1 = (f32[144,512]{1,0:T(8,128)S(1)}, f32[224,512]{1,0:T(8,128)S(1)}) custom-call(f32[512,512]{1,0:T(8,128)} %bitcast.5), custom_call_target="tpu_custom_call" | custom-call | bytes 1048576 | tf_op jit(solution)/shard_map/pieces/pallas_call | solution.py:77
  1.6 2.6 %collective-permute-start.4 = (f32[144,512]{1,0:T(8,128)S(1)}, f32[144,512]{1,0:T(8,128)S(1)}, u32[]{:S(2)}, u32[]{:S(2)}) collective-permute-start(f32[144,512]{1,0:T(8,128)S(1)} %get-tuple-element.31), channel_id=1, source_target_pairs={{0,16},{8,24},{16,0},{24,8},{1,17},{9,25},{17,1},{25,9},{2,18},{10... | collective-permute-start | bytes 884744 | tf_op jit(solution)/shard_map/ppermute | solution.py:40
  4.1 0.1 collective-permute-start.5
  4.9 0.9 %pack_lists.1 = (s32[3,1,96]{2,1,0:T(1,128)S(1)}, s32[3,256]{1,0:T(4,128)S(1)}) custom-call(s32[1]{0:T(128)S(6)} %copy.13.count_ref, s32[1,96]{1,0:T(1,128)} %refs_0_.1, s32[1,96]{1,0:T(1,128)} %refs_1_.1, s32[1,96]{1,0:T(1,128)} %refs_2_, s32[1,32]{1,0:T(1,128)} %bitcast.8, s32[1,8]{1,0:T(1,128)} %refs_4_.1, s32[1,4]{1,0:T(1,128)} %bitcast.9), custom_call_target="tpu_custom_call" | custom-call | bytes 4096 | tf_op jit(solution)/shard_map/pack_lists/pallas_call | solution.py:112
  5.7 2.0 %collective-permute-start = (s32[3,1,96]{2,1,0:T(1,128)S(1)}, s32[3,1,96]{2,1,0:T(1,128)S(1)}, u32[]{:S(2)}, u32[]{:S(2)}) collective-permute-start(s32[3,1,96]{2,1,0:T(1,128)S(1)} %get-tuple-element.33), channel_id=1, source_target_pairs={{0,1},{1,0},{2,3},{3,2},{4,5},{5,4},{6,7},{7,6},{8,9},{9,8},{10,11... | collective-permute-start | bytes 3464 | tf_op jit(solution)/shard_map/ppermute | solution.py:40
  7.8 2.1 %load_amplitudes.2.refs_0_ = bf16[2048,512]{1,0:T(8,128)(2,1)S(1)} custom-call(f32[32,64,512]{2,1,0:T(8,128)} %amp_hbm.3), custom_call_target="tpu_custom_call" | custom-call | bytes 4194304 | tf_op jit(solution)/shard_map/load_amplitudes/pallas_call | solution.py:147
  9.9 0.0 collective-permute-done
  10.0 1.6 %collective-permute-start.1 = (s32[3,2,96]{2,1,0:T(2,128)S(1)}, s32[3,2,96]{2,1,0:T(2,128)S(1)}, u32[]{:S(2)}, u32[]{:S(2)}) collective-permute-start(s32[3,2,96]{2,1,0:T(2,128)S(1)} %pad_add_fusion.2), channel_id=1, source_target_pairs={{0,2},{1,3},{2,0},{3,1},{4,6},{5,7},{6,4},{7,5},{8,10},{9,11},{10,... | collective-permute-start | bytes 6920 | tf_op jit(solution)/shard_map/ppermute | solution.py:40
  11.6 0.4 collective-permute-done.4.rest_0_
  12.0 2.0 %collective-permute-start.6 = (f32[144,512]{1,0:T(8,128)S(1)}, f32[144,512]{1,0:T(8,128)S(1)}, u32[]{:S(2)}, u32[]{:S(2)}) collective-permute-start(f32[144,512]{1,0:T(8,128)S(1)} %collective-permute-done.4.rest_0_), channel_id=1, source_target_pairs={{0,1},{1,0},{2,3},{3,2},{4,5},{5,4},{6,7},{7,6},{8,9},{9,8},{10,11... | collective-permute-start | bytes 884744 | tf_op jit(solution)/shard_map/ppermute | solution.py:40
  14.0 0.0 collective-permute-done.1
  14.0 0.0 copy-start
  14.0 2.7 %collective-permute-start.2 = (s32[3,4,96]{2,1,0:T(4,128)S(1)}, s32[3,4,96]{2,1,0:T(4,128)S(1)}, u32[]{:S(2)}, u32[]{:S(2)}) collective-permute-start(s32[3,4,96]{2,1,0:T(4,128)S(1)} %pad_add_fusion.1), channel_id=1, source_target_pairs={{0,4},{1,5},{2,6},{3,7},{4,0},{5,1},{6,2},{7,3},{8,12},{9,13},{10,... | collective-permute-start | bytes 13832 | tf_op jit(solution)/shard_map/ppermute | solution.py:40
  16.7 2.1 %load_amplitudes.3.refs_1_ = bf16[2048,512]{1,0:T(8,128)(2,1)S(1)} custom-call(f32[32,64,512]{2,1,0:T(8,128)} %amp_hbm.3), custom_call_target="tpu_custom_call" | custom-call | bytes 4194304 | tf_op jit(solution)/shard_map/load_amplitudes/pallas_call | solution.py:147
  18.8 0.0 collective-permute-done.2
  18.8 0.0 collective-permute-done.3.pair_ref
  18.8 0.0 copy-done
  18.8 3.0 %sums.1 = (bf16[256,2048]{1,0:T(8,128)(2,1)S(1)}, bf16[256,2048]{1,0:T(8,128)(2,1)S(1)}, bf16[256,2048]{1,0:T(8,128)(2,1)S(1)}, bf16[256,2048]{1,0:T(8,128)(2,1)...) custom-call(s32[3,8,96]{2,1,0:T(8,128)S(1)} %pad_add_fusion.lists_ref, s32[3,256]{1,0:T(4,128)S(1)} %get-tuple-element.36.table_ref, ...), custom_call_target="tpu_custom_call" | custom-call | bytes 16777216 | tf_op jit(solution)/shard_map/sums/pallas_call | solution.py:262
  21.9 0.0 collective-permute-done.5.rest_1_
  21.9 0.1 collective-permute-start.8
  22.0 0.5 %collective-permute-start.7 = (f32[144,512]{1,0:T(8,128)S(1)}, f32[144,512]{1,0:T(8,128)S(1)}, u32[]{:S(2)}, u32[]{:S(2)}) collective-permute-start(f32[144,512]{1,0:T(8,128)S(1)} %collective-permute-done.4.rest_0_), channel_id=1, source_target_pairs={{0,8},{8,0},{16,24},{24,16},{1,9},{9,1},{17,25},{25,17},{2,10},{10... | collective-permute-start | bytes 884744 | tf_op jit(solution)/shard_map/ppermute | solution.py:40
  22.5 0.0 collective-permute-done.6.rest_2_
  22.5 0.1 collective-permute-start.9
  22.5 1.6 %collective-permute-done.7.rest_3_ = f32[144,512]{1,0:T(8,128)S(1)} collective-permute-done((f32[144,512]{1,0:T(8,128)S(1)}, f32[144,512]{1,0:T(8,128)S(1)}, u32[]{:S(2)}, u32[]{:S(2)}) %collective-permute-start.7) | collective-permute-done | bytes 294944 | tf_op jit(solution)/shard_map/ppermute | solution.py:40
  24.2 0.4 collective-permute-done.9.rest_5_
  24.6 0.0 collective-permute-done.8.rest_4_
  24.6 1.2 %away_products.1 = (f32[1,64,512]{2,1,0:T(8,128)S(1)}, f32[1,64,512]{2,1,0:T(8,128)S(1)}, f32[1,64,512]{2,1,0:T(8,128)S(1)}, f32[1,64,512]{2,1,0:T(8,128)S(1)}, ...) custom-call(bf16[256,2048]{1,0:T(8,128)(2,1)S(1)} %get-tuple-element.40.hi, ...), custom_call_target="tpu_custom_call" | custom-call | flops 805306368 | tf_op jit(solution)/shard_map/away_products/pallas_call | solution.py:303
  25.9 1.5 %collective-permute-start.10 = (f32[1,64,512]{2,1,0:T(8,128)S(1)}, f32[1,64,512]{2,1,0:T(8,128)S(1)}, u32[]{:S(2)}, u32[]{:S(2)}) collective-permute-start(f32[1,64,512]{2,1,0:T(8,128)S(1)} %get-tuple-element.50), channel_id=1, source_target_pairs={{0,1},{1,0},{2,3},{3,2},{4,5},{5,4},{6,7},{7,6},{8,9},{9,8},{10,11... | collective-permute-start | bytes 393224 | tf_op jit(solution)/shard_map/ppermute | solution.py:40
  27.4 0.6 %collective-permute-start.12 = (f32[1,64,512]{2,1,0:T(8,128)S(1)}, f32[1,64,512]{2,1,0:T(8,128)S(1)}, u32[]{:S(2)}, u32[]{:S(2)}) collective-permute-start(f32[1,64,512]{2,1,0:T(8,128)S(1)} %get-tuple-element.52), channel_id=1, source_target_pairs={{0,1},{1,0},{2,3},{3,2},{4,5},{5,4},{6,7},{7,6},{8,9},{9,8},{10,11... | collective-permute-start | bytes 393224 | tf_op jit(solution)/shard_map/ppermute | solution.py:40
  27.9 1.5 %collective-permute-start.14 = (f32[1,64,512]{2,1,0:T(8,128)S(1)}, f32[1,64,512]{2,1,0:T(8,128)S(1)}, u32[]{:S(2)}, u32[]{:S(2)}) collective-permute-start(f32[1,64,512]{2,1,0:T(8,128)S(1)} %get-tuple-element.54), channel_id=1, source_target_pairs={{0,1},{1,0},{2,3},{3,2},{4,5},{5,4},{6,7},{7,6},{8,9},{9,8},{10,11... | collective-permute-start | bytes 393224 | tf_op jit(solution)/shard_map/ppermute | solution.py:40
  29.4 0.6 %collective-permute-start.16 = (f32[1,64,512]{2,1,0:T(8,128)S(1)}, f32[1,64,512]{2,1,0:T(8,128)S(1)}, u32[]{:S(2)}, u32[]{:S(2)}) collective-permute-start(f32[1,64,512]{2,1,0:T(8,128)S(1)} %get-tuple-element.56), channel_id=1, source_target_pairs={{0,1},{1,0},{2,3},{3,2},{4,5},{5,4},{6,7},{7,6},{8,9},{9,8},{10,11... | collective-permute-start | bytes 393224 | tf_op jit(solution)/shard_map/ppermute | solution.py:40
  30.0 0.0 copy-start.1
  30.0 1.0 %side_products.1 = (f32[1,64,512]{2,1,0:T(8,128)S(1)}, f32[1,64,512]{2,1,0:T(8,128)S(1)}, f32[1,64,512]{2,1,0:T(8,128)S(1)}, f32[1,64,512]{2,1,0:T(8,128)S(1)}) custom-call(bf16[256,2048]{1,0:T(8,128)(2,1)S(1)} %get-tuple-element.37.hi, bf16[256,2048]{1,0:T(8,128)(2,1)S(1)} %get-tuple-element.38.lo, f32[256,512]{1,0:T(8,128)S(1)} %get-tuple-element.39.local_ref, ...), custom_call_target="tpu_custom_call" | custom-call | flops 805306368 | tf_op jit(solution)/shard_map/side_products/pallas_call | solution.py:319
  31.0 1.3 %collective-permute-done.10 = f32[1,64,512]{2,1,0:T(8,128)S(1)} collective-permute-done((f32[1,64,512]{2,1,0:T(8,128)S(1)}, f32[1,64,512]{2,1,0:T(8,128)S(1)}, u32[]{:S(2)}, u32[]{:S(2)}) %collective-permute-start.10) | collective-permute-done | bytes 131104 | tf_op jit(solution)/shard_map/ppermute | solution.py:40
  32.3 2.6 %collective-permute-start.11 = (f32[1,64,512]{2,1,0:T(8,128)S(1)}, f32[1,64,512]{2,1,0:T(8,128)S(1)}, u32[]{:S(2)}, u32[]{:S(2)}) collective-permute-start(f32[1,64,512]{2,1,0:T(8,128)S(1)} %add.45), channel_id=1, source_target_pairs={{0,4},{1,5},{2,6},{3,7},{4,0},{5,1},{6,2},{7,3},{8,12},{9,13},{10,... | collective-permute-start | bytes 393224 | tf_op jit(solution)/shard_map/ppermute | solution.py:40
  34.9 0.2 collective-permute-done.12
  35.1 3.6 %collective-permute-start.13 = (f32[1,64,512]{2,1,0:T(8,128)S(1)}, f32[1,64,512]{2,1,0:T(8,128)S(1)}, u32[]{:S(2)}, u32[]{:S(2)}) collective-permute-start(f32[1,64,512]{2,1,0:T(8,128)S(1)} %add.47), channel_id=1, source_target_pairs={{0,6},{1,7},{2,4},{3,5},{4,2},{5,3},{6,0},{7,1},{8,14},{9,15},{10,... | collective-permute-start | bytes 393224 | tf_op jit(solution)/shard_map/ppermute | solution.py:40
  38.7 0.0 collective-permute-done.14
  38.7 0.8 %collective-permute-start.15 = (f32[1,64,512]{2,1,0:T(8,128)S(1)}, f32[1,64,512]{2,1,0:T(8,128)S(1)}, u32[]{:S(2)}, u32[]{:S(2)}) collective-permute-start(f32[1,64,512]{2,1,0:T(8,128)S(1)} %add.49), channel_id=1, source_target_pairs={{0,2},{1,3},{2,0},{3,1},{4,6},{5,7},{6,4},{7,5},{8,10},{9,11},{10,... | collective-permute-start | bytes 393224 | tf_op jit(solution)/shard_map/ppermute | solution.py:40
  39.5 0.3 collective-permute-done.16
  39.9 4.1 %collective-permute-done.11 = f32[1,64,512]{2,1,0:T(8,128)S(1)} collective-permute-done((f32[1,64,512]{2,1,0:T(8,128)S(1)}, f32[1,64,512]{2,1,0:T(8,128)S(1)}, u32[]{:S(2)}, u32[]{:S(2)}) %collective-permute-start.11) | collective-permute-done | bytes 131104 | tf_op jit(solution)/shard_map/ppermute | solution.py:40
  44.0 0.0 collective-permute-done.13
  44.0 1.5 %collective-permute-done.15 = f32[1,64,512]{2,1,0:T(8,128)S(1)} collective-permute-done((f32[1,64,512]{2,1,0:T(8,128)S(1)}, f32[1,64,512]{2,1,0:T(8,128)S(1)}, u32[]{:S(2)}, u32[]{:S(2)}) %collective-permute-start.15) | collective-permute-done | bytes 131104 | tf_op jit(solution)/shard_map/ppermute | solution.py:40
  45.4 0.0 copy-done.1
  45.4 0.0 copy-done.2
  45.4 0.0 copy-done.3
  45.4 0.8 %add_divide_fusion = f32[1,64,512]{2,1,0:T(8,128)} fusion(f32[1,64,512]{2,1,0:T(8,128)S(1)} %get-tuple-element.55, f32[1,64,512]{2,1,0:T(8,128)S(1)} %collective-permute-done.16, f32[1,64,512]{2,1,0:T(8,128)S(1)} %collective-permute-done.15, f32[1,64,512]{2,1,0:T(8,128)S(1)} %collective-permute-done.13, f32[1,64,512]{2,1,0:T(8,128)S(1)} %copy-done.1, ...), kind=kLoop, calls=%fused_computation | loop fusion | flops 229376 | bytes 919808 | tf_op jit(solution)/shard_map/div | solution.py:385
  (8 shorter events, 0.1 us)
Async XLA Ops:
  0.0 18.8 %collective-permute-start.3 = (f32[512,512]{1,0:T(8,128)}, f32[512,512]{1,0:T(8,128)S(1)}, u32[]{:S(2)}, u32[]{:S(2)}) collective-permute-start(f32[512,512]{1,0:T(8,128)} %bitcast.4), channel_id=1, source_target_pairs={{0,8},{8,0},{16,24},{24,16},{1,9},{9,1},{17,25},{25,17},{2,10},{10... | collective-permute-start | bytes 3145736 | tf_op jit(solution)/shard_map/ppermute | solution.py:40
  1.6 10.4 %collective-permute-start.4 = (f32[144,512]{1,0:T(8,128)S(1)}, f32[144,512]{1,0:T(8,128)S(1)}, u32[]{:S(2)}, u32[]{:S(2)}) collective-permute-start(f32[144,512]{1,0:T(8,128)S(1)} %get-tuple-element.31), channel_id=1, source_target_pairs={{0,16},{8,24},{16,0},{24,8},{1,17},{9,25},{17,1},{25,9},{2,18},{10... | collective-permute-start | bytes 884744 | tf_op jit(solution)/shard_map/ppermute | solution.py:40
  4.1 17.7 %collective-permute-start.5 = (f32[224,512]{1,0:T(8,128)S(1)}, f32[224,512]{1,0:T(8,128)S(1)}, u32[]{:S(2)}, u32[]{:S(2)}) collective-permute-start(f32[224,512]{1,0:T(8,128)S(1)} %get-tuple-element.43), channel_id=1, source_target_pairs={{0,16},{8,24},{16,0},{24,8},{1,17},{9,25},{17,1},{25,9},{2,18},{10... | collective-permute-start | bytes 1376264 | tf_op jit(solution)/shard_map/ppermute | solution.py:40
  5.7 4.2 %collective-permute-start = (s32[3,1,96]{2,1,0:T(1,128)S(1)}, s32[3,1,96]{2,1,0:T(1,128)S(1)}, u32[]{:S(2)}, u32[]{:S(2)}) collective-permute-start(s32[3,1,96]{2,1,0:T(1,128)S(1)} %get-tuple-element.33), channel_id=1, source_target_pairs={{0,1},{1,0},{2,3},{3,2},{4,5},{5,4},{6,7},{7,6},{8,9},{9,8},{10,11... | collective-permute-start | bytes 3464 | tf_op jit(solution)/shard_map/ppermute | solution.py:40
  10.0 4.0 %collective-permute-start.1 = (s32[3,2,96]{2,1,0:T(2,128)S(1)}, s32[3,2,96]{2,1,0:T(2,128)S(1)}, u32[]{:S(2)}, u32[]{:S(2)}) collective-permute-start(s32[3,2,96]{2,1,0:T(2,128)S(1)} %pad_add_fusion.2), channel_id=1, source_target_pairs={{0,2},{1,3},{2,0},{3,1},{4,6},{5,7},{6,4},{7,5},{8,10},{9,11},{10,... | collective-permute-start | bytes 6920 | tf_op jit(solution)/shard_map/ppermute | solution.py:40
  12.0 10.5 %collective-permute-start.6 = (f32[144,512]{1,0:T(8,128)S(1)}, f32[144,512]{1,0:T(8,128)S(1)}, u32[]{:S(2)}, u32[]{:S(2)}) collective-permute-start(f32[144,512]{1,0:T(8,128)S(1)} %collective-permute-done.4.rest_0_), channel_id=1, source_target_pairs={{0,1},{1,0},{2,3},{3,2},{4,5},{5,4},{6,7},{7,6},{8,9},{9,8},{10,11... | collective-permute-start | bytes 884744 | tf_op jit(solution)/shard_map/ppermute | solution.py:40
  14.0 4.8 %copy-start = (f32[1,512,512]{2,1,0:T(8,128)S(1)}, f32[1,512,512]{2,1,0:T(8,128)}, u32[]{:S(2)}) copy-start(f32[1,512,512]{2,1,0:T(8,128)} %param.13) | copy-start | bytes 3145732
  14.0 4.8 %collective-permute-start.2 = (s32[3,4,96]{2,1,0:T(4,128)S(1)}, s32[3,4,96]{2,1,0:T(4,128)S(1)}, u32[]{:S(2)}, u32[]{:S(2)}) collective-permute-start(s32[3,4,96]{2,1,0:T(4,128)S(1)} %pad_add_fusion.1), channel_id=1, source_target_pairs={{0,4},{1,5},{2,6},{3,7},{4,0},{5,1},{6,2},{7,3},{8,12},{9,13},{10,... | collective-permute-start | bytes 13832 | tf_op jit(solution)/shard_map/ppermute | solution.py:40
  21.9 2.7 %collective-permute-start.8 = (f32[224,512]{1,0:T(8,128)S(1)}, f32[224,512]{1,0:T(8,128)S(1)}, u32[]{:S(2)}, u32[]{:S(2)}) collective-permute-start(f32[224,512]{1,0:T(8,128)S(1)} %collective-permute-done.5.rest_1_), channel_id=1, source_target_pairs={{0,8},{8,0},{16,24},{24,16},{1,9},{9,1},{17,25},{25,17},{2,10},{10... | collective-permute-start | bytes 1376264 | tf_op jit(solution)/shard_map/ppermute | solution.py:40
  22.0 2.2 %collective-permute-start.7 = (f32[144,512]{1,0:T(8,128)S(1)}, f32[144,512]{1,0:T(8,128)S(1)}, u32[]{:S(2)}, u32[]{:S(2)}) collective-permute-start(f32[144,512]{1,0:T(8,128)S(1)} %collective-permute-done.4.rest_0_), channel_id=1, source_target_pairs={{0,8},{8,0},{16,24},{24,16},{1,9},{9,1},{17,25},{25,17},{2,10},{10... | collective-permute-start | bytes 884744 | tf_op jit(solution)/shard_map/ppermute | solution.py:40
  22.5 2.1 %collective-permute-start.9 = (f32[144,512]{1,0:T(8,128)S(1)}, f32[144,512]{1,0:T(8,128)S(1)}, u32[]{:S(2)}, u32[]{:S(2)}) collective-permute-start(f32[144,512]{1,0:T(8,128)S(1)} %collective-permute-done.6.rest_2_), channel_id=1, source_target_pairs={{0,8},{8,0},{16,24},{24,16},{1,9},{9,1},{17,25},{25,17},{2,10},{10... | collective-permute-start | bytes 884744 | tf_op jit(solution)/shard_map/ppermute | solution.py:40
  25.9 6.4 %collective-permute-start.10 = (f32[1,64,512]{2,1,0:T(8,128)S(1)}, f32[1,64,512]{2,1,0:T(8,128)S(1)}, u32[]{:S(2)}, u32[]{:S(2)}) collective-permute-start(f32[1,64,512]{2,1,0:T(8,128)S(1)} %get-tuple-element.50), channel_id=1, source_target_pairs={{0,1},{1,0},{2,3},{3,2},{4,5},{5,4},{6,7},{7,6},{8,9},{9,8},{10,11... | collective-permute-start | bytes 393224 | tf_op jit(solution)/shard_map/ppermute | solution.py:40
  27.4 7.7 %collective-permute-start.12 = (f32[1,64,512]{2,1,0:T(8,128)S(1)}, f32[1,64,512]{2,1,0:T(8,128)S(1)}, u32[]{:S(2)}, u32[]{:S(2)}) collective-permute-start(f32[1,64,512]{2,1,0:T(8,128)S(1)} %get-tuple-element.52), channel_id=1, source_target_pairs={{0,1},{1,0},{2,3},{3,2},{4,5},{5,4},{6,7},{7,6},{8,9},{9,8},{10,11... | collective-permute-start | bytes 393224 | tf_op jit(solution)/shard_map/ppermute | solution.py:40
  27.9 10.8 %collective-permute-start.14 = (f32[1,64,512]{2,1,0:T(8,128)S(1)}, f32[1,64,512]{2,1,0:T(8,128)S(1)}, u32[]{:S(2)}, u32[]{:S(2)}) collective-permute-start(f32[1,64,512]{2,1,0:T(8,128)S(1)} %get-tuple-element.54), channel_id=1, source_target_pairs={{0,1},{1,0},{2,3},{3,2},{4,5},{5,4},{6,7},{7,6},{8,9},{9,8},{10,11... | collective-permute-start | bytes 393224 | tf_op jit(solution)/shard_map/ppermute | solution.py:40
  29.4 10.5 %collective-permute-start.16 = (f32[1,64,512]{2,1,0:T(8,128)S(1)}, f32[1,64,512]{2,1,0:T(8,128)S(1)}, u32[]{:S(2)}, u32[]{:S(2)}) collective-permute-start(f32[1,64,512]{2,1,0:T(8,128)S(1)} %get-tuple-element.56), channel_id=1, source_target_pairs={{0,1},{1,0},{2,3},{3,2},{4,5},{5,4},{6,7},{7,6},{8,9},{9,8},{10,11... | collective-permute-start | bytes 393224 | tf_op jit(solution)/shard_map/ppermute | solution.py:40
  30.0 15.4 %copy-start.1 = (f32[1,64,512]{2,1,0:T(8,128)S(1)}, f32[1,64,512]{2,1,0:T(8,128)}, u32[]{:S(2)}) copy-start(f32[1,64,512]{2,1,0:T(8,128)} %param.14) | copy-start | bytes 393220
  30.0 15.4 %copy-start.2 = (f32[512]{0:T(512)S(1)}, f32[512]{0:T(512)}, u32[]{:S(2)}) copy-start(f32[512]{0:T(512)} %param.16) | copy-start | bytes 6148
  30.0 15.4 %copy-start.3 = (f32[1,64]{1,0:T(1,128)S(1)}, f32[1,64]{1,0:T(1,128)}, u32[]{:S(2)}) copy-start(f32[1,64]{1,0:T(1,128)} %param.15) | copy-start | bytes 772
  32.3 11.7 %collective-permute-start.11 = (f32[1,64,512]{2,1,0:T(8,128)S(1)}, f32[1,64,512]{2,1,0:T(8,128)S(1)}, u32[]{:S(2)}, u32[]{:S(2)}) collective-permute-start(f32[1,64,512]{2,1,0:T(8,128)S(1)} %add.45), channel_id=1, source_target_pairs={{0,4},{1,5},{2,6},{3,7},{4,0},{5,1},{6,2},{7,3},{8,12},{9,13},{10,... | collective-permute-start | bytes 393224 | tf_op jit(solution)/shard_map/ppermute | solution.py:40
  35.1 8.9 %collective-permute-start.13 = (f32[1,64,512]{2,1,0:T(8,128)S(1)}, f32[1,64,512]{2,1,0:T(8,128)S(1)}, u32[]{:S(2)}, u32[]{:S(2)}) collective-permute-start(f32[1,64,512]{2,1,0:T(8,128)S(1)} %add.47), channel_id=1, source_target_pairs={{0,6},{1,7},{2,4},{3,5},{4,2},{5,3},{6,0},{7,1},{8,14},{9,15},{10,... | collective-permute-start | bytes 393224 | tf_op jit(solution)/shard_map/ppermute | solution.py:40
  38.7 6.7 %collective-permute-start.15 = (f32[1,64,512]{2,1,0:T(8,128)S(1)}, f32[1,64,512]{2,1,0:T(8,128)S(1)}, u32[]{:S(2)}, u32[]{:S(2)}) collective-permute-start(f32[1,64,512]{2,1,0:T(8,128)S(1)} %add.49), channel_id=1, source_target_pairs={{0,2},{1,3},{2,0},{3,1},{4,6},{5,7},{6,4},{7,5},{8,10},{9,11},{10,... | collective-permute-start | bytes 393224 | tf_op jit(solution)/shard_map/ppermute | solution.py:40

commit v6 on v5

--- a/solution.py
+++ b/solution.py
@@ -45,7 +45,8 @@
 
 
 def tile_order(lanes):
-    side = list(range(lanes // 2, lanes, 2)) + list(range(lanes // 2 - 2, -1, -2))
+    half = lanes // 2
+    side = [half] + list(range(half - 2, 0, -2)) + list(range(half + 2, lanes, 2)) + [0]
     return [k + 1 for k in side], side
 
 
@@ -271,59 +272,96 @@
     )(lists, table, own, pair, *[in_vmem(x) for x in rows])
 
 
-def away_kernel(blocks, hi, lo, local_ref, *rest):
-    n = 3 * (blocks - 2)
-    parts, out_refs, (in_hi, in_lo, held) = rest[:n], rest[n:-3], rest[-3:]
-    depth = in_hi.shape[0] // (blocks - 2)
+def split_parts(parts, in_hi, in_lo):
+    depth = sum(x.shape[0] for x in parts[:3])
     mine, theirs = end_offsets(depth)
-    for c in range(blocks - 2):
+    for c in range(len(parts) // 3):
         starts = (mine, row_cuts(depth)[0], theirs)
         for start, part in zip(starts, parts[3 * c : 3 * c + 3]):
-            high, low = split(part[...])
+            hi, lo = split(part[...])
             at = pl.ds(pl.multiple_of(c * depth + start, 16), part.shape[0])
-            in_hi[at, :] = high
-            in_lo[at, :] = low
-    out = passes(hi[:, 2 * depth :], lo[:, 2 * depth :], in_hi[...], in_lo[...])
+            in_hi[at, :] = hi
+            in_lo[at, :] = lo
+
+
+def columns(x, odd, depth):
+    blocks = range(2 + odd, x.shape[1] // depth, 2)
+    return jnp.concatenate([x[:, c * depth : (c + 1) * depth] for c in blocks], axis=1)
+
+
+def fetched_kernel(*refs):
+    sums_refs, local_refs, rest = refs[:4], refs[4:6], refs[6:]
+    parts, out_refs, (in_hi, in_lo) = rest[:-4], rest[-4:-2], rest[-2:]
+    depth = sum(x.shape[0] for x in parts[:3])
+    split_parts(parts, in_hi, in_lo)
+    for k in range(2):
+        hi, lo = (columns(x, 0, depth) for x in sums_refs[2 * k : 2 * k + 2])
+        out_refs[k][...] = local_refs[k][...] + passes(hi, lo, in_hi[...], in_lo[...])
+
+
+def flat(parts):
+    return [x for three in parts for x in three]
+
+
+def fetched_products(held, local, parts):
+    rows, window = local[0].shape
+    depth = sum(x.shape[0] for x in parts[0])
+    half = pltpu.VMEM((len(parts) * depth, window), jnp.bfloat16)
+    return pl.pallas_call(
+        fetched_kernel,
+        out_shape=[pltpu.VMEM((rows, window), jnp.float32)] * 2,
+        in_specs=[VMEM] * (6 + 3 * len(parts)),
+        out_specs=[VMEM] * 2,
+        scratch_shapes=[half] * 2,
+        compiler_params=limit(16 * len(parts) * depth * window),
+        cost_estimate=cost(12 * rows * len(parts) * depth * window, 0),
+        name="fetched_products",
+    )(*[in_vmem(x) for x in (*held, *local)], *flat(parts))
+
+
+def away_kernel(tiles, hi, lo, local_ref, *rest):
+    parts, out_refs, (in_hi, in_lo, held) = rest[: -3 - tiles], rest[-3 - tiles : -3], rest[-3:]
+    split_parts(parts, in_hi, in_lo)
+    depth = sum(x.shape[0] for x in parts[:3])
+    out = passes(columns(hi, 1, depth), columns(lo, 1, depth), in_hi[...], in_lo[...])
     store_tiles(local_ref[...] + out, out_refs, held)
 
 
-def side_kernel(hi, lo, local_ref, in_hi, in_lo, *rest):
+def side_kernel(depth, hi, lo, local_ref, in_hi, in_lo, *rest):
     out_refs, held = rest[:-1], rest[-1]
-    lead = hi.shape[1] - in_hi.shape[0]
-    out = passes(hi[:, lead:], lo[:, lead:], in_hi[...], in_lo[...])
+    out = passes(columns(hi, 1, depth), columns(lo, 1, depth), in_hi[...], in_lo[...])
     store_tiles(local_ref[...] + out, out_refs, held)
 
 
 def away_products(hi, lo, local, parts, tiles):
-    blocks = 2 + len(parts)
-    depth = hi.shape[1] // blocks
     rows, window = local.shape
-    remote = pltpu.VMEM(((blocks - 2) * depth, window), jnp.bfloat16)
+    depth = sum(x.shape[0] for x in parts[0])
+    remote = pltpu.VMEM((len(parts) * depth, window), jnp.bfloat16)
     shapes = [jax.ShapeDtypeStruct((1, rows // tiles, window), jnp.float32)] * tiles
     *out, in_hi, in_lo = pl.pallas_call(
-        functools.partial(away_kernel, blocks),
+        functools.partial(away_kernel, tiles),
         out_shape=shapes + [remote] * 2,
         in_specs=[VMEM] * (3 + 3 * len(parts)),
-        out_specs=[VMEM] * (len(shapes) + 2),
+        out_specs=[VMEM] * (tiles + 2),
         scratch_shapes=[pltpu.VMEM((window // LANES, rows, LANES), jnp.float32)],
-        compiler_params=limit(4 * blocks * depth * window),
-        cost_estimate=cost(6 * rows * (blocks - 2) * depth * window, 0),
+        compiler_params=limit(16 * len(parts) * depth * window),
+        cost_estimate=cost(6 * rows * len(parts) * depth * window, 0),
         name="away_products",
-    )(*[in_vmem(x) for x in (hi, lo, local)], *[x for three in parts for x in three])
+    )(*[in_vmem(x) for x in (hi, lo, local)], *flat(parts))
     return out, in_hi, in_lo
 
 
-def side_products(hi, lo, local, in_hi, in_lo, tiles):
+def side_products(hi, lo, local, in_hi, in_lo, tiles, depth):
     rows, window = local.shape
     shapes = [jax.ShapeDtypeStruct((1, rows // tiles, window), jnp.float32)] * tiles
     return pl.pallas_call(
-        side_kernel,
+        functools.partial(side_kernel, depth),
         out_shape=shapes,
         in_specs=[VMEM] * 5,
-        out_specs=[VMEM] * len(shapes),
+        out_specs=[VMEM] * tiles,
         scratch_shapes=[pltpu.VMEM((window // LANES, rows, LANES), jnp.float32)],
         compiler_params=limit(0),
-        cost_estimate=cost(6 * rows * in_hi.size, 0),
+        cost_estimate=cost(0, 0),
         name="side_products",
     )(*[in_vmem(x) for x in (hi, lo, local, in_hi, in_lo)])
 
@@ -361,22 +399,21 @@
         lists = jnp.concatenate([lists, swap(lists, "wide", k)], axis=1)
         k *= 2
     lists = after(lists, rows[1])
-    away_hi, away_lo, side_hi, side_lo, *local = sums(
+    *held, local_away, local_side = sums(
         lists, table, own, pair, rows, amp_dev, tile_rows, lanes, grps
     )
 
-    parts = [None] * (grps - 2)
+    even, odd = [], []
     for k, (one, two) in fetched.items():
-        three = [one, two, swap(one, "wide", 1)]
-        parts[k - 2] = three
-        parts[k - 1] = [
-            swap(after(x, y), "grp", 1) for x, y in zip(three, (lists, away_hi, away_hi))
-        ]
-
-    away, in_hi, in_lo = away_products(away_hi, away_lo, local[0], parts, half)
-    side = side_products(side_hi, side_lo, local[1], in_hi, in_lo, half)
+        even.append([one, two, swap(one, "wide", 1)])
+        odd.append([swap(after(x, y), "grp", 1) for x, y in zip(even[-1], (lists, held[0], held[0]))])
+
+    local = fetched_products(held, (local_away, local_side), even)
+    away, in_hi, in_lo = away_products(*held[:2], local[0], odd, half)
+    side = side_products(*held[2:], local[1], in_hi, in_lo, half, own.shape[0])
     _, offsets = tile_order(lanes)
-    got = [swap(x, "wide", 1) for x in away]
+    got = [swap(away[0], "wide", 1)]
+    got += [swap(after(x, side[0]), "wide", 1) for x in away[1:]]
     summed = base_residual
     for k, here, there in zip(offsets, side, got):
         part = here + there

time: 46.5 us -> 45.6 us (0.981)
  waiting for transfers between devices: 9.8 us -> 7.78 us
  starting transfers between devices: 23.2 us -> 24.1 us
    ppermute x17, waiting for transfers between devices: 9.8 us -> 7.78 us  [swap(): return lax.ppermute(x, axis, [(i, i ^ k) for i in range(n)])]
    ppermute x17, starting transfers between devices: 23.2 us -> 24.1 us  [swap(): return lax.ppermute(x, axis, [(i, i ^ k) for i in range(n)])]
    pallas_call x2 -> x3, Pallas kernels: 2.23 us -> 2.44 us  [the longest x1 1.12 us: fetched_products(): pl.pallas_call(fetched_kernel, out_shape=[pltpu.VMEM((rows, window), jnp....]
  transfers between devices with their start and end apart: 17 -> 17, of which waited for: 8 -> 7; matrix products, arithmetic and copies ran while one was open for 0% -> 0% of each run, Pallas kernels for 22% -> 24%
where the time goes in v6:
time: 45.6 us; the launch traced here: 45.3 us
  starting transfers between devices  24.1 us (53%)
  Pallas kernels  11.7 us (26%)
  waiting for transfers between devices  7.78 us (17%)
  other arithmetic  0.84 us (2%)
  between operations  0.81 us (2%)
    ppermute x17, starting transfers between devices, swap(): return lax.ppermute(x, axis, [(i, i ^ k) for i in range(n)])  24.1 us
    ppermute x17, waiting for transfers between devices, swap(): return lax.ppermute(x, axis, [(i, i ^ k) for i in range(n)])  7.78 us
    pallas_call x2, Pallas kernels, load(): pl.pallas_call(functools.partial(load_kernel, first), out_shape=pltpu.VME...  4.26 us
    pallas_call x1, Pallas kernels, sums(): pl.pallas_call(functools.partial(sums_kernel, lanes, blocks, amp_dev), ou...  3.03 us
    pallas_call x1, Pallas kernels, pieces(): pl.pallas_call(pieces_kernel, out_shape=[pltpu.VMEM((n, own.shape[1]), ow...  1.12 us
    pallas_call x1, Pallas kernels, fetched_products(): pl.pallas_call(fetched_kernel, out_shape=[pltpu.VMEM((rows, window), jnp....  1.12 us
  transfers between devices with their start and end apart: 17, of which 7 were waited for; matrix products, arithmetic and copies ran while one was open for 0% of the time, Pallas kernels for 24%

profile of v6, /device:TPU:0, one launch (start us, length us, event | category | flops | bytes accessed | tf_op | source)
XLA Modules:
  0.0 45.3 jit_solution(9292855524902391918)
XLA Ops:
  0.0 0.5 collective-permute-start.3
  0.5 1.1 %pieces.1 = (f32[144,512]{1,0:T(8,128)S(1)}, f32[224,512]{1,0:T(8,128)S(1)}) custom-call(f32[512,512]{1,0:T(8,128)} %bitcast.5), custom_call_target="tpu_custom_call" | custom-call | bytes 1048576 | tf_op jit(solution)/shard_map/pieces/pallas_call | solution.py:78
  1.6 2.6 %collective-permute-start.4 = (f32[144,512]{1,0:T(8,128)S(1)}, f32[144,512]{1,0:T(8,128)S(1)}, u32[]{:S(2)}, u32[]{:S(2)}) collective-permute-start(f32[144,512]{1,0:T(8,128)S(1)} %get-tuple-element.36), channel_id=1, source_target_pairs={{0,16},{8,24},{16,0},{24,8},{1,17},{9,25},{17,1},{25,9},{2,18},{10... | collective-permute-start | bytes 884744 | tf_op jit(solution)/shard_map/ppermute | solution.py:40
  4.1 0.1 collective-permute-start.5
  4.9 0.9 %pack_lists.1 = (s32[3,1,96]{2,1,0:T(1,128)S(1)}, s32[3,256]{1,0:T(4,128)S(1)}) custom-call(s32[1]{0:T(128)S(6)} %copy.13.count_ref, s32[1,96]{1,0:T(1,128)} %refs_0_.1, s32[1,96]{1,0:T(1,128)} %refs_1_.1, s32[1,96]{1,0:T(1,128)} %refs_2_, s32[1,32]{1,0:T(1,128)} %bitcast.8, s32[1,8]{1,0:T(1,128)} %refs_4_.1, s32[1,4]{1,0:T(1,128)} %bitcast.9), custom_call_target="tpu_custom_call" | custom-call | bytes 4096 | tf_op jit(solution)/shard_map/pack_lists/pallas_call | solution.py:113
  5.7 2.0 %collective-permute-start = (s32[3,1,96]{2,1,0:T(1,128)S(1)}, s32[3,1,96]{2,1,0:T(1,128)S(1)}, u32[]{:S(2)}, u32[]{:S(2)}) collective-permute-start(s32[3,1,96]{2,1,0:T(1,128)S(1)} %get-tuple-element.38), channel_id=1, source_target_pairs={{0,1},{1,0},{2,3},{3,2},{4,5},{5,4},{6,7},{7,6},{8,9},{9,8},{10,11... | collective-permute-start | bytes 3464 | tf_op jit(solution)/shard_map/ppermute | solution.py:40
  7.8 2.1 %load_amplitudes.2.refs_0_ = bf16[2048,512]{1,0:T(8,128)(2,1)S(1)} custom-call(f32[32,64,512]{2,1,0:T(8,128)} %amp_hbm.3), custom_call_target="tpu_custom_call" | custom-call | bytes 4194304 | tf_op jit(solution)/shard_map/load_amplitudes/pallas_call | solution.py:148
  9.9 0.0 collective-permute-done
  10.0 1.6 %collective-permute-start.1 = (s32[3,2,96]{2,1,0:T(2,128)S(1)}, s32[3,2,96]{2,1,0:T(2,128)S(1)}, u32[]{:S(2)}, u32[]{:S(2)}) collective-permute-start(s32[3,2,96]{2,1,0:T(2,128)S(1)} %pad_add_fusion.2), channel_id=1, source_target_pairs={{0,2},{1,3},{2,0},{3,1},{4,6},{5,7},{6,4},{7,5},{8,10},{9,11},{10,... | collective-permute-start | bytes 6920 | tf_op jit(solution)/shard_map/ppermute | solution.py:40
  11.6 0.4 collective-permute-done.4.refs_6_
  12.0 2.0 %collective-permute-start.6 = (f32[144,512]{1,0:T(8,128)S(1)}, f32[144,512]{1,0:T(8,128)S(1)}, u32[]{:S(2)}, u32[]{:S(2)}) collective-permute-start(f32[144,512]{1,0:T(8,128)S(1)} %collective-permute-done.4.refs_6_), channel_id=1, source_target_pairs={{0,1},{1,0},{2,3},{3,2},{4,5},{5,4},{6,7},{7,6},{8,9},{9,8},{10,11... | collective-permute-start | bytes 884744 | tf_op jit(solution)/shard_map/ppermute | solution.py:40
  14.0 0.0 collective-permute-done.1
  14.0 0.0 copy-start
  14.0 2.7 %collective-permute-start.2 = (s32[3,4,96]{2,1,0:T(4,128)S(1)}, s32[3,4,96]{2,1,0:T(4,128)S(1)}, u32[]{:S(2)}, u32[]{:S(2)}) collective-permute-start(s32[3,4,96]{2,1,0:T(4,128)S(1)} %pad_add_fusion.1), channel_id=1, source_target_pairs={{0,4},{1,5},{2,6},{3,7},{4,0},{5,1},{6,2},{7,3},{8,12},{9,13},{10,... | collective-permute-start | bytes 13832 | tf_op jit(solution)/shard_map/ppermute | solution.py:40
  16.7 2.1 %load_amplitudes.3.refs_1_ = bf16[2048,512]{1,0:T(8,128)(2,1)S(1)} custom-call(f32[32,64,512]{2,1,0:T(8,128)} %amp_hbm.3), custom_call_target="tpu_custom_call" | custom-call | bytes 4194304 | tf_op jit(solution)/shard_map/load_amplitudes/pallas_call | solution.py:148
  18.8 0.0 collective-permute-done.2
  18.8 0.0 collective-permute-done.3.pair_ref
  18.8 0.0 copy-done
  18.8 3.0 %sums.1 = (bf16[256,2048]{1,0:T(8,128)(2,1)S(1)}, bf16[256,2048]{1,0:T(8,128)(2,1)S(1)}, bf16[256,2048]{1,0:T(8,128)(2,1)S(1)}, bf16[256,2048]{1,0:T(8,128)(2,1)...) custom-call(s32[3,8,96]{2,1,0:T(8,128)S(1)} %pad_add_fusion.lists_ref, s32[3,256]{1,0:T(4,128)S(1)} %get-tuple-element.41.table_ref, ...), custom_call_target="tpu_custom_call" | custom-call | bytes 16777216 | tf_op jit(solution)/shard_map/sums/pallas_call | solution.py:263
  21.9 0.0 collective-permute-done.5.refs_7_
  21.9 0.1 collective-permute-start.8
  22.0 0.5 %collective-permute-start.7 = (f32[144,512]{1,0:T(8,128)S(1)}, f32[144,512]{1,0:T(8,128)S(1)}, u32[]{:S(2)}, u32[]{:S(2)}) collective-permute-start(f32[144,512]{1,0:T(8,128)S(1)} %collective-permute-done.4.refs_6_), channel_id=1, source_target_pairs={{0,8},{8,0},{16,24},{24,16},{1,9},{9,1},{17,25},{25,17},{2,10},{10... | collective-permute-start | bytes 884744 | tf_op jit(solution)/shard_map/ppermute | solution.py:40
  22.5 0.0 collective-permute-done.6.refs_8_
  22.5 0.1 collective-permute-start.9
  22.5 1.1 %fetched_products.1 = (f32[256,512]{1,0:T(8,128)S(1)}, f32[256,512]{1,0:T(8,128)S(1)}) custom-call(bf16[256,2048]{1,0:T(8,128)(2,1)S(1)} %get-tuple-element.44.refs_0_.hi, bf16[256,2048]{1,0:T(8,128)(2,1)S(1)} %get-tuple-element.45.refs_1_.lo, bf16[256,2048]{1,0:T(8,128)(2,1)S(1)} %get-tuple-element.42.refs_2_.hi, ...), custom_call_target="tpu_custom_call" | custom-call | flops 805306368 | tf_op jit(solution)/shard_map/fetched_products/pallas_call | solution.py:310
  23.7 0.5 %collective-permute-done.7.rest_0_ = f32[144,512]{1,0:T(8,128)S(1)} collective-permute-done((f32[144,512]{1,0:T(8,128)S(1)}, f32[144,512]{1,0:T(8,128)S(1)}, u32[]{:S(2)}, u32[]{:S(2)}) %collective-permute-start.7) | collective-permute-done | bytes 294944 | tf_op jit(solution)/shard_map/ppermute | solution.py:40
  24.2 0.4 collective-permute-done.9.rest_2_
  24.6 0.0 collective-permute-done.8.rest_1_
  24.6 0.7 %away_products.1 = (f32[1,64,512]{2,1,0:T(8,128)S(1)}, f32[1,64,512]{2,1,0:T(8,128)S(1)}, f32[1,64,512]{2,1,0:T(8,128)S(1)}, f32[1,64,512]{2,1,0:T(8,128)S(1)}, ...) custom-call(bf16[256,2048]{1,0:T(8,128)(2,1)S(1)} %get-tuple-element.44.refs_0_.hi, ...), custom_call_target="tpu_custom_call" | custom-call | flops 402653184 | tf_op jit(solution)/shard_map/away_products/pallas_call | solution.py:341
  25.3 1.5 %collective-permute-start.10 = (f32[1,64,512]{2,1,0:T(8,128)S(1)}, f32[1,64,512]{2,1,0:T(8,128)S(1)}, u32[]{:S(2)}, u32[]{:S(2)}) collective-permute-start(f32[1,64,512]{2,1,0:T(8,128)S(1)} %get-tuple-element.57), channel_id=1, source_target_pairs={{0,1},{1,0},{2,3},{3,2},{4,5},{5,4},{6,7},{7,6},{8,9},{9,8},{10,11... | collective-permute-start | bytes 393224 | tf_op jit(solution)/shard_map/ppermute | solution.py:40
  26.9 0.6 %side_products.1 = (f32[1,64,512]{2,1,0:T(8,128)S(1)}, f32[1,64,512]{2,1,0:T(8,128)S(1)}, f32[1,64,512]{2,1,0:T(8,128)S(1)}, f32[1,64,512]{2,1,0:T(8,128)S(1)}) custom-call(bf16[256,2048]{1,0:T(8,128)(2,1)S(1)} %get-tuple-element.42.refs_2_.hi, bf16[256,2048]{1,0:T(8,128)(2,1)S(1)} %get-tuple-element.43.refs_3_.lo, ...), custom_call_target="tpu_custom_call" | custom-call | tf_op jit(solution)/shard_map/side_products/pallas_call | solution.py:357
  27.5 0.6 %collective-permute-start.12 = (f32[1,64,512]{2,1,0:T(8,128)S(1)}, f32[1,64,512]{2,1,0:T(8,128)S(1)}, u32[]{:S(2)}, u32[]{:S(2)}) collective-permute-start(f32[1,64,512]{2,1,0:T(8,128)S(1)} %get-tuple-element.60), channel_id=1, source_target_pairs={{0,1},{1,0},{2,3},{3,2},{4,5},{5,4},{6,7},{7,6},{8,9},{9,8},{10,11... | collective-permute-start | bytes 393224 | tf_op jit(solution)/shard_map/ppermute | solution.py:40
  28.1 1.5 %collective-permute-start.14 = (f32[1,64,512]{2,1,0:T(8,128)S(1)}, f32[1,64,512]{2,1,0:T(8,128)S(1)}, u32[]{:S(2)}, u32[]{:S(2)}) collective-permute-start(f32[1,64,512]{2,1,0:T(8,128)S(1)} %get-tuple-element.63), channel_id=1, source_target_pairs={{0,1},{1,0},{2,3},{3,2},{4,5},{5,4},{6,7},{7,6},{8,9},{9,8},{10,11... | collective-permute-start | bytes 393224 | tf_op jit(solution)/shard_map/ppermute | solution.py:40
  29.6 0.6 %collective-permute-start.16 = (f32[1,64,512]{2,1,0:T(8,128)S(1)}, f32[1,64,512]{2,1,0:T(8,128)S(1)}, u32[]{:S(2)}, u32[]{:S(2)}) collective-permute-start(f32[1,64,512]{2,1,0:T(8,128)S(1)} %get-tuple-element.66), channel_id=1, source_target_pairs={{0,1},{1,0},{2,3},{3,2},{4,5},{5,4},{6,7},{7,6},{8,9},{9,8},{10,11... | collective-permute-start | bytes 393224 | tf_op jit(solution)/shard_map/ppermute | solution.py:40
  30.1 1.6 %collective-permute-done.10 = f32[1,64,512]{2,1,0:T(8,128)S(1)} collective-permute-done((f32[1,64,512]{2,1,0:T(8,128)S(1)}, f32[1,64,512]{2,1,0:T(8,128)S(1)}, u32[]{:S(2)}, u32[]{:S(2)}) %collective-permute-start.10) | collective-permute-done | bytes 131104 | tf_op jit(solution)/shard_map/ppermute | solution.py:40
  31.8 2.6 %collective-permute-start.11 = (f32[1,64,512]{2,1,0:T(8,128)S(1)}, f32[1,64,512]{2,1,0:T(8,128)S(1)}, u32[]{:S(2)}, u32[]{:S(2)}) collective-permute-start(f32[1,64,512]{2,1,0:T(8,128)S(1)} %add.45), channel_id=1, source_target_pairs={{0,4},{1,5},{2,6},{3,7},{4,0},{5,1},{6,2},{7,3},{8,12},{9,13},{10,... | collective-permute-start | bytes 393224 | tf_op jit(solution)/shard_map/ppermute | solution.py:40
  34.4 0.2 collective-permute-done.12
  34.6 1.6 %collective-permute-start.13 = (f32[1,64,512]{2,1,0:T(8,128)S(1)}, f32[1,64,512]{2,1,0:T(8,128)S(1)}, u32[]{:S(2)}, u32[]{:S(2)}) collective-permute-start(f32[1,64,512]{2,1,0:T(8,128)S(1)} %add.47), channel_id=1, source_target_pairs={{0,2},{1,3},{2,0},{3,1},{4,6},{5,7},{6,4},{7,5},{8,10},{9,11},{10,... | collective-permute-start | bytes 393224 | tf_op jit(solution)/shard_map/ppermute | solution.py:40
  36.2 1.1 %collective-permute-done.14 = f32[1,64,512]{2,1,0:T(8,128)S(1)} collective-permute-done((f32[1,64,512]{2,1,0:T(8,128)S(1)}, f32[1,64,512]{2,1,0:T(8,128)S(1)}, u32[]{:S(2)}, u32[]{:S(2)}) %collective-permute-start.14) | collective-permute-done | bytes 131104 | tf_op jit(solution)/shard_map/ppermute | solution.py:40
  37.4 3.6 %collective-permute-start.15 = (f32[1,64,512]{2,1,0:T(8,128)S(1)}, f32[1,64,512]{2,1,0:T(8,128)S(1)}, u32[]{:S(2)}, u32[]{:S(2)}) collective-permute-start(f32[1,64,512]{2,1,0:T(8,128)S(1)} %add.49), channel_id=1, source_target_pairs={{0,6},{1,7},{2,4},{3,5},{4,2},{5,3},{6,0},{7,1},{8,14},{9,15},{10,... | collective-permute-start | bytes 393224 | tf_op jit(solution)/shard_map/ppermute | solution.py:40
  41.0 0.0 collective-permute-done.16
  41.0 0.0 collective-permute-done.11
  41.0 0.0 collective-permute-done.13
  41.0 3.5 %collective-permute-done.15 = f32[1,64,512]{2,1,0:T(8,128)S(1)} collective-permute-done((f32[1,64,512]{2,1,0:T(8,128)S(1)}, f32[1,64,512]{2,1,0:T(8,128)S(1)}, u32[]{:S(2)}, u32[]{:S(2)}) %collective-permute-start.15) | collective-permute-done | bytes 131104 | tf_op jit(solution)/shard_map/ppermute | solution.py:40
  44.5 0.0 copy-done.1
  44.5 0.0 copy-done.2
  44.5 0.0 copy-done.3
  44.5 0.8 %add_divide_fusion = f32[1,64,512]{2,1,0:T(8,128)} fusion(f32[1,64,512]{2,1,0:T(8,128)S(1)} %get-tuple-element.64, f32[1,64,512]{2,1,0:T(8,128)S(1)} %collective-permute-done.16, f32[1,64,512]{2,1,0:T(8,128)S(1)} %collective-permute-done.15, f32[1,64,512]{2,1,0:T(8,128)S(1)} %collective-permute-done.13, f32[1,64,512]{2,1,0:T(8,128)S(1)} %copy-done.1, ...), kind=kLoop, calls=%fused_computation | loop fusion | flops 229376 | bytes 919808 | tf_op jit(solution)/shard_map/div | solution.py:422
  (9 shorter events, 0.1 us)
Async XLA Ops:
  0.0 18.8 %collective-permute-start.3 = (f32[512,512]{1,0:T(8,128)}, f32[512,512]{1,0:T(8,128)S(1)}, u32[]{:S(2)}, u32[]{:S(2)}) collective-permute-start(f32[512,512]{1,0:T(8,128)} %bitcast.4), channel_id=1, source_target_pairs={{0,8},{8,0},{16,24},{24,16},{1,9},{9,1},{17,25},{25,17},{2,10},{10... | collective-permute-start | bytes 3145736 | tf_op jit(solution)/shard_map/ppermute | solution.py:40
  1.6 10.4 %collective-permute-start.4 = (f32[144,512]{1,0:T(8,128)S(1)}, f32[144,512]{1,0:T(8,128)S(1)}, u32[]{:S(2)}, u32[]{:S(2)}) collective-permute-start(f32[144,512]{1,0:T(8,128)S(1)} %get-tuple-element.36), channel_id=1, source_target_pairs={{0,16},{8,24},{16,0},{24,8},{1,17},{9,25},{17,1},{25,9},{2,18},{10... | collective-permute-start | bytes 884744 | tf_op jit(solution)/shard_map/ppermute | solution.py:40
  4.1 17.7 %collective-permute-start.5 = (f32[224,512]{1,0:T(8,128)S(1)}, f32[224,512]{1,0:T(8,128)S(1)}, u32[]{:S(2)}, u32[]{:S(2)}) collective-permute-start(f32[224,512]{1,0:T(8,128)S(1)} %get-tuple-element.48), channel_id=1, source_target_pairs={{0,16},{8,24},{16,0},{24,8},{1,17},{9,25},{17,1},{25,9},{2,18},{10... | collective-permute-start | bytes 1376264 | tf_op jit(solution)/shard_map/ppermute | solution.py:40
  5.7 4.2 %collective-permute-start = (s32[3,1,96]{2,1,0:T(1,128)S(1)}, s32[3,1,96]{2,1,0:T(1,128)S(1)}, u32[]{:S(2)}, u32[]{:S(2)}) collective-permute-start(s32[3,1,96]{2,1,0:T(1,128)S(1)} %get-tuple-element.38), channel_id=1, source_target_pairs={{0,1},{1,0},{2,3},{3,2},{4,5},{5,4},{6,7},{7,6},{8,9},{9,8},{10,11... | collective-permute-start | bytes 3464 | tf_op jit(solution)/shard_map/ppermute | solution.py:40
  10.0 4.0 %collective-permute-start.1 = (s32[3,2,96]{2,1,0:T(2,128)S(1)}, s32[3,2,96]{2,1,0:T(2,128)S(1)}, u32[]{:S(2)}, u32[]{:S(2)}) collective-permute-start(s32[3,2,96]{2,1,0:T(2,128)S(1)} %pad_add_fusion.2), channel_id=1, source_target_pairs={{0,2},{1,3},{2,0},{3,1},{4,6},{5,7},{6,4},{7,5},{8,10},{9,11},{10,... | collective-permute-start | bytes 6920 | tf_op jit(solution)/shard_map/ppermute | solution.py:40
  12.0 10.5 %collective-permute-start.6 = (f32[144,512]{1,0:T(8,128)S(1)}, f32[144,512]{1,0:T(8,128)S(1)}, u32[]{:S(2)}, u32[]{:S(2)}) collective-permute-start(f32[144,512]{1,0:T(8,128)S(1)} %collective-permute-done.4.refs_6_), channel_id=1, source_target_pairs={{0,1},{1,0},{2,3},{3,2},{4,5},{5,4},{6,7},{7,6},{8,9},{9,8},{10,11... | collective-permute-start | bytes 884744 | tf_op jit(solution)/shard_map/ppermute | solution.py:40
  14.0 4.8 %copy-start = (f32[1,512,512]{2,1,0:T(8,128)S(1)}, f32[1,512,512]{2,1,0:T(8,128)}, u32[]{:S(2)}) copy-start(f32[1,512,512]{2,1,0:T(8,128)} %param.13) | copy-start | bytes 3145732
  14.0 4.8 %collective-permute-start.2 = (s32[3,4,96]{2,1,0:T(4,128)S(1)}, s32[3,4,96]{2,1,0:T(4,128)S(1)}, u32[]{:S(2)}, u32[]{:S(2)}) collective-permute-start(s32[3,4,96]{2,1,0:T(4,128)S(1)} %pad_add_fusion.1), channel_id=1, source_target_pairs={{0,4},{1,5},{2,6},{3,7},{4,0},{5,1},{6,2},{7,3},{8,12},{9,13},{10,... | collective-permute-start | bytes 13832 | tf_op jit(solution)/shard_map/ppermute | solution.py:40
  21.9 2.7 %collective-permute-start.8 = (f32[224,512]{1,0:T(8,128)S(1)}, f32[224,512]{1,0:T(8,128)S(1)}, u32[]{:S(2)}, u32[]{:S(2)}) collective-permute-start(f32[224,512]{1,0:T(8,128)S(1)} %collective-permute-done.5.refs_7_), channel_id=1, source_target_pairs={{0,8},{8,0},{16,24},{24,16},{1,9},{9,1},{17,25},{25,17},{2,10},{10... | collective-permute-start | bytes 1376264 | tf_op jit(solution)/shard_map/ppermute | solution.py:40
  22.0 2.2 %collective-permute-start.7 = (f32[144,512]{1,0:T(8,128)S(1)}, f32[144,512]{1,0:T(8,128)S(1)}, u32[]{:S(2)}, u32[]{:S(2)}) collective-permute-start(f32[144,512]{1,0:T(8,128)S(1)} %collective-permute-done.4.refs_6_), channel_id=1, source_target_pairs={{0,8},{8,0},{16,24},{24,16},{1,9},{9,1},{17,25},{25,17},{2,10},{10... | collective-permute-start | bytes 884744 | tf_op jit(solution)/shard_map/ppermute | solution.py:40
  22.5 2.1 %collective-permute-start.9 = (f32[144,512]{1,0:T(8,128)S(1)}, f32[144,512]{1,0:T(8,128)S(1)}, u32[]{:S(2)}, u32[]{:S(2)}) collective-permute-start(f32[144,512]{1,0:T(8,128)S(1)} %collective-permute-done.6.refs_8_), channel_id=1, source_target_pairs={{0,8},{8,0},{16,24},{24,16},{1,9},{9,1},{17,25},{25,17},{2,10},{10... | collective-permute-start | bytes 884744 | tf_op jit(solution)/shard_map/ppermute | solution.py:40
  25.3 6.4 %collective-permute-start.10 = (f32[1,64,512]{2,1,0:T(8,128)S(1)}, f32[1,64,512]{2,1,0:T(8,128)S(1)}, u32[]{:S(2)}, u32[]{:S(2)}) collective-permute-start(f32[1,64,512]{2,1,0:T(8,128)S(1)} %get-tuple-element.57), channel_id=1, source_target_pairs={{0,1},{1,0},{2,3},{3,2},{4,5},{5,4},{6,7},{7,6},{8,9},{9,8},{10,11... | collective-permute-start | bytes 393224 | tf_op jit(solution)/shard_map/ppermute | solution.py:40
  26.9 17.6 %copy-start.1 = (f32[1,64,512]{2,1,0:T(8,128)S(1)}, f32[1,64,512]{2,1,0:T(8,128)}, u32[]{:S(2)}) copy-start(f32[1,64,512]{2,1,0:T(8,128)} %param.14) | copy-start | bytes 393220
  26.9 17.6 %copy-start.2 = (f32[512]{0:T(512)S(1)}, f32[512]{0:T(512)}, u32[]{:S(2)}) copy-start(f32[512]{0:T(512)} %param.16) | copy-start | bytes 6148
  26.9 17.6 %copy-start.3 = (f32[1,64]{1,0:T(1,128)S(1)}, f32[1,64]{1,0:T(1,128)}, u32[]{:S(2)}) copy-start(f32[1,64]{1,0:T(1,128)} %param.15) | copy-start | bytes 772
  27.5 7.1 %collective-permute-start.12 = (f32[1,64,512]{2,1,0:T(8,128)S(1)}, f32[1,64,512]{2,1,0:T(8,128)S(1)}, u32[]{:S(2)}, u32[]{:S(2)}) collective-permute-start(f32[1,64,512]{2,1,0:T(8,128)S(1)} %get-tuple-element.60), channel_id=1, source_target_pairs={{0,1},{1,0},{2,3},{3,2},{4,5},{5,4},{6,7},{7,6},{8,9},{9,8},{10,11... | collective-permute-start | bytes 393224 | tf_op jit(solution)/shard_map/ppermute | solution.py:40
  28.1 9.3 %collective-permute-start.14 = (f32[1,64,512]{2,1,0:T(8,128)S(1)}, f32[1,64,512]{2,1,0:T(8,128)S(1)}, u32[]{:S(2)}, u32[]{:S(2)}) collective-permute-start(f32[1,64,512]{2,1,0:T(8,128)S(1)} %get-tuple-element.63), channel_id=1, source_target_pairs={{0,1},{1,0},{2,3},{3,2},{4,5},{5,4},{6,7},{7,6},{8,9},{9,8},{10,11... | collective-permute-start | bytes 393224 | tf_op jit(solution)/shard_map/ppermute | solution.py:40
  29.6 11.4 %collective-permute-start.16 = (f32[1,64,512]{2,1,0:T(8,128)S(1)}, f32[1,64,512]{2,1,0:T(8,128)S(1)}, u32[]{:S(2)}, u32[]{:S(2)}) collective-permute-start(f32[1,64,512]{2,1,0:T(8,128)S(1)} %get-tuple-element.66), channel_id=1, source_target_pairs={{0,1},{1,0},{2,3},{3,2},{4,5},{5,4},{6,7},{7,6},{8,9},{9,8},{10,11... | collective-permute-start | bytes 393224 | tf_op jit(solution)/shard_map/ppermute | solution.py:40
  31.8 9.2 %collective-permute-start.11 = (f32[1,64,512]{2,1,0:T(8,128)S(1)}, f32[1,64,512]{2,1,0:T(8,128)S(1)}, u32[]{:S(2)}, u32[]{:S(2)}) collective-permute-start(f32[1,64,512]{2,1,0:T(8,128)S(1)} %add.45), channel_id=1, source_target_pairs={{0,4},{1,5},{2,6},{3,7},{4,0},{5,1},{6,2},{7,3},{8,12},{9,13},{10,... | collective-permute-start | bytes 393224 | tf_op jit(solution)/shard_map/ppermute | solution.py:40
  34.6 6.4 %collective-permute-start.13 = (f32[1,64,512]{2,1,0:T(8,128)S(1)}, f32[1,64,512]{2,1,0:T(8,128)S(1)}, u32[]{:S(2)}, u32[]{:S(2)}) collective-permute-start(f32[1,64,512]{2,1,0:T(8,128)S(1)} %add.47), channel_id=1, source_target_pairs={{0,2},{1,3},{2,0},{3,1},{4,6},{5,7},{6,4},{7,5},{8,10},{9,11},{10,... | collective-permute-start | bytes 393224 | tf_op jit(solution)/shard_map/ppermute | solution.py:40
  37.4 7.1 %collective-permute-start.15 = (f32[1,64,512]{2,1,0:T(8,128)S(1)}, f32[1,64,512]{2,1,0:T(8,128)S(1)}, u32[]{:S(2)}, u32[]{:S(2)}) collective-permute-start(f32[1,64,512]{2,1,0:T(8,128)S(1)} %add.49), channel_id=1, source_target_pairs={{0,6},{1,7},{2,4},{3,5},{4,2},{5,3},{6,0},{7,1},{8,14},{9,15},{10,... | collective-permute-start | bytes 393224 | tf_op jit(solution)/shard_map/ppermute | solution.py:40

commit v7 on v6

--- a/solution.py
+++ b/solution.py
@@ -46,7 +46,7 @@
 
 def tile_order(lanes):
     half = lanes // 2
-    side = [half] + list(range(half - 2, 0, -2)) + list(range(half + 2, lanes, 2)) + [0]
+    side = list(range(half, lanes, 2)) + list(range(half - 2, -1, -2))
     return [k + 1 for k in side], side
 
 
@@ -227,7 +227,7 @@
 
 
 def sums_kernel(lanes, blocks, amp_dev, lists_ref, table_ref, own_ref, pair_ref, *refs):
-    amp_refs, sums_refs, local_refs, (in_hi, in_lo) = refs[:2], refs[2:6], refs[6:8], refs[8:]
+    amp_refs, sums_refs, (local_ref, in_hi, in_lo) = refs[:2], refs[2:6], refs[6:]
     weight = coefficients(lists_ref, table_ref, amp_dev, lanes, blocks)
     depth = own_ref.shape[0]
     step = weight.shape[0] // (2 * blocks)
@@ -249,9 +249,8 @@
         hi, lo = split(ref[...])
         in_hi[c * depth : (c + 1) * depth, :] = hi
         in_lo[c * depth : (c + 1) * depth, :] = lo
-    for k, ref in enumerate(local_refs):
-        hi, lo = (x[:, : 2 * depth] for x in sums_refs[2 * k : 2 * k + 2])
-        ref[...] = passes(hi, lo, in_hi[...], in_lo[...])
+    hi, lo = (x[:, : 2 * depth] for x in sums_refs[:2])
+    local_ref[...] = passes(hi, lo, in_hi[...], in_lo[...])
 
 
 def sums(lists, table, own, pair, rows, amp_dev, tile_rows, lanes, blocks):
@@ -262,10 +261,9 @@
     product = pltpu.VMEM((kept, window), jnp.float32)
     return pl.pallas_call(
         functools.partial(sums_kernel, lanes, blocks, amp_dev),
-        out_shape=[held] * 4 + [product] * 2,
+        out_shape=[held] * 4 + [product] + [local] * 2,
         in_specs=[VMEM] * (4 + len(rows)),
-        out_specs=[VMEM] * 6,
-        scratch_shapes=[local] * 2,
+        out_specs=[VMEM] * 7,
         compiler_params=limit(16 * depth * window),
         cost_estimate=cost(0, 16 * tile_rows * amp_dev * depth),
         name="sums",
@@ -290,13 +288,15 @@
 
 
 def fetched_kernel(*refs):
-    sums_refs, local_refs, rest = refs[:4], refs[4:6], refs[6:]
+    sums_refs, (local_ref, local_hi, local_lo), rest = refs[:4], refs[4:7], refs[7:]
     parts, out_refs, (in_hi, in_lo) = rest[:-4], rest[-4:-2], rest[-2:]
     depth = sum(x.shape[0] for x in parts[:3])
     split_parts(parts, in_hi, in_lo)
-    for k in range(2):
+    hi, lo = (x[:, : 2 * depth] for x in sums_refs[2:])
+    out_refs[1][...] = passes(hi, lo, local_hi[...], local_lo[...])
+    for k, ref in enumerate((local_ref, out_refs[1])):
         hi, lo = (columns(x, 0, depth) for x in sums_refs[2 * k : 2 * k + 2])
-        out_refs[k][...] = local_refs[k][...] + passes(hi, lo, in_hi[...], in_lo[...])
+        out_refs[k][...] = ref[...] + passes(hi, lo, in_hi[...], in_lo[...])
 
 
 def flat(parts):
@@ -310,7 +310,7 @@
     return pl.pallas_call(
         fetched_kernel,
         out_shape=[pltpu.VMEM((rows, window), jnp.float32)] * 2,
-        in_specs=[VMEM] * (6 + 3 * len(parts)),
+        in_specs=[VMEM] * (7 + 3 * len(parts)),
         out_specs=[VMEM] * 2,
         scratch_shapes=[half] * 2,
         compiler_params=limit(16 * len(parts) * depth * window),
@@ -399,7 +399,7 @@
         lists = jnp.concatenate([lists, swap(lists, "wide", k)], axis=1)
         k *= 2
     lists = after(lists, rows[1])
-    *held, local_away, local_side = sums(
+    *held, local_away, local_hi, local_lo = sums(
         lists, table, own, pair, rows, amp_dev, tile_rows, lanes, grps
     )
 
@@ -408,16 +408,20 @@
         even.append([one, two, swap(one, "wide", 1)])
         odd.append([swap(after(x, y), "grp", 1) for x, y in zip(even[-1], (lists, held[0], held[0]))])
 
-    local = fetched_products(held, (local_away, local_side), even)
+    local = fetched_products(held, (local_away, local_hi, local_lo), even)
     away, in_hi, in_lo = away_products(*held[:2], local[0], odd, half)
+    _, offsets = tile_order(lanes)
+    far, near, last = range(lanes // 4), range(lanes // 4, half - 1), half - 1
     side = side_products(*held[2:], local[1], in_hi, in_lo, half, own.shape[0])
-    _, offsets = tile_order(lanes)
-    got = [swap(away[0], "wide", 1)]
-    got += [swap(after(x, side[0]), "wide", 1) for x in away[1:]]
-    summed = base_residual
-    for k, here, there in zip(offsets, side, got):
-        part = here + there
-        summed = summed + (swap(part, "wide", k) if k else part)
+    got = [swap(away[j], "wide", 1) for j in far]
+    summed = base_residual + side[last]
+    for j in far:
+        summed = summed + swap(side[j] + got[j], "wide", offsets[j])
+    rest = away[last]
+    for j in near:
+        summed = summed + swap(side[j], "wide", offsets[j])
+        rest = rest + swap(after(away[j], side[0]), "wide", offsets[j])
+    summed = summed + swap(rest, "wide", 1)
     divisor = occ_gap[:, :, None] + virt_sum[None, None, :]
     return summed / divisor
 

time: 45.6 us -> 45 us (0.987)
    pallas_call x1, Pallas kernels: 3.03 us -> 2.28 us  [sums(): pl.pallas_call(functools.partial(sums_kernel, lanes, blocks, amp_dev), ou...]
    pallas_call x1, Pallas kernels: 1.12 us -> 1.81 us  [fetched_products(): pl.pallas_call(fetched_kernel, out_shape=[pltpu.VMEM((rows, window), jnp....]
  transfers between devices with their start and end apart: 17 -> 17, of which waited for: 7 -> 5; matrix products, arithmetic and copies ran while one was open for 0% -> 0% of each run, Pallas kernels for 24% -> 25%
where the time goes in v7:
time: 45 us; the launch traced here: 44.5 us
  starting transfers between devices  23.7 us (53%)
  Pallas kernels  11.7 us (26%)
  waiting for transfers between devices  7.48 us (17%)
  other arithmetic  0.84 us (2%)
  between operations  0.82 us (2%)
    ppermute x17, starting transfers between devices, swap(): return lax.ppermute(x, axis, [(i, i ^ k) for i in range(n)])  23.7 us
    ppermute x17, waiting for transfers between devices, swap(): return lax.ppermute(x, axis, [(i, i ^ k) for i in range(n)])  7.48 us
    pallas_call x2, Pallas kernels, load(): pl.pallas_call(functools.partial(load_kernel, first), out_shape=pltpu.VME...  4.26 us
    pallas_call x1, Pallas kernels, sums(): pl.pallas_call(functools.partial(sums_kernel, lanes, blocks, amp_dev), ou...  2.28 us
    pallas_call x1, Pallas kernels, fetched_products(): pl.pallas_call(fetched_kernel, out_shape=[pltpu.VMEM((rows, window), jnp....  1.81 us
    pallas_call x1, Pallas kernels, pieces(): pl.pallas_call(pieces_kernel, out_shape=[pltpu.VMEM((n, own.shape[1]), ow...  1.12 us
  transfers between devices with their start and end apart: 17, of which 5 were waited for; matrix products, arithmetic and copies ran while one was open for 0% of the time, Pallas kernels for 25%

profile of v7, /device:TPU:0, one launch (start us, length us, event | category | flops | bytes accessed | tf_op | source)
XLA Modules:
  0.0 44.5 jit_solution(16791641222515363081)
XLA Ops:
  0.0 0.5 %collective-permute-start.3 = (f32[512,512]{1,0:T(8,128)}, f32[512,512]{1,0:T(8,128)S(1)}, u32[]{:S(2)}, u32[]{:S(2)}) collective-permute-start(f32[512,512]{1,0:T(8,128)} %bitcast.4), channel_id=1, source_target_pairs={{0,8},{8,0},{16,24},{24,16},{1,9},{9,1},{17,25},{25,17},{2,10},{10... | collective-permute-start | bytes 3145736 | tf_op jit(solution)/shard_map/ppermute | solution.py:40
  0.5 1.1 %pieces.1 = (f32[144,512]{1,0:T(8,128)S(1)}, f32[224,512]{1,0:T(8,128)S(1)}) custom-call(f32[512,512]{1,0:T(8,128)} %bitcast.5), custom_call_target="tpu_custom_call" | custom-call | bytes 1048576 | tf_op jit(solution)/shard_map/pieces/pallas_call | solution.py:78
  1.6 2.6 %collective-permute-start.4 = (f32[144,512]{1,0:T(8,128)S(1)}, f32[144,512]{1,0:T(8,128)S(1)}, u32[]{:S(2)}, u32[]{:S(2)}) collective-permute-start(f32[144,512]{1,0:T(8,128)S(1)} %get-tuple-element.35), channel_id=1, source_target_pairs={{0,16},{8,24},{16,0},{24,8},{1,17},{9,25},{17,1},{25,9},{2,18},{10... | collective-permute-start | bytes 884744 | tf_op jit(solution)/shard_map/ppermute | solution.py:40
  4.1 0.1 collective-permute-start.5
  4.9 0.9 %pack_lists.1 = (s32[3,1,96]{2,1,0:T(1,128)S(1)}, s32[3,256]{1,0:T(4,128)S(1)}) custom-call(s32[1]{0:T(128)S(6)} %copy.13.count_ref, s32[1,96]{1,0:T(1,128)} %refs_0_.1, s32[1,96]{1,0:T(1,128)} %refs_1_.1, s32[1,96]{1,0:T(1,128)} %refs_2_, s32[1,32]{1,0:T(1,128)} %bitcast.8, s32[1,8]{1,0:T(1,128)} %refs_4_.1, s32[1,4]{1,0:T(1,128)} %bitcast.9), custom_call_target="tpu_custom_call" | custom-call | bytes 4096 | tf_op jit(solution)/shard_map/pack_lists/pallas_call | solution.py:113
  5.7 2.0 %collective-permute-start = (s32[3,1,96]{2,1,0:T(1,128)S(1)}, s32[3,1,96]{2,1,0:T(1,128)S(1)}, u32[]{:S(2)}, u32[]{:S(2)}) collective-permute-start(s32[3,1,96]{2,1,0:T(1,128)S(1)} %get-tuple-element.37), channel_id=1, source_target_pairs={{0,1},{1,0},{2,3},{3,2},{4,5},{5,4},{6,7},{7,6},{8,9},{9,8},{10,11... | collective-permute-start | bytes 3464 | tf_op jit(solution)/shard_map/ppermute | solution.py:40
  7.8 2.1 %load_amplitudes.2.refs_0_ = bf16[2048,512]{1,0:T(8,128)(2,1)S(1)} custom-call(f32[32,64,512]{2,1,0:T(8,128)} %amp_hbm.3), custom_call_target="tpu_custom_call" | custom-call | bytes 4194304 | tf_op jit(solution)/shard_map/load_amplitudes/pallas_call | solution.py:148
  9.9 0.0 collective-permute-done
  10.0 1.6 %collective-permute-start.1 = (s32[3,2,96]{2,1,0:T(2,128)S(1)}, s32[3,2,96]{2,1,0:T(2,128)S(1)}, u32[]{:S(2)}, u32[]{:S(2)}) collective-permute-start(s32[3,2,96]{2,1,0:T(2,128)S(1)} %pad_add_fusion.2), channel_id=1, source_target_pairs={{0,2},{1,3},{2,0},{3,1},{4,6},{5,7},{6,4},{7,5},{8,10},{9,11},{10,... | collective-permute-start | bytes 6920 | tf_op jit(solution)/shard_map/ppermute | solution.py:40
  11.6 0.4 collective-permute-done.4.refs_7_
  12.0 2.0 %collective-permute-start.6 = (f32[144,512]{1,0:T(8,128)S(1)}, f32[144,512]{1,0:T(8,128)S(1)}, u32[]{:S(2)}, u32[]{:S(2)}) collective-permute-start(f32[144,512]{1,0:T(8,128)S(1)} %collective-permute-done.4.refs_7_), channel_id=1, source_target_pairs={{0,1},{1,0},{2,3},{3,2},{4,5},{5,4},{6,7},{7,6},{8,9},{9,8},{10,11... | collective-permute-start | bytes 884744 | tf_op jit(solution)/shard_map/ppermute | solution.py:40
  14.0 0.0 collective-permute-done.1
  14.0 0.0 copy-start
  14.0 2.7 %collective-permute-start.2 = (s32[3,4,96]{2,1,0:T(4,128)S(1)}, s32[3,4,96]{2,1,0:T(4,128)S(1)}, u32[]{:S(2)}, u32[]{:S(2)}) collective-permute-start(s32[3,4,96]{2,1,0:T(4,128)S(1)} %pad_add_fusion.1), channel_id=1, source_target_pairs={{0,4},{1,5},{2,6},{3,7},{4,0},{5,1},{6,2},{7,3},{8,12},{9,13},{10,... | collective-permute-start | bytes 13832 | tf_op jit(solution)/shard_map/ppermute | solution.py:40
  16.7 2.1 %load_amplitudes.3.refs_1_ = bf16[2048,512]{1,0:T(8,128)(2,1)S(1)} custom-call(f32[32,64,512]{2,1,0:T(8,128)} %amp_hbm.3), custom_call_target="tpu_custom_call" | custom-call | bytes 4194304 | tf_op jit(solution)/shard_map/load_amplitudes/pallas_call | solution.py:148
  18.8 0.0 collective-permute-done.2
  18.8 0.0 collective-permute-done.3.pair_ref
  18.8 0.0 copy-done
  18.8 2.3 %sums.1 = (bf16[256,2048]{1,0:T(8,128)(2,1)S(1)}, bf16[256,2048]{1,0:T(8,128)(2,1)S(1)}, bf16[256,2048]{1,0:T(8,128)(2,1)S(1)}, bf16[256,2048]{1,0:T(8,128)(2,1)...) custom-call(s32[3,8,96]{2,1,0:T(8,128)S(1)} %pad_add_fusion.lists_ref, ...), custom_call_target="tpu_custom_call" | custom-call | bytes 16777216 | tf_op jit(solution)/shard_map/sums/pallas_call | solution.py:262
  21.1 0.5 %collective-permute-done.5.refs_8_ = f32[224,512]{1,0:T(8,128)S(1)} collective-permute-done((f32[224,512]{1,0:T(8,128)S(1)}, f32[224,512]{1,0:T(8,128)S(1)}, u32[]{:S(2)}, u32[]{:S(2)}) %collective-permute-start.5) | collective-permute-done | bytes 458784 | tf_op jit(solution)/shard_map/ppermute | solution.py:40
  21.7 0.0 collective-permute-start.8
  21.7 0.5 %collective-permute-start.7 = (f32[144,512]{1,0:T(8,128)S(1)}, f32[144,512]{1,0:T(8,128)S(1)}, u32[]{:S(2)}, u32[]{:S(2)}) collective-permute-start(f32[144,512]{1,0:T(8,128)S(1)} %collective-permute-done.4.refs_7_), channel_id=1, source_target_pairs={{0,8},{8,0},{16,24},{24,16},{1,9},{9,1},{17,25},{25,17},{2,10},{10... | collective-permute-start | bytes 884744 | tf_op jit(solution)/shard_map/ppermute | solution.py:40
  22.2 0.0 collective-permute-done.6.refs_9_
  22.2 0.0 collective-permute-start.9
  22.2 1.8 %fetched_products.1 = (f32[256,512]{1,0:T(8,128)S(1)}, f32[256,512]{1,0:T(8,128)S(1)}) custom-call(bf16[256,2048]{1,0:T(8,128)(2,1)S(1)} %get-tuple-element.43.refs_0_.hi, bf16[256,2048]{1,0:T(8,128)(2,1)S(1)} %get-tuple-element.44.refs_1_.lo, bf16[256,2048]{1,0:T(8,128)(2,1)S(1)} %get-tuple-element.41.refs_2_.hi, ...), custom_call_target="tpu_custom_call" | custom-call | flops 805306368 | tf_op jit(solution)/shard_map/fetched_products/pallas_call | solution.py:310
  24.0 0.0 collective-permute-done.7.rest_0_
  24.0 0.3 collective-permute-done.9.rest_2_
  24.3 0.0 collective-permute-done.8.rest_1_
  24.3 0.7 %away_products.1 = (f32[1,64,512]{2,1,0:T(8,128)S(1)}, f32[1,64,512]{2,1,0:T(8,128)S(1)}, f32[1,64,512]{2,1,0:T(8,128)S(1)}, f32[1,64,512]{2,1,0:T(8,128)S(1)}, ...) custom-call(bf16[256,2048]{1,0:T(8,128)(2,1)S(1)} %get-tuple-element.43.refs_0_.hi, ...), custom_call_target="tpu_custom_call" | custom-call | flops 402653184 | tf_op jit(solution)/shard_map/away_products/pallas_call | solution.py:341
  25.0 1.8 %collective-permute-start.10 = (f32[1,64,512]{2,1,0:T(8,128)S(1)}, f32[1,64,512]{2,1,0:T(8,128)S(1)}, u32[]{:S(2)}, u32[]{:S(2)}) collective-permute-start(f32[1,64,512]{2,1,0:T(8,128)S(1)} %get-tuple-element.58), channel_id=1, source_target_pairs={{0,1},{1,0},{2,3},{3,2},{4,5},{5,4},{6,7},{7,6},{8,9},{9,8},{10,11... | collective-permute-start | bytes 393224 | tf_op jit(solution)/shard_map/ppermute | solution.py:40
  26.9 0.3 collective-permute-start.12
  27.1 0.6 %side_products.1 = (f32[1,64,512]{2,1,0:T(8,128)S(1)}, f32[1,64,512]{2,1,0:T(8,128)S(1)}, f32[1,64,512]{2,1,0:T(8,128)S(1)}, f32[1,64,512]{2,1,0:T(8,128)S(1)}) custom-call(bf16[256,2048]{1,0:T(8,128)(2,1)S(1)} %get-tuple-element.41.refs_2_.hi, bf16[256,2048]{1,0:T(8,128)(2,1)S(1)} %get-tuple-element.42.refs_3_.lo, ...), custom_call_target="tpu_custom_call" | custom-call | tf_op jit(solution)/shard_map/side_products/pallas_call | solution.py:357
  27.7 1.9 %collective-permute-start.15 = (f32[1,64,512]{2,1,0:T(8,128)S(1)}, f32[1,64,512]{2,1,0:T(8,128)S(1)}, u32[]{:S(2)}, u32[]{:S(2)}) collective-permute-start(f32[1,64,512]{2,1,0:T(8,128)S(1)} %get-tuple-element.64), channel_id=1, source_target_pairs={{0,2},{1,3},{2,0},{3,1},{4,6},{5,7},{6,4},{7,5},{8,10},{9,11},{10,... | collective-permute-start | bytes 393224 | tf_op jit(solution)/shard_map/ppermute | solution.py:40
  29.6 0.2 collective-permute-start.14
  29.8 1.6 %collective-permute-done.10 = f32[1,64,512]{2,1,0:T(8,128)S(1)} collective-permute-done((f32[1,64,512]{2,1,0:T(8,128)S(1)}, f32[1,64,512]{2,1,0:T(8,128)S(1)}, u32[]{:S(2)}, u32[]{:S(2)}) %collective-permute-start.10) | collective-permute-done | bytes 131104 | tf_op jit(solution)/shard_map/ppermute | solution.py:40
  31.5 2.9 %collective-permute-start.11 = (f32[1,64,512]{2,1,0:T(8,128)S(1)}, f32[1,64,512]{2,1,0:T(8,128)S(1)}, u32[]{:S(2)}, u32[]{:S(2)}) collective-permute-start(f32[1,64,512]{2,1,0:T(8,128)S(1)} %add.46), channel_id=1, source_target_pairs={{0,4},{1,5},{2,6},{3,7},{4,0},{5,1},{6,2},{7,3},{8,12},{9,13},{10,... | collective-permute-start | bytes 393224 | tf_op jit(solution)/shard_map/ppermute | solution.py:40
  34.4 0.0 collective-permute-done.12
  34.4 3.1 %collective-permute-start.13 = (f32[1,64,512]{2,1,0:T(8,128)S(1)}, f32[1,64,512]{2,1,0:T(8,128)S(1)}, u32[]{:S(2)}, u32[]{:S(2)}) collective-permute-start(f32[1,64,512]{2,1,0:T(8,128)S(1)} %add.48), channel_id=1, source_target_pairs={{0,6},{1,7},{2,4},{3,5},{4,2},{5,3},{6,0},{7,1},{8,14},{9,15},{10,... | collective-permute-start | bytes 393224 | tf_op jit(solution)/shard_map/ppermute | solution.py:40
  37.5 0.0 collective-permute-done.15
  37.5 1.6 %collective-permute-start.16 = (f32[1,64,512]{2,1,0:T(8,128)S(1)}, f32[1,64,512]{2,1,0:T(8,128)S(1)}, u32[]{:S(2)}, u32[]{:S(2)}) collective-permute-start(f32[1,64,512]{2,1,0:T(8,128)S(1)} %add.51), channel_id=1, source_target_pairs={{0,1},{1,0},{2,3},{3,2},{4,5},{5,4},{6,7},{7,6},{8,9},{9,8},{10,11... | collective-permute-start | bytes 393224 | tf_op jit(solution)/shard_map/ppermute | solution.py:40
  39.1 0.0 collective-permute-done.14
  39.1 4.6 %collective-permute-done.11 = f32[1,64,512]{2,1,0:T(8,128)S(1)} collective-permute-done((f32[1,64,512]{2,1,0:T(8,128)S(1)}, f32[1,64,512]{2,1,0:T(8,128)S(1)}, u32[]{:S(2)}, u32[]{:S(2)}) %collective-permute-start.11) | collective-permute-done | bytes 131104 | tf_op jit(solution)/shard_map/ppermute | solution.py:40
  43.7 0.0 collective-permute-done.13
  43.7 0.0 collective-permute-done.16
  43.7 0.0 copy-done.1
  43.7 0.0 copy-done.2
  43.7 0.0 copy-done.3
  43.7 0.8 %add_divide_fusion = f32[1,64,512]{2,1,0:T(8,128)} fusion(f32[1,64,512]{2,1,0:T(8,128)S(1)} %collective-permute-done.16, f32[1,64,512]{2,1,0:T(8,128)S(1)} %collective-permute-done.14, f32[1,64,512]{2,1,0:T(8,128)S(1)} %collective-permute-done.13, f32[1,64,512]{2,1,0:T(8,128)S(1)} %collective-permute-done.11, f32[1,64,512]{2,1,0:T(8,128)S(1)} %copy-done.1, ...), kind=kLoop, calls=%fused_computation | loop fusion | flops 229376 | bytes 919808 | tf_op jit(solution)/shard_map/div | solution.py:426
  (9 shorter events, 0.1 us)
Async XLA Ops:
  0.0 18.8 %collective-permute-start.3 = (f32[512,512]{1,0:T(8,128)}, f32[512,512]{1,0:T(8,128)S(1)}, u32[]{:S(2)}, u32[]{:S(2)}) collective-permute-start(f32[512,512]{1,0:T(8,128)} %bitcast.4), channel_id=1, source_target_pairs={{0,8},{8,0},{16,24},{24,16},{1,9},{9,1},{17,25},{25,17},{2,10},{10... | collective-permute-start | bytes 3145736 | tf_op jit(solution)/shard_map/ppermute | solution.py:40
  1.6 10.4 %collective-permute-start.4 = (f32[144,512]{1,0:T(8,128)S(1)}, f32[144,512]{1,0:T(8,128)S(1)}, u32[]{:S(2)}, u32[]{:S(2)}) collective-permute-start(f32[144,512]{1,0:T(8,128)S(1)} %get-tuple-element.35), channel_id=1, source_target_pairs={{0,16},{8,24},{16,0},{24,8},{1,17},{9,25},{17,1},{25,9},{2,18},{10... | collective-permute-start | bytes 884744 | tf_op jit(solution)/shard_map/ppermute | solution.py:40
  4.1 17.5 %collective-permute-start.5 = (f32[224,512]{1,0:T(8,128)S(1)}, f32[224,512]{1,0:T(8,128)S(1)}, u32[]{:S(2)}, u32[]{:S(2)}) collective-permute-start(f32[224,512]{1,0:T(8,128)S(1)} %get-tuple-element.48), channel_id=1, source_target_pairs={{0,16},{8,24},{16,0},{24,8},{1,17},{9,25},{17,1},{25,9},{2,18},{10... | collective-permute-start | bytes 1376264 | tf_op jit(solution)/shard_map/ppermute | solution.py:40
  5.7 4.2 %collective-permute-start = (s32[3,1,96]{2,1,0:T(1,128)S(1)}, s32[3,1,96]{2,1,0:T(1,128)S(1)}, u32[]{:S(2)}, u32[]{:S(2)}) collective-permute-start(s32[3,1,96]{2,1,0:T(1,128)S(1)} %get-tuple-element.37), channel_id=1, source_target_pairs={{0,1},{1,0},{2,3},{3,2},{4,5},{5,4},{6,7},{7,6},{8,9},{9,8},{10,11... | collective-permute-start | bytes 3464 | tf_op jit(solution)/shard_map/ppermute | solution.py:40
  10.0 4.0 %collective-permute-start.1 = (s32[3,2,96]{2,1,0:T(2,128)S(1)}, s32[3,2,96]{2,1,0:T(2,128)S(1)}, u32[]{:S(2)}, u32[]{:S(2)}) collective-permute-start(s32[3,2,96]{2,1,0:T(2,128)S(1)} %pad_add_fusion.2), channel_id=1, source_target_pairs={{0,2},{1,3},{2,0},{3,1},{4,6},{5,7},{6,4},{7,5},{8,10},{9,11},{10,... | collective-permute-start | bytes 6920 | tf_op jit(solution)/shard_map/ppermute | solution.py:40
  12.0 10.2 %collective-permute-start.6 = (f32[144,512]{1,0:T(8,128)S(1)}, f32[144,512]{1,0:T(8,128)S(1)}, u32[]{:S(2)}, u32[]{:S(2)}) collective-permute-start(f32[144,512]{1,0:T(8,128)S(1)} %collective-permute-done.4.refs_7_), channel_id=1, source_target_pairs={{0,1},{1,0},{2,3},{3,2},{4,5},{5,4},{6,7},{7,6},{8,9},{9,8},{10,11... | collective-permute-start | bytes 884744 | tf_op jit(solution)/shard_map/ppermute | solution.py:40
  14.0 4.8 %copy-start = (f32[1,512,512]{2,1,0:T(8,128)S(1)}, f32[1,512,512]{2,1,0:T(8,128)}, u32[]{:S(2)}) copy-start(f32[1,512,512]{2,1,0:T(8,128)} %param.13) | copy-start | bytes 3145732
  14.0 4.8 %collective-permute-start.2 = (s32[3,4,96]{2,1,0:T(4,128)S(1)}, s32[3,4,96]{2,1,0:T(4,128)S(1)}, u32[]{:S(2)}, u32[]{:S(2)}) collective-permute-start(s32[3,4,96]{2,1,0:T(4,128)S(1)} %pad_add_fusion.1), channel_id=1, source_target_pairs={{0,4},{1,5},{2,6},{3,7},{4,0},{5,1},{6,2},{7,3},{8,12},{9,13},{10,... | collective-permute-start | bytes 13832 | tf_op jit(solution)/shard_map/ppermute | solution.py:40
  21.7 2.7 %collective-permute-start.8 = (f32[224,512]{1,0:T(8,128)S(1)}, f32[224,512]{1,0:T(8,128)S(1)}, u32[]{:S(2)}, u32[]{:S(2)}) collective-permute-start(f32[224,512]{1,0:T(8,128)S(1)} %collective-permute-done.5.refs_8_), channel_id=1, source_target_pairs={{0,8},{8,0},{16,24},{24,16},{1,9},{9,1},{17,25},{25,17},{2,10},{10... | collective-permute-start | bytes 1376264 | tf_op jit(solution)/shard_map/ppermute | solution.py:40
  21.7 2.3 %collective-permute-start.7 = (f32[144,512]{1,0:T(8,128)S(1)}, f32[144,512]{1,0:T(8,128)S(1)}, u32[]{:S(2)}, u32[]{:S(2)}) collective-permute-start(f32[144,512]{1,0:T(8,128)S(1)} %collective-permute-done.4.refs_7_), channel_id=1, source_target_pairs={{0,8},{8,0},{16,24},{24,16},{1,9},{9,1},{17,25},{25,17},{2,10},{10... | collective-permute-start | bytes 884744 | tf_op jit(solution)/shard_map/ppermute | solution.py:40
  22.2 2.1 %collective-permute-start.9 = (f32[144,512]{1,0:T(8,128)S(1)}, f32[144,512]{1,0:T(8,128)S(1)}, u32[]{:S(2)}, u32[]{:S(2)}) collective-permute-start(f32[144,512]{1,0:T(8,128)S(1)} %collective-permute-done.6.refs_9_), channel_id=1, source_target_pairs={{0,8},{8,0},{16,24},{24,16},{1,9},{9,1},{17,25},{25,17},{2,10},{10... | collective-permute-start | bytes 884744 | tf_op jit(solution)/shard_map/ppermute | solution.py:40
  25.0 6.4 %collective-permute-start.10 = (f32[1,64,512]{2,1,0:T(8,128)S(1)}, f32[1,64,512]{2,1,0:T(8,128)S(1)}, u32[]{:S(2)}, u32[]{:S(2)}) collective-permute-start(f32[1,64,512]{2,1,0:T(8,128)S(1)} %get-tuple-element.58), channel_id=1, source_target_pairs={{0,1},{1,0},{2,3},{3,2},{4,5},{5,4},{6,7},{7,6},{8,9},{9,8},{10,11... | collective-permute-start | bytes 393224 | tf_op jit(solution)/shard_map/ppermute | solution.py:40
  26.9 7.5 %collective-permute-start.12 = (f32[1,64,512]{2,1,0:T(8,128)S(1)}, f32[1,64,512]{2,1,0:T(8,128)S(1)}, u32[]{:S(2)}, u32[]{:S(2)}) collective-permute-start(f32[1,64,512]{2,1,0:T(8,128)S(1)} %get-tuple-element.60), channel_id=1, source_target_pairs={{0,1},{1,0},{2,3},{3,2},{4,5},{5,4},{6,7},{7,6},{8,9},{9,8},{10,11... | collective-permute-start | bytes 393224 | tf_op jit(solution)/shard_map/ppermute | solution.py:40
  27.1 16.6 %copy-start.1 = (f32[1,64,512]{2,1,0:T(8,128)S(1)}, f32[1,64,512]{2,1,0:T(8,128)}, u32[]{:S(2)}) copy-start(f32[1,64,512]{2,1,0:T(8,128)} %param.14) | copy-start | bytes 393220
  27.1 16.6 %copy-start.2 = (f32[512]{0:T(512)S(1)}, f32[512]{0:T(512)}, u32[]{:S(2)}) copy-start(f32[512]{0:T(512)} %param.16) | copy-start | bytes 6148
  27.1 16.6 %copy-start.3 = (f32[1,64]{1,0:T(1,128)S(1)}, f32[1,64]{1,0:T(1,128)}, u32[]{:S(2)}) copy-start(f32[1,64]{1,0:T(1,128)} %param.15) | copy-start | bytes 772
  27.7 9.7 %collective-permute-start.15 = (f32[1,64,512]{2,1,0:T(8,128)S(1)}, f32[1,64,512]{2,1,0:T(8,128)S(1)}, u32[]{:S(2)}, u32[]{:S(2)}) collective-permute-start(f32[1,64,512]{2,1,0:T(8,128)S(1)} %get-tuple-element.64), channel_id=1, source_target_pairs={{0,2},{1,3},{2,0},{3,1},{4,6},{5,7},{6,4},{7,5},{8,10},{9,11},{10,... | collective-permute-start | bytes 393224 | tf_op jit(solution)/shard_map/ppermute | solution.py:40
  29.6 9.4 %collective-permute-start.14 = (f32[1,64,512]{2,1,0:T(8,128)S(1)}, f32[1,64,512]{2,1,0:T(8,128)S(1)}, u32[]{:S(2)}, u32[]{:S(2)}) collective-permute-start(f32[1,64,512]{2,1,0:T(8,128)S(1)} %get-tuple-element.61), channel_id=1, source_target_pairs={{0,2},{1,3},{2,0},{3,1},{4,6},{5,7},{6,4},{7,5},{8,10},{9,11},{10,... | collective-permute-start | bytes 393224 | tf_op jit(solution)/shard_map/ppermute | solution.py:40
  31.5 12.2 %collective-permute-start.11 = (f32[1,64,512]{2,1,0:T(8,128)S(1)}, f32[1,64,512]{2,1,0:T(8,128)S(1)}, u32[]{:S(2)}, u32[]{:S(2)}) collective-permute-start(f32[1,64,512]{2,1,0:T(8,128)S(1)} %add.46), channel_id=1, source_target_pairs={{0,4},{1,5},{2,6},{3,7},{4,0},{5,1},{6,2},{7,3},{8,12},{9,13},{10,... | collective-permute-start | bytes 393224 | tf_op jit(solution)/shard_map/ppermute | solution.py:40
  34.4 9.3 %collective-permute-start.13 = (f32[1,64,512]{2,1,0:T(8,128)S(1)}, f32[1,64,512]{2,1,0:T(8,128)S(1)}, u32[]{:S(2)}, u32[]{:S(2)}) collective-permute-start(f32[1,64,512]{2,1,0:T(8,128)S(1)} %add.48), channel_id=1, source_target_pairs={{0,6},{1,7},{2,4},{3,5},{4,2},{5,3},{6,0},{7,1},{8,14},{9,15},{10,... | collective-permute-start | bytes 393224 | tf_op jit(solution)/shard_map/ppermute | solution.py:40
  37.5 6.2 %collective-permute-start.16 = (f32[1,64,512]{2,1,0:T(8,128)S(1)}, f32[1,64,512]{2,1,0:T(8,128)S(1)}, u32[]{:S(2)}, u32[]{:S(2)}) collective-permute-start(f32[1,64,512]{2,1,0:T(8,128)S(1)} %add.51), channel_id=1, source_target_pairs={{0,1},{1,0},{2,3},{3,2},{4,5},{5,4},{6,7},{7,6},{8,9},{9,8},{10,11... | collective-permute-start | bytes 393224 | tf_op jit(solution)/shard_map/ppermute | solution.py:40

commit v8 on v6

--- a/solution.py
+++ b/solution.py
@@ -46,7 +46,7 @@
 
 def tile_order(lanes):
     half = lanes // 2
-    side = [half] + list(range(half - 2, 0, -2)) + list(range(half + 2, lanes, 2)) + [0]
+    side = list(range(half, lanes, 2)) + list(range(half - 2, -1, -2))
     return [k + 1 for k in side], side
 
 
@@ -272,16 +272,18 @@
     )(lists, table, own, pair, *[in_vmem(x) for x in rows])
 
 
-def split_parts(parts, in_hi, in_lo):
-    depth = sum(x.shape[0] for x in parts[:3])
+def split_parts(parts, in_hi, in_lo, cuts):
+    n = sum(cuts)
+    depth = in_hi.shape[0] // (len(parts) // n)
     mine, theirs = end_offsets(depth)
-    for c in range(len(parts) // 3):
-        starts = (mine, row_cuts(depth)[0], theirs)
-        for start, part in zip(starts, parts[3 * c : 3 * c + 3]):
-            hi, lo = split(part[...])
-            at = pl.ds(pl.multiple_of(c * depth + start, 16), part.shape[0])
-            in_hi[at, :] = hi
-            in_lo[at, :] = lo
+    end, middle = row_cuts(depth)
+    places = zip((mine, end, theirs), (end, middle, end), cuts)
+    starts = [first + i * rows // m for first, rows, m in places for i in range(m)]
+    for i, part in enumerate(parts):
+        hi, lo = split(part[...])
+        at = pl.ds(pl.multiple_of(i // n * depth + starts[i % n], 16), part.shape[0])
+        in_hi[at, :] = hi
+        in_lo[at, :] = lo
 
 
 def columns(x, odd, depth):
@@ -293,7 +295,7 @@
     sums_refs, local_refs, rest = refs[:4], refs[4:6], refs[6:]
     parts, out_refs, (in_hi, in_lo) = rest[:-4], rest[-4:-2], rest[-2:]
     depth = sum(x.shape[0] for x in parts[:3])
-    split_parts(parts, in_hi, in_lo)
+    split_parts(parts, in_hi, in_lo, (1, 1, 1))
     for k in range(2):
         hi, lo = (columns(x, 0, depth) for x in sums_refs[2 * k : 2 * k + 2])
         out_refs[k][...] = local_refs[k][...] + passes(hi, lo, in_hi[...], in_lo[...])
@@ -321,8 +323,8 @@
 
 def away_kernel(tiles, hi, lo, local_ref, *rest):
     parts, out_refs, (in_hi, in_lo, held) = rest[: -3 - tiles], rest[-3 - tiles : -3], rest[-3:]
-    split_parts(parts, in_hi, in_lo)
-    depth = sum(x.shape[0] for x in parts[:3])
+    split_parts(parts, in_hi, in_lo, (1, 2, 2))
+    depth = in_hi.shape[0] // (len(parts) // 5)
     out = passes(columns(hi, 1, depth), columns(lo, 1, depth), in_hi[...], in_lo[...])
     store_tiles(local_ref[...] + out, out_refs, held)
 
@@ -341,7 +343,7 @@
     *out, in_hi, in_lo = pl.pallas_call(
         functools.partial(away_kernel, tiles),
         out_shape=shapes + [remote] * 2,
-        in_specs=[VMEM] * (3 + 3 * len(parts)),
+        in_specs=[VMEM] * (3 + 5 * len(parts)),
         out_specs=[VMEM] * (tiles + 2),
         scratch_shapes=[pltpu.VMEM((window // LANES, rows, LANES), jnp.float32)],
         compiler_params=limit(16 * len(parts) * depth * window),
@@ -364,6 +366,25 @@
         cost_estimate=cost(0, 0),
         name="side_products",
     )(*[in_vmem(x) for x in (hi, lo, local, in_hi, in_lo)])
+
+
+def halves_kernel(x, *out_refs):
+    rows = out_refs[0].shape[0]
+    for i, ref in enumerate(out_refs):
+        ref[...] = x[i * rows : (i + 1) * rows, :]
+
+
+def halves(x, nbytes):
+    half = pltpu.VMEM((x.shape[0] // 2, x.shape[1]), x.dtype)
+    return pl.pallas_call(
+        halves_kernel,
+        out_shape=[half, half],
+        in_specs=[VMEM],
+        out_specs=[VMEM] * 2,
+        compiler_params=limit(0),
+        cost_estimate=cost(0, nbytes),
+        name="halves",
+    )(x)
 
 
 def on_device(
@@ -406,18 +427,23 @@
     even, odd = [], []
     for k, (one, two) in fetched.items():
         even.append([one, two, swap(one, "wide", 1)])
-        odd.append([swap(after(x, y), "grp", 1) for x, y in zip(even[-1], (lists, held[0], held[0]))])
+        later = [one, *halves(after(two, held[0]), 0), *halves(after(even[-1][2], held[0]), 0)]
+        odd.append([swap(after(x, held[0]), "grp", 1) for x in later])
 
     local = fetched_products(held, (local_away, local_side), even)
     away, in_hi, in_lo = away_products(*held[:2], local[0], odd, half)
+    _, offsets = tile_order(lanes)
+    far, near, last = range(lanes // 4), range(lanes // 4, half - 1), half - 1
     side = side_products(*held[2:], local[1], in_hi, in_lo, half, own.shape[0])
-    _, offsets = tile_order(lanes)
-    got = [swap(away[0], "wide", 1)]
-    got += [swap(after(x, side[0]), "wide", 1) for x in away[1:]]
-    summed = base_residual
-    for k, here, there in zip(offsets, side, got):
-        part = here + there
-        summed = summed + (swap(part, "wide", k) if k else part)
+    got = [swap(away[j], "wide", 1) for j in far]
+    summed = base_residual + side[last]
+    for j in far:
+        summed = summed + swap(side[j] + got[j], "wide", offsets[j])
+    rest = away[last]
+    for j in near:
+        summed = summed + swap(side[j], "wide", offsets[j])
+        rest = rest + swap(after(away[j], side[0]), "wide", offsets[j])
+    summed = summed + swap(rest, "wide", 1)
     divisor = occ_gap[:, :, None] + virt_sum[None, None, :]
     return summed / divisor
 

time: 45.6 us -> 45.5 us (level)
    ppermute x17 -> x19, starting transfers between devices: 24.1 us -> 23.8 us  [swap(): return lax.ppermute(x, axis, [(i, i ^ k) for i in range(n)])]
    ppermute x17 -> x19, waiting for transfers between devices: 7.78 us -> 7.79 us  [swap(): return lax.ppermute(x, axis, [(i, i ^ k) for i in range(n)])]
  transfers between devices with their start and end apart: 17 -> 19, of which waited for: 7 -> 4; matrix products, arithmetic and copies ran while one was open for 0% -> 0% of each run, Pallas kernels for 24% -> 25%
where the time goes in v8:
time: 45.5 us; the launch traced here: 45.1 us
  starting transfers between devices  23.8 us (52%)
  Pallas kernels  11.8 us (26%)
  waiting for transfers between devices  7.79 us (17%)
  other arithmetic  0.84 us (2%)
  between operations  0.84 us (2%)
    ppermute x19, starting transfers between devices, swap(): return lax.ppermute(x, axis, [(i, i ^ k) for i in range(n)])  23.8 us
    ppermute x19, waiting for transfers between devices, swap(): return lax.ppermute(x, axis, [(i, i ^ k) for i in range(n)])  7.79 us
    pallas_call x2, Pallas kernels, load(): pl.pallas_call(functools.partial(load_kernel, first), out_shape=pltpu.VME...  4.26 us
    pallas_call x1, Pallas kernels, sums(): pl.pallas_call(functools.partial(sums_kernel, lanes, blocks, amp_dev), ou...  3.03 us
    pallas_call x1, Pallas kernels, fetched_products(): pl.pallas_call(fetched_kernel, out_shape=[pltpu.VMEM((rows, window), jnp....  1.13 us
    pallas_call x1, Pallas kernels, pieces(): pl.pallas_call(pieces_kernel, out_shape=[pltpu.VMEM((n, own.shape[1]), ow...  1.12 us
  transfers between devices with their start and end apart: 19, of which 4 were waited for; matrix products, arithmetic and copies ran while one was open for 0% of the time, Pallas kernels for 25%

profile of v8, /device:TPU:0, one launch (start us, length us, event | category | flops | bytes accessed | tf_op | source)
XLA Modules:
  0.0 45.1 jit_solution(2561134849723741328)
XLA Ops:
  0.0 0.5 %collective-permute-start.3 = (f32[512,512]{1,0:T(8,128)}, f32[512,512]{1,0:T(8,128)S(1)}, u32[]{:S(2)}, u32[]{:S(2)}) collective-permute-start(f32[512,512]{1,0:T(8,128)} %bitcast.4), channel_id=1, source_target_pairs={{0,8},{8,0},{16,24},{24,16},{1,9},{9,1},{17,25},{25,17},{2,10},{10... | collective-permute-start | bytes 3145736 | tf_op jit(solution)/shard_map/ppermute | solution.py:40
  0.5 1.1 %pieces.1 = (f32[144,512]{1,0:T(8,128)S(1)}, f32[224,512]{1,0:T(8,128)S(1)}) custom-call(f32[512,512]{1,0:T(8,128)} %bitcast.5), custom_call_target="tpu_custom_call" | custom-call | bytes 1048576 | tf_op jit(solution)/shard_map/pieces/pallas_call | solution.py:78
  1.6 2.6 %collective-permute-start.4 = (f32[144,512]{1,0:T(8,128)S(1)}, f32[144,512]{1,0:T(8,128)S(1)}, u32[]{:S(2)}, u32[]{:S(2)}) collective-permute-start(f32[144,512]{1,0:T(8,128)S(1)} %get-tuple-element.42), channel_id=1, source_target_pairs={{0,16},{8,24},{16,0},{24,8},{1,17},{9,25},{17,1},{25,9},{2,18},{10... | collective-permute-start | bytes 884744 | tf_op jit(solution)/shard_map/ppermute | solution.py:40
  4.1 0.1 collective-permute-start.5
  4.9 0.9 %pack_lists.1 = (s32[3,1,96]{2,1,0:T(1,128)S(1)}, s32[3,256]{1,0:T(4,128)S(1)}) custom-call(s32[1]{0:T(128)S(6)} %copy.13.count_ref, s32[1,96]{1,0:T(1,128)} %refs_0_.1, s32[1,96]{1,0:T(1,128)} %refs_1_.1, s32[1,96]{1,0:T(1,128)} %refs_2_, s32[1,32]{1,0:T(1,128)} %bitcast.8, s32[1,8]{1,0:T(1,128)} %refs_4_.1, s32[1,4]{1,0:T(1,128)} %bitcast.9), custom_call_target="tpu_custom_call" | custom-call | bytes 4096 | tf_op jit(solution)/shard_map/pack_lists/pallas_call | solution.py:113
  5.7 2.0 %collective-permute-start = (s32[3,1,96]{2,1,0:T(1,128)S(1)}, s32[3,1,96]{2,1,0:T(1,128)S(1)}, u32[]{:S(2)}, u32[]{:S(2)}) collective-permute-start(s32[3,1,96]{2,1,0:T(1,128)S(1)} %get-tuple-element.44), channel_id=1, source_target_pairs={{0,1},{1,0},{2,3},{3,2},{4,5},{5,4},{6,7},{7,6},{8,9},{9,8},{10,11... | collective-permute-start | bytes 3464 | tf_op jit(solution)/shard_map/ppermute | solution.py:40
  7.8 2.1 %load_amplitudes.2.refs_0_ = bf16[2048,512]{1,0:T(8,128)(2,1)S(1)} custom-call(f32[32,64,512]{2,1,0:T(8,128)} %amp_hbm.3), custom_call_target="tpu_custom_call" | custom-call | bytes 4194304 | tf_op jit(solution)/shard_map/load_amplitudes/pallas_call | solution.py:148
  9.9 0.0 collective-permute-done
  10.0 1.6 %collective-permute-start.1 = (s32[3,2,96]{2,1,0:T(2,128)S(1)}, s32[3,2,96]{2,1,0:T(2,128)S(1)}, u32[]{:S(2)}, u32[]{:S(2)}) collective-permute-start(s32[3,2,96]{2,1,0:T(2,128)S(1)} %pad_add_fusion.2), channel_id=1, source_target_pairs={{0,2},{1,3},{2,0},{3,1},{4,6},{5,7},{6,4},{7,5},{8,10},{9,11},{10,... | collective-permute-start | bytes 6920 | tf_op jit(solution)/shard_map/ppermute | solution.py:40
  11.6 0.4 collective-permute-done.4.refs_6_
  12.0 2.0 %collective-permute-start.6 = (f32[144,512]{1,0:T(8,128)S(1)}, f32[144,512]{1,0:T(8,128)S(1)}, u32[]{:S(2)}, u32[]{:S(2)}) collective-permute-start(f32[144,512]{1,0:T(8,128)S(1)} %collective-permute-done.4.refs_6_), channel_id=1, source_target_pairs={{0,1},{1,0},{2,3},{3,2},{4,5},{5,4},{6,7},{7,6},{8,9},{9,8},{10,11... | collective-permute-start | bytes 884744 | tf_op jit(solution)/shard_map/ppermute | solution.py:40
  14.0 0.0 collective-permute-done.1
  14.0 0.0 copy-start
  14.0 2.7 %collective-permute-start.2 = (s32[3,4,96]{2,1,0:T(4,128)S(1)}, s32[3,4,96]{2,1,0:T(4,128)S(1)}, u32[]{:S(2)}, u32[]{:S(2)}) collective-permute-start(s32[3,4,96]{2,1,0:T(4,128)S(1)} %pad_add_fusion.1), channel_id=1, source_target_pairs={{0,4},{1,5},{2,6},{3,7},{4,0},{5,1},{6,2},{7,3},{8,12},{9,13},{10,... | collective-permute-start | bytes 13832 | tf_op jit(solution)/shard_map/ppermute | solution.py:40
  16.7 2.1 %load_amplitudes.3.refs_1_ = bf16[2048,512]{1,0:T(8,128)(2,1)S(1)} custom-call(f32[32,64,512]{2,1,0:T(8,128)} %amp_hbm.3), custom_call_target="tpu_custom_call" | custom-call | bytes 4194304 | tf_op jit(solution)/shard_map/load_amplitudes/pallas_call | solution.py:148
  18.8 0.0 collective-permute-done.2
  18.8 0.0 collective-permute-done.3.pair_ref
  18.8 3.0 %sums.1 = (bf16[256,2048]{1,0:T(8,128)(2,1)S(1)}, bf16[256,2048]{1,0:T(8,128)(2,1)S(1)}, bf16[256,2048]{1,0:T(8,128)(2,1)S(1)}, bf16[256,2048]{1,0:T(8,128)(2,1)...) custom-call(s32[3,8,96]{2,1,0:T(8,128)S(1)} %pad_add_fusion.lists_ref, s32[3,256]{1,0:T(4,128)S(1)} %get-tuple-element.47.table_ref, ...), custom_call_target="tpu_custom_call" | custom-call | bytes 16777216 | tf_op jit(solution)/shard_map/sums/pallas_call | solution.py:263
  21.9 0.1 collective-permute-start.7
  22.0 0.0 collective-permute-done.5.refs_7_.x
  22.0 0.5 %collective-permute-start.9 = (f32[112,512]{1,0:T(8,128)S(1)}, f32[112,512]{1,0:T(8,128)S(1)}, u32[]{:S(2)}, u32[]{:S(2)}) collective-permute-start(f32[112,512]{1,0:T(8,128)S(1)} %get-tuple-element.62), channel_id=1, source_target_pairs={{0,8},{8,0},{16,24},{24,16},{1,9},{9,1},{17,25},{25,17},{2,10},{10... | collective-permute-start | bytes 688136 | tf_op jit(solution)/shard_map/ppermute | solution.py:40
  22.6 0.1 collective-permute-start.8
  22.6 0.0 collective-permute-done.6.refs_8_.x
  22.7 0.5 %collective-permute-start.11 = (f32[72,512]{1,0:T(8,128)S(1)}, f32[72,512]{1,0:T(8,128)S(1)}, u32[]{:S(2)}, u32[]{:S(2)}) collective-permute-start(f32[72,512]{1,0:T(8,128)S(1)} %get-tuple-element.67), channel_id=1, source_target_pairs={{0,8},{8,0},{16,24},{24,16},{1,9},{9,1},{17,25},{25,17},{2,10},{10... | collective-permute-start | bytes 442376 | tf_op jit(solution)/shard_map/ppermute | solution.py:40
  23.2 0.1 collective-permute-start.10
  23.2 1.1 %fetched_products.1 = (f32[256,512]{1,0:T(8,128)S(1)}, f32[256,512]{1,0:T(8,128)S(1)}) custom-call(bf16[256,2048]{1,0:T(8,128)(2,1)S(1)} %get-tuple-element.50.refs_0_.hi, bf16[256,2048]{1,0:T(8,128)(2,1)S(1)} %get-tuple-element.51.refs_1_.lo, bf16[256,2048]{1,0:T(8,128)(2,1)S(1)} %get-tuple-element.48.refs_2_.hi, ...), custom_call_target="tpu_custom_call" | custom-call | flops 805306368 | tf_op jit(solution)/shard_map/fetched_products/pallas_call | solution.py:312
  24.4 0.0 collective-permute-done.11.rest_4_
  24.4 0.2 collective-permute-done.10.rest_3_
  24.6 0.0 collective-permute-done.9.rest_2_
  24.6 0.0 collective-permute-done.8.rest_1_
  24.6 0.0 collective-permute-done.7.rest_0_
  24.6 0.7 %away_products.1 = (f32[1,64,512]{2,1,0:T(8,128)S(1)}, f32[1,64,512]{2,1,0:T(8,128)S(1)}, f32[1,64,512]{2,1,0:T(8,128)S(1)}, f32[1,64,512]{2,1,0:T(8,128)S(1)}, ...) custom-call(bf16[256,2048]{1,0:T(8,128)(2,1)S(1)} %get-tuple-element.50.refs_0_.hi, ...), custom_call_target="tpu_custom_call" | custom-call | flops 402653184 | tf_op jit(solution)/shard_map/away_products/pallas_call | solution.py:343
  25.3 1.3 %collective-permute-start.12 = (f32[1,64,512]{2,1,0:T(8,128)S(1)}, f32[1,64,512]{2,1,0:T(8,128)S(1)}, u32[]{:S(2)}, u32[]{:S(2)}) collective-permute-start(f32[1,64,512]{2,1,0:T(8,128)S(1)} %get-tuple-element.72), channel_id=1, source_target_pairs={{0,1},{1,0},{2,3},{3,2},{4,5},{5,4},{6,7},{7,6},{8,9},{9,8},{10,11... | collective-permute-start | bytes 393224 | tf_op jit(solution)/shard_map/ppermute | solution.py:40
  26.6 0.8 %collective-permute-start.14 = (f32[1,64,512]{2,1,0:T(8,128)S(1)}, f32[1,64,512]{2,1,0:T(8,128)S(1)}, u32[]{:S(2)}, u32[]{:S(2)}) collective-permute-start(f32[1,64,512]{2,1,0:T(8,128)S(1)} %get-tuple-element.74), channel_id=1, source_target_pairs={{0,1},{1,0},{2,3},{3,2},{4,5},{5,4},{6,7},{7,6},{8,9},{9,8},{10,11... | collective-permute-start | bytes 393224 | tf_op jit(solution)/shard_map/ppermute | solution.py:40
  27.4 0.6 %side_products.1 = (f32[1,64,512]{2,1,0:T(8,128)S(1)}, f32[1,64,512]{2,1,0:T(8,128)S(1)}, f32[1,64,512]{2,1,0:T(8,128)S(1)}, f32[1,64,512]{2,1,0:T(8,128)S(1)}) custom-call(bf16[256,2048]{1,0:T(8,128)(2,1)S(1)} %get-tuple-element.48.refs_2_.hi, bf16[256,2048]{1,0:T(8,128)(2,1)S(1)} %get-tuple-element.49.refs_3_.lo, ...), custom_call_target="tpu_custom_call" | custom-call | tf_op jit(solution)/shard_map/side_products/pallas_call | solution.py:359
  28.0 1.6 %collective-permute-start.17 = (f32[1,64,512]{2,1,0:T(8,128)S(1)}, f32[1,64,512]{2,1,0:T(8,128)S(1)}, u32[]{:S(2)}, u32[]{:S(2)}) collective-permute-start(f32[1,64,512]{2,1,0:T(8,128)S(1)} %get-tuple-element.78), channel_id=1, source_target_pairs={{0,2},{1,3},{2,0},{3,1},{4,6},{5,7},{6,4},{7,5},{8,10},{9,11},{10,... | collective-permute-start | bytes 393224 | tf_op jit(solution)/shard_map/ppermute | solution.py:40
  29.7 0.4 collective-permute-start.16
  30.1 1.6 %collective-permute-done.12 = f32[1,64,512]{2,1,0:T(8,128)S(1)} collective-permute-done((f32[1,64,512]{2,1,0:T(8,128)S(1)}, f32[1,64,512]{2,1,0:T(8,128)S(1)}, u32[]{:S(2)}, u32[]{:S(2)}) %collective-permute-start.12) | collective-permute-done | bytes 131104 | tf_op jit(solution)/shard_map/ppermute | solution.py:40
  31.8 2.4 %collective-permute-start.13 = (f32[1,64,512]{2,1,0:T(8,128)S(1)}, f32[1,64,512]{2,1,0:T(8,128)S(1)}, u32[]{:S(2)}, u32[]{:S(2)}) collective-permute-start(f32[1,64,512]{2,1,0:T(8,128)S(1)} %add.46), channel_id=1, source_target_pairs={{0,4},{1,5},{2,6},{3,7},{4,0},{5,1},{6,2},{7,3},{8,12},{9,13},{10,... | collective-permute-start | bytes 393224 | tf_op jit(solution)/shard_map/ppermute | solution.py:40
  34.2 0.0 collective-permute-done.14
  34.2 3.1 %collective-permute-start.15 = (f32[1,64,512]{2,1,0:T(8,128)S(1)}, f32[1,64,512]{2,1,0:T(8,128)S(1)}, u32[]{:S(2)}, u32[]{:S(2)}) collective-permute-start(f32[1,64,512]{2,1,0:T(8,128)S(1)} %add.48), channel_id=1, source_target_pairs={{0,6},{1,7},{2,4},{3,5},{4,2},{5,3},{6,0},{7,1},{8,14},{9,15},{10,... | collective-permute-start | bytes 393224 | tf_op jit(solution)/shard_map/ppermute | solution.py:40
  37.3 0.0 collective-permute-done.17
  37.3 1.4 %collective-permute-start.18 = (f32[1,64,512]{2,1,0:T(8,128)S(1)}, f32[1,64,512]{2,1,0:T(8,128)S(1)}, u32[]{:S(2)}, u32[]{:S(2)}) collective-permute-start(f32[1,64,512]{2,1,0:T(8,128)S(1)} %add.51), channel_id=1, source_target_pairs={{0,1},{1,0},{2,3},{3,2},{4,5},{5,4},{6,7},{7,6},{8,9},{9,8},{10,11... | collective-permute-start | bytes 393224 | tf_op jit(solution)/shard_map/ppermute | solution.py:40
  38.8 0.0 collective-permute-done.16
  38.8 5.5 %collective-permute-done.13 = f32[1,64,512]{2,1,0:T(8,128)S(1)} collective-permute-done((f32[1,64,512]{2,1,0:T(8,128)S(1)}, f32[1,64,512]{2,1,0:T(8,128)S(1)}, u32[]{:S(2)}, u32[]{:S(2)}) %collective-permute-start.13) | collective-permute-done | bytes 131104 | tf_op jit(solution)/shard_map/ppermute | solution.py:40
  44.3 0.0 collective-permute-done.15
  44.3 0.0 collective-permute-done.18
  44.4 0.8 %add_divide_fusion = f32[1,64,512]{2,1,0:T(8,128)} fusion(f32[1,64,512]{2,1,0:T(8,128)S(1)} %collective-permute-done.18, f32[1,64,512]{2,1,0:T(8,128)S(1)} %collective-permute-done.16, f32[1,64,512]{2,1,0:T(8,128)S(1)} %collective-permute-done.15, f32[1,64,512]{2,1,0:T(8,128)S(1)} %collective-permute-done.13, f32[1,64,512]{2,1,0:T(8,128)S(1)} %copy-done.1, ...), kind=kLoop, calls=%fused_computation | loop fusion | flops 229376 | bytes 919808 | tf_op jit(solution)/shard_map/div | solution.py:448
  (15 shorter events, 0.2 us)
Async XLA Ops:
  0.0 18.8 %collective-permute-start.3 = (f32[512,512]{1,0:T(8,128)}, f32[512,512]{1,0:T(8,128)S(1)}, u32[]{:S(2)}, u32[]{:S(2)}) collective-permute-start(f32[512,512]{1,0:T(8,128)} %bitcast.4), channel_id=1, source_target_pairs={{0,8},{8,0},{16,24},{24,16},{1,9},{9,1},{17,25},{25,17},{2,10},{10... | collective-permute-start | bytes 3145736 | tf_op jit(solution)/shard_map/ppermute | solution.py:40
  1.6 10.4 %collective-permute-start.4 = (f32[144,512]{1,0:T(8,128)S(1)}, f32[144,512]{1,0:T(8,128)S(1)}, u32[]{:S(2)}, u32[]{:S(2)}) collective-permute-start(f32[144,512]{1,0:T(8,128)S(1)} %get-tuple-element.42), channel_id=1, source_target_pairs={{0,16},{8,24},{16,0},{24,8},{1,17},{9,25},{17,1},{25,9},{2,18},{10... | collective-permute-start | bytes 884744 | tf_op jit(solution)/shard_map/ppermute | solution.py:40
  4.1 17.8 %collective-permute-start.5 = (f32[224,512]{1,0:T(8,128)S(1)}, f32[224,512]{1,0:T(8,128)S(1)}, u32[]{:S(2)}, u32[]{:S(2)}) collective-permute-start(f32[224,512]{1,0:T(8,128)S(1)} %get-tuple-element.54), channel_id=1, source_target_pairs={{0,16},{8,24},{16,0},{24,8},{1,17},{9,25},{17,1},{25,9},{2,18},{10... | collective-permute-start | bytes 1376264 | tf_op jit(solution)/shard_map/ppermute | solution.py:40
  5.7 4.2 %collective-permute-start = (s32[3,1,96]{2,1,0:T(1,128)S(1)}, s32[3,1,96]{2,1,0:T(1,128)S(1)}, u32[]{:S(2)}, u32[]{:S(2)}) collective-permute-start(s32[3,1,96]{2,1,0:T(1,128)S(1)} %get-tuple-element.44), channel_id=1, source_target_pairs={{0,1},{1,0},{2,3},{3,2},{4,5},{5,4},{6,7},{7,6},{8,9},{9,8},{10,11... | collective-permute-start | bytes 3464 | tf_op jit(solution)/shard_map/ppermute | solution.py:40
  10.0 4.0 %collective-permute-start.1 = (s32[3,2,96]{2,1,0:T(2,128)S(1)}, s32[3,2,96]{2,1,0:T(2,128)S(1)}, u32[]{:S(2)}, u32[]{:S(2)}) collective-permute-start(s32[3,2,96]{2,1,0:T(2,128)S(1)} %pad_add_fusion.2), channel_id=1, source_target_pairs={{0,2},{1,3},{2,0},{3,1},{4,6},{5,7},{6,4},{7,5},{8,10},{9,11},{10,... | collective-permute-start | bytes 6920 | tf_op jit(solution)/shard_map/ppermute | solution.py:40
  12.0 10.6 %collective-permute-start.6 = (f32[144,512]{1,0:T(8,128)S(1)}, f32[144,512]{1,0:T(8,128)S(1)}, u32[]{:S(2)}, u32[]{:S(2)}) collective-permute-start(f32[144,512]{1,0:T(8,128)S(1)} %collective-permute-done.4.refs_6_), channel_id=1, source_target_pairs={{0,1},{1,0},{2,3},{3,2},{4,5},{5,4},{6,7},{7,6},{8,9},{9,8},{10,11... | collective-permute-start | bytes 884744 | tf_op jit(solution)/shard_map/ppermute | solution.py:40
  14.0 4.8 %copy-start = (f32[1,512,512]{2,1,0:T(8,128)S(1)}, f32[1,512,512]{2,1,0:T(8,128)}, u32[]{:S(2)}) copy-start(f32[1,512,512]{2,1,0:T(8,128)} %param.13) | copy-start | bytes 3145732
  14.0 4.8 %collective-permute-start.2 = (s32[3,4,96]{2,1,0:T(4,128)S(1)}, s32[3,4,96]{2,1,0:T(4,128)S(1)}, u32[]{:S(2)}, u32[]{:S(2)}) collective-permute-start(s32[3,4,96]{2,1,0:T(4,128)S(1)} %pad_add_fusion.1), channel_id=1, source_target_pairs={{0,4},{1,5},{2,6},{3,7},{4,0},{5,1},{6,2},{7,3},{8,12},{9,13},{10,... | collective-permute-start | bytes 13832 | tf_op jit(solution)/shard_map/ppermute | solution.py:40
  21.9 2.7 %collective-permute-start.7 = (f32[144,512]{1,0:T(8,128)S(1)}, f32[144,512]{1,0:T(8,128)S(1)}, u32[]{:S(2)}, u32[]{:S(2)}) collective-permute-start(f32[144,512]{1,0:T(8,128)S(1)} %collective-permute-done.4.refs_6_), channel_id=1, source_target_pairs={{0,8},{8,0},{16,24},{24,16},{1,9},{9,1},{17,25},{25,17},{2,10},{10... | collective-permute-start | bytes 884744 | tf_op jit(solution)/shard_map/ppermute | solution.py:40
  22.0 2.6 %collective-permute-start.9 = (f32[112,512]{1,0:T(8,128)S(1)}, f32[112,512]{1,0:T(8,128)S(1)}, u32[]{:S(2)}, u32[]{:S(2)}) collective-permute-start(f32[112,512]{1,0:T(8,128)S(1)} %get-tuple-element.62), channel_id=1, source_target_pairs={{0,8},{8,0},{16,24},{24,16},{1,9},{9,1},{17,25},{25,17},{2,10},{10... | collective-permute-start | bytes 688136 | tf_op jit(solution)/shard_map/ppermute | solution.py:40
  22.6 2.1 %collective-permute-start.8 = (f32[112,512]{1,0:T(8,128)S(1)}, f32[112,512]{1,0:T(8,128)S(1)}, u32[]{:S(2)}, u32[]{:S(2)}) collective-permute-start(f32[112,512]{1,0:T(8,128)S(1)} %get-tuple-element.60), channel_id=1, source_target_pairs={{0,8},{8,0},{16,24},{24,16},{1,9},{9,1},{17,25},{25,17},{2,10},{10... | collective-permute-start | bytes 688136 | tf_op jit(solution)/shard_map/ppermute | solution.py:40
  22.7 1.7 %collective-permute-start.11 = (f32[72,512]{1,0:T(8,128)S(1)}, f32[72,512]{1,0:T(8,128)S(1)}, u32[]{:S(2)}, u32[]{:S(2)}) collective-permute-start(f32[72,512]{1,0:T(8,128)S(1)} %get-tuple-element.67), channel_id=1, source_target_pairs={{0,8},{8,0},{16,24},{24,16},{1,9},{9,1},{17,25},{25,17},{2,10},{10... | collective-permute-start | bytes 442376 | tf_op jit(solution)/shard_map/ppermute | solution.py:40
  23.2 1.4 %collective-permute-start.10 = (f32[72,512]{1,0:T(8,128)S(1)}, f32[72,512]{1,0:T(8,128)S(1)}, u32[]{:S(2)}, u32[]{:S(2)}) collective-permute-start(f32[72,512]{1,0:T(8,128)S(1)} %get-tuple-element.65), channel_id=1, source_target_pairs={{0,8},{8,0},{16,24},{24,16},{1,9},{9,1},{17,25},{25,17},{2,10},{10... | collective-permute-start | bytes 442376 | tf_op jit(solution)/shard_map/ppermute | solution.py:40
  25.3 6.4 %collective-permute-start.12 = (f32[1,64,512]{2,1,0:T(8,128)S(1)}, f32[1,64,512]{2,1,0:T(8,128)S(1)}, u32[]{:S(2)}, u32[]{:S(2)}) collective-permute-start(f32[1,64,512]{2,1,0:T(8,128)S(1)} %get-tuple-element.72), channel_id=1, source_target_pairs={{0,1},{1,0},{2,3},{3,2},{4,5},{5,4},{6,7},{7,6},{8,9},{9,8},{10,11... | collective-permute-start | bytes 393224 | tf_op jit(solution)/shard_map/ppermute | solution.py:40
  26.6 7.6 %collective-permute-start.14 = (f32[1,64,512]{2,1,0:T(8,128)S(1)}, f32[1,64,512]{2,1,0:T(8,128)S(1)}, u32[]{:S(2)}, u32[]{:S(2)}) collective-permute-start(f32[1,64,512]{2,1,0:T(8,128)S(1)} %get-tuple-element.74), channel_id=1, source_target_pairs={{0,1},{1,0},{2,3},{3,2},{4,5},{5,4},{6,7},{7,6},{8,9},{9,8},{10,11... | collective-permute-start | bytes 393224 | tf_op jit(solution)/shard_map/ppermute | solution.py:40
  27.4 16.9 %copy-start.1 = (f32[1,64,512]{2,1,0:T(8,128)S(1)}, f32[1,64,512]{2,1,0:T(8,128)}, u32[]{:S(2)}) copy-start(f32[1,64,512]{2,1,0:T(8,128)} %param.14) | copy-start | bytes 393220
  27.4 16.9 %copy-start.2 = (f32[512]{0:T(512)S(1)}, f32[512]{0:T(512)}, u32[]{:S(2)}) copy-start(f32[512]{0:T(512)} %param.16) | copy-start | bytes 6148
  27.4 16.9 %copy-start.3 = (f32[1,64]{1,0:T(1,128)S(1)}, f32[1,64]{1,0:T(1,128)}, u32[]{:S(2)}) copy-start(f32[1,64]{1,0:T(1,128)} %param.15) | copy-start | bytes 772
  28.0 9.3 %collective-permute-start.17 = (f32[1,64,512]{2,1,0:T(8,128)S(1)}, f32[1,64,512]{2,1,0:T(8,128)S(1)}, u32[]{:S(2)}, u32[]{:S(2)}) collective-permute-start(f32[1,64,512]{2,1,0:T(8,128)S(1)} %get-tuple-element.78), channel_id=1, source_target_pairs={{0,2},{1,3},{2,0},{3,1},{4,6},{5,7},{6,4},{7,5},{8,10},{9,11},{10,... | collective-permute-start | bytes 393224 | tf_op jit(solution)/shard_map/ppermute | solution.py:40
  29.7 9.1 %collective-permute-start.16 = (f32[1,64,512]{2,1,0:T(8,128)S(1)}, f32[1,64,512]{2,1,0:T(8,128)S(1)}, u32[]{:S(2)}, u32[]{:S(2)}) collective-permute-start(f32[1,64,512]{2,1,0:T(8,128)S(1)} %get-tuple-element.75), channel_id=1, source_target_pairs={{0,2},{1,3},{2,0},{3,1},{4,6},{5,7},{6,4},{7,5},{8,10},{9,11},{10,... | collective-permute-start | bytes 393224 | tf_op jit(solution)/shard_map/ppermute | solution.py:40
  31.8 12.6 %collective-permute-start.13 = (f32[1,64,512]{2,1,0:T(8,128)S(1)}, f32[1,64,512]{2,1,0:T(8,128)S(1)}, u32[]{:S(2)}, u32[]{:S(2)}) collective-permute-start(f32[1,64,512]{2,1,0:T(8,128)S(1)} %add.46), channel_id=1, source_target_pairs={{0,4},{1,5},{2,6},{3,7},{4,0},{5,1},{6,2},{7,3},{8,12},{9,13},{10,... | collective-permute-start | bytes 393224 | tf_op jit(solution)/shard_map/ppermute | solution.py:40
  34.2 10.1 %collective-permute-start.15 = (f32[1,64,512]{2,1,0:T(8,128)S(1)}, f32[1,64,512]{2,1,0:T(8,128)S(1)}, u32[]{:S(2)}, u32[]{:S(2)}) collective-permute-start(f32[1,64,512]{2,1,0:T(8,128)S(1)} %add.48), channel_id=1, source_target_pairs={{0,6},{1,7},{2,4},{3,5},{4,2},{5,3},{6,0},{7,1},{8,14},{9,15},{10,... | collective-permute-start | bytes 393224 | tf_op jit(solution)/shard_map/ppermute | solution.py:40
  37.3 7.0 %collective-permute-start.18 = (f32[1,64,512]{2,1,0:T(8,128)S(1)}, f32[1,64,512]{2,1,0:T(8,128)S(1)}, u32[]{:S(2)}, u32[]{:S(2)}) collective-permute-start(f32[1,64,512]{2,1,0:T(8,128)S(1)} %add.51), channel_id=1, source_target_pairs={{0,1},{1,0},{2,3},{3,2},{4,5},{5,4},{6,7},{7,6},{8,9},{9,8},{10,11... | collective-permute-start | bytes 393224 | tf_op jit(solution)/shard_map/ppermute | solution.py:40

commit v9 on v7

--- a/solution.py
+++ b/solution.py
@@ -392,12 +392,11 @@
     )
     pair = swap(own, "grp", 1)
     rows = [load(amplitudes, i * tile_rows // 2, tile_rows // 2) for i in range(2)]
-    k = 1
-    while k < lanes:
-        if k == 2:
+    order = [1] + [1 << b for b in range(lanes.bit_length() - 2, 0, -1)]
+    for k in order:
+        if k == order[1]:
             lists = after(lists, rows[0])
         lists = jnp.concatenate([lists, swap(lists, "wide", k)], axis=1)
-        k *= 2
     lists = after(lists, rows[1])
     *held, local_away, local_hi, local_lo = sums(
         lists, table, own, pair, rows, amp_dev, tile_rows, lanes, grps
@@ -413,14 +412,14 @@
     _, offsets = tile_order(lanes)
     far, near, last = range(lanes // 4), range(lanes // 4, half - 1), half - 1
     side = side_products(*held[2:], local[1], in_hi, in_lo, half, own.shape[0])
-    got = [swap(away[j], "wide", 1) for j in far]
+    got = [swap(after(away[j], side[0]) if j else away[j], "wide", 1) for j in far]
     summed = base_residual + side[last]
     for j in far:
         summed = summed + swap(side[j] + got[j], "wide", offsets[j])
     rest = away[last]
     for j in near:
         summed = summed + swap(side[j], "wide", offsets[j])
-        rest = rest + swap(after(away[j], side[0]), "wide", offsets[j])
+        rest = rest + swap(away[j], "wide", offsets[j])
     summed = summed + swap(rest, "wide", 1)
     divisor = occ_gap[:, :, None] + virt_sum[None, None, :]
     return summed / divisor

time: 45 us -> 45 us (level)
  starting transfers between devices: 23.7 us -> 23.2 us
    ppermute x17, starting transfers between devices: 23.7 us -> 23.2 us  [swap(): return lax.ppermute(x, axis, [(i, i ^ k) for i in range(n)])]
  transfers between devices with their start and end apart: 17 -> 17, of which waited for: 5 -> 6; matrix products, arithmetic and copies ran while one was open for 0% -> 0% of each run, Pallas kernels for 25% -> 25%
where the time goes in v9:
time: 45 us; the launch traced here: 44.4 us
  starting transfers between devices  23.2 us (52%)
  Pallas kernels  11.7 us (26%)
  waiting for transfers between devices  7.93 us (18%)
  other arithmetic  0.84 us (2%)
  between operations  0.81 us (2%)
    ppermute x17, starting transfers between devices, swap(): return lax.ppermute(x, axis, [(i, i ^ k) for i in range(n)])  23.2 us
    ppermute x17, waiting for transfers between devices, swap(): return lax.ppermute(x, axis, [(i, i ^ k) for i in range(n)])  7.93 us
    pallas_call x2, Pallas kernels, load(): pl.pallas_call(functools.partial(load_kernel, first), out_shape=pltpu.VME...  4.26 us
    pallas_call x1, Pallas kernels, sums(): pl.pallas_call(functools.partial(sums_kernel, lanes, blocks, amp_dev), ou...  2.28 us
    pallas_call x1, Pallas kernels, fetched_products(): pl.pallas_call(fetched_kernel, out_shape=[pltpu.VMEM((rows, window), jnp....  1.81 us
    pallas_call x1, Pallas kernels, pieces(): pl.pallas_call(pieces_kernel, out_shape=[pltpu.VMEM((n, own.shape[1]), ow...  1.12 us
  transfers between devices with their start and end apart: 17, of which 6 were waited for; matrix products, arithmetic and copies ran while one was open for 0% of the time, Pallas kernels for 25%

profile of v9, /device:TPU:0, one launch (start us, length us, event | category | flops | bytes accessed | tf_op | source)
XLA Modules:
  0.0 44.4 jit_solution(12647620511189786455)
XLA Ops:
  0.0 0.5 %collective-permute-start.3 = (f32[512,512]{1,0:T(8,128)}, f32[512,512]{1,0:T(8,128)S(1)}, u32[]{:S(2)}, u32[]{:S(2)}) collective-permute-start(f32[512,512]{1,0:T(8,128)} %bitcast.4), channel_id=1, source_target_pairs={{0,8},{8,0},{16,24},{24,16},{1,9},{9,1},{17,25},{25,17},{2,10},{10... | collective-permute-start | bytes 3145736 | tf_op jit(solution)/shard_map/ppermute | solution.py:40
  0.5 1.1 %pieces.1 = (f32[144,512]{1,0:T(8,128)S(1)}, f32[224,512]{1,0:T(8,128)S(1)}) custom-call(f32[512,512]{1,0:T(8,128)} %bitcast.5), custom_call_target="tpu_custom_call" | custom-call | bytes 1048576 | tf_op jit(solution)/shard_map/pieces/pallas_call | solution.py:78
  1.6 2.6 %collective-permute-start.4 = (f32[144,512]{1,0:T(8,128)S(1)}, f32[144,512]{1,0:T(8,128)S(1)}, u32[]{:S(2)}, u32[]{:S(2)}) collective-permute-start(f32[144,512]{1,0:T(8,128)S(1)} %get-tuple-element.35), channel_id=1, source_target_pairs={{0,16},{8,24},{16,0},{24,8},{1,17},{9,25},{17,1},{25,9},{2,18},{10... | collective-permute-start | bytes 884744 | tf_op jit(solution)/shard_map/ppermute | solution.py:40
  4.1 0.1 collective-permute-start.5
  4.9 0.9 %pack_lists.1 = (s32[3,1,96]{2,1,0:T(1,128)S(1)}, s32[3,256]{1,0:T(4,128)S(1)}) custom-call(s32[1]{0:T(128)S(6)} %copy.13.count_ref, s32[1,96]{1,0:T(1,128)} %refs_0_.1, s32[1,96]{1,0:T(1,128)} %refs_1_.1, s32[1,96]{1,0:T(1,128)} %refs_2_, s32[1,32]{1,0:T(1,128)} %bitcast.8, s32[1,8]{1,0:T(1,128)} %refs_4_.1, s32[1,4]{1,0:T(1,128)} %bitcast.9), custom_call_target="tpu_custom_call" | custom-call | bytes 4096 | tf_op jit(solution)/shard_map/pack_lists/pallas_call | solution.py:113
  5.7 2.0 %collective-permute-start = (s32[3,1,96]{2,1,0:T(1,128)S(1)}, s32[3,1,96]{2,1,0:T(1,128)S(1)}, u32[]{:S(2)}, u32[]{:S(2)}) collective-permute-start(s32[3,1,96]{2,1,0:T(1,128)S(1)} %get-tuple-element.37), channel_id=1, source_target_pairs={{0,1},{1,0},{2,3},{3,2},{4,5},{5,4},{6,7},{7,6},{8,9},{9,8},{10,11... | collective-permute-start | bytes 3464 | tf_op jit(solution)/shard_map/ppermute | solution.py:40
  7.8 2.1 %load_amplitudes.2.refs_0_ = bf16[2048,512]{1,0:T(8,128)(2,1)S(1)} custom-call(f32[32,64,512]{2,1,0:T(8,128)} %amp_hbm.3), custom_call_target="tpu_custom_call" | custom-call | bytes 4194304 | tf_op jit(solution)/shard_map/load_amplitudes/pallas_call | solution.py:148
  9.9 0.0 collective-permute-done
  10.0 2.7 %collective-permute-start.1 = (s32[3,2,96]{2,1,0:T(2,128)S(1)}, s32[3,2,96]{2,1,0:T(2,128)S(1)}, u32[]{:S(2)}, u32[]{:S(2)}) collective-permute-start(s32[3,2,96]{2,1,0:T(2,128)S(1)} %pad_add_fusion.2), channel_id=1, source_target_pairs={{0,4},{1,5},{2,6},{3,7},{4,0},{5,1},{6,2},{7,3},{8,12},{9,13},{10,... | collective-permute-start | bytes 6920 | tf_op jit(solution)/shard_map/ppermute | solution.py:40
  12.6 0.0 collective-permute-done.4.refs_7_
  12.6 1.4 %collective-permute-start.6 = (f32[144,512]{1,0:T(8,128)S(1)}, f32[144,512]{1,0:T(8,128)S(1)}, u32[]{:S(2)}, u32[]{:S(2)}) collective-permute-start(f32[144,512]{1,0:T(8,128)S(1)} %collective-permute-done.4.refs_7_), channel_id=1, source_target_pairs={{0,1},{1,0},{2,3},{3,2},{4,5},{5,4},{6,7},{7,6},{8,9},{9,8},{10,11... | collective-permute-start | bytes 884744 | tf_op jit(solution)/shard_map/ppermute | solution.py:40
  14.0 0.5 %collective-permute-done.1 = s32[3,2,96]{2,1,0:T(2,128)S(1)} collective-permute-done((s32[3,2,96]{2,1,0:T(2,128)S(1)}, s32[3,2,96]{2,1,0:T(2,128)S(1)}, u32[]{:S(2)}, u32[]{:S(2)}) %collective-permute-start.1) | collective-permute-done | bytes 2336 | tf_op jit(solution)/shard_map/ppermute | solution.py:40
  14.5 0.0 copy-start
  14.5 1.6 %collective-permute-start.2 = (s32[3,4,96]{2,1,0:T(4,128)S(1)}, s32[3,4,96]{2,1,0:T(4,128)S(1)}, u32[]{:S(2)}, u32[]{:S(2)}) collective-permute-start(s32[3,4,96]{2,1,0:T(4,128)S(1)} %pad_add_fusion.1), channel_id=1, source_target_pairs={{0,2},{1,3},{2,0},{3,1},{4,6},{5,7},{6,4},{7,5},{8,10},{9,11},{10,... | collective-permute-start | bytes 13832 | tf_op jit(solution)/shard_map/ppermute | solution.py:40
  16.2 2.1 %load_amplitudes.3.refs_1_ = bf16[2048,512]{1,0:T(8,128)(2,1)S(1)} custom-call(f32[32,64,512]{2,1,0:T(8,128)} %amp_hbm.3), custom_call_target="tpu_custom_call" | custom-call | bytes 4194304 | tf_op jit(solution)/shard_map/load_amplitudes/pallas_call | solution.py:148
  18.3 0.0 collective-permute-done.2
  18.4 0.0 collective-permute-done.3.pair_ref
  18.4 0.0 copy-done
  18.4 2.3 %sums.1 = (bf16[256,2048]{1,0:T(8,128)(2,1)S(1)}, bf16[256,2048]{1,0:T(8,128)(2,1)S(1)}, bf16[256,2048]{1,0:T(8,128)(2,1)S(1)}, bf16[256,2048]{1,0:T(8,128)(2,1)...) custom-call(s32[3,8,96]{2,1,0:T(8,128)S(1)} %pad_add_fusion.lists_ref, ...), custom_call_target="tpu_custom_call" | custom-call | bytes 16777216 | tf_op jit(solution)/shard_map/sums/pallas_call | solution.py:262
  20.6 1.0 %collective-permute-done.5.refs_8_ = f32[224,512]{1,0:T(8,128)S(1)} collective-permute-done((f32[224,512]{1,0:T(8,128)S(1)}, f32[224,512]{1,0:T(8,128)S(1)}, u32[]{:S(2)}, u32[]{:S(2)}) %collective-permute-start.5) | collective-permute-done | bytes 458784 | tf_op jit(solution)/shard_map/ppermute | solution.py:40
  21.7 0.0 collective-permute-start.8
  21.7 0.5 %collective-permute-start.7 = (f32[144,512]{1,0:T(8,128)S(1)}, f32[144,512]{1,0:T(8,128)S(1)}, u32[]{:S(2)}, u32[]{:S(2)}) collective-permute-start(f32[144,512]{1,0:T(8,128)S(1)} %collective-permute-done.4.refs_7_), channel_id=1, source_target_pairs={{0,8},{8,0},{16,24},{24,16},{1,9},{9,1},{17,25},{25,17},{2,10},{10... | collective-permute-start | bytes 884744 | tf_op jit(solution)/shard_map/ppermute | solution.py:40
  22.2 0.0 collective-permute-done.6.refs_9_
  22.2 0.0 collective-permute-start.9
  22.2 1.8 %fetched_products.1 = (f32[256,512]{1,0:T(8,128)S(1)}, f32[256,512]{1,0:T(8,128)S(1)}) custom-call(bf16[256,2048]{1,0:T(8,128)(2,1)S(1)} %get-tuple-element.43.refs_0_.hi, bf16[256,2048]{1,0:T(8,128)(2,1)S(1)} %get-tuple-element.44.refs_1_.lo, bf16[256,2048]{1,0:T(8,128)(2,1)S(1)} %get-tuple-element.41.refs_2_.hi, ...), custom_call_target="tpu_custom_call" | custom-call | flops 805306368 | tf_op jit(solution)/shard_map/fetched_products/pallas_call | solution.py:310
  24.0 0.0 collective-permute-done.7.rest_0_
  24.0 0.3 collective-permute-done.9.rest_2_
  24.3 0.0 collective-permute-done.8.rest_1_
  24.3 0.7 %away_products.1 = (f32[1,64,512]{2,1,0:T(8,128)S(1)}, f32[1,64,512]{2,1,0:T(8,128)S(1)}, f32[1,64,512]{2,1,0:T(8,128)S(1)}, f32[1,64,512]{2,1,0:T(8,128)S(1)}, ...) custom-call(bf16[256,2048]{1,0:T(8,128)(2,1)S(1)} %get-tuple-element.43.refs_0_.hi, ...), custom_call_target="tpu_custom_call" | custom-call | flops 402653184 | tf_op jit(solution)/shard_map/away_products/pallas_call | solution.py:341
  25.0 1.8 %collective-permute-start.10 = (f32[1,64,512]{2,1,0:T(8,128)S(1)}, f32[1,64,512]{2,1,0:T(8,128)S(1)}, u32[]{:S(2)}, u32[]{:S(2)}) collective-permute-start(f32[1,64,512]{2,1,0:T(8,128)S(1)} %get-tuple-element.58), channel_id=1, source_target_pairs={{0,1},{1,0},{2,3},{3,2},{4,5},{5,4},{6,7},{7,6},{8,9},{9,8},{10,11... | collective-permute-start | bytes 393224 | tf_op jit(solution)/shard_map/ppermute | solution.py:40
  26.9 0.6 %side_products.1 = (f32[1,64,512]{2,1,0:T(8,128)S(1)}, f32[1,64,512]{2,1,0:T(8,128)S(1)}, f32[1,64,512]{2,1,0:T(8,128)S(1)}, f32[1,64,512]{2,1,0:T(8,128)S(1)}) custom-call(bf16[256,2048]{1,0:T(8,128)(2,1)S(1)} %get-tuple-element.41.refs_2_.hi, bf16[256,2048]{1,0:T(8,128)(2,1)S(1)} %get-tuple-element.42.refs_3_.lo, ...), custom_call_target="tpu_custom_call" | custom-call | tf_op jit(solution)/shard_map/side_products/pallas_call | solution.py:357
  27.5 0.3 collective-permute-start.12
  27.8 1.8 %collective-permute-start.15 = (f32[1,64,512]{2,1,0:T(8,128)S(1)}, f32[1,64,512]{2,1,0:T(8,128)S(1)}, u32[]{:S(2)}, u32[]{:S(2)}) collective-permute-start(f32[1,64,512]{2,1,0:T(8,128)S(1)} %get-tuple-element.64), channel_id=1, source_target_pairs={{0,2},{1,3},{2,0},{3,1},{4,6},{5,7},{6,4},{7,5},{8,10},{9,11},{10,... | collective-permute-start | bytes 393224 | tf_op jit(solution)/shard_map/ppermute | solution.py:40
  29.6 0.2 collective-permute-start.14
  29.8 1.5 %collective-permute-done.10 = f32[1,64,512]{2,1,0:T(8,128)S(1)} collective-permute-done((f32[1,64,512]{2,1,0:T(8,128)S(1)}, f32[1,64,512]{2,1,0:T(8,128)S(1)}, u32[]{:S(2)}, u32[]{:S(2)}) %collective-permute-start.10) | collective-permute-done | bytes 131104 | tf_op jit(solution)/shard_map/ppermute | solution.py:40
  31.4 3.0 %collective-permute-start.11 = (f32[1,64,512]{2,1,0:T(8,128)S(1)}, f32[1,64,512]{2,1,0:T(8,128)S(1)}, u32[]{:S(2)}, u32[]{:S(2)}) collective-permute-start(f32[1,64,512]{2,1,0:T(8,128)S(1)} %add.46), channel_id=1, source_target_pairs={{0,4},{1,5},{2,6},{3,7},{4,0},{5,1},{6,2},{7,3},{8,12},{9,13},{10,... | collective-permute-start | bytes 393224 | tf_op jit(solution)/shard_map/ppermute | solution.py:40
  34.4 0.0 collective-permute-done.12
  34.4 3.1 %collective-permute-start.13 = (f32[1,64,512]{2,1,0:T(8,128)S(1)}, f32[1,64,512]{2,1,0:T(8,128)S(1)}, u32[]{:S(2)}, u32[]{:S(2)}) collective-permute-start(f32[1,64,512]{2,1,0:T(8,128)S(1)} %add.48), channel_id=1, source_target_pairs={{0,6},{1,7},{2,4},{3,5},{4,2},{5,3},{6,0},{7,1},{8,14},{9,15},{10,... | collective-permute-start | bytes 393224 | tf_op jit(solution)/shard_map/ppermute | solution.py:40
  37.5 0.0 collective-permute-done.15
  37.5 1.6 %collective-permute-start.16 = (f32[1,64,512]{2,1,0:T(8,128)S(1)}, f32[1,64,512]{2,1,0:T(8,128)S(1)}, u32[]{:S(2)}, u32[]{:S(2)}) collective-permute-start(f32[1,64,512]{2,1,0:T(8,128)S(1)} %add.51), channel_id=1, source_target_pairs={{0,1},{1,0},{2,3},{3,2},{4,5},{5,4},{6,7},{7,6},{8,9},{9,8},{10,11... | collective-permute-start | bytes 393224 | tf_op jit(solution)/shard_map/ppermute | solution.py:40
  39.1 0.0 collective-permute-done.14
  39.1 0.2 collective-permute-done.11
  39.3 4.4 %collective-permute-done.13 = f32[1,64,512]{2,1,0:T(8,128)S(1)} collective-permute-done((f32[1,64,512]{2,1,0:T(8,128)S(1)}, f32[1,64,512]{2,1,0:T(8,128)S(1)}, u32[]{:S(2)}, u32[]{:S(2)}) %collective-permute-start.13) | collective-permute-done | bytes 131104 | tf_op jit(solution)/shard_map/ppermute | solution.py:40
  43.7 0.0 collective-permute-done.16
  43.7 0.0 copy-done.1
  43.7 0.0 copy-done.2
  43.7 0.0 copy-done.3
  43.7 0.8 %add_divide_fusion = f32[1,64,512]{2,1,0:T(8,128)} fusion(f32[1,64,512]{2,1,0:T(8,128)S(1)} %collective-permute-done.16, f32[1,64,512]{2,1,0:T(8,128)S(1)} %collective-permute-done.14, f32[1,64,512]{2,1,0:T(8,128)S(1)} %collective-permute-done.13, f32[1,64,512]{2,1,0:T(8,128)S(1)} %collective-permute-done.11, f32[1,64,512]{2,1,0:T(8,128)S(1)} %copy-done.1, ...), kind=kLoop, calls=%fused_computation | loop fusion | flops 229376 | bytes 919808 | tf_op jit(solution)/shard_map/div | solution.py:425
  (9 shorter events, 0.1 us)
Async XLA Ops:
  0.0 18.4 %collective-permute-start.3 = (f32[512,512]{1,0:T(8,128)}, f32[512,512]{1,0:T(8,128)S(1)}, u32[]{:S(2)}, u32[]{:S(2)}) collective-permute-start(f32[512,512]{1,0:T(8,128)} %bitcast.4), channel_id=1, source_target_pairs={{0,8},{8,0},{16,24},{24,16},{1,9},{9,1},{17,25},{25,17},{2,10},{10... | collective-permute-start | bytes 3145736 | tf_op jit(solution)/shard_map/ppermute | solution.py:40
  1.6 11.0 %collective-permute-start.4 = (f32[144,512]{1,0:T(8,128)S(1)}, f32[144,512]{1,0:T(8,128)S(1)}, u32[]{:S(2)}, u32[]{:S(2)}) collective-permute-start(f32[144,512]{1,0:T(8,128)S(1)} %get-tuple-element.35), channel_id=1, source_target_pairs={{0,16},{8,24},{16,0},{24,8},{1,17},{9,25},{17,1},{25,9},{2,18},{10... | collective-permute-start | bytes 884744 | tf_op jit(solution)/shard_map/ppermute | solution.py:40
  4.1 17.5 %collective-permute-start.5 = (f32[224,512]{1,0:T(8,128)S(1)}, f32[224,512]{1,0:T(8,128)S(1)}, u32[]{:S(2)}, u32[]{:S(2)}) collective-permute-start(f32[224,512]{1,0:T(8,128)S(1)} %get-tuple-element.48), channel_id=1, source_target_pairs={{0,16},{8,24},{16,0},{24,8},{1,17},{9,25},{17,1},{25,9},{2,18},{10... | collective-permute-start | bytes 1376264 | tf_op jit(solution)/shard_map/ppermute | solution.py:40
  5.7 4.2 %collective-permute-start = (s32[3,1,96]{2,1,0:T(1,128)S(1)}, s32[3,1,96]{2,1,0:T(1,128)S(1)}, u32[]{:S(2)}, u32[]{:S(2)}) collective-permute-start(s32[3,1,96]{2,1,0:T(1,128)S(1)} %get-tuple-element.37), channel_id=1, source_target_pairs={{0,1},{1,0},{2,3},{3,2},{4,5},{5,4},{6,7},{7,6},{8,9},{9,8},{10,11... | collective-permute-start | bytes 3464 | tf_op jit(solution)/shard_map/ppermute | solution.py:40
  10.0 4.6 %collective-permute-start.1 = (s32[3,2,96]{2,1,0:T(2,128)S(1)}, s32[3,2,96]{2,1,0:T(2,128)S(1)}, u32[]{:S(2)}, u32[]{:S(2)}) collective-permute-start(s32[3,2,96]{2,1,0:T(2,128)S(1)} %pad_add_fusion.2), channel_id=1, source_target_pairs={{0,4},{1,5},{2,6},{3,7},{4,0},{5,1},{6,2},{7,3},{8,12},{9,13},{10,... | collective-permute-start | bytes 6920 | tf_op jit(solution)/shard_map/ppermute | solution.py:40
  12.6 9.6 %collective-permute-start.6 = (f32[144,512]{1,0:T(8,128)S(1)}, f32[144,512]{1,0:T(8,128)S(1)}, u32[]{:S(2)}, u32[]{:S(2)}) collective-permute-start(f32[144,512]{1,0:T(8,128)S(1)} %collective-permute-done.4.refs_7_), channel_id=1, source_target_pairs={{0,1},{1,0},{2,3},{3,2},{4,5},{5,4},{6,7},{7,6},{8,9},{9,8},{10,11... | collective-permute-start | bytes 884744 | tf_op jit(solution)/shard_map/ppermute | solution.py:40
  14.5 3.8 %copy-start = (f32[1,512,512]{2,1,0:T(8,128)S(1)}, f32[1,512,512]{2,1,0:T(8,128)}, u32[]{:S(2)}) copy-start(f32[1,512,512]{2,1,0:T(8,128)} %param.13) | copy-start | bytes 3145732
  14.5 3.8 %collective-permute-start.2 = (s32[3,4,96]{2,1,0:T(4,128)S(1)}, s32[3,4,96]{2,1,0:T(4,128)S(1)}, u32[]{:S(2)}, u32[]{:S(2)}) collective-permute-start(s32[3,4,96]{2,1,0:T(4,128)S(1)} %pad_add_fusion.1), channel_id=1, source_target_pairs={{0,2},{1,3},{2,0},{3,1},{4,6},{5,7},{6,4},{7,5},{8,10},{9,11},{10,... | collective-permute-start | bytes 13832 | tf_op jit(solution)/shard_map/ppermute | solution.py:40
  21.7 2.7 %collective-permute-start.8 = (f32[224,512]{1,0:T(8,128)S(1)}, f32[224,512]{1,0:T(8,128)S(1)}, u32[]{:S(2)}, u32[]{:S(2)}) collective-permute-start(f32[224,512]{1,0:T(8,128)S(1)} %collective-permute-done.5.refs_8_), channel_id=1, source_target_pairs={{0,8},{8,0},{16,24},{24,16},{1,9},{9,1},{17,25},{25,17},{2,10},{10... | collective-permute-start | bytes 1376264 | tf_op jit(solution)/shard_map/ppermute | solution.py:40
  21.7 2.3 %collective-permute-start.7 = (f32[144,512]{1,0:T(8,128)S(1)}, f32[144,512]{1,0:T(8,128)S(1)}, u32[]{:S(2)}, u32[]{:S(2)}) collective-permute-start(f32[144,512]{1,0:T(8,128)S(1)} %collective-permute-done.4.refs_7_), channel_id=1, source_target_pairs={{0,8},{8,0},{16,24},{24,16},{1,9},{9,1},{17,25},{25,17},{2,10},{10... | collective-permute-start | bytes 884744 | tf_op jit(solution)/shard_map/ppermute | solution.py:40
  22.2 2.1 %collective-permute-start.9 = (f32[144,512]{1,0:T(8,128)S(1)}, f32[144,512]{1,0:T(8,128)S(1)}, u32[]{:S(2)}, u32[]{:S(2)}) collective-permute-start(f32[144,512]{1,0:T(8,128)S(1)} %collective-permute-done.6.refs_9_), channel_id=1, source_target_pairs={{0,8},{8,0},{16,24},{24,16},{1,9},{9,1},{17,25},{25,17},{2,10},{10... | collective-permute-start | bytes 884744 | tf_op jit(solution)/shard_map/ppermute | solution.py:40
  25.0 6.3 %collective-permute-start.10 = (f32[1,64,512]{2,1,0:T(8,128)S(1)}, f32[1,64,512]{2,1,0:T(8,128)S(1)}, u32[]{:S(2)}, u32[]{:S(2)}) collective-permute-start(f32[1,64,512]{2,1,0:T(8,128)S(1)} %get-tuple-element.58), channel_id=1, source_target_pairs={{0,1},{1,0},{2,3},{3,2},{4,5},{5,4},{6,7},{7,6},{8,9},{9,8},{10,11... | collective-permute-start | bytes 393224 | tf_op jit(solution)/shard_map/ppermute | solution.py:40
  26.9 16.8 %copy-start.1 = (f32[1,64,512]{2,1,0:T(8,128)S(1)}, f32[1,64,512]{2,1,0:T(8,128)}, u32[]{:S(2)}) copy-start(f32[1,64,512]{2,1,0:T(8,128)} %param.14) | copy-start | bytes 393220
  26.9 16.8 %copy-start.2 = (f32[512]{0:T(512)S(1)}, f32[512]{0:T(512)}, u32[]{:S(2)}) copy-start(f32[512]{0:T(512)} %param.16) | copy-start | bytes 6148
  26.9 16.8 %copy-start.3 = (f32[1,64]{1,0:T(1,128)S(1)}, f32[1,64]{1,0:T(1,128)}, u32[]{:S(2)}) copy-start(f32[1,64]{1,0:T(1,128)} %param.15) | copy-start | bytes 772
  27.5 6.9 %collective-permute-start.12 = (f32[1,64,512]{2,1,0:T(8,128)S(1)}, f32[1,64,512]{2,1,0:T(8,128)S(1)}, u32[]{:S(2)}, u32[]{:S(2)}) collective-permute-start(f32[1,64,512]{2,1,0:T(8,128)S(1)} %get-tuple-element.61), channel_id=1, source_target_pairs={{0,1},{1,0},{2,3},{3,2},{4,5},{5,4},{6,7},{7,6},{8,9},{9,8},{10,11... | collective-permute-start | bytes 393224 | tf_op jit(solution)/shard_map/ppermute | solution.py:40
  27.8 9.7 %collective-permute-start.15 = (f32[1,64,512]{2,1,0:T(8,128)S(1)}, f32[1,64,512]{2,1,0:T(8,128)S(1)}, u32[]{:S(2)}, u32[]{:S(2)}) collective-permute-start(f32[1,64,512]{2,1,0:T(8,128)S(1)} %get-tuple-element.64), channel_id=1, source_target_pairs={{0,2},{1,3},{2,0},{3,1},{4,6},{5,7},{6,4},{7,5},{8,10},{9,11},{10,... | collective-permute-start | bytes 393224 | tf_op jit(solution)/shard_map/ppermute | solution.py:40
  29.6 9.4 %collective-permute-start.14 = (f32[1,64,512]{2,1,0:T(8,128)S(1)}, f32[1,64,512]{2,1,0:T(8,128)S(1)}, u32[]{:S(2)}, u32[]{:S(2)}) collective-permute-start(f32[1,64,512]{2,1,0:T(8,128)S(1)} %get-tuple-element.62), channel_id=1, source_target_pairs={{0,2},{1,3},{2,0},{3,1},{4,6},{5,7},{6,4},{7,5},{8,10},{9,11},{10,... | collective-permute-start | bytes 393224 | tf_op jit(solution)/shard_map/ppermute | solution.py:40
  31.4 7.9 %collective-permute-start.11 = (f32[1,64,512]{2,1,0:T(8,128)S(1)}, f32[1,64,512]{2,1,0:T(8,128)S(1)}, u32[]{:S(2)}, u32[]{:S(2)}) collective-permute-start(f32[1,64,512]{2,1,0:T(8,128)S(1)} %add.46), channel_id=1, source_target_pairs={{0,4},{1,5},{2,6},{3,7},{4,0},{5,1},{6,2},{7,3},{8,12},{9,13},{10,... | collective-permute-start | bytes 393224 | tf_op jit(solution)/shard_map/ppermute | solution.py:40
  34.4 9.3 %collective-permute-start.13 = (f32[1,64,512]{2,1,0:T(8,128)S(1)}, f32[1,64,512]{2,1,0:T(8,128)S(1)}, u32[]{:S(2)}, u32[]{:S(2)}) collective-permute-start(f32[1,64,512]{2,1,0:T(8,128)S(1)} %add.48), channel_id=1, source_target_pairs={{0,6},{1,7},{2,4},{3,5},{4,2},{5,3},{6,0},{7,1},{8,14},{9,15},{10,... | collective-permute-start | bytes 393224 | tf_op jit(solution)/shard_map/ppermute | solution.py:40
  37.5 6.2 %collective-permute-start.16 = (f32[1,64,512]{2,1,0:T(8,128)S(1)}, f32[1,64,512]{2,1,0:T(8,128)S(1)}, u32[]{:S(2)}, u32[]{:S(2)}) collective-permute-start(f32[1,64,512]{2,1,0:T(8,128)S(1)} %add.51), channel_id=1, source_target_pairs={{0,1},{1,0},{2,3},{3,2},{4,5},{5,4},{6,7},{7,6},{8,9},{9,8},{10,11... | collective-permute-start | bytes 393224 | tf_op jit(solution)/shard_map/ppermute | solution.py:40

commit v10 on v9

--- a/solution.py
+++ b/solution.py
@@ -61,29 +61,25 @@
     return pl.multiple_of(low * last, 16), pl.multiple_of(last - low * last, 16)
 
 
-def pieces_kernel(own_hbm, one_ref, two_ref, sems):
-    end, middle = one_ref.shape[0], two_ref.shape[0]
-    mine, _ = end_offsets(own_hbm.shape[0])
-    copies = [
-        pltpu.make_async_copy(own_hbm.at[pl.ds(mine, end), :], one_ref, sems.at[0]),
-        pltpu.make_async_copy(own_hbm.at[pl.ds(end, middle), :], two_ref, sems.at[1]),
-    ]
-    for copy in copies:
-        copy.start()
-    for copy in copies:
-        copy.wait()
-
-
-def pieces(own):
-    return pl.pallas_call(
-        pieces_kernel,
-        out_shape=[pltpu.VMEM((n, own.shape[1]), own.dtype) for n in row_cuts(own.shape[0])],
+def piece_kernel(ends, own_hbm, out_ref, sem):
+    rows = out_ref.shape[0]
+    start = end_offsets(own_hbm.shape[0])[0] if ends else (own_hbm.shape[0] - rows) // 2
+    copy = pltpu.make_async_copy(own_hbm.at[pl.ds(start, rows), :], out_ref, sem)
+    copy.start()
+    copy.wait()
+
+
+def piece(own, ends):
+    rows = row_cuts(own.shape[0])[0 if ends else 1]
+    return pl.pallas_call(
+        functools.partial(piece_kernel, ends),
+        out_shape=pltpu.VMEM((rows, own.shape[1]), own.dtype),
         in_specs=[HBM],
-        out_specs=[VMEM] * 2,
-        scratch_shapes=[pltpu.SemaphoreType.DMA((2,))],
+        out_specs=VMEM,
+        scratch_shapes=[pltpu.SemaphoreType.DMA],
         compiler_params=limit(0),
         cost_estimate=cost(0, own.size * 4),
-        name="pieces",
+        name="piece",
     )(in_hbm(own))
 
 
@@ -385,7 +381,7 @@
     amp_dev, tile_rows, _ = amplitudes.shape
     half = lanes // 2
     own = integrals[0]
-    one, two = pieces(own)
+    one, two = piece(own, True), piece(own, False)
     fetched = {k: [swap(x, "grp", k) for x in (one, two)] for k in range(2, grps, 2)}
     lists, table = pack_lists(
         task_amp, task_int, after(task_res, one), task_count, amp_label, res_owner, int_label

time: 45 us -> 45.2 us (level)
  Pallas kernels: 11.7 us -> 12.5 us
  waiting for transfers between devices: 7.93 us -> 7.43 us
    pallas_call x1 -> x2, Pallas kernels: 1.12 us -> 1.99 us  [piece(): pl.pallas_call(functools.partial(piece_kernel, ends), out_shape=pltpu.VME...]
    ppermute x17, waiting for transfers between devices: 7.93 us -> 7.43 us  [swap(): return lax.ppermute(x, axis, [(i, i ^ k) for i in range(n)])]
  transfers between devices with their start and end apart: 17 -> 17, of which waited for: 6 -> 4; matrix products, arithmetic and copies ran while one was open for 0% -> 0% of each run, Pallas kernels for 25% -> 26%
where the time goes in v10:
time: 45.2 us; the launch traced here: 44.8 us
  starting transfers between devices  23.1 us (51%)
  Pallas kernels  12.5 us (28%)
  waiting for transfers between devices  7.43 us (16%)
  other arithmetic  0.84 us (2%)
  between operations  0.84 us (2%)
    ppermute x17, starting transfers between devices, swap(): return lax.ppermute(x, axis, [(i, i ^ k) for i in range(n)])  23.1 us
    ppermute x17, waiting for transfers between devices, swap(): return lax.ppermute(x, axis, [(i, i ^ k) for i in range(n)])  7.43 us
    pallas_call x2, Pallas kernels, load(): pl.pallas_call(functools.partial(load_kernel, first), out_shape=pltpu.VME...  4.26 us
    pallas_call x1, Pallas kernels, sums(): pl.pallas_call(functools.partial(sums_kernel, lanes, blocks, amp_dev), ou...  2.28 us
    pallas_call x2, Pallas kernels, piece(): pl.pallas_call(functools.partial(piece_kernel, ends), out_shape=pltpu.VME...  1.99 us
    pallas_call x1, Pallas kernels, fetched_products(): pl.pallas_call(fetched_kernel, out_shape=[pltpu.VMEM((rows, window), jnp....  1.79 us
  transfers between devices with their start and end apart: 17, of which 4 were waited for; matrix products, arithmetic and copies ran while one was open for 0% of the time, Pallas kernels for 26%

profile of v10, /device:TPU:0, one launch (start us, length us, event | category | flops | bytes accessed | tf_op | source)
XLA Modules:
  0.0 44.8 jit_solution(8682261481312942576)
XLA Ops:
  0.0 0.5 %collective-permute-start.3 = (f32[512,512]{1,0:T(8,128)}, f32[512,512]{1,0:T(8,128)S(1)}, u32[]{:S(2)}, u32[]{:S(2)}) collective-permute-start(f32[512,512]{1,0:T(8,128)} %bitcast.4), channel_id=1, source_target_pairs={{0,8},{8,0},{16,24},{24,16},{1,9},{9,1},{17,25},{25,17},{2,10},{10... | collective-permute-start | bytes 3145736 | tf_op jit(solution)/shard_map/ppermute | solution.py:40
  0.5 1.0 %piece.2 = f32[144,512]{1,0:T(8,128)S(1)} custom-call(f32[512,512]{1,0:T(8,128)} %bitcast.5), custom_call_target="tpu_custom_call" | custom-call | bytes 1048576 | tf_op jit(solution)/shard_map/piece/pallas_call | solution.py:74
  1.4 2.6 %collective-permute-start.4 = (f32[144,512]{1,0:T(8,128)S(1)}, f32[144,512]{1,0:T(8,128)S(1)}, u32[]{:S(2)}, u32[]{:S(2)}) collective-permute-start(f32[144,512]{1,0:T(8,128)S(1)} %piece.2), channel_id=1, source_target_pairs={{0,16},{8,24},{16,0},{24,8},{1,17},{9,25},{17,1},{25,9},{2,18},{10... | collective-permute-start | bytes 884744 | tf_op jit(solution)/shard_map/ppermute | solution.py:40
  4.0 1.0 %piece.3 = f32[224,512]{1,0:T(8,128)S(1)} custom-call(f32[512,512]{1,0:T(8,128)} %bitcast.6), custom_call_target="tpu_custom_call" | custom-call | bytes 1048576 | tf_op jit(solution)/shard_map/piece/pallas_call | solution.py:74
  5.0 0.1 collective-permute-start.5
  5.8 0.9 %pack_lists.1 = (s32[3,1,96]{2,1,0:T(1,128)S(1)}, s32[3,256]{1,0:T(4,128)S(1)}) custom-call(s32[1]{0:T(128)S(6)} %copy.13.count_ref, s32[1,96]{1,0:T(1,128)} %refs_0_.1, s32[1,96]{1,0:T(1,128)} %refs_1_.1, s32[1,96]{1,0:T(1,128)} %refs_2_, s32[1,32]{1,0:T(1,128)} %bitcast.9, s32[1,8]{1,0:T(1,128)} %refs_4_.1, s32[1,4]{1,0:T(1,128)} %bitcast.10), custom_call_target="tpu_custom_call" | custom-call | bytes 4096 | tf_op jit(solution)/shard_map/pack_lists/pallas_call | solution.py:109
  6.6 2.1 %collective-permute-start = (s32[3,1,96]{2,1,0:T(1,128)S(1)}, s32[3,1,96]{2,1,0:T(1,128)S(1)}, u32[]{:S(2)}, u32[]{:S(2)}) collective-permute-start(s32[3,1,96]{2,1,0:T(1,128)S(1)} %get-tuple-element.34), channel_id=1, source_target_pairs={{0,1},{1,0},{2,3},{3,2},{4,5},{5,4},{6,7},{7,6},{8,9},{9,8},{10,11... | collective-permute-start | bytes 3464 | tf_op jit(solution)/shard_map/ppermute | solution.py:40
  8.7 2.1 %load_amplitudes.2.refs_0_ = bf16[2048,512]{1,0:T(8,128)(2,1)S(1)} custom-call(f32[32,64,512]{2,1,0:T(8,128)} %amp_hbm.3), custom_call_target="tpu_custom_call" | custom-call | bytes 4194304 | tf_op jit(solution)/shard_map/load_amplitudes/pallas_call | solution.py:144
  10.9 0.0 collective-permute-done
  10.9 2.7 %collective-permute-start.1 = (s32[3,2,96]{2,1,0:T(2,128)S(1)}, s32[3,2,96]{2,1,0:T(2,128)S(1)}, u32[]{:S(2)}, u32[]{:S(2)}) collective-permute-start(s32[3,2,96]{2,1,0:T(2,128)S(1)} %pad_add_fusion.2), channel_id=1, source_target_pairs={{0,4},{1,5},{2,6},{3,7},{4,0},{5,1},{6,2},{7,3},{8,12},{9,13},{10,... | collective-permute-start | bytes 6920 | tf_op jit(solution)/shard_map/ppermute | solution.py:40
  13.6 0.0 collective-permute-done.4.refs_7_
  13.6 1.4 %collective-permute-start.6 = (f32[144,512]{1,0:T(8,128)S(1)}, f32[144,512]{1,0:T(8,128)S(1)}, u32[]{:S(2)}, u32[]{:S(2)}) collective-permute-start(f32[144,512]{1,0:T(8,128)S(1)} %collective-permute-done.4.refs_7_), channel_id=1, source_target_pairs={{0,1},{1,0},{2,3},{3,2},{4,5},{5,4},{6,7},{7,6},{8,9},{9,8},{10,11... | collective-permute-start | bytes 884744 | tf_op jit(solution)/shard_map/ppermute | solution.py:40
  15.0 0.5 %collective-permute-done.1 = s32[3,2,96]{2,1,0:T(2,128)S(1)} collective-permute-done((s32[3,2,96]{2,1,0:T(2,128)S(1)}, s32[3,2,96]{2,1,0:T(2,128)S(1)}, u32[]{:S(2)}, u32[]{:S(2)}) %collective-permute-start.1) | collective-permute-done | bytes 2336 | tf_op jit(solution)/shard_map/ppermute | solution.py:40
  15.5 0.0 copy-start
  15.5 1.6 %collective-permute-start.2 = (s32[3,4,96]{2,1,0:T(4,128)S(1)}, s32[3,4,96]{2,1,0:T(4,128)S(1)}, u32[]{:S(2)}, u32[]{:S(2)}) collective-permute-start(s32[3,4,96]{2,1,0:T(4,128)S(1)} %pad_add_fusion.1), channel_id=1, source_target_pairs={{0,2},{1,3},{2,0},{3,1},{4,6},{5,7},{6,4},{7,5},{8,10},{9,11},{10,... | collective-permute-start | bytes 13832 | tf_op jit(solution)/shard_map/ppermute | solution.py:40
  17.1 2.1 %load_amplitudes.3.refs_1_ = bf16[2048,512]{1,0:T(8,128)(2,1)S(1)} custom-call(f32[32,64,512]{2,1,0:T(8,128)} %amp_hbm.3), custom_call_target="tpu_custom_call" | custom-call | bytes 4194304 | tf_op jit(solution)/shard_map/load_amplitudes/pallas_call | solution.py:144
  19.3 0.0 collective-permute-done.2
  19.3 0.0 collective-permute-done.3.pair_ref
  19.3 0.0 copy-done
  19.3 2.3 %sums.1 = (bf16[256,2048]{1,0:T(8,128)(2,1)S(1)}, bf16[256,2048]{1,0:T(8,128)(2,1)S(1)}, bf16[256,2048]{1,0:T(8,128)(2,1)S(1)}, bf16[256,2048]{1,0:T(8,128)(2,1)...) custom-call(s32[3,8,96]{2,1,0:T(8,128)S(1)} %pad_add_fusion.lists_ref, ...), custom_call_target="tpu_custom_call" | custom-call | bytes 16777216 | tf_op jit(solution)/shard_map/sums/pallas_call | solution.py:258
  21.6 0.0 collective-permute-done.5.refs_8_
  21.6 0.1 collective-permute-start.8
  21.7 0.5 %collective-permute-start.7 = (f32[144,512]{1,0:T(8,128)S(1)}, f32[144,512]{1,0:T(8,128)S(1)}, u32[]{:S(2)}, u32[]{:S(2)}) collective-permute-start(f32[144,512]{1,0:T(8,128)S(1)} %collective-permute-done.4.refs_7_), channel_id=1, source_target_pairs={{0,8},{8,0},{16,24},{24,16},{1,9},{9,1},{17,25},{25,17},{2,10},{10... | collective-permute-start | bytes 884744 | tf_op jit(solution)/shard_map/ppermute | solution.py:40
  22.2 0.0 collective-permute-done.6.refs_9_
  22.2 0.1 collective-permute-start.9
  22.3 1.8 %fetched_products.1 = (f32[256,512]{1,0:T(8,128)S(1)}, f32[256,512]{1,0:T(8,128)S(1)}) custom-call(bf16[256,2048]{1,0:T(8,128)(2,1)S(1)} %get-tuple-element.40.refs_0_.hi, bf16[256,2048]{1,0:T(8,128)(2,1)S(1)} %get-tuple-element.41.refs_1_.lo, bf16[256,2048]{1,0:T(8,128)(2,1)S(1)} %get-tuple-element.38.refs_2_.hi, ...), custom_call_target="tpu_custom_call" | custom-call | flops 805306368 | tf_op jit(solution)/shard_map/fetched_products/pallas_call | solution.py:306
  24.1 0.0 collective-permute-done.7.rest_0_
  24.1 0.3 collective-permute-done.9.rest_2_
  24.3 0.0 collective-permute-done.8.rest_1_
  24.3 0.7 %away_products.1 = (f32[1,64,512]{2,1,0:T(8,128)S(1)}, f32[1,64,512]{2,1,0:T(8,128)S(1)}, f32[1,64,512]{2,1,0:T(8,128)S(1)}, f32[1,64,512]{2,1,0:T(8,128)S(1)}, ...) custom-call(bf16[256,2048]{1,0:T(8,128)(2,1)S(1)} %get-tuple-element.40.refs_0_.hi, ...), custom_call_target="tpu_custom_call" | custom-call | flops 402653184 | tf_op jit(solution)/shard_map/away_products/pallas_call | solution.py:337
  25.1 1.7 %collective-permute-start.10 = (f32[1,64,512]{2,1,0:T(8,128)S(1)}, f32[1,64,512]{2,1,0:T(8,128)S(1)}, u32[]{:S(2)}, u32[]{:S(2)}) collective-permute-start(f32[1,64,512]{2,1,0:T(8,128)S(1)} %get-tuple-element.54), channel_id=1, source_target_pairs={{0,1},{1,0},{2,3},{3,2},{4,5},{5,4},{6,7},{7,6},{8,9},{9,8},{10,11... | collective-permute-start | bytes 393224 | tf_op jit(solution)/shard_map/ppermute | solution.py:40
  26.7 0.6 %side_products.1 = (f32[1,64,512]{2,1,0:T(8,128)S(1)}, f32[1,64,512]{2,1,0:T(8,128)S(1)}, f32[1,64,512]{2,1,0:T(8,128)S(1)}, f32[1,64,512]{2,1,0:T(8,128)S(1)}) custom-call(bf16[256,2048]{1,0:T(8,128)(2,1)S(1)} %get-tuple-element.38.refs_2_.hi, bf16[256,2048]{1,0:T(8,128)(2,1)S(1)} %get-tuple-element.39.refs_3_.lo, ...), custom_call_target="tpu_custom_call" | custom-call | tf_op jit(solution)/shard_map/side_products/pallas_call | solution.py:353
  27.3 0.5 %collective-permute-start.12 = (f32[1,64,512]{2,1,0:T(8,128)S(1)}, f32[1,64,512]{2,1,0:T(8,128)S(1)}, u32[]{:S(2)}, u32[]{:S(2)}) collective-permute-start(f32[1,64,512]{2,1,0:T(8,128)S(1)} %get-tuple-element.57), channel_id=1, source_target_pairs={{0,1},{1,0},{2,3},{3,2},{4,5},{5,4},{6,7},{7,6},{8,9},{9,8},{10,11... | collective-permute-start | bytes 393224 | tf_op jit(solution)/shard_map/ppermute | solution.py:40
  27.8 1.6 %collective-permute-start.15 = (f32[1,64,512]{2,1,0:T(8,128)S(1)}, f32[1,64,512]{2,1,0:T(8,128)S(1)}, u32[]{:S(2)}, u32[]{:S(2)}) collective-permute-start(f32[1,64,512]{2,1,0:T(8,128)S(1)} %get-tuple-element.60), channel_id=1, source_target_pairs={{0,2},{1,3},{2,0},{3,1},{4,6},{5,7},{6,4},{7,5},{8,10},{9,11},{10,... | collective-permute-start | bytes 393224 | tf_op jit(solution)/shard_map/ppermute | solution.py:40
  29.5 0.4 collective-permute-start.14
  29.9 1.6 %collective-permute-done.10 = f32[1,64,512]{2,1,0:T(8,128)S(1)} collective-permute-done((f32[1,64,512]{2,1,0:T(8,128)S(1)}, f32[1,64,512]{2,1,0:T(8,128)S(1)}, u32[]{:S(2)}, u32[]{:S(2)}) %collective-permute-start.10) | collective-permute-done | bytes 131104 | tf_op jit(solution)/shard_map/ppermute | solution.py:40
  31.5 2.7 %collective-permute-start.11 = (f32[1,64,512]{2,1,0:T(8,128)S(1)}, f32[1,64,512]{2,1,0:T(8,128)S(1)}, u32[]{:S(2)}, u32[]{:S(2)}) collective-permute-start(f32[1,64,512]{2,1,0:T(8,128)S(1)} %add.46), channel_id=1, source_target_pairs={{0,4},{1,5},{2,6},{3,7},{4,0},{5,1},{6,2},{7,3},{8,12},{9,13},{10,... | collective-permute-start | bytes 393224 | tf_op jit(solution)/shard_map/ppermute | solution.py:40
  34.2 0.0 collective-permute-done.12
  34.2 3.1 %collective-permute-start.13 = (f32[1,64,512]{2,1,0:T(8,128)S(1)}, f32[1,64,512]{2,1,0:T(8,128)S(1)}, u32[]{:S(2)}, u32[]{:S(2)}) collective-permute-start(f32[1,64,512]{2,1,0:T(8,128)S(1)} %add.48), channel_id=1, source_target_pairs={{0,6},{1,7},{2,4},{3,5},{4,2},{5,3},{6,0},{7,1},{8,14},{9,15},{10,... | collective-permute-start | bytes 393224 | tf_op jit(solution)/shard_map/ppermute | solution.py:40
  37.3 0.0 collective-permute-done.15
  37.3 1.6 %collective-permute-start.16 = (f32[1,64,512]{2,1,0:T(8,128)S(1)}, f32[1,64,512]{2,1,0:T(8,128)S(1)}, u32[]{:S(2)}, u32[]{:S(2)}) collective-permute-start(f32[1,64,512]{2,1,0:T(8,128)S(1)} %add.51), channel_id=1, source_target_pairs={{0,1},{1,0},{2,3},{3,2},{4,5},{5,4},{6,7},{7,6},{8,9},{9,8},{10,11... | collective-permute-start | bytes 393224 | tf_op jit(solution)/shard_map/ppermute | solution.py:40
  38.9 0.0 collective-permute-done.14
  38.9 5.1 %collective-permute-done.11 = f32[1,64,512]{2,1,0:T(8,128)S(1)} collective-permute-done((f32[1,64,512]{2,1,0:T(8,128)S(1)}, f32[1,64,512]{2,1,0:T(8,128)S(1)}, u32[]{:S(2)}, u32[]{:S(2)}) %collective-permute-start.11) | collective-permute-done | bytes 131104 | tf_op jit(solution)/shard_map/ppermute | solution.py:40
  44.0 0.0 collective-permute-done.13
  44.0 0.0 collective-permute-done.16
  44.0 0.0 copy-done.1
  44.0 0.0 copy-done.2
  44.0 0.8 %add_divide_fusion = f32[1,64,512]{2,1,0:T(8,128)} fusion(f32[1,64,512]{2,1,0:T(8,128)S(1)} %collective-permute-done.16, f32[1,64,512]{2,1,0:T(8,128)S(1)} %collective-permute-done.14, f32[1,64,512]{2,1,0:T(8,128)S(1)} %collective-permute-done.13, f32[1,64,512]{2,1,0:T(8,128)S(1)} %collective-permute-done.11, f32[1,64,512]{2,1,0:T(8,128)S(1)} %copy-done.1, ...), kind=kLoop, calls=%fused_computation | loop fusion | flops 229376 | bytes 919808 | tf_op jit(solution)/shard_map/div | solution.py:421
  (10 shorter events, 0.1 us)
Async XLA Ops:
  0.0 19.3 %collective-permute-start.3 = (f32[512,512]{1,0:T(8,128)}, f32[512,512]{1,0:T(8,128)S(1)}, u32[]{:S(2)}, u32[]{:S(2)}) collective-permute-start(f32[512,512]{1,0:T(8,128)} %bitcast.4), channel_id=1, source_target_pairs={{0,8},{8,0},{16,24},{24,16},{1,9},{9,1},{17,25},{25,17},{2,10},{10... | collective-permute-start | bytes 3145736 | tf_op jit(solution)/shard_map/ppermute | solution.py:40
  1.4 12.1 %collective-permute-start.4 = (f32[144,512]{1,0:T(8,128)S(1)}, f32[144,512]{1,0:T(8,128)S(1)}, u32[]{:S(2)}, u32[]{:S(2)}) collective-permute-start(f32[144,512]{1,0:T(8,128)S(1)} %piece.2), channel_id=1, source_target_pairs={{0,16},{8,24},{16,0},{24,8},{1,17},{9,25},{17,1},{25,9},{2,18},{10... | collective-permute-start | bytes 884744 | tf_op jit(solution)/shard_map/ppermute | solution.py:40
  5.0 16.6 %collective-permute-start.5 = (f32[224,512]{1,0:T(8,128)S(1)}, f32[224,512]{1,0:T(8,128)S(1)}, u32[]{:S(2)}, u32[]{:S(2)}) collective-permute-start(f32[224,512]{1,0:T(8,128)S(1)} %piece.3), channel_id=1, source_target_pairs={{0,16},{8,24},{16,0},{24,8},{1,17},{9,25},{17,1},{25,9},{2,18},{10... | collective-permute-start | bytes 1376264 | tf_op jit(solution)/shard_map/ppermute | solution.py:40
  6.6 4.2 %collective-permute-start = (s32[3,1,96]{2,1,0:T(1,128)S(1)}, s32[3,1,96]{2,1,0:T(1,128)S(1)}, u32[]{:S(2)}, u32[]{:S(2)}) collective-permute-start(s32[3,1,96]{2,1,0:T(1,128)S(1)} %get-tuple-element.34), channel_id=1, source_target_pairs={{0,1},{1,0},{2,3},{3,2},{4,5},{5,4},{6,7},{7,6},{8,9},{9,8},{10,11... | collective-permute-start | bytes 3464 | tf_op jit(solution)/shard_map/ppermute | solution.py:40
  10.9 4.6 %collective-permute-start.1 = (s32[3,2,96]{2,1,0:T(2,128)S(1)}, s32[3,2,96]{2,1,0:T(2,128)S(1)}, u32[]{:S(2)}, u32[]{:S(2)}) collective-permute-start(s32[3,2,96]{2,1,0:T(2,128)S(1)} %pad_add_fusion.2), channel_id=1, source_target_pairs={{0,4},{1,5},{2,6},{3,7},{4,0},{5,1},{6,2},{7,3},{8,12},{9,13},{10,... | collective-permute-start | bytes 6920 | tf_op jit(solution)/shard_map/ppermute | solution.py:40
  13.6 8.6 %collective-permute-start.6 = (f32[144,512]{1,0:T(8,128)S(1)}, f32[144,512]{1,0:T(8,128)S(1)}, u32[]{:S(2)}, u32[]{:S(2)}) collective-permute-start(f32[144,512]{1,0:T(8,128)S(1)} %collective-permute-done.4.refs_7_), channel_id=1, source_target_pairs={{0,1},{1,0},{2,3},{3,2},{4,5},{5,4},{6,7},{7,6},{8,9},{9,8},{10,11... | collective-permute-start | bytes 884744 | tf_op jit(solution)/shard_map/ppermute | solution.py:40
  15.5 3.8 %copy-start = (f32[1,512,512]{2,1,0:T(8,128)S(1)}, f32[1,512,512]{2,1,0:T(8,128)}, u32[]{:S(2)}) copy-start(f32[1,512,512]{2,1,0:T(8,128)} %param.13) | copy-start | bytes 3145732
  15.5 3.8 %collective-permute-start.2 = (s32[3,4,96]{2,1,0:T(4,128)S(1)}, s32[3,4,96]{2,1,0:T(4,128)S(1)}, u32[]{:S(2)}, u32[]{:S(2)}) collective-permute-start(s32[3,4,96]{2,1,0:T(4,128)S(1)} %pad_add_fusion.1), channel_id=1, source_target_pairs={{0,2},{1,3},{2,0},{3,1},{4,6},{5,7},{6,4},{7,5},{8,10},{9,11},{10,... | collective-permute-start | bytes 13832 | tf_op jit(solution)/shard_map/ppermute | solution.py:40
  21.6 2.7 %collective-permute-start.8 = (f32[224,512]{1,0:T(8,128)S(1)}, f32[224,512]{1,0:T(8,128)S(1)}, u32[]{:S(2)}, u32[]{:S(2)}) collective-permute-start(f32[224,512]{1,0:T(8,128)S(1)} %collective-permute-done.5.refs_8_), channel_id=1, source_target_pairs={{0,8},{8,0},{16,24},{24,16},{1,9},{9,1},{17,25},{25,17},{2,10},{10... | collective-permute-start | bytes 1376264 | tf_op jit(solution)/shard_map/ppermute | solution.py:40
  21.7 2.4 %collective-permute-start.7 = (f32[144,512]{1,0:T(8,128)S(1)}, f32[144,512]{1,0:T(8,128)S(1)}, u32[]{:S(2)}, u32[]{:S(2)}) collective-permute-start(f32[144,512]{1,0:T(8,128)S(1)} %collective-permute-done.4.refs_7_), channel_id=1, source_target_pairs={{0,8},{8,0},{16,24},{24,16},{1,9},{9,1},{17,25},{25,17},{2,10},{10... | collective-permute-start | bytes 884744 | tf_op jit(solution)/shard_map/ppermute | solution.py:40
  22.2 2.1 %collective-permute-start.9 = (f32[144,512]{1,0:T(8,128)S(1)}, f32[144,512]{1,0:T(8,128)S(1)}, u32[]{:S(2)}, u32[]{:S(2)}) collective-permute-start(f32[144,512]{1,0:T(8,128)S(1)} %collective-permute-done.6.refs_9_), channel_id=1, source_target_pairs={{0,8},{8,0},{16,24},{24,16},{1,9},{9,1},{17,25},{25,17},{2,10},{10... | collective-permute-start | bytes 884744 | tf_op jit(solution)/shard_map/ppermute | solution.py:40
  25.1 6.4 %collective-permute-start.10 = (f32[1,64,512]{2,1,0:T(8,128)S(1)}, f32[1,64,512]{2,1,0:T(8,128)S(1)}, u32[]{:S(2)}, u32[]{:S(2)}) collective-permute-start(f32[1,64,512]{2,1,0:T(8,128)S(1)} %get-tuple-element.54), channel_id=1, source_target_pairs={{0,1},{1,0},{2,3},{3,2},{4,5},{5,4},{6,7},{7,6},{8,9},{9,8},{10,11... | collective-permute-start | bytes 393224 | tf_op jit(solution)/shard_map/ppermute | solution.py:40
  26.7 17.3 %copy-start.1 = (f32[1,64,512]{2,1,0:T(8,128)S(1)}, f32[1,64,512]{2,1,0:T(8,128)}, u32[]{:S(2)}) copy-start(f32[1,64,512]{2,1,0:T(8,128)} %param.14) | copy-start | bytes 393220
  26.7 17.3 %copy-start.2 = (f32[512]{0:T(512)S(1)}, f32[512]{0:T(512)}, u32[]{:S(2)}) copy-start(f32[512]{0:T(512)} %param.16) | copy-start | bytes 6148
  26.7 17.3 %copy-start.3 = (f32[1,64]{1,0:T(1,128)S(1)}, f32[1,64]{1,0:T(1,128)}, u32[]{:S(2)}) copy-start(f32[1,64]{1,0:T(1,128)} %param.15) | copy-start | bytes 772
  27.3 6.9 %collective-permute-start.12 = (f32[1,64,512]{2,1,0:T(8,128)S(1)}, f32[1,64,512]{2,1,0:T(8,128)S(1)}, u32[]{:S(2)}, u32[]{:S(2)}) collective-permute-start(f32[1,64,512]{2,1,0:T(8,128)S(1)} %get-tuple-element.57), channel_id=1, source_target_pairs={{0,1},{1,0},{2,3},{3,2},{4,5},{5,4},{6,7},{7,6},{8,9},{9,8},{10,11... | collective-permute-start | bytes 393224 | tf_op jit(solution)/shard_map/ppermute | solution.py:40
  27.8 9.5 %collective-permute-start.15 = (f32[1,64,512]{2,1,0:T(8,128)S(1)}, f32[1,64,512]{2,1,0:T(8,128)S(1)}, u32[]{:S(2)}, u32[]{:S(2)}) collective-permute-start(f32[1,64,512]{2,1,0:T(8,128)S(1)} %get-tuple-element.60), channel_id=1, source_target_pairs={{0,2},{1,3},{2,0},{3,1},{4,6},{5,7},{6,4},{7,5},{8,10},{9,11},{10,... | collective-permute-start | bytes 393224 | tf_op jit(solution)/shard_map/ppermute | solution.py:40
  29.5 9.4 %collective-permute-start.14 = (f32[1,64,512]{2,1,0:T(8,128)S(1)}, f32[1,64,512]{2,1,0:T(8,128)S(1)}, u32[]{:S(2)}, u32[]{:S(2)}) collective-permute-start(f32[1,64,512]{2,1,0:T(8,128)S(1)} %get-tuple-element.58), channel_id=1, source_target_pairs={{0,2},{1,3},{2,0},{3,1},{4,6},{5,7},{6,4},{7,5},{8,10},{9,11},{10,... | collective-permute-start | bytes 393224 | tf_op jit(solution)/shard_map/ppermute | solution.py:40
  31.5 12.5 %collective-permute-start.11 = (f32[1,64,512]{2,1,0:T(8,128)S(1)}, f32[1,64,512]{2,1,0:T(8,128)S(1)}, u32[]{:S(2)}, u32[]{:S(2)}) collective-permute-start(f32[1,64,512]{2,1,0:T(8,128)S(1)} %add.46), channel_id=1, source_target_pairs={{0,4},{1,5},{2,6},{3,7},{4,0},{5,1},{6,2},{7,3},{8,12},{9,13},{10,... | collective-permute-start | bytes 393224 | tf_op jit(solution)/shard_map/ppermute | solution.py:40
  34.2 9.7 %collective-permute-start.13 = (f32[1,64,512]{2,1,0:T(8,128)S(1)}, f32[1,64,512]{2,1,0:T(8,128)S(1)}, u32[]{:S(2)}, u32[]{:S(2)}) collective-permute-start(f32[1,64,512]{2,1,0:T(8,128)S(1)} %add.48), channel_id=1, source_target_pairs={{0,6},{1,7},{2,4},{3,5},{4,2},{5,3},{6,0},{7,1},{8,14},{9,15},{10,... | collective-permute-start | bytes 393224 | tf_op jit(solution)/shard_map/ppermute | solution.py:40
  37.3 6.6 %collective-permute-start.16 = (f32[1,64,512]{2,1,0:T(8,128)S(1)}, f32[1,64,512]{2,1,0:T(8,128)S(1)}, u32[]{:S(2)}, u32[]{:S(2)}) collective-permute-start(f32[1,64,512]{2,1,0:T(8,128)S(1)} %add.51), channel_id=1, source_target_pairs={{0,1},{1,0},{2,3},{3,2},{4,5},{5,4},{6,7},{7,6},{8,9},{9,8},{10,11... | collective-permute-start | bytes 393224 | tf_op jit(solution)/shard_map/ppermute | solution.py:40
